TPU v7x, 32 devices: a whole 2x2x4 slice. The times are simulated.
32 devices in a mesh: row: 16 (over z, y, core), col: 2 (over x).
Axes of the slice: x: 2, y: 2, z: 4, core: 2. Of those that a mesh axis runs over, the one named last changes fastest.
Arguments:
- vectors: float32 [32, 65536], P(None, ('row', 'col')), may hold values from -6 to 6
- block_values: bfloat16 [8192, 128, 128], P(('row', 'col')), may hold values from -0.15625 to 0.15625
- block_rows: int32 [8192], P(('row', 'col')), may hold values from 0 to 31, as said below
- block_cols: int32 [8192], P(('row', 'col')), may hold values from 0 to 255, as said below
- block_counts: int32 [32], P(('row', 'col')), may hold values from 32 to 256, as said below
- center: float32 [1], replicated, may hold values from -0.5 to 0.5
- radius: float32 [1], replicated, may hold values from 1.5 to 3
Outputs:
- filtered: float32 [32, 65536], P(None, ('row', 'col'))
Inputs may be any that keep to these rules, and one draw needn't show every extreme that they name: `block_counts`: live slots of each device; some device fills all 256 slots. `block_rows`: Block-row inside the row group; slots may repeat a position. `block_cols`: Block-column inside the col group; slots may repeat a position.
All inputs are finite; a program needn't handle non-finite values.
Results may differ from a plain program's by a relative error of at most 0.02.
Values may be sent and summed in bfloat16 or wider, within the bound.
No kernel may reach another device: no remote copies, remote signals or barrier semaphores. Data moves between devices by JAX's collectives and lax.ppermute only.
A program may use at most 128 MiB of HBM per device.

v0:
```python
import functools

import jax
import jax.numpy as jnp
from jax import lax
from jax.experimental import pallas as pl
from jax.experimental.pallas import tpu as pltpu
from jax.sharding import PartitionSpec as P

CHUNK = 32
UNROLL = 32


def product_kernel(contract, inputs, outputs, count_ref, take_ref, put_ref, *refs):
    n_in = len(inputs)
    pieces = refs[:n_in]
    blocks = refs[n_in]
    outs = refs[n_in + 1 : n_in + 1 + len(outputs)]
    held, held_blocks, total, block_sems = refs[n_in + 1 + len(outputs) :]
    capacity, size_block = blocks.shape[0], blocks.shape[1]
    per_piece = held.shape[2] // size_block
    chunks = capacity // CHUNK
    count = count_ref[0]

    def block_copy(g):
        part = pl.ds(g * CHUNK, CHUNK)
        return pltpu.make_async_copy(blocks.at[part], held_blocks.at[part], block_sems.at[g])

    for g in range(chunks):
        @pl.when(g * CHUNK < count)
        def _(g=g):
            block_copy(g).start()

    total[...] = jnp.zeros_like(total)
    for part, held_pieces in zip(pieces, inputs):
        for n, p in enumerate(held_pieces):
            held[p] = part[n]

    def place(index):
        column = pl.multiple_of((index % per_piece) * size_block, size_block)
        return index // per_piece, slice(None), pl.ds(column, size_block)

    def group(first):
        products = []
        for n in range(0, UNROLL, 2):
            slot = first + n
            picked = jnp.concatenate([held[place(take_ref[slot])], held[place(take_ref[slot + 1])]], axis=0)
            if contract == 0:
                pair = jnp.concatenate([held_blocks[slot], held_blocks[slot + 1]], axis=1)
            else:
                pair = held_blocks[pl.ds(slot, 2)].reshape(2 * size_block, size_block)
            product = lax.dot_general(
                picked, pair, (((1,), (contract,)), ((), ())), preferred_element_type=jnp.float32
            )
            rows = product.shape[0] // 2
            products += [product[:rows, :size_block], product[rows:, size_block:]]
        for n, product in enumerate(products):
            total[place(put_ref[first + n])] += product

    @pl.loop(0, (count + CHUNK - 1) // CHUNK)
    def _(g):
        block_copy(g).wait()
        for n in range(0, CHUNK, UNROLL):
            group(g * CHUNK + n)

    for out, held_pieces in zip(outs, outputs):
        for n, p in enumerate(held_pieces):
            out[n] = total[p].astype(out.dtype)


def block_product(contract, inputs, outputs, dtypes, n_put, count, take, put, pieces, blocks):
    capacity, size_block = blocks.shape[0], blocks.shape[1]
    vector_count, own_rows = pieces[0].shape[-2:]
    pieces = [part.reshape(-1, vector_count, own_rows) for part in pieces]
    n_in = sum(part.shape[0] for part in pieces)
    smem = pl.BlockSpec(memory_space=pltpu.SMEM)
    vmem = pl.BlockSpec(memory_space=pltpu.VMEM)
    hbm = pl.BlockSpec(memory_space=pltpu.HBM)
    return pl.pallas_call(
        functools.partial(product_kernel, contract, inputs, outputs),
        out_shape=[
            jax.ShapeDtypeStruct((len(held), vector_count, own_rows), dtype) for held, dtype in zip(outputs, dtypes)
        ],
        in_specs=[smem] * 3 + [vmem] * len(pieces) + [hbm],
        out_specs=[pl.BlockSpec(memory_space=pltpu.VMEM)] * len(outputs),
        scratch_shapes=[
            pltpu.VMEM((n_in, vector_count, own_rows), jnp.bfloat16),
            pltpu.VMEM(blocks.shape, blocks.dtype),
            pltpu.VMEM((n_put + 1, vector_count, own_rows), jnp.float32),
            pltpu.SemaphoreType.DMA((capacity // CHUNK,)),
        ],
        compiler_params=pltpu.CompilerParams(vmem_limit_bytes=40 * 1024 * 1024),
        cost_estimate=pl.CostEstimate(
            flops=2 * capacity * size_block * size_block * 256,
            bytes_accessed=2 * blocks.size + 2 * n_in * vector_count * own_rows,
            transcendentals=0,
        ),
        name="mirror" if contract == 0 else "forward",
    )(count, take, put, *pieces, pltpu.with_memory_space_constraint(blocks, pltpu.HBM))


def shards(n_row, n_col, vectors, block_values, block_rows, block_cols, block_counts, center, radius):
    size_block = block_values.shape[1]
    own_rows = vectors.shape[1]
    per_piece = own_rows // size_block
    center_value = center[0]
    radius_value = radius[0]

    n_c = 2 if n_row % 2 == 0 else 1
    n_a = 4 if (n_row // n_c) % 4 == 0 else n_row // n_c
    n_b = n_row // n_c // n_a

    def at(a, b, c):
        return ((a % n_a) * n_b + b % n_b) * n_c + c % n_c

    spots = [(a, b, c) for a in range(n_a) for b in range(n_b) for c in range(n_c)]

    def shift(value, da=0, db=0, dc=0):
        pairs = [(at(a, b, c), at(a + da, b + db, c + dc)) for a, b, c in spots]
        return lax.ppermute(value, "row", pairs)

    def shift_col(value, d):
        return lax.ppermute(value, "col", [(j, (j + d) % n_col) for j in range(n_col)])

    row_index = lax.axis_index("row").astype(jnp.int32)
    col_index = lax.axis_index("col").astype(jnp.int32)
    my_c, my_b, my_a = row_index % n_c, row_index // n_c % n_b, row_index // (n_c * n_b)

    def piece(da, db, dc):
        return (dc * n_b + db) * n_a + da

    owner = block_cols // per_piece
    owner_c, owner_b, owner_a = owner % n_c, owner // n_c % n_b, owner // (n_c * n_b)
    place_cols = (
        piece((my_a - owner_a + n_a) % n_a, (my_b - owner_b + n_b) % n_b, (my_c - owner_c + n_c) % n_c) * per_piece
        + block_cols % per_piece
    )
    place_rows = (col_index - block_rows // per_piece + n_col) % n_col * per_piece + block_rows % per_piece
    live = jnp.arange(block_rows.shape[0], dtype=jnp.int32) < block_counts[0]
    put_cols = jnp.where(live, place_cols, n_row * per_piece)
    put_rows = jnp.where(live, place_rows, n_col * per_piece)

    mirror_outputs = [[piece(a, b, c) for b in range(n_b) for a in range(n_a)] for c in range(n_c)]
    forward_outputs = [[j] for j in range(n_col)]
    mirror_inputs = [[j] for j in range(n_col)]
    forward_inputs = []
    for c in range(n_c):
        forward_inputs.append([piece(0, b, c) for b in range(n_b)] + [piece(a, 0, c) for a in range(1, n_a)])
        if n_b > 1:
            forward_inputs.append([piece(a, b, c) for b in range(1, n_b) for a in range(1, n_a)])

    def apply_operator(narrow):
        by_col = [narrow] + [shift_col(narrow, j) for j in range(1, n_col)]
        near = [narrow] + [shift(narrow, db=b) for b in range(1, n_b)]
        far = [[shift(part, da=a) for a in range(1, n_a)] for part in near]
        mirrors = block_product(
            0, mirror_inputs, mirror_outputs, [jnp.bfloat16] * len(mirror_outputs), n_row,
            block_counts, place_rows, put_cols, by_col, block_values,
        )
        far[0], mirrors = lax.optimization_barrier((far[0], mirrors))

        shares = mirrors[0].astype(jnp.float32)
        for c in range(1, n_c):
            shares += shift(mirrors[c], dc=-c).astype(jnp.float32)
        by_b = [shares[b * n_a : (b + 1) * n_a] for b in range(n_b)]
        others = [shift(by_b[b].astype(jnp.bfloat16), db=-b) for b in range(1, n_b)]

        early = jnp.stack(near + far[0])
        late = [part for behind in far[1:] for part in behind]
        late = [jnp.stack(late)] if late else []
        by_row = [early] + late
        for c in range(1, n_c):
            by_row += [shift(part, dc=c) for part in [early] + late]
        by_row, others = lax.optimization_barrier((by_row, others))

        share = by_b[0]
        for other in others:
            share += other.astype(jnp.float32)
        back = [shift(share[a].astype(jnp.bfloat16), da=-a) for a in range(1, n_a)]

        forwards = block_product(
            1, forward_inputs, forward_outputs, [jnp.float32] + [jnp.bfloat16] * (n_col - 1), n_col,
            block_counts, place_cols, put_rows, by_row, block_values,
        )
        back, forwards = lax.optimization_barrier((back, forwards))
        forward_sum = forwards[0][0]
        for j in range(1, n_col):
            forward_sum += shift_col(forwards[j][0], -j).astype(jnp.float32)
        mirror_sum = share[0]
        for other in back:
            mirror_sum += other.astype(jnp.float32)
        return forward_sum + mirror_sum

    current = (apply_operator(vectors.astype(jnp.bfloat16)) - center_value * vectors) / radius_value
    return 2.0 * (apply_operator(current.astype(jnp.bfloat16)) - center_value * current) / radius_value - vectors


def solution(mesh):
    return jax.shard_map(
        functools.partial(shards, mesh.shape["row"], mesh.shape["col"]),
        mesh=mesh,
        in_specs=(
            P(None, ("row", "col")),
            P(("row", "col"), None, None),
            P(("row", "col")),
            P(("row", "col")),
            P(("row", "col")),
            P(),
            P(),
        ),
        out_specs=P(None, ("row", "col")),
        check_vma=False,
    )
```

profile of v0, /device:TPU:0, one launch (start us, length us, event | category | flops | bytes accessed | tf_op | source)
XLA Modules:
  0.0 105.3 jit_solution(7661139159772529953)
XLA Ops:
  1.0 3.0 %collective-permute-start.3 = (bf16[32,2048]{1,0:T(8,128)(2,1)S(1)}, bf16[32,2048]{1,0:T(8,128)(2,1)S(1)}, u32[]{:S(2)}, u32[]{:S(2)}) collective-permute-start(bf16[32,2048]{1,0:T(8,128)(2,1)S(1)} %get-tuple-element.91), channel_id=1, source_target_pairs={{0,1},{1,0},{2,3},{3,2},{4,5},{5,4},{6,7},{7,6},{8,9},{9,8},{10,11... | collective-permute-start | bytes 393224 | tf_op jit(solution)/shard_map/ppermute | solution.py:123
  5.6 2.6 %collective-permute-start.1 = (bf16[32,2048]{1,0:T(8,128)(2,1)S(1)}, bf16[32,2048]{1,0:T(8,128)(2,1)S(1)}, u32[]{:S(2)}, u32[]{:S(2)}) collective-permute-start(bf16[32,2048]{1,0:T(8,128)(2,1)S(1)} %get-tuple-element.91), channel_id=1, source_target_pairs={{0,16},{2,18},{4,20},{6,22},{8,24},{10,26},{12,28},{14,30},{16,0},... | collective-permute-start | bytes 393224 | tf_op jit(solution)/shard_map/ppermute | solution.py:120
  12.4 5.4 %mirror.2 = (bf16[8,32,2048]{2,1,0:T(8,128)(2,1)S(1)}, bf16[8,32,2048]{2,1,0:T(8,128)(2,1)S(1)}) custom-call(s32[1]{0:T(128)} %copy.16.count_ref, s32[256]{0:T(256)S(1)} %get-tuple-element.87.take_ref, s32[256]{0:T(256)S(1)} %get-tuple-element.100.put_ref, bf16[1,32,2048]{2,1,0:T(8,128)(2,1)S(1)} %bitcast.93, bf16[1,32,2048]{2,1,0:T(8,128)(2,1)S(1)} %bitcast.94, ...), custom_call_target="tpu_custom_call" | custom-call | flops 2147483648 | bytes 8650752 | tf_op jit(solution)/shard_map/mirror/pallas_call | solution.py:79
  18.6 1.9 %collective-permute-start.6 = (bf16[32,2048]{1,0:T(8,128)(2,1)S(1)}, bf16[32,2048]{1,0:T(8,128)(2,1)S(1)}, u32[]{:S(2)}, u32[]{:S(2)}) collective-permute-start(bf16[32,2048]{1,0:T(8,128)(2,1)S(1)} %collective-permute-done.5), channel_id=1, source_target_pairs={{0,8},{2,10},{4,12},{6,14},{8,16},{10,18},{12,20},{14,22},{16,24},... | collective-permute-start | bytes 393224 | tf_op jit(solution)/shard_map/ppermute | solution.py:120
  20.5 1.6 %collective-permute-start.7 = (bf16[32,2048]{1,0:T(8,128)(2,1)S(1)}, bf16[32,2048]{1,0:T(8,128)(2,1)S(1)}, u32[]{:S(2)}, u32[]{:S(2)}) collective-permute-start(bf16[32,2048]{1,0:T(8,128)(2,1)S(1)} %collective-permute-done.5), channel_id=1, source_target_pairs={{0,16},{2,18},{4,20},{6,22},{8,24},{10,26},{12,28},{14,30},{16,0},... | collective-permute-start | bytes 393224 | tf_op jit(solution)/shard_map/ppermute | solution.py:120
  24.9 1.9 %collective-permute-done.6 = bf16[32,2048]{1,0:T(8,128)(2,1)S(1)} collective-permute-done((bf16[32,2048]{1,0:T(8,128)(2,1)S(1)}, bf16[32,2048]{1,0:T(8,128)(2,1)S(1)}, u32[]{:S(2)}, u32[]{:S(2)}) %collective-permute-start.6) | collective-permute-done | bytes 131104 | tf_op jit(solution)/shard_map/ppermute | solution.py:120
  26.8 4.7 %collective-permute-done.7 = bf16[32,2048]{1,0:T(8,128)(2,1)S(1)} collective-permute-done((bf16[32,2048]{1,0:T(8,128)(2,1)S(1)}, bf16[32,2048]{1,0:T(8,128)(2,1)S(1)}, u32[]{:S(2)}, u32[]{:S(2)}) %collective-permute-start.7) | collective-permute-done | bytes 131104 | tf_op jit(solution)/shard_map/ppermute | solution.py:120
  31.7 1.7 %collective-permute-done.10.refs_3_ = bf16[3,32,2048]{2,1,0:T(8,128)(2,1)S(1)} collective-permute-done((bf16[3,32,2048]{2,1,0:T(8,128)(2,1)S(1)}, bf16[3,32,2048]{2,1,0:T(8,128)(2,1)S(1)}, u32[]{:S(2)}, u32[]{:S(2)}) %collective-permute-start.10) | collective-permute-done | bytes 393248 | tf_op jit(solution)/shard_map/ppermute | solution.py:120
  33.4 3.4 %collective-permute-done.11 = bf16[4,32,2048]{2,1,0:T(8,128)(2,1)S(1)} collective-permute-done((bf16[4,32,2048]{2,1,0:T(8,128)(2,1)S(1)}, bf16[4,32,2048]{2,1,0:T(8,128)(2,1)S(1)}, u32[]{:S(2)}, u32[]{:S(2)}) %collective-permute-start.11) | collective-permute-done | bytes 524320 | tf_op jit(solution)/shard_map/ppermute | solution.py:120
  37.0 1.7 %collective-permute-start.12 = (bf16[32,2048]{1,0:T(8,128)(2,1)S(1)}, bf16[32,2048]{1,0:T(8,128)(2,1)S(1)}, u32[]{:S(2)}, u32[]{:S(2)}) collective-permute-start(bf16[32,2048]{1,0:T(8,128)(2,1)S(1)} %get-tuple-element.99), channel_id=1, source_target_pairs={{0,24},{2,26},{4,28},{6,30},{8,0},{10,2},{12,4},{14,6},{16,8},{18,... | collective-permute-start | bytes 393224 | tf_op jit(solution)/shard_map/ppermute | solution.py:120
  40.2 5.4 %forward.2 = (f32[1,32,2048]{2,1,0:T(8,128)S(1)}, bf16[1,32,2048]{2,1,0:T(8,128)(2,1)S(1)}) custom-call(s32[1]{0:T(128)} %copy.16.count_ref, s32[256]{0:T(256)S(1)} %get-tuple-element.101.take_ref, s32[256]{0:T(256)S(1)} %get-tuple-element.86.put_ref, bf16[5,32,2048]{2,1,0:T(8,128)(2,1)S(1)} %bitcast_dynamic-update-slice_fusion.4.refs_0_, ...), custom_call_target="tpu_custom_call" | custom-call | flops 2147483648 | bytes 10485760 | tf_op jit(solution)/shard_map/forward/pallas_call | solution.py:79
  45.7 4.7 %collective-permute-done.13 = bf16[32,2048]{1,0:T(8,128)(2,1)S(1)} collective-permute-done((bf16[32,2048]{1,0:T(8,128)(2,1)S(1)}, bf16[32,2048]{1,0:T(8,128)(2,1)S(1)}, u32[]{:S(2)}, u32[]{:S(2)}) %collective-permute-start.13) | collective-permute-done | bytes 131104 | tf_op jit(solution)/shard_map/ppermute | solution.py:120
  52.0 3.3 %collective-permute-done.15 = bf16[32,2048]{1,0:T(8,128)(2,1)S(1)} collective-permute-done((bf16[32,2048]{1,0:T(8,128)(2,1)S(1)}, bf16[32,2048]{1,0:T(8,128)(2,1)S(1)}, u32[]{:S(2)}, u32[]{:S(2)}) %collective-permute-start.15) | collective-permute-done | bytes 131104 | tf_op jit(solution)/shard_map/ppermute | solution.py:123
  57.1 2.9 %collective-permute-start.18 = (bf16[32,2048]{1,0:T(8,128)(2,1)S(1)}, bf16[32,2048]{1,0:T(8,128)(2,1)S(1)}, u32[]{:S(2)}, u32[]{:S(2)}) collective-permute-start(bf16[32,2048]{1,0:T(8,128)(2,1)S(1)} %get-tuple-element.84), channel_id=1, source_target_pairs={{0,24},{2,26},{4,28},{6,30},{8,0},{10,2},{12,4},{14,6},{16,8},{18,... | collective-permute-start | bytes 393224 | tf_op jit(solution)/shard_map/ppermute | solution.py:120
  61.6 5.4 %mirror.3 = (bf16[8,32,2048]{2,1,0:T(8,128)(2,1)S(1)}, bf16[8,32,2048]{2,1,0:T(8,128)(2,1)S(1)}) custom-call(s32[1]{0:T(128)} %copy.16.count_ref, s32[256]{0:T(256)S(1)} %get-tuple-element.87.take_ref, s32[256]{0:T(256)S(1)} %get-tuple-element.100.put_ref, bf16[1,32,2048]{2,1,0:T(8,128)(2,1)S(1)} %bitcast.92, bf16[1,32,2048]{2,1,0:T(8,128)(2,1)S(1)} %bitcast.95, ...), custom_call_target="tpu_custom_call" | custom-call | flops 2147483648 | bytes 8650752 | tf_op jit(solution)/shard_map/mirror/pallas_call | solution.py:79
  68.9 2.2 %collective-permute-start.23 = (bf16[32,2048]{1,0:T(8,128)(2,1)S(1)}, bf16[32,2048]{1,0:T(8,128)(2,1)S(1)}, u32[]{:S(2)}, u32[]{:S(2)}) collective-permute-start(bf16[32,2048]{1,0:T(8,128)(2,1)S(1)} %collective-permute-done.21), channel_id=1, source_target_pairs={{0,16},{2,18},{4,20},{6,22},{8,24},{10,26},{12,28},{14,30},{16,0},... | collective-permute-start | bytes 393224 | tf_op jit(solution)/shard_map/ppermute | solution.py:120
  73.3 2.7 %collective-permute-done.22 = bf16[32,2048]{1,0:T(8,128)(2,1)S(1)} collective-permute-done((bf16[32,2048]{1,0:T(8,128)(2,1)S(1)}, bf16[32,2048]{1,0:T(8,128)(2,1)S(1)}, u32[]{:S(2)}, u32[]{:S(2)}) %collective-permute-start.22) | collective-permute-done | bytes 131104 | tf_op jit(solution)/shard_map/ppermute | solution.py:120
  76.0 4.7 %collective-permute-done.23 = bf16[32,2048]{1,0:T(8,128)(2,1)S(1)} collective-permute-done((bf16[32,2048]{1,0:T(8,128)(2,1)S(1)}, bf16[32,2048]{1,0:T(8,128)(2,1)S(1)}, u32[]{:S(2)}, u32[]{:S(2)}) %collective-permute-start.23) | collective-permute-done | bytes 131104 | tf_op jit(solution)/shard_map/ppermute | solution.py:120
  80.8 1.7 %collective-permute-done.26.refs_3_ = bf16[3,32,2048]{2,1,0:T(8,128)(2,1)S(1)} collective-permute-done((bf16[3,32,2048]{2,1,0:T(8,128)(2,1)S(1)}, bf16[3,32,2048]{2,1,0:T(8,128)(2,1)S(1)}, u32[]{:S(2)}, u32[]{:S(2)}) %collective-permute-start.26) | collective-permute-done | bytes 393248 | tf_op jit(solution)/shard_map/ppermute | solution.py:120
  82.5 2.8 %collective-permute-done.27 = bf16[4,32,2048]{2,1,0:T(8,128)(2,1)S(1)} collective-permute-done((bf16[4,32,2048]{2,1,0:T(8,128)(2,1)S(1)}, bf16[4,32,2048]{2,1,0:T(8,128)(2,1)S(1)}, u32[]{:S(2)}, u32[]{:S(2)}) %collective-permute-start.27) | collective-permute-done | bytes 524320 | tf_op jit(solution)/shard_map/ppermute | solution.py:120
  85.6 1.7 %collective-permute-start.28 = (bf16[32,2048]{1,0:T(8,128)(2,1)S(1)}, bf16[32,2048]{1,0:T(8,128)(2,1)S(1)}, u32[]{:S(2)}, u32[]{:S(2)}) collective-permute-start(bf16[32,2048]{1,0:T(8,128)(2,1)S(1)} %get-tuple-element.96), channel_id=1, source_target_pairs={{0,24},{2,26},{4,28},{6,30},{8,0},{10,2},{12,4},{14,6},{16,8},{18,... | collective-permute-start | bytes 393224 | tf_op jit(solution)/shard_map/ppermute | solution.py:120
  89.4 5.4 %forward.3 = (f32[1,32,2048]{2,1,0:T(8,128)S(1)}, bf16[1,32,2048]{2,1,0:T(8,128)(2,1)S(1)}) custom-call(s32[1]{0:T(128)} %copy.16.count_ref, s32[256]{0:T(256)S(1)} %get-tuple-element.101.take_ref, s32[256]{0:T(256)S(1)} %get-tuple-element.86.put_ref, bf16[5,32,2048]{2,1,0:T(8,128)(2,1)S(1)} %bitcast_dynamic-update-slice_fusion.refs_0_, ...), custom_call_target="tpu_custom_call" | custom-call | flops 2147483648 | bytes 10485760 | tf_op jit(solution)/shard_map/forward/pallas_call | solution.py:79
  94.8 4.7 %collective-permute-done.29 = bf16[32,2048]{1,0:T(8,128)(2,1)S(1)} collective-permute-done((bf16[32,2048]{1,0:T(8,128)(2,1)S(1)}, bf16[32,2048]{1,0:T(8,128)(2,1)S(1)}, u32[]{:S(2)}, u32[]{:S(2)}) %collective-permute-start.29) | collective-permute-done | bytes 131104 | tf_op jit(solution)/shard_map/ppermute | solution.py:120
  100.5 4.0 %collective-permute-done.31 = bf16[32,2048]{1,0:T(8,128)(2,1)S(1)} collective-permute-done((bf16[32,2048]{1,0:T(8,128)(2,1)S(1)}, bf16[32,2048]{1,0:T(8,128)(2,1)S(1)}, u32[]{:S(2)}, u32[]{:S(2)}) %collective-permute-start.31) | collective-permute-done | bytes 131104 | tf_op jit(solution)/shard_map/ppermute | solution.py:123
  (68 shorter events, 23.5 us)
Async XLA Ops:
  1.0 11.4 %collective-permute-start.3 = (bf16[32,2048]{1,0:T(8,128)(2,1)S(1)}, bf16[32,2048]{1,0:T(8,128)(2,1)S(1)}, u32[]{:S(2)}, u32[]{:S(2)}) collective-permute-start(bf16[32,2048]{1,0:T(8,128)(2,1)S(1)} %get-tuple-element.91), channel_id=1, source_target_pairs={{0,1},{1,0},{2,3},{3,2},{4,5},{5,4},{6,7},{7,6},{8,9},{9,8},{10,11... | collective-permute-start | bytes 393224 | tf_op jit(solution)/shard_map/ppermute | solution.py:123
  4.0 13.8 %collective-permute-start = (bf16[32,2048]{1,0:T(8,128)(2,1)S(1)}, bf16[32,2048]{1,0:T(8,128)(2,1)S(1)}, u32[]{:S(2)}, u32[]{:S(2)}) collective-permute-start(bf16[32,2048]{1,0:T(8,128)(2,1)S(1)} %get-tuple-element.91), channel_id=1, source_target_pairs={{0,8},{2,10},{4,12},{6,14},{8,16},{10,18},{12,20},{14,22},{16,24},... | collective-permute-start | bytes 393224 | tf_op jit(solution)/shard_map/ppermute | solution.py:120
  5.6 12.3 %collective-permute-start.1 = (bf16[32,2048]{1,0:T(8,128)(2,1)S(1)}, bf16[32,2048]{1,0:T(8,128)(2,1)S(1)}, u32[]{:S(2)}, u32[]{:S(2)}) collective-permute-start(bf16[32,2048]{1,0:T(8,128)(2,1)S(1)} %get-tuple-element.91), channel_id=1, source_target_pairs={{0,16},{2,18},{4,20},{6,22},{8,24},{10,26},{12,28},{14,30},{16,0},... | collective-permute-start | bytes 393224 | tf_op jit(solution)/shard_map/ppermute | solution.py:120
  8.1 9.7 %collective-permute-start.2 = (bf16[32,2048]{1,0:T(8,128)(2,1)S(1)}, bf16[32,2048]{1,0:T(8,128)(2,1)S(1)}, u32[]{:S(2)}, u32[]{:S(2)}) collective-permute-start(bf16[32,2048]{1,0:T(8,128)(2,1)S(1)} %get-tuple-element.91), channel_id=1, source_target_pairs={{0,24},{2,26},{4,28},{6,30},{8,0},{10,2},{12,4},{14,6},{16,8},{18,... | collective-permute-start | bytes 393224 | tf_op jit(solution)/shard_map/ppermute | solution.py:120
  9.5 8.4 %collective-permute-start.5 = (bf16[32,2048]{1,0:T(8,128)(2,1)S(1)}, bf16[32,2048]{1,0:T(8,128)(2,1)S(1)}, u32[]{:S(2)}, u32[]{:S(2)}) collective-permute-start(bf16[32,2048]{1,0:T(8,128)(2,1)S(1)} %get-tuple-element.91), channel_id=1, source_target_pairs={{0,4},{2,6},{4,0},{6,2},{8,12},{10,14},{12,8},{14,10},{16,20},{18,... | collective-permute-start | bytes 393224 | tf_op jit(solution)/shard_map/ppermute | solution.py:120
  18.0 15.4 %collective-permute-start.9 = (bf16[5,32,2048]{2,1,0:T(8,128)(2,1)S(1)}, bf16[5,32,2048]{2,1,0:T(8,128)(2,1)S(1)}, u32[]{:S(2)}, u32[]{:S(2)}) collective-permute-start(bf16[5,32,2048]{2,1,0:T(8,128)(2,1)S(1)} %bitcast_dynamic-update-slice_fusion.4.refs_0_), channel_id=1, source_target_pairs={{0,2},{2,0},{4,6},{6,4},{8,10},{10,8},{12,14},{14,12},{16,18},{18,... | collective-permute-start | bytes 1966088 | tf_op jit(solution)/shard_map/ppermute | solution.py:120
  18.6 8.2 %collective-permute-start.6 = (bf16[32,2048]{1,0:T(8,128)(2,1)S(1)}, bf16[32,2048]{1,0:T(8,128)(2,1)S(1)}, u32[]{:S(2)}, u32[]{:S(2)}) collective-permute-start(bf16[32,2048]{1,0:T(8,128)(2,1)S(1)} %collective-permute-done.5), channel_id=1, source_target_pairs={{0,8},{2,10},{4,12},{6,14},{8,16},{10,18},{12,20},{14,22},{16,24},... | collective-permute-start | bytes 393224 | tf_op jit(solution)/shard_map/ppermute | solution.py:120
  20.5 11.1 %collective-permute-start.7 = (bf16[32,2048]{1,0:T(8,128)(2,1)S(1)}, bf16[32,2048]{1,0:T(8,128)(2,1)S(1)}, u32[]{:S(2)}, u32[]{:S(2)}) collective-permute-start(bf16[32,2048]{1,0:T(8,128)(2,1)S(1)} %collective-permute-done.5), channel_id=1, source_target_pairs={{0,16},{2,18},{4,20},{6,22},{8,24},{10,26},{12,28},{14,30},{16,0},... | collective-permute-start | bytes 393224 | tf_op jit(solution)/shard_map/ppermute | solution.py:120
  22.1 9.5 %collective-permute-start.8 = (bf16[32,2048]{1,0:T(8,128)(2,1)S(1)}, bf16[32,2048]{1,0:T(8,128)(2,1)S(1)}, u32[]{:S(2)}, u32[]{:S(2)}) collective-permute-start(bf16[32,2048]{1,0:T(8,128)(2,1)S(1)} %collective-permute-done.5), channel_id=1, source_target_pairs={{0,24},{2,26},{4,28},{6,30},{8,0},{10,2},{12,4},{14,6},{16,8},{18,... | collective-permute-start | bytes 393224 | tf_op jit(solution)/shard_map/ppermute | solution.py:120
  23.3 13.5 %collective-permute-start.11 = (bf16[4,32,2048]{2,1,0:T(8,128)(2,1)S(1)}, bf16[4,32,2048]{2,1,0:T(8,128)(2,1)S(1)}, u32[]{:S(2)}, u32[]{:S(2)}) collective-permute-start(bf16[4,32,2048]{2,1,0:T(8,128)(2,1)S(1)} %slice.109), channel_id=1, source_target_pairs={{0,4},{2,6},{4,0},{6,2},{8,12},{10,14},{12,8},{14,10},{16,20},{18,... | collective-permute-start | bytes 1572872 | tf_op jit(solution)/shard_map/ppermute | solution.py:120
  37.0 8.7 %collective-permute-start.12 = (bf16[32,2048]{1,0:T(8,128)(2,1)S(1)}, bf16[32,2048]{1,0:T(8,128)(2,1)S(1)}, u32[]{:S(2)}, u32[]{:S(2)}) collective-permute-start(bf16[32,2048]{1,0:T(8,128)(2,1)S(1)} %get-tuple-element.99), channel_id=1, source_target_pairs={{0,24},{2,26},{4,28},{6,30},{8,0},{10,2},{12,4},{14,6},{16,8},{18,... | collective-permute-start | bytes 393224 | tf_op jit(solution)/shard_map/ppermute | solution.py:120
  38.7 11.6 %collective-permute-start.13 = (bf16[32,2048]{1,0:T(8,128)(2,1)S(1)}, bf16[32,2048]{1,0:T(8,128)(2,1)S(1)}, u32[]{:S(2)}, u32[]{:S(2)}) collective-permute-start(bf16[32,2048]{1,0:T(8,128)(2,1)S(1)} %get-tuple-element.98), channel_id=1, source_target_pairs={{0,16},{2,18},{4,20},{6,22},{8,24},{10,26},{12,28},{14,30},{16,0},... | collective-permute-start | bytes 393224 | tf_op jit(solution)/shard_map/ppermute | solution.py:120
  39.4 11.0 %collective-permute-start.14 = (bf16[32,2048]{1,0:T(8,128)(2,1)S(1)}, bf16[32,2048]{1,0:T(8,128)(2,1)S(1)}, u32[]{:S(2)}, u32[]{:S(2)}) collective-permute-start(bf16[32,2048]{1,0:T(8,128)(2,1)S(1)} %get-tuple-element.97), channel_id=1, source_target_pairs={{0,8},{2,10},{4,12},{6,14},{8,16},{10,18},{12,20},{14,22},{16,24},... | collective-permute-start | bytes 393224 | tf_op jit(solution)/shard_map/ppermute | solution.py:120
  55.9 11.1 %collective-permute-start.16 = (bf16[32,2048]{1,0:T(8,128)(2,1)S(1)}, bf16[32,2048]{1,0:T(8,128)(2,1)S(1)}, u32[]{:S(2)}, u32[]{:S(2)}) collective-permute-start(bf16[32,2048]{1,0:T(8,128)(2,1)S(1)} %get-tuple-element.84), channel_id=1, source_target_pairs={{0,8},{2,10},{4,12},{6,14},{8,16},{10,18},{12,20},{14,22},{16,24},... | collective-permute-start | bytes 393224 | tf_op jit(solution)/shard_map/ppermute | solution.py:120
  55.9 11.1 %collective-permute-start.17 = (bf16[32,2048]{1,0:T(8,128)(2,1)S(1)}, bf16[32,2048]{1,0:T(8,128)(2,1)S(1)}, u32[]{:S(2)}, u32[]{:S(2)}) collective-permute-start(bf16[32,2048]{1,0:T(8,128)(2,1)S(1)} %get-tuple-element.84), channel_id=1, source_target_pairs={{0,16},{2,18},{4,20},{6,22},{8,24},{10,26},{12,28},{14,30},{16,0},... | collective-permute-start | bytes 393224 | tf_op jit(solution)/shard_map/ppermute | solution.py:120
  57.1 9.9 %collective-permute-start.18 = (bf16[32,2048]{1,0:T(8,128)(2,1)S(1)}, bf16[32,2048]{1,0:T(8,128)(2,1)S(1)}, u32[]{:S(2)}, u32[]{:S(2)}) collective-permute-start(bf16[32,2048]{1,0:T(8,128)(2,1)S(1)} %get-tuple-element.84), channel_id=1, source_target_pairs={{0,24},{2,26},{4,28},{6,30},{8,0},{10,2},{12,4},{14,6},{16,8},{18,... | collective-permute-start | bytes 393224 | tf_op jit(solution)/shard_map/ppermute | solution.py:120
  67.2 15.4 %collective-permute-start.25 = (bf16[5,32,2048]{2,1,0:T(8,128)(2,1)S(1)}, bf16[5,32,2048]{2,1,0:T(8,128)(2,1)S(1)}, u32[]{:S(2)}, u32[]{:S(2)}) collective-permute-start(bf16[5,32,2048]{2,1,0:T(8,128)(2,1)S(1)} %bitcast_dynamic-update-slice_fusion.refs_0_), channel_id=1, source_target_pairs={{0,2},{2,0},{4,6},{6,4},{8,10},{10,8},{12,14},{14,12},{16,18},{18,... | collective-permute-start | bytes 1966088 | tf_op jit(solution)/shard_map/ppermute | solution.py:120
  67.7 8.2 %collective-permute-start.22 = (bf16[32,2048]{1,0:T(8,128)(2,1)S(1)}, bf16[32,2048]{1,0:T(8,128)(2,1)S(1)}, u32[]{:S(2)}, u32[]{:S(2)}) collective-permute-start(bf16[32,2048]{1,0:T(8,128)(2,1)S(1)} %collective-permute-done.21), channel_id=1, source_target_pairs={{0,8},{2,10},{4,12},{6,14},{8,16},{10,18},{12,20},{14,22},{16,24},... | collective-permute-start | bytes 393224 | tf_op jit(solution)/shard_map/ppermute | solution.py:120
  68.9 11.8 %collective-permute-start.23 = (bf16[32,2048]{1,0:T(8,128)(2,1)S(1)}, bf16[32,2048]{1,0:T(8,128)(2,1)S(1)}, u32[]{:S(2)}, u32[]{:S(2)}) collective-permute-start(bf16[32,2048]{1,0:T(8,128)(2,1)S(1)} %collective-permute-done.21), channel_id=1, source_target_pairs={{0,16},{2,18},{4,20},{6,22},{8,24},{10,26},{12,28},{14,30},{16,0},... | collective-permute-start | bytes 393224 | tf_op jit(solution)/shard_map/ppermute | solution.py:120
  71.1 9.6 %collective-permute-start.24 = (bf16[32,2048]{1,0:T(8,128)(2,1)S(1)}, bf16[32,2048]{1,0:T(8,128)(2,1)S(1)}, u32[]{:S(2)}, u32[]{:S(2)}) collective-permute-start(bf16[32,2048]{1,0:T(8,128)(2,1)S(1)} %collective-permute-done.21), channel_id=1, source_target_pairs={{0,24},{2,26},{4,28},{6,30},{8,0},{10,2},{12,4},{14,6},{16,8},{18,... | collective-permute-start | bytes 393224 | tf_op jit(solution)/shard_map/ppermute | solution.py:120
  72.0 13.4 %collective-permute-start.27 = (bf16[4,32,2048]{2,1,0:T(8,128)(2,1)S(1)}, bf16[4,32,2048]{2,1,0:T(8,128)(2,1)S(1)}, u32[]{:S(2)}, u32[]{:S(2)}) collective-permute-start(bf16[4,32,2048]{2,1,0:T(8,128)(2,1)S(1)} %slice.108), channel_id=1, source_target_pairs={{0,4},{2,6},{4,0},{6,2},{8,12},{10,14},{12,8},{14,10},{16,20},{18,... | collective-permute-start | bytes 1572872 | tf_op jit(solution)/shard_map/ppermute | solution.py:120
  85.6 9.2 %collective-permute-start.28 = (bf16[32,2048]{1,0:T(8,128)(2,1)S(1)}, bf16[32,2048]{1,0:T(8,128)(2,1)S(1)}, u32[]{:S(2)}, u32[]{:S(2)}) collective-permute-start(bf16[32,2048]{1,0:T(8,128)(2,1)S(1)} %get-tuple-element.96), channel_id=1, source_target_pairs={{0,24},{2,26},{4,28},{6,30},{8,0},{10,2},{12,4},{14,6},{16,8},{18,... | collective-permute-start | bytes 393224 | tf_op jit(solution)/shard_map/ppermute | solution.py:120
  87.3 12.2 %collective-permute-start.29 = (bf16[32,2048]{1,0:T(8,128)(2,1)S(1)}, bf16[32,2048]{1,0:T(8,128)(2,1)S(1)}, u32[]{:S(2)}, u32[]{:S(2)}) collective-permute-start(bf16[32,2048]{1,0:T(8,128)(2,1)S(1)} %get-tuple-element.95), channel_id=1, source_target_pairs={{0,16},{2,18},{4,20},{6,22},{8,24},{10,26},{12,28},{14,30},{16,0},... | collective-permute-start | bytes 393224 | tf_op jit(solution)/shard_map/ppermute | solution.py:120
  88.4 11.1 %collective-permute-start.30 = (bf16[32,2048]{1,0:T(8,128)(2,1)S(1)}, bf16[32,2048]{1,0:T(8,128)(2,1)S(1)}, u32[]{:S(2)}, u32[]{:S(2)}) collective-permute-start(bf16[32,2048]{1,0:T(8,128)(2,1)S(1)} %get-tuple-element.94), channel_id=1, source_target_pairs={{0,8},{2,10},{4,12},{6,14},{8,16},{10,18},{12,20},{14,22},{16,24},... | collective-permute-start | bytes 393224 | tf_op jit(solution)/shard_map/ppermute | solution.py:120
  (9 other events, 51.3 us)
where the time goes:
time: 106 us; the launch traced here: 105 us
  waiting for transfers between devices  40.4 us (38%)
  starting transfers between devices  37 us (35%)
  Pallas kernels  21.5 us (20%)
  other arithmetic  3.79 us (4%)
  between operations  2.28 us (2%)
    ppermute x28, waiting for transfers between devices, shift(): return lax.ppermute(value, 'row', pairs)  33.1 us
    ppermute x28, starting transfers between devices, shift(): return lax.ppermute(value, 'row', pairs)  32.3 us
    pallas_call x4, Pallas kernels, block_product(): pl.pallas_call(functools.partial(product_kernel, contract, inputs, output...  21.5 us
    ppermute x4, waiting for transfers between devices, shift_col(): lax.ppermute(value, 'col', [(j, (j + d) % n_col) for j in range(n_col)])  7.29 us
    ppermute x4, starting transfers between devices, shift_col(): lax.ppermute(value, 'col', [(j, (j + d) % n_col) for j in range(n_col)])  4.77 us
  transfers between devices with their start and end apart: 32, of which 12 were waited for; matrix products, arithmetic and copies ran while one was open for 2% of the time, Pallas kernels for 20%

commit v1 on v0

--- a/solution.py
+++ b/solution.py
@@ -182,8 +182,8 @@
             1, forward_inputs, forward_outputs, [jnp.float32] + [jnp.bfloat16] * (n_col - 1), n_col,
             block_counts, place_cols, put_rows, by_row, block_values,
         )
-        back, forwards = lax.optimization_barrier((back, forwards))
-        forward_sum = forwards[0][0]
+        back, own = lax.optimization_barrier((back, forwards[0]))
+        forward_sum = own[0]
         for j in range(1, n_col):
             forward_sum += shift_col(forwards[j][0], -j).astype(jnp.float32)
         mirror_sum = share[0]

time: 106 us -> 97.5 us (0.920)
  Pallas kernels: 21.5 us -> 12.5 us
  starting transfers between devices: 37 us -> 38.5 us
  waiting for transfers between devices: 40.4 us -> 39.1 us
    pallas_call x4, Pallas kernels: 21.5 us -> 12.5 us  [block_product(): pl.pallas_call(functools.partial(product_kernel, contract, inputs, output...]
    ppermute x4, waiting for transfers between devices: 7.29 us -> 0.01 us  [shift_col(): lax.ppermute(value, 'col', [(j, (j + d) % n_col) for j in range(n_col)])]
    ppermute x28, waiting for transfers between devices: 33.1 us -> 39.1 us  [shift(): return lax.ppermute(value, 'row', pairs)]
    ppermute x28, starting transfers between devices: 32.3 us -> 33.8 us  [shift(): return lax.ppermute(value, 'row', pairs)]
  transfers between devices with their start and end apart: 32 -> 32, of which waited for: 12 -> 12; matrix products, arithmetic and copies ran while one was open for 2% -> 2% of each run, Pallas kernels for 20% -> 13%
where the time goes in v1:
time: 97.5 us; the launch traced here: 96.5 us
  waiting for transfers between devices  39.1 us (40%)
  starting transfers between devices  38.5 us (39%)
  Pallas kernels  12.5 us (13%)
  other arithmetic  3.8 us (4%)
  between operations  2.22 us (2%)
    ppermute x28, waiting for transfers between devices, shift(): return lax.ppermute(value, 'row', pairs)  39.1 us
    ppermute x28, starting transfers between devices, shift(): return lax.ppermute(value, 'row', pairs)  33.8 us
    pallas_call x4, Pallas kernels, block_product(): pl.pallas_call(functools.partial(product_kernel, contract, inputs, output...  12.5 us
    ppermute x4, starting transfers between devices, shift_col(): lax.ppermute(value, 'col', [(j, (j + d) % n_col) for j in range(n_col)])  4.8 us
  transfers between devices with their start and end apart: 32, of which 12 were waited for; matrix products, arithmetic and copies ran while one was open for 2% of the time, Pallas kernels for 13%

profile of v1, /device:TPU:0, one launch (start us, length us, event | category | flops | bytes accessed | tf_op | source)
XLA Modules:
  0.0 96.5 jit_solution(14284077340328340032)
XLA Ops:
  1.0 3.0 %collective-permute-start.3 = (bf16[32,2048]{1,0:T(8,128)(2,1)S(1)}, bf16[32,2048]{1,0:T(8,128)(2,1)S(1)}, u32[]{:S(2)}, u32[]{:S(2)}) collective-permute-start(bf16[32,2048]{1,0:T(8,128)(2,1)S(1)} %get-tuple-element.87), channel_id=1, source_target_pairs={{0,1},{1,0},{2,3},{3,2},{4,5},{5,4},{6,7},{7,6},{8,9},{9,8},{10,11... | collective-permute-start | bytes 393224 | tf_op jit(solution)/shard_map/ppermute | solution.py:123
  4.0 1.6 %collective-permute-start = (bf16[32,2048]{1,0:T(8,128)(2,1)S(1)}, bf16[32,2048]{1,0:T(8,128)(2,1)S(1)}, u32[]{:S(2)}, u32[]{:S(2)}) collective-permute-start(bf16[32,2048]{1,0:T(8,128)(2,1)S(1)} %get-tuple-element.87), channel_id=1, source_target_pairs={{0,8},{2,10},{4,12},{6,14},{8,16},{10,18},{12,20},{14,22},{16,24},... | collective-permute-start | bytes 393224 | tf_op jit(solution)/shard_map/ppermute | solution.py:120
  5.6 2.6 %collective-permute-start.1 = (bf16[32,2048]{1,0:T(8,128)(2,1)S(1)}, bf16[32,2048]{1,0:T(8,128)(2,1)S(1)}, u32[]{:S(2)}, u32[]{:S(2)}) collective-permute-start(bf16[32,2048]{1,0:T(8,128)(2,1)S(1)} %get-tuple-element.87), channel_id=1, source_target_pairs={{0,16},{2,18},{4,20},{6,22},{8,24},{10,26},{12,28},{14,30},{16,0},... | collective-permute-start | bytes 393224 | tf_op jit(solution)/shard_map/ppermute | solution.py:120
  12.4 3.2 %mirror.2 = (bf16[8,32,2048]{2,1,0:T(8,128)(2,1)S(1)}, bf16[8,32,2048]{2,1,0:T(8,128)(2,1)S(1)}) custom-call(s32[1]{0:T(128)} %copy.16.count_ref, s32[256]{0:T(256)S(1)} %get-tuple-element.83.take_ref, s32[256]{0:T(256)S(1)} %get-tuple-element.96.put_ref, bf16[1,32,2048]{2,1,0:T(8,128)(2,1)S(1)} %bitcast.93, bf16[1,32,2048]{2,1,0:T(8,128)(2,1)S(1)} %bitcast.94, ...), custom_call_target="tpu_custom_call" | custom-call | flops 2147483648 | bytes 8650752 | tf_op jit(solution)/shard_map/mirror/pallas_call | solution.py:79
  17.2 3.3 %collective-permute-start.6 = (bf16[32,2048]{1,0:T(8,128)(2,1)S(1)}, bf16[32,2048]{1,0:T(8,128)(2,1)S(1)}, u32[]{:S(2)}, u32[]{:S(2)}) collective-permute-start(bf16[32,2048]{1,0:T(8,128)(2,1)S(1)} %collective-permute-done.5), channel_id=1, source_target_pairs={{0,8},{2,10},{4,12},{6,14},{8,16},{10,18},{12,20},{14,22},{16,24},... | collective-permute-start | bytes 393224 | tf_op jit(solution)/shard_map/ppermute | solution.py:120
  20.5 1.6 %collective-permute-start.7 = (bf16[32,2048]{1,0:T(8,128)(2,1)S(1)}, bf16[32,2048]{1,0:T(8,128)(2,1)S(1)}, u32[]{:S(2)}, u32[]{:S(2)}) collective-permute-start(bf16[32,2048]{1,0:T(8,128)(2,1)S(1)} %collective-permute-done.5), channel_id=1, source_target_pairs={{0,16},{2,18},{4,20},{6,22},{8,24},{10,26},{12,28},{14,30},{16,0},... | collective-permute-start | bytes 393224 | tf_op jit(solution)/shard_map/ppermute | solution.py:120
  23.3 1.5 %collective-permute-start.11 = (bf16[4,32,2048]{2,1,0:T(8,128)(2,1)S(1)}, bf16[4,32,2048]{2,1,0:T(8,128)(2,1)S(1)}, u32[]{:S(2)}, u32[]{:S(2)}) collective-permute-start(bf16[4,32,2048]{2,1,0:T(8,128)(2,1)S(1)} %slice.109), channel_id=1, source_target_pairs={{0,4},{2,6},{4,0},{6,2},{8,12},{10,14},{12,8},{14,10},{16,20},{18,... | collective-permute-start | bytes 1572872 | tf_op jit(solution)/shard_map/ppermute | solution.py:120
  25.9 5.0 %collective-permute-done.7 = bf16[32,2048]{1,0:T(8,128)(2,1)S(1)} collective-permute-done((bf16[32,2048]{1,0:T(8,128)(2,1)S(1)}, bf16[32,2048]{1,0:T(8,128)(2,1)S(1)}, u32[]{:S(2)}, u32[]{:S(2)}) %collective-permute-start.7) | collective-permute-done | bytes 131104 | tf_op jit(solution)/shard_map/ppermute | solution.py:120
  31.1 1.7 %collective-permute-done.10.refs_3_ = bf16[3,32,2048]{2,1,0:T(8,128)(2,1)S(1)} collective-permute-done((bf16[3,32,2048]{2,1,0:T(8,128)(2,1)S(1)}, bf16[3,32,2048]{2,1,0:T(8,128)(2,1)S(1)}, u32[]{:S(2)}, u32[]{:S(2)}) %collective-permute-start.10) | collective-permute-done | bytes 393248 | tf_op jit(solution)/shard_map/ppermute | solution.py:120
  32.8 4.0 %collective-permute-done.11 = bf16[4,32,2048]{2,1,0:T(8,128)(2,1)S(1)} collective-permute-done((bf16[4,32,2048]{2,1,0:T(8,128)(2,1)S(1)}, bf16[4,32,2048]{2,1,0:T(8,128)(2,1)S(1)}, u32[]{:S(2)}, u32[]{:S(2)}) %collective-permute-start.11) | collective-permute-done | bytes 524320 | tf_op jit(solution)/shard_map/ppermute | solution.py:120
  37.0 1.7 %collective-permute-start.12 = (bf16[32,2048]{1,0:T(8,128)(2,1)S(1)}, bf16[32,2048]{1,0:T(8,128)(2,1)S(1)}, u32[]{:S(2)}, u32[]{:S(2)}) collective-permute-start(bf16[32,2048]{1,0:T(8,128)(2,1)S(1)} %get-tuple-element.95), channel_id=1, source_target_pairs={{0,24},{2,26},{4,28},{6,30},{8,0},{10,2},{12,4},{14,6},{16,8},{18,... | collective-permute-start | bytes 393224 | tf_op jit(solution)/shard_map/ppermute | solution.py:120
  39.7 3.1 %forward.2 = (f32[1,32,2048]{2,1,0:T(8,128)S(1)}, bf16[1,32,2048]{2,1,0:T(8,128)(2,1)S(1)}) custom-call(s32[1]{0:T(128)} %copy.16.count_ref, s32[256]{0:T(256)S(1)} %get-tuple-element.97.take_ref, s32[256]{0:T(256)S(1)} %get-tuple-element.82.put_ref, bf16[5,32,2048]{2,1,0:T(8,128)(2,1)S(1)} %bitcast_dynamic-update-slice_fusion.4.refs_0_, ...), custom_call_target="tpu_custom_call" | custom-call | flops 2147483648 | bytes 10485760 | tf_op jit(solution)/shard_map/forward/pallas_call | solution.py:79
  44.2 5.9 %collective-permute-done.13 = bf16[32,2048]{1,0:T(8,128)(2,1)S(1)} collective-permute-done((bf16[32,2048]{1,0:T(8,128)(2,1)S(1)}, bf16[32,2048]{1,0:T(8,128)(2,1)S(1)}, u32[]{:S(2)}, u32[]{:S(2)}) %collective-permute-start.13) | collective-permute-done | bytes 131104 | tf_op jit(solution)/shard_map/ppermute | solution.py:120
  50.9 1.5 %collective-permute-start.16 = (bf16[32,2048]{1,0:T(8,128)(2,1)S(1)}, bf16[32,2048]{1,0:T(8,128)(2,1)S(1)}, u32[]{:S(2)}, u32[]{:S(2)}) collective-permute-start(bf16[32,2048]{1,0:T(8,128)(2,1)S(1)} %get-tuple-element.80), channel_id=1, source_target_pairs={{0,8},{2,10},{4,12},{6,14},{8,16},{10,18},{12,20},{14,22},{16,24},... | collective-permute-start | bytes 393224 | tf_op jit(solution)/shard_map/ppermute | solution.py:120
  53.9 2.8 %collective-permute-start.18 = (bf16[32,2048]{1,0:T(8,128)(2,1)S(1)}, bf16[32,2048]{1,0:T(8,128)(2,1)S(1)}, u32[]{:S(2)}, u32[]{:S(2)}) collective-permute-start(bf16[32,2048]{1,0:T(8,128)(2,1)S(1)} %get-tuple-element.80), channel_id=1, source_target_pairs={{0,24},{2,26},{4,28},{6,30},{8,0},{10,2},{12,4},{14,6},{16,8},{18,... | collective-permute-start | bytes 393224 | tf_op jit(solution)/shard_map/ppermute | solution.py:120
  56.8 3.2 %mirror.3 = (bf16[8,32,2048]{2,1,0:T(8,128)(2,1)S(1)}, bf16[8,32,2048]{2,1,0:T(8,128)(2,1)S(1)}) custom-call(s32[1]{0:T(128)} %copy.16.count_ref, s32[256]{0:T(256)S(1)} %get-tuple-element.83.take_ref, s32[256]{0:T(256)S(1)} %get-tuple-element.96.put_ref, bf16[1,32,2048]{2,1,0:T(8,128)(2,1)S(1)} %bitcast.92, bf16[1,32,2048]{2,1,0:T(8,128)(2,1)S(1)} %bitcast.95, ...), custom_call_target="tpu_custom_call" | custom-call | flops 2147483648 | bytes 8650752 | tf_op jit(solution)/shard_map/mirror/pallas_call | solution.py:79
  60.0 2.3 %collective-permute-done.17 = bf16[32,2048]{1,0:T(8,128)(2,1)S(1)} collective-permute-done((bf16[32,2048]{1,0:T(8,128)(2,1)S(1)}, bf16[32,2048]{1,0:T(8,128)(2,1)S(1)}, u32[]{:S(2)}, u32[]{:S(2)}) %collective-permute-start.17) | collective-permute-done | bytes 131104 | tf_op jit(solution)/shard_map/ppermute | solution.py:120
  62.9 3.2 %collective-permute-start.22 = (bf16[32,2048]{1,0:T(8,128)(2,1)S(1)}, bf16[32,2048]{1,0:T(8,128)(2,1)S(1)}, u32[]{:S(2)}, u32[]{:S(2)}) collective-permute-start(bf16[32,2048]{1,0:T(8,128)(2,1)S(1)} %collective-permute-done.21), channel_id=1, source_target_pairs={{0,8},{2,10},{4,12},{6,14},{8,16},{10,18},{12,20},{14,22},{16,24},... | collective-permute-start | bytes 393224 | tf_op jit(solution)/shard_map/ppermute | solution.py:120
  71.2 5.0 %collective-permute-done.23 = bf16[32,2048]{1,0:T(8,128)(2,1)S(1)} collective-permute-done((bf16[32,2048]{1,0:T(8,128)(2,1)S(1)}, bf16[32,2048]{1,0:T(8,128)(2,1)S(1)}, u32[]{:S(2)}, u32[]{:S(2)}) %collective-permute-start.23) | collective-permute-done | bytes 131104 | tf_op jit(solution)/shard_map/ppermute | solution.py:120
  76.4 1.7 %collective-permute-done.26.refs_3_ = bf16[3,32,2048]{2,1,0:T(8,128)(2,1)S(1)} collective-permute-done((bf16[3,32,2048]{2,1,0:T(8,128)(2,1)S(1)}, bf16[3,32,2048]{2,1,0:T(8,128)(2,1)S(1)}, u32[]{:S(2)}, u32[]{:S(2)}) %collective-permute-start.26) | collective-permute-done | bytes 393248 | tf_op jit(solution)/shard_map/ppermute | solution.py:120
  78.1 4.3 %collective-permute-done.27 = bf16[4,32,2048]{2,1,0:T(8,128)(2,1)S(1)} collective-permute-done((bf16[4,32,2048]{2,1,0:T(8,128)(2,1)S(1)}, bf16[4,32,2048]{2,1,0:T(8,128)(2,1)S(1)}, u32[]{:S(2)}, u32[]{:S(2)}) %collective-permute-start.27) | collective-permute-done | bytes 524320 | tf_op jit(solution)/shard_map/ppermute | solution.py:120
  82.7 1.6 %collective-permute-start.28 = (bf16[32,2048]{1,0:T(8,128)(2,1)S(1)}, bf16[32,2048]{1,0:T(8,128)(2,1)S(1)}, u32[]{:S(2)}, u32[]{:S(2)}) collective-permute-start(bf16[32,2048]{1,0:T(8,128)(2,1)S(1)} %get-tuple-element.92), channel_id=1, source_target_pairs={{0,24},{2,26},{4,28},{6,30},{8,0},{10,2},{12,4},{14,6},{16,8},{18,... | collective-permute-start | bytes 393224 | tf_op jit(solution)/shard_map/ppermute | solution.py:120
  85.1 3.1 %forward.3 = (f32[1,32,2048]{2,1,0:T(8,128)S(1)}, bf16[1,32,2048]{2,1,0:T(8,128)(2,1)S(1)}) custom-call(s32[1]{0:T(128)} %copy.16.count_ref, s32[256]{0:T(256)S(1)} %get-tuple-element.97.take_ref, s32[256]{0:T(256)S(1)} %get-tuple-element.82.put_ref, bf16[5,32,2048]{2,1,0:T(8,128)(2,1)S(1)} %bitcast_dynamic-update-slice_fusion.refs_0_, ...), custom_call_target="tpu_custom_call" | custom-call | flops 2147483648 | bytes 10485760 | tf_op jit(solution)/shard_map/forward/pallas_call | solution.py:79
  89.3 6.3 %collective-permute-done.29 = bf16[32,2048]{1,0:T(8,128)(2,1)S(1)} collective-permute-done((bf16[32,2048]{1,0:T(8,128)(2,1)S(1)}, bf16[32,2048]{1,0:T(8,128)(2,1)S(1)}, u32[]{:S(2)}, u32[]{:S(2)}) %collective-permute-start.29) | collective-permute-done | bytes 131104 | tf_op jit(solution)/shard_map/ppermute | solution.py:120
  (68 shorter events, 21.0 us)
Async XLA Ops:
  1.0 11.4 %collective-permute-start.3 = (bf16[32,2048]{1,0:T(8,128)(2,1)S(1)}, bf16[32,2048]{1,0:T(8,128)(2,1)S(1)}, u32[]{:S(2)}, u32[]{:S(2)}) collective-permute-start(bf16[32,2048]{1,0:T(8,128)(2,1)S(1)} %get-tuple-element.87), channel_id=1, source_target_pairs={{0,1},{1,0},{2,3},{3,2},{4,5},{5,4},{6,7},{7,6},{8,9},{9,8},{10,11... | collective-permute-start | bytes 393224 | tf_op jit(solution)/shard_map/ppermute | solution.py:123
  4.0 11.6 %collective-permute-start = (bf16[32,2048]{1,0:T(8,128)(2,1)S(1)}, bf16[32,2048]{1,0:T(8,128)(2,1)S(1)}, u32[]{:S(2)}, u32[]{:S(2)}) collective-permute-start(bf16[32,2048]{1,0:T(8,128)(2,1)S(1)} %get-tuple-element.87), channel_id=1, source_target_pairs={{0,8},{2,10},{4,12},{6,14},{8,16},{10,18},{12,20},{14,22},{16,24},... | collective-permute-start | bytes 393224 | tf_op jit(solution)/shard_map/ppermute | solution.py:120
  5.6 11.0 %collective-permute-start.1 = (bf16[32,2048]{1,0:T(8,128)(2,1)S(1)}, bf16[32,2048]{1,0:T(8,128)(2,1)S(1)}, u32[]{:S(2)}, u32[]{:S(2)}) collective-permute-start(bf16[32,2048]{1,0:T(8,128)(2,1)S(1)} %get-tuple-element.87), channel_id=1, source_target_pairs={{0,16},{2,18},{4,20},{6,22},{8,24},{10,26},{12,28},{14,30},{16,0},... | collective-permute-start | bytes 393224 | tf_op jit(solution)/shard_map/ppermute | solution.py:120
  8.1 8.4 %collective-permute-start.2 = (bf16[32,2048]{1,0:T(8,128)(2,1)S(1)}, bf16[32,2048]{1,0:T(8,128)(2,1)S(1)}, u32[]{:S(2)}, u32[]{:S(2)}) collective-permute-start(bf16[32,2048]{1,0:T(8,128)(2,1)S(1)} %get-tuple-element.87), channel_id=1, source_target_pairs={{0,24},{2,26},{4,28},{6,30},{8,0},{10,2},{12,4},{14,6},{16,8},{18,... | collective-permute-start | bytes 393224 | tf_op jit(solution)/shard_map/ppermute | solution.py:120
  9.5 7.4 %collective-permute-start.5 = (bf16[32,2048]{1,0:T(8,128)(2,1)S(1)}, bf16[32,2048]{1,0:T(8,128)(2,1)S(1)}, u32[]{:S(2)}, u32[]{:S(2)}) collective-permute-start(bf16[32,2048]{1,0:T(8,128)(2,1)S(1)} %get-tuple-element.87), channel_id=1, source_target_pairs={{0,4},{2,6},{4,0},{6,2},{8,12},{10,14},{12,8},{14,10},{16,20},{18,... | collective-permute-start | bytes 393224 | tf_op jit(solution)/shard_map/ppermute | solution.py:120
  17.0 15.8 %collective-permute-start.9 = (bf16[5,32,2048]{2,1,0:T(8,128)(2,1)S(1)}, bf16[5,32,2048]{2,1,0:T(8,128)(2,1)S(1)}, u32[]{:S(2)}, u32[]{:S(2)}) collective-permute-start(bf16[5,32,2048]{2,1,0:T(8,128)(2,1)S(1)} %bitcast_dynamic-update-slice_fusion.4.refs_0_), channel_id=1, source_target_pairs={{0,2},{2,0},{4,6},{6,4},{8,10},{10,8},{12,14},{14,12},{16,18},{18,... | collective-permute-start | bytes 1966088 | tf_op jit(solution)/shard_map/ppermute | solution.py:120
  17.2 8.7 %collective-permute-start.6 = (bf16[32,2048]{1,0:T(8,128)(2,1)S(1)}, bf16[32,2048]{1,0:T(8,128)(2,1)S(1)}, u32[]{:S(2)}, u32[]{:S(2)}) collective-permute-start(bf16[32,2048]{1,0:T(8,128)(2,1)S(1)} %collective-permute-done.5), channel_id=1, source_target_pairs={{0,8},{2,10},{4,12},{6,14},{8,16},{10,18},{12,20},{14,22},{16,24},... | collective-permute-start | bytes 393224 | tf_op jit(solution)/shard_map/ppermute | solution.py:120
  20.5 10.5 %collective-permute-start.7 = (bf16[32,2048]{1,0:T(8,128)(2,1)S(1)}, bf16[32,2048]{1,0:T(8,128)(2,1)S(1)}, u32[]{:S(2)}, u32[]{:S(2)}) collective-permute-start(bf16[32,2048]{1,0:T(8,128)(2,1)S(1)} %collective-permute-done.5), channel_id=1, source_target_pairs={{0,16},{2,18},{4,20},{6,22},{8,24},{10,26},{12,28},{14,30},{16,0},... | collective-permute-start | bytes 393224 | tf_op jit(solution)/shard_map/ppermute | solution.py:120
  22.1 8.9 %collective-permute-start.8 = (bf16[32,2048]{1,0:T(8,128)(2,1)S(1)}, bf16[32,2048]{1,0:T(8,128)(2,1)S(1)}, u32[]{:S(2)}, u32[]{:S(2)}) collective-permute-start(bf16[32,2048]{1,0:T(8,128)(2,1)S(1)} %collective-permute-done.5), channel_id=1, source_target_pairs={{0,24},{2,26},{4,28},{6,30},{8,0},{10,2},{12,4},{14,6},{16,8},{18,... | collective-permute-start | bytes 393224 | tf_op jit(solution)/shard_map/ppermute | solution.py:120
  23.3 13.4 %collective-permute-start.11 = (bf16[4,32,2048]{2,1,0:T(8,128)(2,1)S(1)}, bf16[4,32,2048]{2,1,0:T(8,128)(2,1)S(1)}, u32[]{:S(2)}, u32[]{:S(2)}) collective-permute-start(bf16[4,32,2048]{2,1,0:T(8,128)(2,1)S(1)} %slice.109), channel_id=1, source_target_pairs={{0,4},{2,6},{4,0},{6,2},{8,12},{10,14},{12,8},{14,10},{16,20},{18,... | collective-permute-start | bytes 1572872 | tf_op jit(solution)/shard_map/ppermute | solution.py:120
  38.7 11.4 %collective-permute-start.13 = (bf16[32,2048]{1,0:T(8,128)(2,1)S(1)}, bf16[32,2048]{1,0:T(8,128)(2,1)S(1)}, u32[]{:S(2)}, u32[]{:S(2)}) collective-permute-start(bf16[32,2048]{1,0:T(8,128)(2,1)S(1)} %get-tuple-element.94), channel_id=1, source_target_pairs={{0,16},{2,18},{4,20},{6,22},{8,24},{10,26},{12,28},{14,30},{16,0},... | collective-permute-start | bytes 393224 | tf_op jit(solution)/shard_map/ppermute | solution.py:120
  39.4 10.8 %collective-permute-start.14 = (bf16[32,2048]{1,0:T(8,128)(2,1)S(1)}, bf16[32,2048]{1,0:T(8,128)(2,1)S(1)}, u32[]{:S(2)}, u32[]{:S(2)}) collective-permute-start(bf16[32,2048]{1,0:T(8,128)(2,1)S(1)} %get-tuple-element.93), channel_id=1, source_target_pairs={{0,8},{2,10},{4,12},{6,14},{8,16},{10,18},{12,20},{14,22},{16,24},... | collective-permute-start | bytes 393224 | tf_op jit(solution)/shard_map/ppermute | solution.py:120
  42.8 7.3 %collective-permute-start.15 = (bf16[32,2048]{1,0:T(8,128)(2,1)S(1)}, bf16[32,2048]{1,0:T(8,128)(2,1)S(1)}, u32[]{:S(2)}, u32[]{:S(2)}) collective-permute-start(bf16[32,2048]{1,0:T(8,128)(2,1)S(1)} %bitcast.97), channel_id=1, source_target_pairs={{0,1},{1,0},{2,3},{3,2},{4,5},{5,4},{6,7},{7,6},{8,9},{9,8},{10,11... | collective-permute-start | bytes 393224 | tf_op jit(solution)/shard_map/ppermute | solution.py:123
  50.9 9.1 %collective-permute-start.16 = (bf16[32,2048]{1,0:T(8,128)(2,1)S(1)}, bf16[32,2048]{1,0:T(8,128)(2,1)S(1)}, u32[]{:S(2)}, u32[]{:S(2)}) collective-permute-start(bf16[32,2048]{1,0:T(8,128)(2,1)S(1)} %get-tuple-element.80), channel_id=1, source_target_pairs={{0,8},{2,10},{4,12},{6,14},{8,16},{10,18},{12,20},{14,22},{16,24},... | collective-permute-start | bytes 393224 | tf_op jit(solution)/shard_map/ppermute | solution.py:120
  52.4 9.8 %collective-permute-start.17 = (bf16[32,2048]{1,0:T(8,128)(2,1)S(1)}, bf16[32,2048]{1,0:T(8,128)(2,1)S(1)}, u32[]{:S(2)}, u32[]{:S(2)}) collective-permute-start(bf16[32,2048]{1,0:T(8,128)(2,1)S(1)} %get-tuple-element.80), channel_id=1, source_target_pairs={{0,16},{2,18},{4,20},{6,22},{8,24},{10,26},{12,28},{14,30},{16,0},... | collective-permute-start | bytes 393224 | tf_op jit(solution)/shard_map/ppermute | solution.py:120
  53.9 8.3 %collective-permute-start.18 = (bf16[32,2048]{1,0:T(8,128)(2,1)S(1)}, bf16[32,2048]{1,0:T(8,128)(2,1)S(1)}, u32[]{:S(2)}, u32[]{:S(2)}) collective-permute-start(bf16[32,2048]{1,0:T(8,128)(2,1)S(1)} %get-tuple-element.80), channel_id=1, source_target_pairs={{0,24},{2,26},{4,28},{6,30},{8,0},{10,2},{12,4},{14,6},{16,8},{18,... | collective-permute-start | bytes 393224 | tf_op jit(solution)/shard_map/ppermute | solution.py:120
  62.3 15.8 %collective-permute-start.25 = (bf16[5,32,2048]{2,1,0:T(8,128)(2,1)S(1)}, bf16[5,32,2048]{2,1,0:T(8,128)(2,1)S(1)}, u32[]{:S(2)}, u32[]{:S(2)}) collective-permute-start(bf16[5,32,2048]{2,1,0:T(8,128)(2,1)S(1)} %bitcast_dynamic-update-slice_fusion.refs_0_), channel_id=1, source_target_pairs={{0,2},{2,0},{4,6},{6,4},{8,10},{10,8},{12,14},{14,12},{16,18},{18,... | collective-permute-start | bytes 1966088 | tf_op jit(solution)/shard_map/ppermute | solution.py:120
  62.9 8.3 %collective-permute-start.22 = (bf16[32,2048]{1,0:T(8,128)(2,1)S(1)}, bf16[32,2048]{1,0:T(8,128)(2,1)S(1)}, u32[]{:S(2)}, u32[]{:S(2)}) collective-permute-start(bf16[32,2048]{1,0:T(8,128)(2,1)S(1)} %collective-permute-done.21), channel_id=1, source_target_pairs={{0,8},{2,10},{4,12},{6,14},{8,16},{10,18},{12,20},{14,22},{16,24},... | collective-permute-start | bytes 393224 | tf_op jit(solution)/shard_map/ppermute | solution.py:120
  66.1 10.2 %collective-permute-start.23 = (bf16[32,2048]{1,0:T(8,128)(2,1)S(1)}, bf16[32,2048]{1,0:T(8,128)(2,1)S(1)}, u32[]{:S(2)}, u32[]{:S(2)}) collective-permute-start(bf16[32,2048]{1,0:T(8,128)(2,1)S(1)} %collective-permute-done.21), channel_id=1, source_target_pairs={{0,16},{2,18},{4,20},{6,22},{8,24},{10,26},{12,28},{14,30},{16,0},... | collective-permute-start | bytes 393224 | tf_op jit(solution)/shard_map/ppermute | solution.py:120
  67.4 8.9 %collective-permute-start.24 = (bf16[32,2048]{1,0:T(8,128)(2,1)S(1)}, bf16[32,2048]{1,0:T(8,128)(2,1)S(1)}, u32[]{:S(2)}, u32[]{:S(2)}) collective-permute-start(bf16[32,2048]{1,0:T(8,128)(2,1)S(1)} %collective-permute-done.21), channel_id=1, source_target_pairs={{0,24},{2,26},{4,28},{6,30},{8,0},{10,2},{12,4},{14,6},{16,8},{18,... | collective-permute-start | bytes 393224 | tf_op jit(solution)/shard_map/ppermute | solution.py:120
  69.3 13.1 %collective-permute-start.27 = (bf16[4,32,2048]{2,1,0:T(8,128)(2,1)S(1)}, bf16[4,32,2048]{2,1,0:T(8,128)(2,1)S(1)}, u32[]{:S(2)}, u32[]{:S(2)}) collective-permute-start(bf16[4,32,2048]{2,1,0:T(8,128)(2,1)S(1)} %slice.108), channel_id=1, source_target_pairs={{0,4},{2,6},{4,0},{6,2},{8,12},{10,14},{12,8},{14,10},{16,20},{18,... | collective-permute-start | bytes 1572872 | tf_op jit(solution)/shard_map/ppermute | solution.py:120
  84.3 11.3 %collective-permute-start.29 = (bf16[32,2048]{1,0:T(8,128)(2,1)S(1)}, bf16[32,2048]{1,0:T(8,128)(2,1)S(1)}, u32[]{:S(2)}, u32[]{:S(2)}) collective-permute-start(bf16[32,2048]{1,0:T(8,128)(2,1)S(1)} %get-tuple-element.91), channel_id=1, source_target_pairs={{0,16},{2,18},{4,20},{6,22},{8,24},{10,26},{12,28},{14,30},{16,0},... | collective-permute-start | bytes 393224 | tf_op jit(solution)/shard_map/ppermute | solution.py:120
  84.7 10.9 %collective-permute-start.30 = (bf16[32,2048]{1,0:T(8,128)(2,1)S(1)}, bf16[32,2048]{1,0:T(8,128)(2,1)S(1)}, u32[]{:S(2)}, u32[]{:S(2)}) collective-permute-start(bf16[32,2048]{1,0:T(8,128)(2,1)S(1)} %get-tuple-element.90), channel_id=1, source_target_pairs={{0,8},{2,10},{4,12},{6,14},{8,16},{10,18},{12,20},{14,22},{16,24},... | collective-permute-start | bytes 393224 | tf_op jit(solution)/shard_map/ppermute | solution.py:120
  88.2 7.4 %collective-permute-start.31 = (bf16[32,2048]{1,0:T(8,128)(2,1)S(1)}, bf16[32,2048]{1,0:T(8,128)(2,1)S(1)}, u32[]{:S(2)}, u32[]{:S(2)}) collective-permute-start(bf16[32,2048]{1,0:T(8,128)(2,1)S(1)} %bitcast.96), channel_id=1, source_target_pairs={{0,1},{1,0},{2,3},{3,2},{4,5},{5,4},{6,7},{7,6},{8,9},{9,8},{10,11... | collective-permute-start | bytes 393224 | tf_op jit(solution)/shard_map/ppermute | solution.py:123
  (9 other events, 52.9 us)

commit v2 on v1

--- a/solution.py
+++ b/solution.py
@@ -140,55 +140,67 @@
     put_cols = jnp.where(live, place_cols, n_row * per_piece)
     put_rows = jnp.where(live, place_rows, n_col * per_piece)
 
-    mirror_outputs = [[piece(a, b, c) for b in range(n_b) for a in range(n_a)] for c in range(n_c)]
+    order = list(range(1, n_a)) + [0]
+    halves = [order[: n_a // 2], order[n_a // 2 :]] if n_a > 1 else [order]
+    mirror_outputs = [[piece(a, b, c) for b in range(n_b) for a in order] for c in range(n_c)]
     forward_outputs = [[j] for j in range(n_col)]
     mirror_inputs = [[j] for j in range(n_col)]
     forward_inputs = []
     for c in range(n_c):
-        forward_inputs.append([piece(0, b, c) for b in range(n_b)] + [piece(a, 0, c) for a in range(1, n_a)])
+        forward_inputs.append([piece(a, 0, c) for a in range(n_a)])
         if n_b > 1:
-            forward_inputs.append([piece(a, b, c) for b in range(1, n_b) for a in range(1, n_a)])
+            forward_inputs.append([piece(a, b, c) for b in range(1, n_b) for a in range(n_a)])
 
     def apply_operator(narrow):
         by_col = [narrow] + [shift_col(narrow, j) for j in range(1, n_col)]
-        near = [narrow] + [shift(narrow, db=b) for b in range(1, n_b)]
-        far = [[shift(part, da=a) for a in range(1, n_a)] for part in near]
+        along_a = [shift(narrow, da=a) for a in range(1, n_a)]
+        along_b = [shift(narrow, db=b) for b in range(1, n_b)]
         mirrors = block_product(
             0, mirror_inputs, mirror_outputs, [jnp.bfloat16] * len(mirror_outputs), n_row,
             block_counts, place_rows, put_cols, by_col, block_values,
         )
-        far[0], mirrors = lax.optimization_barrier((far[0], mirrors))
+        by_col, along_a, along_b, mirrors = lax.optimization_barrier((by_col, along_a, along_b, mirrors))
 
         shares = mirrors[0].astype(jnp.float32)
         for c in range(1, n_c):
             shares += shift(mirrors[c], dc=-c).astype(jnp.float32)
-        by_b = [shares[b * n_a : (b + 1) * n_a] for b in range(n_b)]
-        others = [shift(by_b[b].astype(jnp.bfloat16), db=-b) for b in range(1, n_b)]
-
-        early = jnp.stack(near + far[0])
-        late = [part for behind in far[1:] for part in behind]
-        late = [jnp.stack(late)] if late else []
-        by_row = [early] + late
+        parts = []
+        for b in range(n_b):
+            first = b * n_a
+            for half in halves:
+                parts.append(shares[first : first + len(half)])
+                first += len(half)
+        kept = parts[: len(halves)]
+        sends = [part.astype(jnp.bfloat16) for part in parts[len(halves) :]]
+
+        early = jnp.stack([narrow] + along_a)
+        along_both = [shift(early[1:], db=b) for b in range(1, n_b)]
+        sends, along_both = lax.optimization_barrier((sends, along_both))
+        others = [shift(send, db=-(n // len(halves) + 1)) for n, send in enumerate(sends)]
+        by_row = [early]
+        if n_b > 1:
+            late = []
+            for one, rest in zip(along_b, along_both):
+                late += [one[None], rest]
+            by_row.append(jnp.concatenate(late))
         for c in range(1, n_c):
-            by_row += [shift(part, dc=c) for part in [early] + late]
-        by_row, others = lax.optimization_barrier((by_row, others))
-
-        share = by_b[0]
-        for other in others:
-            share += other.astype(jnp.float32)
-        back = [shift(share[a].astype(jnp.bfloat16), da=-a) for a in range(1, n_a)]
-
+            by_row += [shift(part, dc=c) for part in by_row[: len(by_row) // c]]
         forwards = block_product(
             1, forward_inputs, forward_outputs, [jnp.float32] + [jnp.bfloat16] * (n_col - 1), n_col,
             block_counts, place_cols, put_rows, by_row, block_values,
         )
-        back, own = lax.optimization_barrier((back, forwards[0]))
+        others, own = lax.optimization_barrier((others, forwards[0]))
+
+        mirror_sum = 0.0
+        for h, half in enumerate(halves):
+            share = kept[h]
+            for other in others[h :: len(halves)]:
+                share += other.astype(jnp.float32)
+            for n, a in enumerate(half):
+                mirror_sum += shift(share[n].astype(jnp.bfloat16), da=-a).astype(jnp.float32) if a else share[n]
         forward_sum = own[0]
         for j in range(1, n_col):
             forward_sum += shift_col(forwards[j][0], -j).astype(jnp.float32)
-        mirror_sum = share[0]
-        for other in back:
-            mirror_sum += other.astype(jnp.float32)
         return forward_sum + mirror_sum
 
     current = (apply_operator(vectors.astype(jnp.bfloat16)) - center_value * vectors) / radius_value

time: 97.5 us -> 113 us (1.16)
  Pallas kernels: 12.5 us -> 21.5 us
  waiting for transfers between devices: 39.1 us -> 46.5 us
  starting transfers between devices: 38.5 us -> 36.3 us
  other arithmetic: 3.8 us -> 5.07 us
    pallas_call x4, Pallas kernels: 12.5 us -> 21.5 us  [block_product(): pl.pallas_call(functools.partial(product_kernel, contract, inputs, output...]
    ppermute x28 -> x26, waiting for transfers between devices: 39.1 us -> 46.5 us  [shift(): return lax.ppermute(value, 'row', pairs)]
    ppermute x28 -> x26, starting transfers between devices: 33.8 us -> 28.6 us  [shift(): return lax.ppermute(value, 'row', pairs)]
    ppermute x4, starting transfers between devices: 4.8 us -> 7.72 us  [shift_col(): lax.ppermute(value, 'col', [(j, (j + d) % n_col) for j in range(n_col)])]
  transfers between devices with their start and end apart: 32 -> 30, of which waited for: 12 -> 13; matrix products, arithmetic and copies ran while one was open for 2% -> 3% of each run, Pallas kernels for 13% -> 19%
where the time goes in v2:
time: 113 us; the launch traced here: 112 us
  waiting for transfers between devices  46.5 us (41%)
  starting transfers between devices  36.3 us (32%)
  Pallas kernels  21.5 us (19%)
  other arithmetic  5.07 us (4%)
  between operations  2.23 us (2%)
    ppermute x26, waiting for transfers between devices, shift(): return lax.ppermute(value, 'row', pairs)  46.5 us
    ppermute x26, starting transfers between devices, shift(): return lax.ppermute(value, 'row', pairs)  28.6 us
    pallas_call x4, Pallas kernels, block_product(): pl.pallas_call(functools.partial(product_kernel, contract, inputs, output...  21.5 us
    ppermute x4, starting transfers between devices, shift_col(): lax.ppermute(value, 'col', [(j, (j + d) % n_col) for j in range(n_col)])  7.72 us
  transfers between devices with their start and end apart: 30, of which 13 were waited for; matrix products, arithmetic and copies ran while one was open for 3% of the time, Pallas kernels for 19%

profile of v2, /device:TPU:0, one launch (start us, length us, event | category | flops | bytes accessed | tf_op | source)
XLA Modules:
  0.0 111.8 jit_solution(18203483493806441978)
XLA Ops:
  1.0 3.0 %collective-permute-start = (bf16[32,2048]{1,0:T(8,128)(2,1)S(1)}, bf16[32,2048]{1,0:T(8,128)(2,1)S(1)}, u32[]{:S(2)}, u32[]{:S(2)}) collective-permute-start(bf16[32,2048]{1,0:T(8,128)(2,1)S(1)} %convert_element_type.82), channel_id=1, source_target_pairs={{0,1},{1,0},{2,3},{3,2},{4,5},{5,4},{6,7},{7,6},{8,9},{9,8},{10,11... | collective-permute-start | bytes 393224 | tf_op jit(solution)/shard_map/ppermute | solution.py:123
  5.5 2.6 %collective-permute-start.2 = (bf16[32,2048]{1,0:T(8,128)(2,1)S(1)}, bf16[32,2048]{1,0:T(8,128)(2,1)S(1)}, u32[]{:S(2)}, u32[]{:S(2)}) collective-permute-start(bf16[32,2048]{1,0:T(8,128)(2,1)S(1)} %convert_element_type.82), channel_id=1, source_target_pairs={{0,16},{2,18},{4,20},{6,22},{8,24},{10,26},{12,28},{14,30},{16,0},... | collective-permute-start | bytes 393224 | tf_op jit(solution)/shard_map/ppermute | solution.py:120
  13.4 5.4 %mirror.2 = (bf16[8,32,2048]{2,1,0:T(8,128)(2,1)S(1)}, bf16[8,32,2048]{2,1,0:T(8,128)(2,1)S(1)}) custom-call(s32[1]{0:T(128)} %copy.8.count_ref, s32[256]{0:T(256)S(1)} %get-tuple-element.72.take_ref, s32[256]{0:T(256)S(1)} %get-tuple-element.91.put_ref, bf16[1,32,2048]{2,1,0:T(8,128)(2,1)S(1)} %convert_bitcast_fusion.refs_0_, ...), custom_call_target="tpu_custom_call" | custom-call | flops 2147483648 | bytes 8650752 | tf_op jit(solution)/shard_map/mirror/pallas_call | solution.py:79
  19.7 1.9 %collective-permute-done.5 = bf16[8,32,2048]{2,1,0:T(8,128)(2,1)S(1)} collective-permute-done((bf16[8,32,2048]{2,1,0:T(8,128)(2,1)S(1)}, bf16[8,32,2048]{2,1,0:T(8,128)(2,1)S(1)}, u32[]{:S(2)}, u32[]{:S(2)}) %collective-permute-start.5) | collective-permute-done | bytes 1048608 | tf_op jit(solution)/shard_map/ppermute | solution.py:120
  22.0 8.5 %collective-permute-done.6 = bf16[3,32,2048]{2,1,0:T(8,128)(2,1)S(1)} collective-permute-done((bf16[3,32,2048]{2,1,0:T(8,128)(2,1)S(1)}, bf16[3,32,2048]{2,1,0:T(8,128)(2,1)S(1)}, u32[]{:S(2)}, u32[]{:S(2)}) %collective-permute-start.6) | collective-permute-done | bytes 393248 | tf_op jit(solution)/shard_map/ppermute | solution.py:120
  31.0 1.7 %collective-permute-start.8 = (bf16[2,32,2048]{2,1,0:T(8,128)(2,1)S(1)}, bf16[2,32,2048]{2,1,0:T(8,128)(2,1)S(1)}, u32[]{:S(2)}, u32[]{:S(2)}) collective-permute-start(bf16[2,32,2048]{2,1,0:T(8,128)(2,1)S(1)} %get-tuple-element.45), channel_id=1, source_target_pairs={{0,4},{2,6},{4,0},{6,2},{8,12},{10,14},{12,8},{14,10},{16,20},{18,... | collective-permute-start | bytes 786440 | tf_op jit(solution)/shard_map/ppermute | solution.py:120
  32.8 5.4 %forward.2 = (f32[1,32,2048]{2,1,0:T(8,128)S(1)}, bf16[1,32,2048]{2,1,0:T(8,128)(2,1)S(1)}) custom-call(s32[1]{0:T(128)} %copy.8.count_ref, s32[256]{0:T(256)S(1)} %get-tuple-element.92.take_ref, s32[256]{0:T(256)S(1)} %get-tuple-element.71.put_ref, bf16[4,32,2048]{2,1,0:T(8,128)(2,1)S(1)} %pad_maximum_fusion.refs_0_, ...), custom_call_target="tpu_custom_call" | custom-call | flops 2147483648 | bytes 10485760 | tf_op jit(solution)/shard_map/forward/pallas_call | solution.py:79
  38.2 1.7 %collective-permute-done.7 = bf16[2,32,2048]{2,1,0:T(8,128)(2,1)S(1)} collective-permute-done((bf16[2,32,2048]{2,1,0:T(8,128)(2,1)S(1)}, bf16[2,32,2048]{2,1,0:T(8,128)(2,1)S(1)}, u32[]{:S(2)}, u32[]{:S(2)}) %collective-permute-start.7) | collective-permute-done | bytes 262176 | tf_op jit(solution)/shard_map/ppermute | solution.py:120
  39.8 5.2 %collective-permute-done.8 = bf16[2,32,2048]{2,1,0:T(8,128)(2,1)S(1)} collective-permute-done((bf16[2,32,2048]{2,1,0:T(8,128)(2,1)S(1)}, bf16[2,32,2048]{2,1,0:T(8,128)(2,1)S(1)}, u32[]{:S(2)}, u32[]{:S(2)}) %collective-permute-start.8) | collective-permute-done | bytes 262176 | tf_op jit(solution)/shard_map/ppermute | solution.py:120
  46.2 1.7 %collective-permute-start.13 = (bf16[32,2048]{1,0:T(8,128)(2,1)S(1)}, bf16[32,2048]{1,0:T(8,128)(2,1)S(1)}, u32[]{:S(2)}, u32[]{:S(2)}) collective-permute-start(bf16[32,2048]{1,0:T(8,128)(2,1)S(1)} %get-tuple-element.90), channel_id=1, source_target_pairs={{0,16},{2,18},{4,20},{6,22},{8,24},{10,26},{12,28},{14,30},{16,0},... | collective-permute-start | bytes 393224 | tf_op jit(solution)/shard_map/ppermute | solution.py:120
  49.2 1.7 %collective-permute-start.11 = (bf16[32,2048]{1,0:T(8,128)(2,1)S(1)}, bf16[32,2048]{1,0:T(8,128)(2,1)S(1)}, u32[]{:S(2)}, u32[]{:S(2)}) collective-permute-start(bf16[32,2048]{1,0:T(8,128)(2,1)S(1)} %bitcast.74), channel_id=1, source_target_pairs={{0,1},{1,0},{2,3},{3,2},{4,5},{5,4},{6,7},{7,6},{8,9},{9,8},{10,11... | collective-permute-start | bytes 393224 | tf_op jit(solution)/shard_map/ppermute | solution.py:123
  53.5 4.3 %collective-permute-done.13 = bf16[32,2048]{1,0:T(8,128)(2,1)S(1)} collective-permute-done((bf16[32,2048]{1,0:T(8,128)(2,1)S(1)}, bf16[32,2048]{1,0:T(8,128)(2,1)S(1)}, u32[]{:S(2)}, u32[]{:S(2)}) %collective-permute-start.13) | collective-permute-done | bytes 131104 | tf_op jit(solution)/shard_map/ppermute | solution.py:120
  57.9 1.8 %collective-permute-start.15 = (bf16[32,2048]{1,0:T(8,128)(2,1)S(1)}, bf16[32,2048]{1,0:T(8,128)(2,1)S(1)}, u32[]{:S(2)}, u32[]{:S(2)}) collective-permute-start(bf16[32,2048]{1,0:T(8,128)(2,1)S(1)} %get-tuple-element.69), channel_id=1, source_target_pairs={{0,1},{1,0},{2,3},{3,2},{4,5},{5,4},{6,7},{7,6},{8,9},{9,8},{10,11... | collective-permute-start | bytes 393224 | tf_op jit(solution)/shard_map/ppermute | solution.py:123
  59.7 2.4 %collective-permute-start.16 = (bf16[32,2048]{1,0:T(8,128)(2,1)S(1)}, bf16[32,2048]{1,0:T(8,128)(2,1)S(1)}, u32[]{:S(2)}, u32[]{:S(2)}) collective-permute-start(bf16[32,2048]{1,0:T(8,128)(2,1)S(1)} %get-tuple-element.69), channel_id=1, source_target_pairs={{0,8},{2,10},{4,12},{6,14},{8,16},{10,18},{12,20},{14,22},{16,24},... | collective-permute-start | bytes 393224 | tf_op jit(solution)/shard_map/ppermute | solution.py:120
  62.5 2.0 %collective-permute-start.18 = (bf16[32,2048]{1,0:T(8,128)(2,1)S(1)}, bf16[32,2048]{1,0:T(8,128)(2,1)S(1)}, u32[]{:S(2)}, u32[]{:S(2)}) collective-permute-start(bf16[32,2048]{1,0:T(8,128)(2,1)S(1)} %get-tuple-element.69), channel_id=1, source_target_pairs={{0,24},{2,26},{4,28},{6,30},{8,0},{10,2},{12,4},{14,6},{16,8},{18,... | collective-permute-start | bytes 393224 | tf_op jit(solution)/shard_map/ppermute | solution.py:120
  65.5 5.4 %mirror.3 = (bf16[8,32,2048]{2,1,0:T(8,128)(2,1)S(1)}, bf16[8,32,2048]{2,1,0:T(8,128)(2,1)S(1)}) custom-call(s32[1]{0:T(128)} %copy.8.count_ref, s32[256]{0:T(256)S(1)} %get-tuple-element.72.take_ref, s32[256]{0:T(256)S(1)} %get-tuple-element.91.put_ref, bf16[1,32,2048]{2,1,0:T(8,128)(2,1)S(1)} %bitcast.69, bf16[1,32,2048]{2,1,0:T(8,128)(2,1)S(1)} %bitcast.72, ...), custom_call_target="tpu_custom_call" | custom-call | flops 2147483648 | bytes 8650752 | tf_op jit(solution)/shard_map/mirror/pallas_call | solution.py:79
  74.7 8.5 %collective-permute-done.21 = bf16[3,32,2048]{2,1,0:T(8,128)(2,1)S(1)} collective-permute-done((bf16[3,32,2048]{2,1,0:T(8,128)(2,1)S(1)}, bf16[3,32,2048]{2,1,0:T(8,128)(2,1)S(1)}, u32[]{:S(2)}, u32[]{:S(2)}) %collective-permute-start.21) | collective-permute-done | bytes 393248 | tf_op jit(solution)/shard_map/ppermute | solution.py:120
  85.4 5.4 %forward.3 = (f32[1,32,2048]{2,1,0:T(8,128)S(1)}, bf16[1,32,2048]{2,1,0:T(8,128)(2,1)S(1)}) custom-call(s32[1]{0:T(128)} %copy.8.count_ref, s32[256]{0:T(256)S(1)} %get-tuple-element.92.take_ref, s32[256]{0:T(256)S(1)} %get-tuple-element.71.put_ref, bf16[4,32,2048]{2,1,0:T(8,128)(2,1)S(1)} %pad_maximum_fusion.2.refs_0_, ...), custom_call_target="tpu_custom_call" | custom-call | flops 2147483648 | bytes 10485760 | tf_op jit(solution)/shard_map/forward/pallas_call | solution.py:79
  90.8 1.7 %collective-permute-done.22 = bf16[2,32,2048]{2,1,0:T(8,128)(2,1)S(1)} collective-permute-done((bf16[2,32,2048]{2,1,0:T(8,128)(2,1)S(1)}, bf16[2,32,2048]{2,1,0:T(8,128)(2,1)S(1)}, u32[]{:S(2)}, u32[]{:S(2)}) %collective-permute-start.22) | collective-permute-done | bytes 262176 | tf_op jit(solution)/shard_map/ppermute | solution.py:120
  92.5 5.2 %collective-permute-done.23 = bf16[2,32,2048]{2,1,0:T(8,128)(2,1)S(1)} collective-permute-done((bf16[2,32,2048]{2,1,0:T(8,128)(2,1)S(1)}, bf16[2,32,2048]{2,1,0:T(8,128)(2,1)S(1)}, u32[]{:S(2)}, u32[]{:S(2)}) %collective-permute-start.23) | collective-permute-done | bytes 262176 | tf_op jit(solution)/shard_map/ppermute | solution.py:120
  97.8 3.0 %collective-permute-start.29 = (bf16[32,2048]{1,0:T(8,128)(2,1)S(1)}, bf16[32,2048]{1,0:T(8,128)(2,1)S(1)}, u32[]{:S(2)}, u32[]{:S(2)}) collective-permute-start(bf16[32,2048]{1,0:T(8,128)(2,1)S(1)} %fusion.13), channel_id=1, source_target_pairs={{0,8},{2,10},{4,12},{6,14},{8,16},{10,18},{12,20},{14,22},{16,24},... | collective-permute-start | bytes 393224 | tf_op jit(solution)/shard_map/ppermute | solution.py:120
  100.8 1.7 %collective-permute-start.28 = (bf16[32,2048]{1,0:T(8,128)(2,1)S(1)}, bf16[32,2048]{1,0:T(8,128)(2,1)S(1)}, u32[]{:S(2)}, u32[]{:S(2)}) collective-permute-start(bf16[32,2048]{1,0:T(8,128)(2,1)S(1)} %get-tuple-element.88), channel_id=1, source_target_pairs={{0,16},{2,18},{4,20},{6,22},{8,24},{10,26},{12,28},{14,30},{16,0},... | collective-permute-start | bytes 393224 | tf_op jit(solution)/shard_map/ppermute | solution.py:120
  104.6 1.8 %collective-permute-done.29 = bf16[32,2048]{1,0:T(8,128)(2,1)S(1)} collective-permute-done((bf16[32,2048]{1,0:T(8,128)(2,1)S(1)}, bf16[32,2048]{1,0:T(8,128)(2,1)S(1)}, u32[]{:S(2)}, u32[]{:S(2)}) %collective-permute-start.29) | collective-permute-done | bytes 131104 | tf_op jit(solution)/shard_map/ppermute | solution.py:120
  106.3 4.6 %collective-permute-done.28 = bf16[32,2048]{1,0:T(8,128)(2,1)S(1)} collective-permute-done((bf16[32,2048]{1,0:T(8,128)(2,1)S(1)}, bf16[32,2048]{1,0:T(8,128)(2,1)S(1)}, u32[]{:S(2)}, u32[]{:S(2)}) %collective-permute-start.28) | collective-permute-done | bytes 131104 | tf_op jit(solution)/shard_map/ppermute | solution.py:120
  (63 shorter events, 23.3 us)
Async XLA Ops:
  1.0 12.4 %collective-permute-start = (bf16[32,2048]{1,0:T(8,128)(2,1)S(1)}, bf16[32,2048]{1,0:T(8,128)(2,1)S(1)}, u32[]{:S(2)}, u32[]{:S(2)}) collective-permute-start(bf16[32,2048]{1,0:T(8,128)(2,1)S(1)} %convert_element_type.82), channel_id=1, source_target_pairs={{0,1},{1,0},{2,3},{3,2},{4,5},{5,4},{6,7},{7,6},{8,9},{9,8},{10,11... | collective-permute-start | bytes 393224 | tf_op jit(solution)/shard_map/ppermute | solution.py:123
  4.0 14.8 %collective-permute-start.1 = (bf16[32,2048]{1,0:T(8,128)(2,1)S(1)}, bf16[32,2048]{1,0:T(8,128)(2,1)S(1)}, u32[]{:S(2)}, u32[]{:S(2)}) collective-permute-start(bf16[32,2048]{1,0:T(8,128)(2,1)S(1)} %convert_element_type.82), channel_id=1, source_target_pairs={{0,8},{2,10},{4,12},{6,14},{8,16},{10,18},{12,20},{14,22},{16,24},... | collective-permute-start | bytes 393224 | tf_op jit(solution)/shard_map/ppermute | solution.py:120
  5.5 13.2 %collective-permute-start.2 = (bf16[32,2048]{1,0:T(8,128)(2,1)S(1)}, bf16[32,2048]{1,0:T(8,128)(2,1)S(1)}, u32[]{:S(2)}, u32[]{:S(2)}) collective-permute-start(bf16[32,2048]{1,0:T(8,128)(2,1)S(1)} %convert_element_type.82), channel_id=1, source_target_pairs={{0,16},{2,18},{4,20},{6,22},{8,24},{10,26},{12,28},{14,30},{16,0},... | collective-permute-start | bytes 393224 | tf_op jit(solution)/shard_map/ppermute | solution.py:120
  8.1 10.7 %collective-permute-start.3 = (bf16[32,2048]{1,0:T(8,128)(2,1)S(1)}, bf16[32,2048]{1,0:T(8,128)(2,1)S(1)}, u32[]{:S(2)}, u32[]{:S(2)}) collective-permute-start(bf16[32,2048]{1,0:T(8,128)(2,1)S(1)} %convert_element_type.82), channel_id=1, source_target_pairs={{0,24},{2,26},{4,28},{6,30},{8,0},{10,2},{12,4},{14,6},{16,8},{18,... | collective-permute-start | bytes 393224 | tf_op jit(solution)/shard_map/ppermute | solution.py:120
  9.5 9.3 %collective-permute-start.4 = (bf16[32,2048]{1,0:T(8,128)(2,1)S(1)}, bf16[32,2048]{1,0:T(8,128)(2,1)S(1)}, u32[]{:S(2)}, u32[]{:S(2)}) collective-permute-start(bf16[32,2048]{1,0:T(8,128)(2,1)S(1)} %convert_element_type.82), channel_id=1, source_target_pairs={{0,4},{2,6},{4,0},{6,2},{8,12},{10,14},{12,8},{14,10},{16,20},{18,... | collective-permute-start | bytes 393224 | tf_op jit(solution)/shard_map/ppermute | solution.py:120
  19.0 11.6 %collective-permute-start.6 = (bf16[3,32,2048]{2,1,0:T(8,128)(2,1)S(1)}, bf16[3,32,2048]{2,1,0:T(8,128)(2,1)S(1)}, u32[]{:S(2)}, u32[]{:S(2)}) collective-permute-start(bf16[3,32,2048]{2,1,0:T(8,128)(2,1)S(1)} %pad_maximum_fusion.4), channel_id=1, source_target_pairs={{0,4},{2,6},{4,0},{6,2},{8,12},{10,14},{12,8},{14,10},{16,20},{18,... | collective-permute-start | bytes 1179656 | tf_op jit(solution)/shard_map/ppermute | solution.py:120
  19.1 13.6 %collective-permute-start.9 = (bf16[4,32,2048]{2,1,0:T(8,128)(2,1)S(1)}, bf16[4,32,2048]{2,1,0:T(8,128)(2,1)S(1)}, u32[]{:S(2)}, u32[]{:S(2)}) collective-permute-start(bf16[4,32,2048]{2,1,0:T(8,128)(2,1)S(1)} %pad_maximum_fusion.refs_0_), channel_id=1, source_target_pairs={{0,2},{2,0},{4,6},{6,4},{8,10},{10,8},{12,14},{14,12},{16,18},{18,... | collective-permute-start | bytes 1572872 | tf_op jit(solution)/shard_map/ppermute | solution.py:120
  30.7 9.2 %collective-permute-start.7 = (bf16[2,32,2048]{2,1,0:T(8,128)(2,1)S(1)}, bf16[2,32,2048]{2,1,0:T(8,128)(2,1)S(1)}, u32[]{:S(2)}, u32[]{:S(2)}) collective-permute-start(bf16[2,32,2048]{2,1,0:T(8,128)(2,1)S(1)} %get-tuple-element.44), channel_id=1, source_target_pairs={{0,4},{2,6},{4,0},{6,2},{8,12},{10,14},{12,8},{14,10},{16,20},{18,... | collective-permute-start | bytes 786440 | tf_op jit(solution)/shard_map/ppermute | solution.py:120
  31.0 14.0 %collective-permute-start.8 = (bf16[2,32,2048]{2,1,0:T(8,128)(2,1)S(1)}, bf16[2,32,2048]{2,1,0:T(8,128)(2,1)S(1)}, u32[]{:S(2)}, u32[]{:S(2)}) collective-permute-start(bf16[2,32,2048]{2,1,0:T(8,128)(2,1)S(1)} %get-tuple-element.45), channel_id=1, source_target_pairs={{0,4},{2,6},{4,0},{6,2},{8,12},{10,14},{12,8},{14,10},{16,20},{18,... | collective-permute-start | bytes 786440 | tf_op jit(solution)/shard_map/ppermute | solution.py:120
  45.2 8.3 %collective-permute-start.14 = (bf16[32,2048]{1,0:T(8,128)(2,1)S(1)}, bf16[32,2048]{1,0:T(8,128)(2,1)S(1)}, u32[]{:S(2)}, u32[]{:S(2)}) collective-permute-start(bf16[32,2048]{1,0:T(8,128)(2,1)S(1)} %fusion.12), channel_id=1, source_target_pairs={{0,8},{2,10},{4,12},{6,14},{8,16},{10,18},{12,20},{14,22},{16,24},... | collective-permute-start | bytes 393224 | tf_op jit(solution)/shard_map/ppermute | solution.py:120
  46.2 11.6 %collective-permute-start.13 = (bf16[32,2048]{1,0:T(8,128)(2,1)S(1)}, bf16[32,2048]{1,0:T(8,128)(2,1)S(1)}, u32[]{:S(2)}, u32[]{:S(2)}) collective-permute-start(bf16[32,2048]{1,0:T(8,128)(2,1)S(1)} %get-tuple-element.90), channel_id=1, source_target_pairs={{0,16},{2,18},{4,20},{6,22},{8,24},{10,26},{12,28},{14,30},{16,0},... | collective-permute-start | bytes 393224 | tf_op jit(solution)/shard_map/ppermute | solution.py:120
  47.8 10.0 %collective-permute-start.12 = (bf16[32,2048]{1,0:T(8,128)(2,1)S(1)}, bf16[32,2048]{1,0:T(8,128)(2,1)S(1)}, u32[]{:S(2)}, u32[]{:S(2)}) collective-permute-start(bf16[32,2048]{1,0:T(8,128)(2,1)S(1)} %get-tuple-element.89), channel_id=1, source_target_pairs={{0,24},{2,26},{4,28},{6,30},{8,0},{10,2},{12,4},{14,6},{16,8},{18,... | collective-permute-start | bytes 393224 | tf_op jit(solution)/shard_map/ppermute | solution.py:120
  49.2 8.6 %collective-permute-start.11 = (bf16[32,2048]{1,0:T(8,128)(2,1)S(1)}, bf16[32,2048]{1,0:T(8,128)(2,1)S(1)}, u32[]{:S(2)}, u32[]{:S(2)}) collective-permute-start(bf16[32,2048]{1,0:T(8,128)(2,1)S(1)} %bitcast.74), channel_id=1, source_target_pairs={{0,1},{1,0},{2,3},{3,2},{4,5},{5,4},{6,7},{7,6},{8,9},{9,8},{10,11... | collective-permute-start | bytes 393224 | tf_op jit(solution)/shard_map/ppermute | solution.py:123
  59.7 11.2 %collective-permute-start.16 = (bf16[32,2048]{1,0:T(8,128)(2,1)S(1)}, bf16[32,2048]{1,0:T(8,128)(2,1)S(1)}, u32[]{:S(2)}, u32[]{:S(2)}) collective-permute-start(bf16[32,2048]{1,0:T(8,128)(2,1)S(1)} %get-tuple-element.69), channel_id=1, source_target_pairs={{0,8},{2,10},{4,12},{6,14},{8,16},{10,18},{12,20},{14,22},{16,24},... | collective-permute-start | bytes 393224 | tf_op jit(solution)/shard_map/ppermute | solution.py:120
  62.1 9.4 %collective-permute-start.17 = (bf16[32,2048]{1,0:T(8,128)(2,1)S(1)}, bf16[32,2048]{1,0:T(8,128)(2,1)S(1)}, u32[]{:S(2)}, u32[]{:S(2)}) collective-permute-start(bf16[32,2048]{1,0:T(8,128)(2,1)S(1)} %get-tuple-element.69), channel_id=1, source_target_pairs={{0,16},{2,18},{4,20},{6,22},{8,24},{10,26},{12,28},{14,30},{16,0},... | collective-permute-start | bytes 393224 | tf_op jit(solution)/shard_map/ppermute | solution.py:120
  62.5 9.0 %collective-permute-start.18 = (bf16[32,2048]{1,0:T(8,128)(2,1)S(1)}, bf16[32,2048]{1,0:T(8,128)(2,1)S(1)}, u32[]{:S(2)}, u32[]{:S(2)}) collective-permute-start(bf16[32,2048]{1,0:T(8,128)(2,1)S(1)} %get-tuple-element.69), channel_id=1, source_target_pairs={{0,24},{2,26},{4,28},{6,30},{8,0},{10,2},{12,4},{14,6},{16,8},{18,... | collective-permute-start | bytes 393224 | tf_op jit(solution)/shard_map/ppermute | solution.py:120
  71.6 11.6 %collective-permute-start.21 = (bf16[3,32,2048]{2,1,0:T(8,128)(2,1)S(1)}, bf16[3,32,2048]{2,1,0:T(8,128)(2,1)S(1)}, u32[]{:S(2)}, u32[]{:S(2)}) collective-permute-start(bf16[3,32,2048]{2,1,0:T(8,128)(2,1)S(1)} %pad_maximum_fusion.5), channel_id=1, source_target_pairs={{0,4},{2,6},{4,0},{6,2},{8,12},{10,14},{12,8},{14,10},{16,20},{18,... | collective-permute-start | bytes 1179656 | tf_op jit(solution)/shard_map/ppermute | solution.py:120
  72.6 12.8 %collective-permute-start.24 = (bf16[4,32,2048]{2,1,0:T(8,128)(2,1)S(1)}, bf16[4,32,2048]{2,1,0:T(8,128)(2,1)S(1)}, u32[]{:S(2)}, u32[]{:S(2)}) collective-permute-start(bf16[4,32,2048]{2,1,0:T(8,128)(2,1)S(1)} %pad_maximum_fusion.2.refs_0_), channel_id=1, source_target_pairs={{0,2},{2,0},{4,6},{6,4},{8,10},{10,8},{12,14},{14,12},{16,18},{18,... | collective-permute-start | bytes 1572872 | tf_op jit(solution)/shard_map/ppermute | solution.py:120
  83.3 9.2 %collective-permute-start.22 = (bf16[2,32,2048]{2,1,0:T(8,128)(2,1)S(1)}, bf16[2,32,2048]{2,1,0:T(8,128)(2,1)S(1)}, u32[]{:S(2)}, u32[]{:S(2)}) collective-permute-start(bf16[2,32,2048]{2,1,0:T(8,128)(2,1)S(1)} %get-tuple-element.60), channel_id=1, source_target_pairs={{0,4},{2,6},{4,0},{6,2},{8,12},{10,14},{12,8},{14,10},{16,20},{18,... | collective-permute-start | bytes 786440 | tf_op jit(solution)/shard_map/ppermute | solution.py:120
  84.3 13.4 %collective-permute-start.23 = (bf16[2,32,2048]{2,1,0:T(8,128)(2,1)S(1)}, bf16[2,32,2048]{2,1,0:T(8,128)(2,1)S(1)}, u32[]{:S(2)}, u32[]{:S(2)}) collective-permute-start(bf16[2,32,2048]{2,1,0:T(8,128)(2,1)S(1)} %get-tuple-element.61), channel_id=1, source_target_pairs={{0,4},{2,6},{4,0},{6,2},{8,12},{10,14},{12,8},{14,10},{16,20},{18,... | collective-permute-start | bytes 786440 | tf_op jit(solution)/shard_map/ppermute | solution.py:120
  97.8 8.5 %collective-permute-start.29 = (bf16[32,2048]{1,0:T(8,128)(2,1)S(1)}, bf16[32,2048]{1,0:T(8,128)(2,1)S(1)}, u32[]{:S(2)}, u32[]{:S(2)}) collective-permute-start(bf16[32,2048]{1,0:T(8,128)(2,1)S(1)} %fusion.13), channel_id=1, source_target_pairs={{0,8},{2,10},{4,12},{6,14},{8,16},{10,18},{12,20},{14,22},{16,24},... | collective-permute-start | bytes 393224 | tf_op jit(solution)/shard_map/ppermute | solution.py:120
  100.8 10.1 %collective-permute-start.28 = (bf16[32,2048]{1,0:T(8,128)(2,1)S(1)}, bf16[32,2048]{1,0:T(8,128)(2,1)S(1)}, u32[]{:S(2)}, u32[]{:S(2)}) collective-permute-start(bf16[32,2048]{1,0:T(8,128)(2,1)S(1)} %get-tuple-element.88), channel_id=1, source_target_pairs={{0,16},{2,18},{4,20},{6,22},{8,24},{10,26},{12,28},{14,30},{16,0},... | collective-permute-start | bytes 393224 | tf_op jit(solution)/shard_map/ppermute | solution.py:120
  102.5 8.4 %collective-permute-start.27 = (bf16[32,2048]{1,0:T(8,128)(2,1)S(1)}, bf16[32,2048]{1,0:T(8,128)(2,1)S(1)}, u32[]{:S(2)}, u32[]{:S(2)}) collective-permute-start(bf16[32,2048]{1,0:T(8,128)(2,1)S(1)} %get-tuple-element.87), channel_id=1, source_target_pairs={{0,24},{2,26},{4,28},{6,30},{8,0},{10,2},{12,4},{14,6},{16,8},{18,... | collective-permute-start | bytes 393224 | tf_op jit(solution)/shard_map/ppermute | solution.py:120
  103.3 7.7 %collective-permute-start.26 = (bf16[32,2048]{1,0:T(8,128)(2,1)S(1)}, bf16[32,2048]{1,0:T(8,128)(2,1)S(1)}, u32[]{:S(2)}, u32[]{:S(2)}) collective-permute-start(bf16[32,2048]{1,0:T(8,128)(2,1)S(1)} %bitcast.73), channel_id=1, source_target_pairs={{0,1},{1,0},{2,3},{3,2},{4,5},{5,4},{6,7},{7,6},{8,9},{9,8},{10,11... | collective-permute-start | bytes 393224 | tf_op jit(solution)/shard_map/ppermute | solution.py:123
  (7 other events, 44.0 us)

commit v3 on v2

--- a/solution.py
+++ b/solution.py
@@ -145,21 +145,19 @@
     mirror_outputs = [[piece(a, b, c) for b in range(n_b) for a in order] for c in range(n_c)]
     forward_outputs = [[j] for j in range(n_col)]
     mirror_inputs = [[j] for j in range(n_col)]
-    forward_inputs = []
-    for c in range(n_c):
-        forward_inputs.append([piece(a, 0, c) for a in range(n_a)])
-        if n_b > 1:
-            forward_inputs.append([piece(a, b, c) for b in range(1, n_b) for a in range(n_a)])
+    chip = [(0, b) for b in range(n_b)] + [(a, b) for b in range(n_b) for a in range(1, n_a)]
+    forward_inputs = [[piece(a, b, c) for a, b in chip] for c in range(n_c)]
 
     def apply_operator(narrow):
         by_col = [narrow] + [shift_col(narrow, j) for j in range(1, n_col)]
-        along_a = [shift(narrow, da=a) for a in range(1, n_a)]
-        along_b = [shift(narrow, db=b) for b in range(1, n_b)]
+        near = [narrow] + [shift(narrow, db=b) for b in range(1, n_b)]
+        far = [shift(narrow, da=a) for a in range(1, n_a)]
         mirrors = block_product(
             0, mirror_inputs, mirror_outputs, [jnp.bfloat16] * len(mirror_outputs), n_row,
             block_counts, place_rows, put_cols, by_col, block_values,
         )
-        by_col, along_a, along_b, mirrors = lax.optimization_barrier((by_col, along_a, along_b, mirrors))
+        by_col, far, near, mirrors = lax.optimization_barrier((by_col, far, near, mirrors))
+        far_b = [shift(part, da=a) for part in near[1:] for a in range(1, n_a)]
 
         shares = mirrors[0].astype(jnp.float32)
         for c in range(1, n_c):
@@ -171,36 +169,38 @@
                 parts.append(shares[first : first + len(half)])
                 first += len(half)
         kept = parts[: len(halves)]
-        sends = [part.astype(jnp.bfloat16) for part in parts[len(halves) :]]
-
-        early = jnp.stack([narrow] + along_a)
-        along_both = [shift(early[1:], db=b) for b in range(1, n_b)]
-        sends, along_both = lax.optimization_barrier((sends, along_both))
-        others = [shift(send, db=-(n // len(halves) + 1)) for n, send in enumerate(sends)]
-        by_row = [early]
-        if n_b > 1:
-            late = []
-            for one, rest in zip(along_b, along_both):
-                late += [one[None], rest]
-            by_row.append(jnp.concatenate(late))
-        for c in range(1, n_c):
-            by_row += [shift(part, dc=c) for part in by_row[: len(by_row) // c]]
+        others = [
+            shift(part.astype(jnp.bfloat16), db=-(n // len(halves) + 1)) for n, part in enumerate(parts[len(halves) :])
+        ]
+        firsts, rest = others[:: len(halves)], others[1 :: len(halves)]
+        firsts, far_b = lax.optimization_barrier((firsts, far_b))
+
+
+        by_chip = jnp.stack(near + far + far_b)
+        by_row = [by_chip] + [shift(by_chip, dc=c) for c in range(1, n_c)]
+
+        own = []
+        back = []
+        for share, received, half in zip(kept, [firsts, rest], halves):
+            for other in received:
+                share += other.astype(jnp.float32)
+            for n, a in enumerate(half):
+                if a:
+                    back.append(shift(share[n].astype(jnp.bfloat16), da=-a))
+                else:
+                    own.append(share[n])
+
         forwards = block_product(
             1, forward_inputs, forward_outputs, [jnp.float32] + [jnp.bfloat16] * (n_col - 1), n_col,
             block_counts, place_cols, put_rows, by_row, block_values,
         )
-        others, own = lax.optimization_barrier((others, forwards[0]))
-
-        mirror_sum = 0.0
-        for h, half in enumerate(halves):
-            share = kept[h]
-            for other in others[h :: len(halves)]:
-                share += other.astype(jnp.float32)
-            for n, a in enumerate(half):
-                mirror_sum += shift(share[n].astype(jnp.bfloat16), da=-a).astype(jnp.float32) if a else share[n]
-        forward_sum = own[0]
+        back, mine = lax.optimization_barrier((back, forwards[0]))
+        forward_sum = mine[0]
         for j in range(1, n_col):
             forward_sum += shift_col(forwards[j][0], -j).astype(jnp.float32)
+        mirror_sum = sum(own)
+        for other in back:
+            mirror_sum += other.astype(jnp.float32)
         return forward_sum + mirror_sum
 
     current = (apply_operator(vectors.astype(jnp.bfloat16)) - center_value * vectors) / radius_value

time: 113 us -> 105 us (0.929)
  Pallas kernels: 21.5 us -> 10.2 us
  starting transfers between devices: 36.3 us -> 42.9 us
  waiting for transfers between devices: 46.5 us -> 43.9 us
    pallas_call x4, Pallas kernels: 21.5 us -> 10.2 us  [block_product(): pl.pallas_call(functools.partial(product_kernel, contract, inputs, output...]
    ppermute x26 -> x28, starting transfers between devices: 28.6 us -> 38.7 us  [shift(): return lax.ppermute(value, 'row', pairs)]
    ppermute x4, starting transfers between devices: 7.72 us -> 4.26 us  [shift_col(): lax.ppermute(value, 'col', [(j, (j + d) % n_col) for j in range(n_col)])]
    ppermute x26 -> x28, waiting for transfers between devices: 46.5 us -> 43.9 us  [shift(): return lax.ppermute(value, 'row', pairs)]
  transfers between devices with their start and end apart: 30 -> 32, of which waited for: 13 -> 12; matrix products, arithmetic and copies ran while one was open for 3% -> 3% of each run, Pallas kernels for 19% -> 10%
where the time goes in v3:
time: 105 us; the launch traced here: 104 us
  waiting for transfers between devices  43.9 us (42%)
  starting transfers between devices  42.9 us (41%)
  Pallas kernels  10.2 us (10%)
  other arithmetic  4.67 us (4%)
  between operations  2.27 us (2%)
    ppermute x28, waiting for transfers between devices, shift(): return lax.ppermute(value, 'row', pairs)  43.9 us
    ppermute x28, starting transfers between devices, shift(): return lax.ppermute(value, 'row', pairs)  38.7 us
    pallas_call x4, Pallas kernels, block_product(): pl.pallas_call(functools.partial(product_kernel, contract, inputs, output...  10.2 us
    ppermute x4, starting transfers between devices, shift_col(): lax.ppermute(value, 'col', [(j, (j + d) % n_col) for j in range(n_col)])  4.26 us
  transfers between devices with their start and end apart: 32, of which 12 were waited for; matrix products, arithmetic and copies ran while one was open for 3% of the time, Pallas kernels for 10%

profile of v3, /device:TPU:0, one launch (start us, length us, event | category | flops | bytes accessed | tf_op | source)
XLA Modules:
  0.0 104.2 jit_solution(4768266349005961843)
XLA Ops:
  1.0 3.0 %collective-permute-start = (bf16[32,2048]{1,0:T(8,128)(2,1)S(1)}, bf16[32,2048]{1,0:T(8,128)(2,1)S(1)}, u32[]{:S(2)}, u32[]{:S(2)}) collective-permute-start(bf16[32,2048]{1,0:T(8,128)(2,1)S(1)} %convert_element_type.82), channel_id=1, source_target_pairs={{0,1},{1,0},{2,3},{3,2},{4,5},{5,4},{6,7},{7,6},{8,9},{9,8},{10,11... | collective-permute-start | bytes 393224 | tf_op jit(solution)/shard_map/ppermute | solution.py:123
  5.5 2.6 %collective-permute-start.2 = (bf16[32,2048]{1,0:T(8,128)(2,1)S(1)}, bf16[32,2048]{1,0:T(8,128)(2,1)S(1)}, u32[]{:S(2)}, u32[]{:S(2)}) collective-permute-start(bf16[32,2048]{1,0:T(8,128)(2,1)S(1)} %convert_element_type.82), channel_id=1, source_target_pairs={{0,16},{2,18},{4,20},{6,22},{8,24},{10,26},{12,28},{14,30},{16,0},... | collective-permute-start | bytes 393224 | tf_op jit(solution)/shard_map/ppermute | solution.py:120
  13.4 2.6 %mirror.2 = (bf16[8,32,2048]{2,1,0:T(8,128)(2,1)S(1)}, bf16[8,32,2048]{2,1,0:T(8,128)(2,1)S(1)}) custom-call(s32[1]{0:T(128)} %copy.22.count_ref, s32[256]{0:T(256)S(1)} %get-tuple-element.84.take_ref, s32[256]{0:T(256)S(1)} %get-tuple-element.103.put_ref, bf16[1,32,2048]{2,1,0:T(8,128)(2,1)S(1)} %convert_bitcast_fusion.refs_0_, ...), custom_call_target="tpu_custom_call" | custom-call | flops 2147483648 | bytes 8650752 | tf_op jit(solution)/shard_map/mirror/pallas_call | solution.py:79
  16.5 3.3 %collective-permute-start.7 = (bf16[32,2048]{1,0:T(8,128)(2,1)S(1)}, bf16[32,2048]{1,0:T(8,128)(2,1)S(1)}, u32[]{:S(2)}, u32[]{:S(2)}) collective-permute-start(bf16[32,2048]{1,0:T(8,128)(2,1)S(1)} %collective-permute-done.4), channel_id=1, source_target_pairs={{0,8},{2,10},{4,12},{6,14},{8,16},{10,18},{12,20},{14,22},{16,24},... | collective-permute-start | bytes 393224 | tf_op jit(solution)/shard_map/ppermute | solution.py:120
  22.3 2.6 %collective-permute-done.5 = bf16[8,32,2048]{2,1,0:T(8,128)(2,1)S(1)} collective-permute-done((bf16[8,32,2048]{2,1,0:T(8,128)(2,1)S(1)}, bf16[8,32,2048]{2,1,0:T(8,128)(2,1)S(1)}, u32[]{:S(2)}, u32[]{:S(2)}) %collective-permute-start.5) | collective-permute-done | bytes 1048608 | tf_op jit(solution)/shard_map/ppermute | solution.py:120
  25.3 2.2 %collective-permute-start.6 = (bf16[2,32,2048]{2,1,0:T(8,128)(2,1)S(1)}, bf16[2,32,2048]{2,1,0:T(8,128)(2,1)S(1)}, u32[]{:S(2)}, u32[]{:S(2)}) collective-permute-start(bf16[2,32,2048]{2,1,0:T(8,128)(2,1)S(1)} %get-tuple-element.98), channel_id=1, source_target_pairs={{0,4},{2,6},{4,0},{6,2},{8,12},{10,14},{12,8},{14,10},{16,20},{18,... | collective-permute-start | bytes 786440 | tf_op jit(solution)/shard_map/ppermute | solution.py:120
  27.6 2.1 %collective-permute-done.8 = bf16[32,2048]{1,0:T(8,128)(2,1)S(1)} collective-permute-done((bf16[32,2048]{1,0:T(8,128)(2,1)S(1)}, bf16[32,2048]{1,0:T(8,128)(2,1)S(1)}, u32[]{:S(2)}, u32[]{:S(2)}) %collective-permute-start.8) | collective-permute-done | bytes 131104 | tf_op jit(solution)/shard_map/ppermute | solution.py:120
  29.7 4.9 %collective-permute-done.6 = bf16[2,32,2048]{2,1,0:T(8,128)(2,1)S(1)} collective-permute-done((bf16[2,32,2048]{2,1,0:T(8,128)(2,1)S(1)}, bf16[2,32,2048]{2,1,0:T(8,128)(2,1)S(1)}, u32[]{:S(2)}, u32[]{:S(2)}) %collective-permute-start.6) | collective-permute-done | bytes 262176 | tf_op jit(solution)/shard_map/ppermute | solution.py:120
  34.7 5.0 %collective-permute-done.12 = bf16[2,32,2048]{2,1,0:T(8,128)(2,1)S(1)} collective-permute-done((bf16[2,32,2048]{2,1,0:T(8,128)(2,1)S(1)}, bf16[2,32,2048]{2,1,0:T(8,128)(2,1)S(1)}, u32[]{:S(2)}, u32[]{:S(2)}) %collective-permute-start.12) | collective-permute-done | bytes 262176 | tf_op jit(solution)/shard_map/ppermute | solution.py:120
  39.9 1.7 %collective-permute-start.10 = (bf16[32,2048]{1,0:T(8,128)(2,1)S(1)}, bf16[32,2048]{1,0:T(8,128)(2,1)S(1)}, u32[]{:S(2)}, u32[]{:S(2)}) collective-permute-start(bf16[32,2048]{1,0:T(8,128)(2,1)S(1)} %get-tuple-element.102), channel_id=1, source_target_pairs={{0,24},{2,26},{4,28},{6,30},{8,0},{10,2},{12,4},{14,6},{16,8},{18,... | collective-permute-start | bytes 393224 | tf_op jit(solution)/shard_map/ppermute | solution.py:120
  42.3 1.8 %collective-permute-start.13 = (bf16[32,2048]{1,0:T(8,128)(2,1)S(1)}, bf16[32,2048]{1,0:T(8,128)(2,1)S(1)}, u32[]{:S(2)}, u32[]{:S(2)}) collective-permute-start(bf16[32,2048]{1,0:T(8,128)(2,1)S(1)} %fusion.16), channel_id=1, source_target_pairs={{0,8},{2,10},{4,12},{6,14},{8,16},{10,18},{12,20},{14,22},{16,24},... | collective-permute-start | bytes 393224 | tf_op jit(solution)/shard_map/ppermute | solution.py:120
  44.0 2.5 %forward.2 = (f32[1,32,2048]{2,1,0:T(8,128)S(1)}, bf16[1,32,2048]{2,1,0:T(8,128)(2,1)S(1)}) custom-call(s32[1]{0:T(128)} %copy.22.count_ref, s32[256]{0:T(256)S(1)} %get-tuple-element.104.take_ref, s32[256]{0:T(256)S(1)} %get-tuple-element.83.put_ref, bf16[8,32,2048]{2,1,0:T(8,128)(2,1)S(1)} %bitcast_dynamic-update-slice_fusion.8.refs_0_, ...), custom_call_target="tpu_custom_call" | custom-call | flops 2147483648 | bytes 10485760 | tf_op jit(solution)/shard_map/forward/pallas_call | solution.py:79
  47.9 5.8 %collective-permute-done.11 = bf16[32,2048]{1,0:T(8,128)(2,1)S(1)} collective-permute-done((bf16[32,2048]{1,0:T(8,128)(2,1)S(1)}, bf16[32,2048]{1,0:T(8,128)(2,1)S(1)}, u32[]{:S(2)}, u32[]{:S(2)}) %collective-permute-start.11) | collective-permute-done | bytes 131104 | tf_op jit(solution)/shard_map/ppermute | solution.py:120
  56.2 2.6 %collective-permute-start.19 = (bf16[32,2048]{1,0:T(8,128)(2,1)S(1)}, bf16[32,2048]{1,0:T(8,128)(2,1)S(1)}, u32[]{:S(2)}, u32[]{:S(2)}) collective-permute-start(bf16[32,2048]{1,0:T(8,128)(2,1)S(1)} %get-tuple-element.68), channel_id=1, source_target_pairs={{0,24},{2,26},{4,28},{6,30},{8,0},{10,2},{12,4},{14,6},{16,8},{18,... | collective-permute-start | bytes 393224 | tf_op jit(solution)/shard_map/ppermute | solution.py:120
  58.8 3.1 %collective-permute-start.20 = (bf16[32,2048]{1,0:T(8,128)(2,1)S(1)}, bf16[32,2048]{1,0:T(8,128)(2,1)S(1)}, u32[]{:S(2)}, u32[]{:S(2)}) collective-permute-start(bf16[32,2048]{1,0:T(8,128)(2,1)S(1)} %get-tuple-element.68), channel_id=1, source_target_pairs={{0,4},{2,6},{4,0},{6,2},{8,12},{10,14},{12,8},{14,10},{16,20},{18,... | collective-permute-start | bytes 393224 | tf_op jit(solution)/shard_map/ppermute | solution.py:120
  61.9 2.6 %mirror.3 = (bf16[8,32,2048]{2,1,0:T(8,128)(2,1)S(1)}, bf16[8,32,2048]{2,1,0:T(8,128)(2,1)S(1)}) custom-call(s32[1]{0:T(128)} %copy.22.count_ref, s32[256]{0:T(256)S(1)} %get-tuple-element.84.take_ref, s32[256]{0:T(256)S(1)} %get-tuple-element.103.put_ref, bf16[1,32,2048]{2,1,0:T(8,128)(2,1)S(1)} %bitcast.101, bf16[1,32,2048]{2,1,0:T(8,128)(2,1)S(1)} %bitcast.103, ...), custom_call_target="tpu_custom_call" | custom-call | flops 2147483648 | bytes 8650752 | tf_op jit(solution)/shard_map/mirror/pallas_call | solution.py:79
  66.3 3.3 %collective-permute-start.23 = (bf16[32,2048]{1,0:T(8,128)(2,1)S(1)}, bf16[32,2048]{1,0:T(8,128)(2,1)S(1)}, u32[]{:S(2)}, u32[]{:S(2)}) collective-permute-start(bf16[32,2048]{1,0:T(8,128)(2,1)S(1)} %collective-permute-done.20), channel_id=1, source_target_pairs={{0,8},{2,10},{4,12},{6,14},{8,16},{10,18},{12,20},{14,22},{16,24},... | collective-permute-start | bytes 393224 | tf_op jit(solution)/shard_map/ppermute | solution.py:120
  72.0 2.6 %collective-permute-done.21 = bf16[8,32,2048]{2,1,0:T(8,128)(2,1)S(1)} collective-permute-done((bf16[8,32,2048]{2,1,0:T(8,128)(2,1)S(1)}, bf16[8,32,2048]{2,1,0:T(8,128)(2,1)S(1)}, u32[]{:S(2)}, u32[]{:S(2)}) %collective-permute-start.21) | collective-permute-done | bytes 1048608 | tf_op jit(solution)/shard_map/ppermute | solution.py:120
  77.2 2.1 %collective-permute-done.24 = bf16[32,2048]{1,0:T(8,128)(2,1)S(1)} collective-permute-done((bf16[32,2048]{1,0:T(8,128)(2,1)S(1)}, bf16[32,2048]{1,0:T(8,128)(2,1)S(1)}, u32[]{:S(2)}, u32[]{:S(2)}) %collective-permute-start.24) | collective-permute-done | bytes 131104 | tf_op jit(solution)/shard_map/ppermute | solution.py:120
  79.3 5.0 %collective-permute-done.22 = bf16[2,32,2048]{2,1,0:T(8,128)(2,1)S(1)} collective-permute-done((bf16[2,32,2048]{2,1,0:T(8,128)(2,1)S(1)}, bf16[2,32,2048]{2,1,0:T(8,128)(2,1)S(1)}, u32[]{:S(2)}, u32[]{:S(2)}) %collective-permute-start.22) | collective-permute-done | bytes 262176 | tf_op jit(solution)/shard_map/ppermute | solution.py:120
  84.4 4.7 %collective-permute-done.28 = bf16[2,32,2048]{2,1,0:T(8,128)(2,1)S(1)} collective-permute-done((bf16[2,32,2048]{2,1,0:T(8,128)(2,1)S(1)}, bf16[2,32,2048]{2,1,0:T(8,128)(2,1)S(1)}, u32[]{:S(2)}, u32[]{:S(2)}) %collective-permute-start.28) | collective-permute-done | bytes 262176 | tf_op jit(solution)/shard_map/ppermute | solution.py:120
  89.2 2.1 %collective-permute-start.26 = (bf16[32,2048]{1,0:T(8,128)(2,1)S(1)}, bf16[32,2048]{1,0:T(8,128)(2,1)S(1)}, u32[]{:S(2)}, u32[]{:S(2)}) collective-permute-start(bf16[32,2048]{1,0:T(8,128)(2,1)S(1)} %get-tuple-element.100), channel_id=1, source_target_pairs={{0,24},{2,26},{4,28},{6,30},{8,0},{10,2},{12,4},{14,6},{16,8},{18,... | collective-permute-start | bytes 393224 | tf_op jit(solution)/shard_map/ppermute | solution.py:120
  93.1 2.5 %forward.3 = (f32[1,32,2048]{2,1,0:T(8,128)S(1)}, bf16[1,32,2048]{2,1,0:T(8,128)(2,1)S(1)}) custom-call(s32[1]{0:T(128)} %copy.22.count_ref, s32[256]{0:T(256)S(1)} %get-tuple-element.104.take_ref, s32[256]{0:T(256)S(1)} %get-tuple-element.83.put_ref, bf16[8,32,2048]{2,1,0:T(8,128)(2,1)S(1)} %bitcast_dynamic-update-slice_fusion.refs_0_, ...), custom_call_target="tpu_custom_call" | custom-call | flops 2147483648 | bytes 10485760 | tf_op jit(solution)/shard_map/forward/pallas_call | solution.py:79
  96.4 7.0 %collective-permute-done.27 = bf16[32,2048]{1,0:T(8,128)(2,1)S(1)} collective-permute-done((bf16[32,2048]{1,0:T(8,128)(2,1)S(1)}, bf16[32,2048]{1,0:T(8,128)(2,1)S(1)}, u32[]{:S(2)}, u32[]{:S(2)}) %collective-permute-start.27) | collective-permute-done | bytes 131104 | tf_op jit(solution)/shard_map/ppermute | solution.py:120
  (77 shorter events, 24.6 us)
Async XLA Ops:
  1.0 12.4 %collective-permute-start = (bf16[32,2048]{1,0:T(8,128)(2,1)S(1)}, bf16[32,2048]{1,0:T(8,128)(2,1)S(1)}, u32[]{:S(2)}, u32[]{:S(2)}) collective-permute-start(bf16[32,2048]{1,0:T(8,128)(2,1)S(1)} %convert_element_type.82), channel_id=1, source_target_pairs={{0,1},{1,0},{2,3},{3,2},{4,5},{5,4},{6,7},{7,6},{8,9},{9,8},{10,11... | collective-permute-start | bytes 393224 | tf_op jit(solution)/shard_map/ppermute | solution.py:123
  4.0 12.1 %collective-permute-start.1 = (bf16[32,2048]{1,0:T(8,128)(2,1)S(1)}, bf16[32,2048]{1,0:T(8,128)(2,1)S(1)}, u32[]{:S(2)}, u32[]{:S(2)}) collective-permute-start(bf16[32,2048]{1,0:T(8,128)(2,1)S(1)} %convert_element_type.82), channel_id=1, source_target_pairs={{0,8},{2,10},{4,12},{6,14},{8,16},{10,18},{12,20},{14,22},{16,24},... | collective-permute-start | bytes 393224 | tf_op jit(solution)/shard_map/ppermute | solution.py:120
  5.5 11.0 %collective-permute-start.2 = (bf16[32,2048]{1,0:T(8,128)(2,1)S(1)}, bf16[32,2048]{1,0:T(8,128)(2,1)S(1)}, u32[]{:S(2)}, u32[]{:S(2)}) collective-permute-start(bf16[32,2048]{1,0:T(8,128)(2,1)S(1)} %convert_element_type.82), channel_id=1, source_target_pairs={{0,16},{2,18},{4,20},{6,22},{8,24},{10,26},{12,28},{14,30},{16,0},... | collective-permute-start | bytes 393224 | tf_op jit(solution)/shard_map/ppermute | solution.py:120
  8.1 8.4 %collective-permute-start.3 = (bf16[32,2048]{1,0:T(8,128)(2,1)S(1)}, bf16[32,2048]{1,0:T(8,128)(2,1)S(1)}, u32[]{:S(2)}, u32[]{:S(2)}) collective-permute-start(bf16[32,2048]{1,0:T(8,128)(2,1)S(1)} %convert_element_type.82), channel_id=1, source_target_pairs={{0,24},{2,26},{4,28},{6,30},{8,0},{10,2},{12,4},{14,6},{16,8},{18,... | collective-permute-start | bytes 393224 | tf_op jit(solution)/shard_map/ppermute | solution.py:120
  16.5 11.1 %collective-permute-start.7 = (bf16[32,2048]{1,0:T(8,128)(2,1)S(1)}, bf16[32,2048]{1,0:T(8,128)(2,1)S(1)}, u32[]{:S(2)}, u32[]{:S(2)}) collective-permute-start(bf16[32,2048]{1,0:T(8,128)(2,1)S(1)} %collective-permute-done.4), channel_id=1, source_target_pairs={{0,8},{2,10},{4,12},{6,14},{8,16},{10,18},{12,20},{14,22},{16,24},... | collective-permute-start | bytes 393224 | tf_op jit(solution)/shard_map/ppermute | solution.py:120
  19.8 9.9 %collective-permute-start.8 = (bf16[32,2048]{1,0:T(8,128)(2,1)S(1)}, bf16[32,2048]{1,0:T(8,128)(2,1)S(1)}, u32[]{:S(2)}, u32[]{:S(2)}) collective-permute-start(bf16[32,2048]{1,0:T(8,128)(2,1)S(1)} %collective-permute-done.4), channel_id=1, source_target_pairs={{0,16},{2,18},{4,20},{6,22},{8,24},{10,26},{12,28},{14,30},{16,0},... | collective-permute-start | bytes 393224 | tf_op jit(solution)/shard_map/ppermute | solution.py:120
  21.4 8.3 %collective-permute-start.9 = (bf16[32,2048]{1,0:T(8,128)(2,1)S(1)}, bf16[32,2048]{1,0:T(8,128)(2,1)S(1)}, u32[]{:S(2)}, u32[]{:S(2)}) collective-permute-start(bf16[32,2048]{1,0:T(8,128)(2,1)S(1)} %collective-permute-done.4), channel_id=1, source_target_pairs={{0,24},{2,26},{4,28},{6,30},{8,0},{10,2},{12,4},{14,6},{16,8},{18,... | collective-permute-start | bytes 393224 | tf_op jit(solution)/shard_map/ppermute | solution.py:120
  25.3 9.3 %collective-permute-start.6 = (bf16[2,32,2048]{2,1,0:T(8,128)(2,1)S(1)}, bf16[2,32,2048]{2,1,0:T(8,128)(2,1)S(1)}, u32[]{:S(2)}, u32[]{:S(2)}) collective-permute-start(bf16[2,32,2048]{2,1,0:T(8,128)(2,1)S(1)} %get-tuple-element.98), channel_id=1, source_target_pairs={{0,4},{2,6},{4,0},{6,2},{8,12},{10,14},{12,8},{14,10},{16,20},{18,... | collective-permute-start | bytes 786440 | tf_op jit(solution)/shard_map/ppermute | solution.py:120
  27.5 12.2 %collective-permute-start.12 = (bf16[2,32,2048]{2,1,0:T(8,128)(2,1)S(1)}, bf16[2,32,2048]{2,1,0:T(8,128)(2,1)S(1)}, u32[]{:S(2)}, u32[]{:S(2)}) collective-permute-start(bf16[2,32,2048]{2,1,0:T(8,128)(2,1)S(1)} %get-tuple-element.97), channel_id=1, source_target_pairs={{0,4},{2,6},{4,0},{6,2},{8,12},{10,14},{12,8},{14,10},{16,20},{18,... | collective-permute-start | bytes 786440 | tf_op jit(solution)/shard_map/ppermute | solution.py:120
  34.7 9.4 %collective-permute-start.14 = (bf16[8,32,2048]{2,1,0:T(8,128)(2,1)S(1)}, bf16[8,32,2048]{2,1,0:T(8,128)(2,1)S(1)}, u32[]{:S(2)}, u32[]{:S(2)}) collective-permute-start(bf16[8,32,2048]{2,1,0:T(8,128)(2,1)S(1)} %bitcast_dynamic-update-slice_fusion.8.refs_0_), channel_id=1, source_target_pairs={{0,2},{2,0},{4,6},{6,4},{8,10},{10,8},{12,14},{14,12},{16,18},{18,... | collective-permute-start | bytes 3145736 | tf_op jit(solution)/shard_map/ppermute | solution.py:120
  41.6 12.1 %collective-permute-start.11 = (bf16[32,2048]{1,0:T(8,128)(2,1)S(1)}, bf16[32,2048]{1,0:T(8,128)(2,1)S(1)}, u32[]{:S(2)}, u32[]{:S(2)}) collective-permute-start(bf16[32,2048]{1,0:T(8,128)(2,1)S(1)} %get-tuple-element.101), channel_id=1, source_target_pairs={{0,16},{2,18},{4,20},{6,22},{8,24},{10,26},{12,28},{14,30},{16,0},... | collective-permute-start | bytes 393224 | tf_op jit(solution)/shard_map/ppermute | solution.py:120
  42.3 11.4 %collective-permute-start.13 = (bf16[32,2048]{1,0:T(8,128)(2,1)S(1)}, bf16[32,2048]{1,0:T(8,128)(2,1)S(1)}, u32[]{:S(2)}, u32[]{:S(2)}) collective-permute-start(bf16[32,2048]{1,0:T(8,128)(2,1)S(1)} %fusion.16), channel_id=1, source_target_pairs={{0,8},{2,10},{4,12},{6,14},{8,16},{10,18},{12,20},{14,22},{16,24},... | collective-permute-start | bytes 393224 | tf_op jit(solution)/shard_map/ppermute | solution.py:120
  53.8 8.1 %collective-permute-start.16 = (bf16[32,2048]{1,0:T(8,128)(2,1)S(1)}, bf16[32,2048]{1,0:T(8,128)(2,1)S(1)}, u32[]{:S(2)}, u32[]{:S(2)}) collective-permute-start(bf16[32,2048]{1,0:T(8,128)(2,1)S(1)} %get-tuple-element.68), channel_id=1, source_target_pairs={{0,1},{1,0},{2,3},{3,2},{4,5},{5,4},{6,7},{7,6},{8,9},{9,8},{10,11... | collective-permute-start | bytes 393224 | tf_op jit(solution)/shard_map/ppermute | solution.py:123
  54.2 10.3 %collective-permute-start.17 = (bf16[32,2048]{1,0:T(8,128)(2,1)S(1)}, bf16[32,2048]{1,0:T(8,128)(2,1)S(1)}, u32[]{:S(2)}, u32[]{:S(2)}) collective-permute-start(bf16[32,2048]{1,0:T(8,128)(2,1)S(1)} %get-tuple-element.68), channel_id=1, source_target_pairs={{0,8},{2,10},{4,12},{6,14},{8,16},{10,18},{12,20},{14,22},{16,24},... | collective-permute-start | bytes 393224 | tf_op jit(solution)/shard_map/ppermute | solution.py:120
  55.2 11.1 %collective-permute-start.18 = (bf16[32,2048]{1,0:T(8,128)(2,1)S(1)}, bf16[32,2048]{1,0:T(8,128)(2,1)S(1)}, u32[]{:S(2)}, u32[]{:S(2)}) collective-permute-start(bf16[32,2048]{1,0:T(8,128)(2,1)S(1)} %get-tuple-element.68), channel_id=1, source_target_pairs={{0,16},{2,18},{4,20},{6,22},{8,24},{10,26},{12,28},{14,30},{16,0},... | collective-permute-start | bytes 393224 | tf_op jit(solution)/shard_map/ppermute | solution.py:120
  56.2 10.0 %collective-permute-start.19 = (bf16[32,2048]{1,0:T(8,128)(2,1)S(1)}, bf16[32,2048]{1,0:T(8,128)(2,1)S(1)}, u32[]{:S(2)}, u32[]{:S(2)}) collective-permute-start(bf16[32,2048]{1,0:T(8,128)(2,1)S(1)} %get-tuple-element.68), channel_id=1, source_target_pairs={{0,24},{2,26},{4,28},{6,30},{8,0},{10,2},{12,4},{14,6},{16,8},{18,... | collective-permute-start | bytes 393224 | tf_op jit(solution)/shard_map/ppermute | solution.py:120
  66.3 11.0 %collective-permute-start.23 = (bf16[32,2048]{1,0:T(8,128)(2,1)S(1)}, bf16[32,2048]{1,0:T(8,128)(2,1)S(1)}, u32[]{:S(2)}, u32[]{:S(2)}) collective-permute-start(bf16[32,2048]{1,0:T(8,128)(2,1)S(1)} %collective-permute-done.20), channel_id=1, source_target_pairs={{0,8},{2,10},{4,12},{6,14},{8,16},{10,18},{12,20},{14,22},{16,24},... | collective-permute-start | bytes 393224 | tf_op jit(solution)/shard_map/ppermute | solution.py:120
  69.5 9.7 %collective-permute-start.24 = (bf16[32,2048]{1,0:T(8,128)(2,1)S(1)}, bf16[32,2048]{1,0:T(8,128)(2,1)S(1)}, u32[]{:S(2)}, u32[]{:S(2)}) collective-permute-start(bf16[32,2048]{1,0:T(8,128)(2,1)S(1)} %collective-permute-done.20), channel_id=1, source_target_pairs={{0,16},{2,18},{4,20},{6,22},{8,24},{10,26},{12,28},{14,30},{16,0},... | collective-permute-start | bytes 393224 | tf_op jit(solution)/shard_map/ppermute | solution.py:120
  71.2 8.1 %collective-permute-start.25 = (bf16[32,2048]{1,0:T(8,128)(2,1)S(1)}, bf16[32,2048]{1,0:T(8,128)(2,1)S(1)}, u32[]{:S(2)}, u32[]{:S(2)}) collective-permute-start(bf16[32,2048]{1,0:T(8,128)(2,1)S(1)} %collective-permute-done.20), channel_id=1, source_target_pairs={{0,24},{2,26},{4,28},{6,30},{8,0},{10,2},{12,4},{14,6},{16,8},{18,... | collective-permute-start | bytes 393224 | tf_op jit(solution)/shard_map/ppermute | solution.py:120
  75.0 9.2 %collective-permute-start.22 = (bf16[2,32,2048]{2,1,0:T(8,128)(2,1)S(1)}, bf16[2,32,2048]{2,1,0:T(8,128)(2,1)S(1)}, u32[]{:S(2)}, u32[]{:S(2)}) collective-permute-start(bf16[2,32,2048]{2,1,0:T(8,128)(2,1)S(1)} %get-tuple-element.95), channel_id=1, source_target_pairs={{0,4},{2,6},{4,0},{6,2},{8,12},{10,14},{12,8},{14,10},{16,20},{18,... | collective-permute-start | bytes 786440 | tf_op jit(solution)/shard_map/ppermute | solution.py:120
  76.7 12.4 %collective-permute-start.28 = (bf16[2,32,2048]{2,1,0:T(8,128)(2,1)S(1)}, bf16[2,32,2048]{2,1,0:T(8,128)(2,1)S(1)}, u32[]{:S(2)}, u32[]{:S(2)}) collective-permute-start(bf16[2,32,2048]{2,1,0:T(8,128)(2,1)S(1)} %get-tuple-element.96), channel_id=1, source_target_pairs={{0,4},{2,6},{4,0},{6,2},{8,12},{10,14},{12,8},{14,10},{16,20},{18,... | collective-permute-start | bytes 786440 | tf_op jit(solution)/shard_map/ppermute | solution.py:120
  84.3 8.8 %collective-permute-start.30 = (bf16[8,32,2048]{2,1,0:T(8,128)(2,1)S(1)}, bf16[8,32,2048]{2,1,0:T(8,128)(2,1)S(1)}, u32[]{:S(2)}, u32[]{:S(2)}) collective-permute-start(bf16[8,32,2048]{2,1,0:T(8,128)(2,1)S(1)} %bitcast_dynamic-update-slice_fusion.refs_0_), channel_id=1, source_target_pairs={{0,2},{2,0},{4,6},{6,4},{8,10},{10,8},{12,14},{14,12},{16,18},{18,... | collective-permute-start | bytes 3145736 | tf_op jit(solution)/shard_map/ppermute | solution.py:120
  91.3 12.1 %collective-permute-start.27 = (bf16[32,2048]{1,0:T(8,128)(2,1)S(1)}, bf16[32,2048]{1,0:T(8,128)(2,1)S(1)}, u32[]{:S(2)}, u32[]{:S(2)}) collective-permute-start(bf16[32,2048]{1,0:T(8,128)(2,1)S(1)} %get-tuple-element.99), channel_id=1, source_target_pairs={{0,16},{2,18},{4,20},{6,22},{8,24},{10,26},{12,28},{14,30},{16,0},... | collective-permute-start | bytes 393224 | tf_op jit(solution)/shard_map/ppermute | solution.py:120
  92.0 11.4 %collective-permute-start.29 = (bf16[32,2048]{1,0:T(8,128)(2,1)S(1)}, bf16[32,2048]{1,0:T(8,128)(2,1)S(1)}, u32[]{:S(2)}, u32[]{:S(2)}) collective-permute-start(bf16[32,2048]{1,0:T(8,128)(2,1)S(1)} %fusion.17), channel_id=1, source_target_pairs={{0,8},{2,10},{4,12},{6,14},{8,16},{10,18},{12,20},{14,22},{16,24},... | collective-permute-start | bytes 393224 | tf_op jit(solution)/shard_map/ppermute | solution.py:120
  (9 other events, 59.6 us)

commit v4 on v1

--- a/solution.py
+++ b/solution.py
@@ -135,9 +135,12 @@
         piece((my_a - owner_a + n_a) % n_a, (my_b - owner_b + n_b) % n_b, (my_c - owner_c + n_c) % n_c) * per_piece
         + block_cols % per_piece
     )
+    sum_cols = (
+        piece(owner_a, (my_b - owner_b + n_b) % n_b, (my_c - owner_c + n_c) % n_c) * per_piece + block_cols % per_piece
+    )
     place_rows = (col_index - block_rows // per_piece + n_col) % n_col * per_piece + block_rows % per_piece
     live = jnp.arange(block_rows.shape[0], dtype=jnp.int32) < block_counts[0]
-    put_cols = jnp.where(live, place_cols, n_row * per_piece)
+    put_cols = jnp.where(live, sum_cols, n_row * per_piece)
     put_rows = jnp.where(live, place_rows, n_col * per_piece)
 
     mirror_outputs = [[piece(a, b, c) for b in range(n_b) for a in range(n_a)] for c in range(n_c)]
@@ -176,7 +179,8 @@
         share = by_b[0]
         for other in others:
             share += other.astype(jnp.float32)
-        back = [shift(share[a].astype(jnp.bfloat16), da=-a) for a in range(1, n_a)]
+        lines = [[at(a, b, c) for a in range(n_a)] for b in range(n_b) for c in range(n_c)]
+        back = lax.all_to_all(share.astype(jnp.bfloat16), "row", 0, 0, axis_index_groups=lines)
 
         forwards = block_product(
             1, forward_inputs, forward_outputs, [jnp.float32] + [jnp.bfloat16] * (n_col - 1), n_col,
@@ -186,9 +190,7 @@
         forward_sum = own[0]
         for j in range(1, n_col):
             forward_sum += shift_col(forwards[j][0], -j).astype(jnp.float32)
-        mirror_sum = share[0]
-        for other in back:
-            mirror_sum += other.astype(jnp.float32)
+        mirror_sum = jnp.sum(back.astype(jnp.float32), axis=0)
         return forward_sum + mirror_sum
 
     current = (apply_operator(vectors.astype(jnp.bfloat16)) - center_value * vectors) / radius_value

time: 97.5 us -> 112 us (1.15)
  Pallas kernels: 12.5 us -> 26.1 us
  starting transfers between devices: 38.5 us -> 31.5 us
  other arithmetic: 3.8 us -> 8.94 us
  waiting for transfers between devices: 39.1 us -> 41.9 us
    all_to_all x0 -> x2, waiting for transfers between devices: none -> 14.1 us  [apply_operator(): lax.all_to_all(share.astype(jnp.bfloat16), 'row', 0, 0, axis_index_groups...]
    pallas_call x4, Pallas kernels: 12.5 us -> 26.1 us  [block_product(): pl.pallas_call(functools.partial(product_kernel, contract, inputs, output...]
    ppermute x28 -> x22, starting transfers between devices: 33.8 us -> 20.7 us  [shift(): return lax.ppermute(value, 'row', pairs)]
    ppermute x28 -> x22, waiting for transfers between devices: 39.1 us -> 27.2 us  [shift(): return lax.ppermute(value, 'row', pairs)]
    all_to_all x0 -> x2, starting transfers between devices: none -> 9.13 us  [apply_operator(): lax.all_to_all(share.astype(jnp.bfloat16), 'row', 0, 0, axis_index_groups...]
    ppermute x4, starting transfers between devices: 4.8 us -> 1.7 us  [shift_col(): lax.ppermute(value, 'col', [(j, (j + d) % n_col) for j in range(n_col)])]
    reduce_sum x0 -> x2, other arithmetic: none -> 2.28 us  [apply_operator(): mirror_sum = jnp.sum(back.astype(jnp.float32), axis=0)]
    convert_element_type x0 -> x2, other arithmetic: none -> 1.83 us  [apply_operator(): share.astype(jnp.bfloat16)]
  transfers between devices with their start and end apart: 32 -> 28, of which waited for: 12 -> 12; matrix products, arithmetic and copies ran while one was open for 2% -> 5% of each run, Pallas kernels for 13% -> 24%
where the time goes in v4:
time: 112 us; the launch traced here: 111 us
  waiting for transfers between devices  41.9 us (37%)
  starting transfers between devices  31.5 us (28%)
  Pallas kernels  26.1 us (23%)
  other arithmetic  8.94 us (8%)
  between operations  2.27 us (2%)
    ppermute x22, waiting for transfers between devices, shift(): return lax.ppermute(value, 'row', pairs)  27.2 us
    pallas_call x4, Pallas kernels, block_product(): pl.pallas_call(functools.partial(product_kernel, contract, inputs, output...  26.1 us
    ppermute x22, starting transfers between devices, shift(): return lax.ppermute(value, 'row', pairs)  20.7 us
    all_to_all x2, waiting for transfers between devices, apply_operator(): lax.all_to_all(share.astype(jnp.bfloat16), 'row', 0, 0, axis_index_groups...  14.1 us
    all_to_all x2, starting transfers between devices, apply_operator(): lax.all_to_all(share.astype(jnp.bfloat16), 'row', 0, 0, axis_index_groups...  9.13 us
    reduce_sum x2, other arithmetic, apply_operator(): mirror_sum = jnp.sum(back.astype(jnp.float32), axis=0)  2.28 us
  transfers between devices with their start and end apart: 28, of which 12 were waited for; matrix products, arithmetic and copies ran while one was open for 5% of the time, Pallas kernels for 24%

profile of v4, /device:TPU:0, one launch (start us, length us, event | category | flops | bytes accessed | tf_op | source)
XLA Modules:
  0.0 110.9 jit_solution(7812681851137187011)
XLA Ops:
  1.0 3.1 %collective-permute-start = (bf16[32,2048]{1,0:T(8,128)(2,1)S(1)}, bf16[32,2048]{1,0:T(8,128)(2,1)S(1)}, u32[]{:S(2)}, u32[]{:S(2)}) collective-permute-start(bf16[32,2048]{1,0:T(8,128)(2,1)S(1)} %get-tuple-element.77), channel_id=1, source_target_pairs={{0,8},{2,10},{4,12},{6,14},{8,16},{10,18},{12,20},{14,22},{16,24},... | collective-permute-start | bytes 393224 | tf_op jit(solution)/shard_map/ppermute | solution.py:120
  4.0 2.6 %collective-permute-start.1 = (bf16[32,2048]{1,0:T(8,128)(2,1)S(1)}, bf16[32,2048]{1,0:T(8,128)(2,1)S(1)}, u32[]{:S(2)}, u32[]{:S(2)}) collective-permute-start(bf16[32,2048]{1,0:T(8,128)(2,1)S(1)} %get-tuple-element.77), channel_id=1, source_target_pairs={{0,16},{2,18},{4,20},{6,22},{8,24},{10,26},{12,28},{14,30},{16,0},... | collective-permute-start | bytes 393224 | tf_op jit(solution)/shard_map/ppermute | solution.py:120
  6.6 1.3 %collective-permute-start.2 = (bf16[32,2048]{1,0:T(8,128)(2,1)S(1)}, bf16[32,2048]{1,0:T(8,128)(2,1)S(1)}, u32[]{:S(2)}, u32[]{:S(2)}) collective-permute-start(bf16[32,2048]{1,0:T(8,128)(2,1)S(1)} %get-tuple-element.77), channel_id=1, source_target_pairs={{0,24},{2,26},{4,28},{6,30},{8,0},{10,2},{12,4},{14,6},{16,8},{18,... | collective-permute-start | bytes 393224 | tf_op jit(solution)/shard_map/ppermute | solution.py:120
  8.0 1.5 %collective-permute-start.3 = (bf16[32,2048]{1,0:T(8,128)(2,1)S(1)}, bf16[32,2048]{1,0:T(8,128)(2,1)S(1)}, u32[]{:S(2)}, u32[]{:S(2)}) collective-permute-start(bf16[32,2048]{1,0:T(8,128)(2,1)S(1)} %get-tuple-element.77), channel_id=1, source_target_pairs={{0,1},{1,0},{2,3},{3,2},{4,5},{5,4},{6,7},{7,6},{8,9},{9,8},{10,11... | collective-permute-start | bytes 393224 | tf_op jit(solution)/shard_map/ppermute | solution.py:123
  9.5 1.5 %collective-permute-start.5 = (bf16[32,2048]{1,0:T(8,128)(2,1)S(1)}, bf16[32,2048]{1,0:T(8,128)(2,1)S(1)}, u32[]{:S(2)}, u32[]{:S(2)}) collective-permute-start(bf16[32,2048]{1,0:T(8,128)(2,1)S(1)} %get-tuple-element.77), channel_id=1, source_target_pairs={{0,4},{2,6},{4,0},{6,2},{8,12},{10,14},{12,8},{14,10},{16,20},{18,... | collective-permute-start | bytes 393224 | tf_op jit(solution)/shard_map/ppermute | solution.py:120
  13.8 6.5 %mirror.2 = (bf16[8,32,2048]{2,1,0:T(8,128)(2,1)S(1)}, bf16[8,32,2048]{2,1,0:T(8,128)(2,1)S(1)}) custom-call(s32[1]{0:T(128)} %copy.16.count_ref, s32[256]{0:T(256)S(1)} %get-tuple-element.72.take_ref, s32[256]{0:T(256)S(1)} %add_select_fusion.put_ref, bf16[1,32,2048]{2,1,0:T(8,128)(2,1)S(1)} %bitcast.64, bf16[1,32,2048]{2,1,0:T(8,128)(2,1)S(1)} %bitcast.66, ...), custom_call_target="tpu_custom_call" | custom-call | flops 2147483648 | bytes 8650752 | tf_op jit(solution)/shard_map/mirror/pallas_call | solution.py:79
  21.0 2.1 %collective-permute-start.7 = (bf16[32,2048]{1,0:T(8,128)(2,1)S(1)}, bf16[32,2048]{1,0:T(8,128)(2,1)S(1)}, u32[]{:S(2)}, u32[]{:S(2)}) collective-permute-start(bf16[32,2048]{1,0:T(8,128)(2,1)S(1)} %collective-permute-done.5), channel_id=1, source_target_pairs={{0,16},{2,18},{4,20},{6,22},{8,24},{10,26},{12,28},{14,30},{16,0},... | collective-permute-start | bytes 393224 | tf_op jit(solution)/shard_map/ppermute | solution.py:120
  23.8 2.7 %collective-permute-done.8 = bf16[32,2048]{1,0:T(8,128)(2,1)S(1)} collective-permute-done((bf16[32,2048]{1,0:T(8,128)(2,1)S(1)}, bf16[32,2048]{1,0:T(8,128)(2,1)S(1)}, u32[]{:S(2)}, u32[]{:S(2)}) %collective-permute-start.8) | collective-permute-done | bytes 131104 | tf_op jit(solution)/shard_map/ppermute | solution.py:120
  26.6 8.5 %collective-permute-done.7 = bf16[32,2048]{1,0:T(8,128)(2,1)S(1)} collective-permute-done((bf16[32,2048]{1,0:T(8,128)(2,1)S(1)}, bf16[32,2048]{1,0:T(8,128)(2,1)S(1)}, u32[]{:S(2)}, u32[]{:S(2)}) %collective-permute-start.7) | collective-permute-done | bytes 131104 | tf_op jit(solution)/shard_map/ppermute | solution.py:120
  35.2 1.7 %collective-permute-done.10.refs_3_ = bf16[3,32,2048]{2,1,0:T(8,128)(2,1)S(1)} collective-permute-done((bf16[3,32,2048]{2,1,0:T(8,128)(2,1)S(1)}, bf16[3,32,2048]{2,1,0:T(8,128)(2,1)S(1)}, u32[]{:S(2)}, u32[]{:S(2)}) %collective-permute-start.10) | collective-permute-done | bytes 393248 | tf_op jit(solution)/shard_map/ppermute | solution.py:120
  38.4 4.3 %all-to-all-start = ((bf16[4,32,2048]{2,1,0:T(8,128)(2,1)}), bf16[4,32,2048]{2,1,0:T(8,128)(2,1)}, u32[]{:S(2)}, u32[]{:S(2)}) async-start(bf16[4,32,2048]{2,1,0:T(8,128)(2,1)} %fusion.1), calls=%async_computation | async-start | bytes 1048576 | tf_op jit(solution)/shard_map/all_to_all | solution.py:183
  44.0 6.6 %forward.2 = (f32[1,32,2048]{2,1,0:T(8,128)S(1)}, bf16[1,32,2048]{2,1,0:T(8,128)(2,1)S(1)}) custom-call(s32[1]{0:T(128)} %copy.16.count_ref, s32[256]{0:T(256)S(1)} %get-tuple-element.73.take_ref, s32[256]{0:T(256)S(1)} %get-tuple-element.71.put_ref, bf16[5,32,2048]{2,1,0:T(8,128)(2,1)S(1)} %bitcast_dynamic-update-slice_fusion.4.refs_0_, ...), custom_call_target="tpu_custom_call" | custom-call | flops 2147483648 | bytes 10485760 | tf_op jit(solution)/shard_map/forward/pallas_call | solution.py:79
  50.7 6.4 %all-to-all-done = bf16[4,32,2048]{2,1,0:T(8,128)(2,1)} async-done(((bf16[4,32,2048]{2,1,0:T(8,128)(2,1)}), bf16[4,32,2048]{2,1,0:T(8,128)(2,1)}, u32[]{:S(2)}, u32[]{:S(2)}) %all-to-all-start) | async-done | bytes 524320 | tf_op jit(solution)/shard_map/all_to_all | solution.py:183
  58.5 2.0 %collective-permute-start.14 = (bf16[32,2048]{1,0:T(8,128)(2,1)S(1)}, bf16[32,2048]{1,0:T(8,128)(2,1)S(1)}, u32[]{:S(2)}, u32[]{:S(2)}) collective-permute-start(bf16[32,2048]{1,0:T(8,128)(2,1)S(1)} %get-tuple-element.70), channel_id=1, source_target_pairs={{0,16},{2,18},{4,20},{6,22},{8,24},{10,26},{12,28},{14,30},{16,0},... | collective-permute-start | bytes 393224 | tf_op jit(solution)/shard_map/ppermute | solution.py:120
  60.5 1.8 %collective-permute-start.15 = (bf16[32,2048]{1,0:T(8,128)(2,1)S(1)}, bf16[32,2048]{1,0:T(8,128)(2,1)S(1)}, u32[]{:S(2)}, u32[]{:S(2)}) collective-permute-start(bf16[32,2048]{1,0:T(8,128)(2,1)S(1)} %get-tuple-element.70), channel_id=1, source_target_pairs={{0,24},{2,26},{4,28},{6,30},{8,0},{10,2},{12,4},{14,6},{16,8},{18,... | collective-permute-start | bytes 393224 | tf_op jit(solution)/shard_map/ppermute | solution.py:120
  63.3 6.5 %mirror.3 = (bf16[8,32,2048]{2,1,0:T(8,128)(2,1)S(1)}, bf16[8,32,2048]{2,1,0:T(8,128)(2,1)S(1)}) custom-call(s32[1]{0:T(128)} %copy.16.count_ref, s32[256]{0:T(256)S(1)} %get-tuple-element.72.take_ref, s32[256]{0:T(256)S(1)} %add_select_fusion.put_ref, bf16[1,32,2048]{2,1,0:T(8,128)(2,1)S(1)} %bitcast.65, bf16[1,32,2048]{2,1,0:T(8,128)(2,1)S(1)} %bitcast.67, ...), custom_call_target="tpu_custom_call" | custom-call | flops 2147483648 | bytes 8650752 | tf_op jit(solution)/shard_map/mirror/pallas_call | solution.py:79
  71.1 2.4 %collective-permute-start.21 = (bf16[32,2048]{1,0:T(8,128)(2,1)S(1)}, bf16[32,2048]{1,0:T(8,128)(2,1)S(1)}, u32[]{:S(2)}, u32[]{:S(2)}) collective-permute-start(bf16[32,2048]{1,0:T(8,128)(2,1)S(1)} %collective-permute-done.18), channel_id=1, source_target_pairs={{0,24},{2,26},{4,28},{6,30},{8,0},{10,2},{12,4},{14,6},{16,8},{18,... | collective-permute-start | bytes 393224 | tf_op jit(solution)/shard_map/ppermute | solution.py:120
  73.6 1.4 %collective-permute-start.20 = (bf16[32,2048]{1,0:T(8,128)(2,1)S(1)}, bf16[32,2048]{1,0:T(8,128)(2,1)S(1)}, u32[]{:S(2)}, u32[]{:S(2)}) collective-permute-start(bf16[32,2048]{1,0:T(8,128)(2,1)S(1)} %collective-permute-done.18), channel_id=1, source_target_pairs={{0,16},{2,18},{4,20},{6,22},{8,24},{10,26},{12,28},{14,30},{16,0},... | collective-permute-start | bytes 393224 | tf_op jit(solution)/shard_map/ppermute | solution.py:120
  75.7 1.8 %collective-permute-done.21 = bf16[32,2048]{1,0:T(8,128)(2,1)S(1)} collective-permute-done((bf16[32,2048]{1,0:T(8,128)(2,1)S(1)}, bf16[32,2048]{1,0:T(8,128)(2,1)S(1)}, u32[]{:S(2)}, u32[]{:S(2)}) %collective-permute-start.21) | collective-permute-done | bytes 131104 | tf_op jit(solution)/shard_map/ppermute | solution.py:120
  77.5 9.3 %collective-permute-done.20 = bf16[32,2048]{1,0:T(8,128)(2,1)S(1)} collective-permute-done((bf16[32,2048]{1,0:T(8,128)(2,1)S(1)}, bf16[32,2048]{1,0:T(8,128)(2,1)S(1)}, u32[]{:S(2)}, u32[]{:S(2)}) %collective-permute-start.20) | collective-permute-done | bytes 131104 | tf_op jit(solution)/shard_map/ppermute | solution.py:120
  87.0 1.7 %collective-permute-done.23.refs_3_ = bf16[3,32,2048]{2,1,0:T(8,128)(2,1)S(1)} collective-permute-done((bf16[3,32,2048]{2,1,0:T(8,128)(2,1)S(1)}, bf16[3,32,2048]{2,1,0:T(8,128)(2,1)S(1)}, u32[]{:S(2)}, u32[]{:S(2)}) %collective-permute-start.23) | collective-permute-done | bytes 393248 | tf_op jit(solution)/shard_map/ppermute | solution.py:120
  89.7 4.8 %all-to-all-start.1 = ((bf16[4,32,2048]{2,1,0:T(8,128)(2,1)}), bf16[4,32,2048]{2,1,0:T(8,128)(2,1)}, u32[]{:S(2)}, u32[]{:S(2)}) async-start(bf16[4,32,2048]{2,1,0:T(8,128)(2,1)} %fusion), calls=%async_computation.1 | async-start | bytes 1048576 | tf_op jit(solution)/shard_map/all_to_all | solution.py:183
  94.5 6.6 %forward.3 = (f32[1,32,2048]{2,1,0:T(8,128)S(1)}, bf16[1,32,2048]{2,1,0:T(8,128)(2,1)S(1)}) custom-call(s32[1]{0:T(128)} %copy.16.count_ref, s32[256]{0:T(256)S(1)} %get-tuple-element.73.take_ref, s32[256]{0:T(256)S(1)} %get-tuple-element.71.put_ref, bf16[5,32,2048]{2,1,0:T(8,128)(2,1)S(1)} %bitcast_dynamic-update-slice_fusion.refs_0_, ...), custom_call_target="tpu_custom_call" | custom-call | flops 2147483648 | bytes 10485760 | tf_op jit(solution)/shard_map/forward/pallas_call | solution.py:79
  101.2 7.7 %all-to-all-done.1 = bf16[4,32,2048]{2,1,0:T(8,128)(2,1)} async-done(((bf16[4,32,2048]{2,1,0:T(8,128)(2,1)}), bf16[4,32,2048]{2,1,0:T(8,128)(2,1)}, u32[]{:S(2)}, u32[]{:S(2)}) %all-to-all-start.1) | async-done | bytes 524320 | tf_op jit(solution)/shard_map/all_to_all | solution.py:183
  (62 shorter events, 13.8 us)
Async XLA Ops:
  1.0 19.3 %collective-permute-start = (bf16[32,2048]{1,0:T(8,128)(2,1)S(1)}, bf16[32,2048]{1,0:T(8,128)(2,1)S(1)}, u32[]{:S(2)}, u32[]{:S(2)}) collective-permute-start(bf16[32,2048]{1,0:T(8,128)(2,1)S(1)} %get-tuple-element.77), channel_id=1, source_target_pairs={{0,8},{2,10},{4,12},{6,14},{8,16},{10,18},{12,20},{14,22},{16,24},... | collective-permute-start | bytes 393224 | tf_op jit(solution)/shard_map/ppermute | solution.py:120
  4.0 16.2 %collective-permute-start.1 = (bf16[32,2048]{1,0:T(8,128)(2,1)S(1)}, bf16[32,2048]{1,0:T(8,128)(2,1)S(1)}, u32[]{:S(2)}, u32[]{:S(2)}) collective-permute-start(bf16[32,2048]{1,0:T(8,128)(2,1)S(1)} %get-tuple-element.77), channel_id=1, source_target_pairs={{0,16},{2,18},{4,20},{6,22},{8,24},{10,26},{12,28},{14,30},{16,0},... | collective-permute-start | bytes 393224 | tf_op jit(solution)/shard_map/ppermute | solution.py:120
  6.6 13.7 %collective-permute-start.2 = (bf16[32,2048]{1,0:T(8,128)(2,1)S(1)}, bf16[32,2048]{1,0:T(8,128)(2,1)S(1)}, u32[]{:S(2)}, u32[]{:S(2)}) collective-permute-start(bf16[32,2048]{1,0:T(8,128)(2,1)S(1)} %get-tuple-element.77), channel_id=1, source_target_pairs={{0,24},{2,26},{4,28},{6,30},{8,0},{10,2},{12,4},{14,6},{16,8},{18,... | collective-permute-start | bytes 393224 | tf_op jit(solution)/shard_map/ppermute | solution.py:120
  8.0 5.8 %collective-permute-start.3 = (bf16[32,2048]{1,0:T(8,128)(2,1)S(1)}, bf16[32,2048]{1,0:T(8,128)(2,1)S(1)}, u32[]{:S(2)}, u32[]{:S(2)}) collective-permute-start(bf16[32,2048]{1,0:T(8,128)(2,1)S(1)} %get-tuple-element.77), channel_id=1, source_target_pairs={{0,1},{1,0},{2,3},{3,2},{4,5},{5,4},{6,7},{7,6},{8,9},{9,8},{10,11... | collective-permute-start | bytes 393224 | tf_op jit(solution)/shard_map/ppermute | solution.py:123
  9.5 10.9 %collective-permute-start.5 = (bf16[32,2048]{1,0:T(8,128)(2,1)S(1)}, bf16[32,2048]{1,0:T(8,128)(2,1)S(1)}, u32[]{:S(2)}, u32[]{:S(2)}) collective-permute-start(bf16[32,2048]{1,0:T(8,128)(2,1)S(1)} %get-tuple-element.77), channel_id=1, source_target_pairs={{0,4},{2,6},{4,0},{6,2},{8,12},{10,14},{12,8},{14,10},{16,20},{18,... | collective-permute-start | bytes 393224 | tf_op jit(solution)/shard_map/ppermute | solution.py:120
  20.5 16.4 %collective-permute-start.9 = (bf16[5,32,2048]{2,1,0:T(8,128)(2,1)S(1)}, bf16[5,32,2048]{2,1,0:T(8,128)(2,1)S(1)}, u32[]{:S(2)}, u32[]{:S(2)}) collective-permute-start(bf16[5,32,2048]{2,1,0:T(8,128)(2,1)S(1)} %bitcast_dynamic-update-slice_fusion.4.refs_0_), channel_id=1, source_target_pairs={{0,2},{2,0},{4,6},{6,4},{8,10},{10,8},{12,14},{14,12},{16,18},{18,... | collective-permute-start | bytes 1966088 | tf_op jit(solution)/shard_map/ppermute | solution.py:120
  21.0 5.5 %collective-permute-start.8 = (bf16[32,2048]{1,0:T(8,128)(2,1)S(1)}, bf16[32,2048]{1,0:T(8,128)(2,1)S(1)}, u32[]{:S(2)}, u32[]{:S(2)}) collective-permute-start(bf16[32,2048]{1,0:T(8,128)(2,1)S(1)} %collective-permute-done.5), channel_id=1, source_target_pairs={{0,24},{2,26},{4,28},{6,30},{8,0},{10,2},{12,4},{14,6},{16,8},{18,... | collective-permute-start | bytes 393224 | tf_op jit(solution)/shard_map/ppermute | solution.py:120
  21.0 14.0 %collective-permute-start.7 = (bf16[32,2048]{1,0:T(8,128)(2,1)S(1)}, bf16[32,2048]{1,0:T(8,128)(2,1)S(1)}, u32[]{:S(2)}, u32[]{:S(2)}) collective-permute-start(bf16[32,2048]{1,0:T(8,128)(2,1)S(1)} %collective-permute-done.5), channel_id=1, source_target_pairs={{0,16},{2,18},{4,20},{6,22},{8,24},{10,26},{12,28},{14,30},{16,0},... | collective-permute-start | bytes 393224 | tf_op jit(solution)/shard_map/ppermute | solution.py:120
  23.2 11.9 %collective-permute-start.6 = (bf16[32,2048]{1,0:T(8,128)(2,1)S(1)}, bf16[32,2048]{1,0:T(8,128)(2,1)S(1)}, u32[]{:S(2)}, u32[]{:S(2)}) collective-permute-start(bf16[32,2048]{1,0:T(8,128)(2,1)S(1)} %collective-permute-done.5), channel_id=1, source_target_pairs={{0,8},{2,10},{4,12},{6,14},{8,16},{10,18},{12,20},{14,22},{16,24},... | collective-permute-start | bytes 393224 | tf_op jit(solution)/shard_map/ppermute | solution.py:120
  23.6 13.9 %collective-permute-start.11 = (bf16[4,32,2048]{2,1,0:T(8,128)(2,1)S(1)}, bf16[4,32,2048]{2,1,0:T(8,128)(2,1)S(1)}, u32[]{:S(2)}, u32[]{:S(2)}) collective-permute-start(bf16[4,32,2048]{2,1,0:T(8,128)(2,1)S(1)} %slice.31), channel_id=1, source_target_pairs={{0,4},{2,6},{4,0},{6,2},{8,12},{10,14},{12,8},{14,10},{16,20},{18,... | collective-permute-start | bytes 1572872 | tf_op jit(solution)/shard_map/ppermute | solution.py:120
  38.4 18.7 %all-to-all-start = ((bf16[4,32,2048]{2,1,0:T(8,128)(2,1)}), bf16[4,32,2048]{2,1,0:T(8,128)(2,1)}, u32[]{:S(2)}, u32[]{:S(2)}) async-start(bf16[4,32,2048]{2,1,0:T(8,128)(2,1)} %fusion.1), calls=%async_computation | async-start | bytes 1048576 | tf_op jit(solution)/shard_map/all_to_all | solution.py:183
  50.6 7.6 %collective-permute-start.12 = (bf16[32,2048]{1,0:T(8,128)(2,1)S(1)}, bf16[32,2048]{1,0:T(8,128)(2,1)S(1)}, u32[]{:S(2)}, u32[]{:S(2)}) collective-permute-start(bf16[32,2048]{1,0:T(8,128)(2,1)S(1)} %bitcast.69), channel_id=1, source_target_pairs={{0,1},{1,0},{2,3},{3,2},{4,5},{5,4},{6,7},{7,6},{8,9},{9,8},{10,11... | collective-permute-start | bytes 393224 | tf_op jit(solution)/shard_map/ppermute | solution.py:123
  58.3 5.0 %collective-permute-start.16 = (bf16[32,2048]{1,0:T(8,128)(2,1)S(1)}, bf16[32,2048]{1,0:T(8,128)(2,1)S(1)}, u32[]{:S(2)}, u32[]{:S(2)}) collective-permute-start(bf16[32,2048]{1,0:T(8,128)(2,1)S(1)} %get-tuple-element.70), channel_id=1, source_target_pairs={{0,1},{1,0},{2,3},{3,2},{4,5},{5,4},{6,7},{7,6},{8,9},{9,8},{10,11... | collective-permute-start | bytes 393224 | tf_op jit(solution)/shard_map/ppermute | solution.py:123
  58.4 11.4 %collective-permute-start.13 = (bf16[32,2048]{1,0:T(8,128)(2,1)S(1)}, bf16[32,2048]{1,0:T(8,128)(2,1)S(1)}, u32[]{:S(2)}, u32[]{:S(2)}) collective-permute-start(bf16[32,2048]{1,0:T(8,128)(2,1)S(1)} %get-tuple-element.70), channel_id=1, source_target_pairs={{0,8},{2,10},{4,12},{6,14},{8,16},{10,18},{12,20},{14,22},{16,24},... | collective-permute-start | bytes 393224 | tf_op jit(solution)/shard_map/ppermute | solution.py:120
  58.5 12.0 %collective-permute-start.14 = (bf16[32,2048]{1,0:T(8,128)(2,1)S(1)}, bf16[32,2048]{1,0:T(8,128)(2,1)S(1)}, u32[]{:S(2)}, u32[]{:S(2)}) collective-permute-start(bf16[32,2048]{1,0:T(8,128)(2,1)S(1)} %get-tuple-element.70), channel_id=1, source_target_pairs={{0,16},{2,18},{4,20},{6,22},{8,24},{10,26},{12,28},{14,30},{16,0},... | collective-permute-start | bytes 393224 | tf_op jit(solution)/shard_map/ppermute | solution.py:120
  60.5 10.0 %collective-permute-start.15 = (bf16[32,2048]{1,0:T(8,128)(2,1)S(1)}, bf16[32,2048]{1,0:T(8,128)(2,1)S(1)}, u32[]{:S(2)}, u32[]{:S(2)}) collective-permute-start(bf16[32,2048]{1,0:T(8,128)(2,1)S(1)} %get-tuple-element.70), channel_id=1, source_target_pairs={{0,24},{2,26},{4,28},{6,30},{8,0},{10,2},{12,4},{14,6},{16,8},{18,... | collective-permute-start | bytes 393224 | tf_op jit(solution)/shard_map/ppermute | solution.py:120
  62.3 8.2 %collective-permute-start.18 = (bf16[32,2048]{1,0:T(8,128)(2,1)S(1)}, bf16[32,2048]{1,0:T(8,128)(2,1)S(1)}, u32[]{:S(2)}, u32[]{:S(2)}) collective-permute-start(bf16[32,2048]{1,0:T(8,128)(2,1)S(1)} %get-tuple-element.70), channel_id=1, source_target_pairs={{0,4},{2,6},{4,0},{6,2},{8,12},{10,14},{12,8},{14,10},{16,20},{18,... | collective-permute-start | bytes 393224 | tf_op jit(solution)/shard_map/ppermute | solution.py:120
  70.6 18.1 %collective-permute-start.22 = (bf16[5,32,2048]{2,1,0:T(8,128)(2,1)S(1)}, bf16[5,32,2048]{2,1,0:T(8,128)(2,1)S(1)}, u32[]{:S(2)}, u32[]{:S(2)}) collective-permute-start(bf16[5,32,2048]{2,1,0:T(8,128)(2,1)S(1)} %bitcast_dynamic-update-slice_fusion.refs_0_), channel_id=1, source_target_pairs={{0,2},{2,0},{4,6},{6,4},{8,10},{10,8},{12,14},{14,12},{16,18},{18,... | collective-permute-start | bytes 1966088 | tf_op jit(solution)/shard_map/ppermute | solution.py:120
  71.1 6.4 %collective-permute-start.21 = (bf16[32,2048]{1,0:T(8,128)(2,1)S(1)}, bf16[32,2048]{1,0:T(8,128)(2,1)S(1)}, u32[]{:S(2)}, u32[]{:S(2)}) collective-permute-start(bf16[32,2048]{1,0:T(8,128)(2,1)S(1)} %collective-permute-done.18), channel_id=1, source_target_pairs={{0,24},{2,26},{4,28},{6,30},{8,0},{10,2},{12,4},{14,6},{16,8},{18,... | collective-permute-start | bytes 393224 | tf_op jit(solution)/shard_map/ppermute | solution.py:120
  73.6 13.3 %collective-permute-start.20 = (bf16[32,2048]{1,0:T(8,128)(2,1)S(1)}, bf16[32,2048]{1,0:T(8,128)(2,1)S(1)}, u32[]{:S(2)}, u32[]{:S(2)}) collective-permute-start(bf16[32,2048]{1,0:T(8,128)(2,1)S(1)} %collective-permute-done.18), channel_id=1, source_target_pairs={{0,16},{2,18},{4,20},{6,22},{8,24},{10,26},{12,28},{14,30},{16,0},... | collective-permute-start | bytes 393224 | tf_op jit(solution)/shard_map/ppermute | solution.py:120
  75.0 11.9 %collective-permute-start.19 = (bf16[32,2048]{1,0:T(8,128)(2,1)S(1)}, bf16[32,2048]{1,0:T(8,128)(2,1)S(1)}, u32[]{:S(2)}, u32[]{:S(2)}) collective-permute-start(bf16[32,2048]{1,0:T(8,128)(2,1)S(1)} %collective-permute-done.18), channel_id=1, source_target_pairs={{0,8},{2,10},{4,12},{6,14},{8,16},{10,18},{12,20},{14,22},{16,24},... | collective-permute-start | bytes 393224 | tf_op jit(solution)/shard_map/ppermute | solution.py:120
  75.4 13.4 %collective-permute-start.24 = (bf16[4,32,2048]{2,1,0:T(8,128)(2,1)S(1)}, bf16[4,32,2048]{2,1,0:T(8,128)(2,1)S(1)}, u32[]{:S(2)}, u32[]{:S(2)}) collective-permute-start(bf16[4,32,2048]{2,1,0:T(8,128)(2,1)S(1)} %slice.30), channel_id=1, source_target_pairs={{0,4},{2,6},{4,0},{6,2},{8,12},{10,14},{12,8},{14,10},{16,20},{18,... | collective-permute-start | bytes 1572872 | tf_op jit(solution)/shard_map/ppermute | solution.py:120
  89.7 19.1 %all-to-all-start.1 = ((bf16[4,32,2048]{2,1,0:T(8,128)(2,1)}), bf16[4,32,2048]{2,1,0:T(8,128)(2,1)}, u32[]{:S(2)}, u32[]{:S(2)}) async-start(bf16[4,32,2048]{2,1,0:T(8,128)(2,1)} %fusion), calls=%async_computation.1 | async-start | bytes 1048576 | tf_op jit(solution)/shard_map/all_to_all | solution.py:183
  101.1 8.9 %collective-permute-start.25 = (bf16[32,2048]{1,0:T(8,128)(2,1)S(1)}, bf16[32,2048]{1,0:T(8,128)(2,1)S(1)}, u32[]{:S(2)}, u32[]{:S(2)}) collective-permute-start(bf16[32,2048]{1,0:T(8,128)(2,1)S(1)} %bitcast.68), channel_id=1, source_target_pairs={{0,1},{1,0},{2,3},{3,2},{4,5},{5,4},{6,7},{7,6},{8,9},{9,8},{10,11... | collective-permute-start | bytes 393224 | tf_op jit(solution)/shard_map/ppermute | solution.py:123
  (5 other events, 25.1 us)

commit v5 on v3

--- a/solution.py
+++ b/solution.py
@@ -91,8 +91,8 @@
         ],
         compiler_params=pltpu.CompilerParams(vmem_limit_bytes=40 * 1024 * 1024),
         cost_estimate=pl.CostEstimate(
-            flops=2 * capacity * size_block * size_block * 256,
-            bytes_accessed=2 * blocks.size + 2 * n_in * vector_count * own_rows,
+            flops=size_block,
+            bytes_accessed=size_block,
             transcendentals=0,
         ),
         name="mirror" if contract == 0 else "forward",
@@ -141,12 +141,16 @@
     put_rows = jnp.where(live, place_rows, n_col * per_piece)
 
     order = list(range(1, n_a)) + [0]
-    halves = [order[: n_a // 2], order[n_a // 2 :]] if n_a > 1 else [order]
+    halves = [order]
     mirror_outputs = [[piece(a, b, c) for b in range(n_b) for a in order] for c in range(n_c)]
     forward_outputs = [[j] for j in range(n_col)]
     mirror_inputs = [[j] for j in range(n_col)]
-    chip = [(0, b) for b in range(n_b)] + [(a, b) for b in range(n_b) for a in range(1, n_a)]
-    forward_inputs = [[piece(a, b, c) for a, b in chip] for c in range(n_c)]
+    chip = [[(0, b) for b in range(n_b)] + [(a, 0) for a in range(1, n_a)]]
+    rest_of_chip = [(a, b) for b in range(1, n_b) for a in range(1, n_a) if a != n_a // 2]
+    rest_of_chip += [(n_a // 2, b) for b in range(1, n_b) if n_a > 1]
+    if rest_of_chip:
+        chip.append(rest_of_chip)
+    forward_inputs = [[piece(a, b, c) for a, b in part] for c in range(n_c) for part in chip]
 
     def apply_operator(narrow):
         by_col = [narrow] + [shift_col(narrow, j) for j in range(1, n_col)]
@@ -157,7 +161,8 @@
             block_counts, place_rows, put_cols, by_col, block_values,
         )
         by_col, far, near, mirrors = lax.optimization_barrier((by_col, far, near, mirrors))
-        far_b = [shift(part, da=a) for part in near[1:] for a in range(1, n_a)]
+        middle = n_a // 2
+        across = [shift(far[middle - 1], db=b) for b in range(1, n_b)] if middle else []
 
         shares = mirrors[0].astype(jnp.float32)
         for c in range(1, n_c):
@@ -169,19 +174,21 @@
                 parts.append(shares[first : first + len(half)])
                 first += len(half)
         kept = parts[: len(halves)]
-        others = [
-            shift(part.astype(jnp.bfloat16), db=-(n // len(halves) + 1)) for n, part in enumerate(parts[len(halves) :])
-        ]
-        firsts, rest = others[:: len(halves)], others[1 :: len(halves)]
-        firsts, far_b = lax.optimization_barrier((firsts, far_b))
-
-
-        by_chip = jnp.stack(near + far + far_b)
-        by_row = [by_chip] + [shift(by_chip, dc=c) for c in range(1, n_c)]
+        sends = [part.astype(jnp.bfloat16) for part in parts[len(halves) :]]
+        others = [shift(send, db=-(n // len(halves) + 1)) for n, send in enumerate(sends)]
+        firsts = others
+        far_b = [shift(part, da=a) for part in near[1:] for a in range(1, n_a) if a != middle]
+        early = jnp.stack(near + far)
+        by_row = [[early] + [shift(early, dc=c) for c in range(1, n_c)]]
+        if far_b + across:
+            last = jnp.stack(far_b + across)
+            by_row.append([last] + [shift(last, dc=c) for c in range(1, n_c)])
+        by_row = [part[c] for c in range(n_c) for part in by_row]
 
         own = []
         back = []
-        for share, received, half in zip(kept, [firsts, rest], halves):
+
+        def add_up(share, received, half):
             for other in received:
                 share += other.astype(jnp.float32)
             for n, a in enumerate(half):
@@ -194,7 +201,8 @@
             1, forward_inputs, forward_outputs, [jnp.float32] + [jnp.bfloat16] * (n_col - 1), n_col,
             block_counts, place_cols, put_rows, by_row, block_values,
         )
-        back, mine = lax.optimization_barrier((back, forwards[0]))
+        firsts, mine = lax.optimization_barrier((firsts, forwards[0]))
+        add_up(kept[0], firsts, halves[0])
         forward_sum = mine[0]
         for j in range(1, n_col):
             forward_sum += shift_col(forwards[j][0], -j).astype(jnp.float32)

time: 105 us -> 107 us (1.019)
  Pallas kernels: 10.2 us -> 23.8 us
  starting transfers between devices: 42.9 us -> 34.1 us
  waiting for transfers between devices: 43.9 us -> 41.3 us
    pallas_call x4, Pallas kernels: 10.2 us -> 23.8 us  [block_product(): pl.pallas_call(functools.partial(product_kernel, contract, inputs, output...]
    ppermute x28, starting transfers between devices: 38.7 us -> 31 us  [shift(): return lax.ppermute(value, 'row', pairs)]
    ppermute x28, waiting for transfers between devices: 43.9 us -> 39.6 us  [shift(): return lax.ppermute(value, 'row', pairs)]
    ppermute x4, waiting for transfers between devices: 0.01 us -> 1.7 us  [shift_col(): lax.ppermute(value, 'col', [(j, (j + d) % n_col) for j in range(n_col)])]
    ppermute x4, starting transfers between devices: 4.26 us -> 3.09 us  [shift_col(): lax.ppermute(value, 'col', [(j, (j + d) % n_col) for j in range(n_col)])]
  transfers between devices with their start and end apart: 32 -> 32, of which waited for: 12 -> 17; matrix products, arithmetic and copies ran while one was open for 3% -> 3% of each run, Pallas kernels for 10% -> 22%
where the time goes in v5:
time: 107 us
  waiting for transfers between devices  41.3 us (39%)
  starting transfers between devices  34.1 us (32%)
  Pallas kernels  23.8 us (22%)
  other arithmetic  4.73 us (4%)
  between operations  2.29 us (2%)
    ppermute x28, waiting for transfers between devices, shift(): return lax.ppermute(value, 'row', pairs)  39.6 us
    ppermute x28, starting transfers between devices, shift(): return lax.ppermute(value, 'row', pairs)  31 us
    pallas_call x4, Pallas kernels, block_product(): pl.pallas_call(functools.partial(product_kernel, contract, inputs, output...  23.8 us
    ppermute x4, starting transfers between devices, shift_col(): lax.ppermute(value, 'col', [(j, (j + d) % n_col) for j in range(n_col)])  3.09 us
  transfers between devices with their start and end apart: 32, of which 17 were waited for; matrix products, arithmetic and copies ran while one was open for 3% of the time, Pallas kernels for 22%

profile of v5, /device:TPU:0, one launch (start us, length us, event | category | flops | bytes accessed | tf_op | source)
XLA Modules:
  0.0 106.6 jit_solution(4553253005768285205)
XLA Ops:
  1.0 3.0 %collective-permute-start.4 = (bf16[32,2048]{1,0:T(8,128)(2,1)S(1)}, bf16[32,2048]{1,0:T(8,128)(2,1)S(1)}, u32[]{:S(2)}, u32[]{:S(2)}) collective-permute-start(bf16[32,2048]{1,0:T(8,128)(2,1)S(1)} %convert_element_type.74), channel_id=1, source_target_pairs={{0,4},{2,6},{4,0},{6,2},{8,12},{10,14},{12,8},{14,10},{16,20},{18,... | collective-permute-start | bytes 393224 | tf_op jit(solution)/shard_map/ppermute | solution.py:120
  4.0 3.6 %collective-permute-start.3 = (bf16[32,2048]{1,0:T(8,128)(2,1)S(1)}, bf16[32,2048]{1,0:T(8,128)(2,1)S(1)}, u32[]{:S(2)}, u32[]{:S(2)}) collective-permute-start(bf16[32,2048]{1,0:T(8,128)(2,1)S(1)} %convert_element_type.74), channel_id=1, source_target_pairs={{0,24},{2,26},{4,28},{6,30},{8,0},{10,2},{12,4},{14,6},{16,8},{18,... | collective-permute-start | bytes 393224 | tf_op jit(solution)/shard_map/ppermute | solution.py:120
  13.6 5.9 %mirror.2 = (bf16[8,32,2048]{2,1,0:T(8,128)(2,1)S(1)}, bf16[8,32,2048]{2,1,0:T(8,128)(2,1)S(1)}) custom-call(s32[1]{0:T(128)} %copy.16.count_ref, s32[256]{0:T(256)S(1)} %get-tuple-element.64.take_ref, s32[256]{0:T(256)S(1)} %get-tuple-element.73.put_ref, bf16[1,32,2048]{2,1,0:T(8,128)(2,1)S(1)} %convert_bitcast_fusion.refs_0_, ...), custom_call_target="tpu_custom_call" | custom-call | flops 128 | bytes 128 | tf_op jit(solution)/shard_map/mirror/pallas_call | solution.py:79
  19.6 3.4 %collective-permute-start.8 = (bf16[32,2048]{1,0:T(8,128)(2,1)S(1)}, bf16[32,2048]{1,0:T(8,128)(2,1)S(1)}, u32[]{:S(2)}, u32[]{:S(2)}) collective-permute-start(bf16[32,2048]{1,0:T(8,128)(2,1)S(1)} %collective-permute-done.4), channel_id=1, source_target_pairs={{0,24},{2,26},{4,28},{6,30},{8,0},{10,2},{12,4},{14,6},{16,8},{18,... | collective-permute-start | bytes 393224 | tf_op jit(solution)/shard_map/ppermute | solution.py:120
  23.7 2.0 %collective-permute-done.5 = bf16[8,32,2048]{2,1,0:T(8,128)(2,1)S(1)} collective-permute-done((bf16[8,32,2048]{2,1,0:T(8,128)(2,1)S(1)}, bf16[8,32,2048]{2,1,0:T(8,128)(2,1)S(1)}, u32[]{:S(2)}, u32[]{:S(2)}) %collective-permute-start.5) | collective-permute-done | bytes 1048608 | tf_op jit(solution)/shard_map/ppermute | solution.py:120
  26.2 2.1 %collective-permute-start.6 = (bf16[4,32,2048]{2,1,0:T(8,128)(2,1)S(1)}, bf16[4,32,2048]{2,1,0:T(8,128)(2,1)S(1)}, u32[]{:S(2)}, u32[]{:S(2)}) collective-permute-start(bf16[4,32,2048]{2,1,0:T(8,128)(2,1)S(1)} %slice.109), channel_id=1, source_target_pairs={{0,4},{2,6},{4,0},{6,2},{8,12},{10,14},{12,8},{14,10},{16,20},{18,... | collective-permute-start | bytes 1572872 | tf_op jit(solution)/shard_map/ppermute | solution.py:120
  31.6 6.0 %forward.2 = (f32[1,32,2048]{2,1,0:T(8,128)S(1)}, bf16[1,32,2048]{2,1,0:T(8,128)(2,1)S(1)}) custom-call(s32[1]{0:T(128)} %copy.16.count_ref, s32[256]{0:T(256)S(1)} %get-tuple-element.74.take_ref, s32[256]{0:T(256)S(1)} %get-tuple-element.63.put_ref, bf16[5,32,2048]{2,1,0:T(8,128)(2,1)S(1)} %bitcast_dynamic-update-slice_fusion.5.refs_0_, ...), custom_call_target="tpu_custom_call" | custom-call | flops 128 | bytes 128 | tf_op jit(solution)/shard_map/forward/pallas_call | solution.py:79
  37.7 2.8 %collective-permute-done.6 = bf16[4,32,2048]{2,1,0:T(8,128)(2,1)S(1)} collective-permute-done((bf16[4,32,2048]{2,1,0:T(8,128)(2,1)S(1)}, bf16[4,32,2048]{2,1,0:T(8,128)(2,1)S(1)}, u32[]{:S(2)}, u32[]{:S(2)}) %collective-permute-start.6) | collective-permute-done | bytes 524320 | tf_op jit(solution)/shard_map/ppermute | solution.py:120
  40.7 3.9 %collective-permute-start.13 = (bf16[32,2048]{1,0:T(8,128)(2,1)S(1)}, bf16[32,2048]{1,0:T(8,128)(2,1)S(1)}, u32[]{:S(2)}, u32[]{:S(2)}) collective-permute-start(bf16[32,2048]{1,0:T(8,128)(2,1)S(1)} %get-tuple-element.70), channel_id=1, source_target_pairs={{0,24},{2,26},{4,28},{6,30},{8,0},{10,2},{12,4},{14,6},{16,8},{18,... | collective-permute-start | bytes 393224 | tf_op jit(solution)/shard_map/ppermute | solution.py:120
  46.5 2.0 %collective-permute-done.13 = bf16[32,2048]{1,0:T(8,128)(2,1)S(1)} collective-permute-done((bf16[32,2048]{1,0:T(8,128)(2,1)S(1)}, bf16[32,2048]{1,0:T(8,128)(2,1)S(1)}, u32[]{:S(2)}, u32[]{:S(2)}) %collective-permute-start.13) | collective-permute-done | bytes 131104 | tf_op jit(solution)/shard_map/ppermute | solution.py:120
  48.5 4.1 %collective-permute-done.15 = bf16[32,2048]{1,0:T(8,128)(2,1)S(1)} collective-permute-done((bf16[32,2048]{1,0:T(8,128)(2,1)S(1)}, bf16[32,2048]{1,0:T(8,128)(2,1)S(1)}, u32[]{:S(2)}, u32[]{:S(2)}) %collective-permute-start.15) | collective-permute-done | bytes 131104 | tf_op jit(solution)/shard_map/ppermute | solution.py:120
  52.6 3.2 %collective-permute-done.14 = bf16[32,2048]{1,0:T(8,128)(2,1)S(1)} collective-permute-done((bf16[32,2048]{1,0:T(8,128)(2,1)S(1)}, bf16[32,2048]{1,0:T(8,128)(2,1)S(1)}, u32[]{:S(2)}, u32[]{:S(2)}) %collective-permute-start.14) | collective-permute-done | bytes 131104 | tf_op jit(solution)/shard_map/ppermute | solution.py:120
  58.0 1.8 %collective-permute-start.19 = (bf16[32,2048]{1,0:T(8,128)(2,1)S(1)}, bf16[32,2048]{1,0:T(8,128)(2,1)S(1)}, u32[]{:S(2)}, u32[]{:S(2)}) collective-permute-start(bf16[32,2048]{1,0:T(8,128)(2,1)S(1)} %get-tuple-element.48), channel_id=1, source_target_pairs={{0,24},{2,26},{4,28},{6,30},{8,0},{10,2},{12,4},{14,6},{16,8},{18,... | collective-permute-start | bytes 393224 | tf_op jit(solution)/shard_map/ppermute | solution.py:120
  61.0 5.9 %mirror.3 = (bf16[8,32,2048]{2,1,0:T(8,128)(2,1)S(1)}, bf16[8,32,2048]{2,1,0:T(8,128)(2,1)S(1)}) custom-call(s32[1]{0:T(128)} %copy.16.count_ref, s32[256]{0:T(256)S(1)} %get-tuple-element.64.take_ref, s32[256]{0:T(256)S(1)} %get-tuple-element.73.put_ref, bf16[1,32,2048]{2,1,0:T(8,128)(2,1)S(1)} %bitcast.95, bf16[1,32,2048]{2,1,0:T(8,128)(2,1)S(1)} %bitcast.97, ...), custom_call_target="tpu_custom_call" | custom-call | flops 128 | bytes 128 | tf_op jit(solution)/shard_map/mirror/pallas_call | solution.py:79
  66.9 3.0 %collective-permute-done.18 = bf16[32,2048]{1,0:T(8,128)(2,1)S(1)} collective-permute-done((bf16[32,2048]{1,0:T(8,128)(2,1)S(1)}, bf16[32,2048]{1,0:T(8,128)(2,1)S(1)}, u32[]{:S(2)}, u32[]{:S(2)}) %collective-permute-start.18) | collective-permute-done | bytes 131104 | tf_op jit(solution)/shard_map/ppermute | solution.py:120
  69.9 1.9 %collective-permute-start.24 = (bf16[32,2048]{1,0:T(8,128)(2,1)S(1)}, bf16[32,2048]{1,0:T(8,128)(2,1)S(1)}, u32[]{:S(2)}, u32[]{:S(2)}) collective-permute-start(bf16[32,2048]{1,0:T(8,128)(2,1)S(1)} %collective-permute-done.20), channel_id=1, source_target_pairs={{0,24},{2,26},{4,28},{6,30},{8,0},{10,2},{12,4},{14,6},{16,8},{18,... | collective-permute-start | bytes 393224 | tf_op jit(solution)/shard_map/ppermute | solution.py:120
  74.3 2.0 %collective-permute-done.21 = bf16[8,32,2048]{2,1,0:T(8,128)(2,1)S(1)} collective-permute-done((bf16[8,32,2048]{2,1,0:T(8,128)(2,1)S(1)}, bf16[8,32,2048]{2,1,0:T(8,128)(2,1)S(1)}, u32[]{:S(2)}, u32[]{:S(2)}) %collective-permute-start.21) | collective-permute-done | bytes 1048608 | tf_op jit(solution)/shard_map/ppermute | solution.py:120
  77.2 2.1 %collective-permute-done.23 = bf16[32,2048]{1,0:T(8,128)(2,1)S(1)} collective-permute-done((bf16[32,2048]{1,0:T(8,128)(2,1)S(1)}, bf16[32,2048]{1,0:T(8,128)(2,1)S(1)}, u32[]{:S(2)}, u32[]{:S(2)}) %collective-permute-start.23) | collective-permute-done | bytes 131104 | tf_op jit(solution)/shard_map/ppermute | solution.py:120
  81.2 6.0 %forward.3 = (f32[1,32,2048]{2,1,0:T(8,128)S(1)}, bf16[1,32,2048]{2,1,0:T(8,128)(2,1)S(1)}) custom-call(s32[1]{0:T(128)} %copy.16.count_ref, s32[256]{0:T(256)S(1)} %get-tuple-element.74.take_ref, s32[256]{0:T(256)S(1)} %get-tuple-element.63.put_ref, bf16[5,32,2048]{2,1,0:T(8,128)(2,1)S(1)} %bitcast_dynamic-update-slice_fusion.refs_0_, ...), custom_call_target="tpu_custom_call" | custom-call | flops 128 | bytes 128 | tf_op jit(solution)/shard_map/forward/pallas_call | solution.py:79
  87.2 3.6 %collective-permute-done.22 = bf16[4,32,2048]{2,1,0:T(8,128)(2,1)S(1)} collective-permute-done((bf16[4,32,2048]{2,1,0:T(8,128)(2,1)S(1)}, bf16[4,32,2048]{2,1,0:T(8,128)(2,1)S(1)}, u32[]{:S(2)}, u32[]{:S(2)}) %collective-permute-start.22) | collective-permute-done | bytes 524320 | tf_op jit(solution)/shard_map/ppermute | solution.py:120
  91.0 3.8 %collective-permute-start.29 = (bf16[32,2048]{1,0:T(8,128)(2,1)S(1)}, bf16[32,2048]{1,0:T(8,128)(2,1)S(1)}, u32[]{:S(2)}, u32[]{:S(2)}) collective-permute-start(bf16[32,2048]{1,0:T(8,128)(2,1)S(1)} %get-tuple-element.67), channel_id=1, source_target_pairs={{0,24},{2,26},{4,28},{6,30},{8,0},{10,2},{12,4},{14,6},{16,8},{18,... | collective-permute-start | bytes 393224 | tf_op jit(solution)/shard_map/ppermute | solution.py:120
  95.9 2.9 %collective-permute-done.29 = bf16[32,2048]{1,0:T(8,128)(2,1)S(1)} collective-permute-done((bf16[32,2048]{1,0:T(8,128)(2,1)S(1)}, bf16[32,2048]{1,0:T(8,128)(2,1)S(1)}, u32[]{:S(2)}, u32[]{:S(2)}) %collective-permute-start.29) | collective-permute-done | bytes 131104 | tf_op jit(solution)/shard_map/ppermute | solution.py:120
  98.8 3.8 %collective-permute-done.31 = bf16[32,2048]{1,0:T(8,128)(2,1)S(1)} collective-permute-done((bf16[32,2048]{1,0:T(8,128)(2,1)S(1)}, bf16[32,2048]{1,0:T(8,128)(2,1)S(1)}, u32[]{:S(2)}, u32[]{:S(2)}) %collective-permute-start.31) | collective-permute-done | bytes 131104 | tf_op jit(solution)/shard_map/ppermute | solution.py:120
  102.6 3.2 %collective-permute-done.30 = bf16[32,2048]{1,0:T(8,128)(2,1)S(1)} collective-permute-done((bf16[32,2048]{1,0:T(8,128)(2,1)S(1)}, bf16[32,2048]{1,0:T(8,128)(2,1)S(1)}, u32[]{:S(2)}, u32[]{:S(2)}) %collective-permute-start.30) | collective-permute-done | bytes 131104 | tf_op jit(solution)/shard_map/ppermute | solution.py:120
  (71 shorter events, 22.3 us)
Async XLA Ops:
  1.0 18.5 %collective-permute-start.4 = (bf16[32,2048]{1,0:T(8,128)(2,1)S(1)}, bf16[32,2048]{1,0:T(8,128)(2,1)S(1)}, u32[]{:S(2)}, u32[]{:S(2)}) collective-permute-start(bf16[32,2048]{1,0:T(8,128)(2,1)S(1)} %convert_element_type.74), channel_id=1, source_target_pairs={{0,4},{2,6},{4,0},{6,2},{8,12},{10,14},{12,8},{14,10},{16,20},{18,... | collective-permute-start | bytes 393224 | tf_op jit(solution)/shard_map/ppermute | solution.py:120
  4.0 15.5 %collective-permute-start.3 = (bf16[32,2048]{1,0:T(8,128)(2,1)S(1)}, bf16[32,2048]{1,0:T(8,128)(2,1)S(1)}, u32[]{:S(2)}, u32[]{:S(2)}) collective-permute-start(bf16[32,2048]{1,0:T(8,128)(2,1)S(1)} %convert_element_type.74), channel_id=1, source_target_pairs={{0,24},{2,26},{4,28},{6,30},{8,0},{10,2},{12,4},{14,6},{16,8},{18,... | collective-permute-start | bytes 393224 | tf_op jit(solution)/shard_map/ppermute | solution.py:120
  7.6 11.9 %collective-permute-start.2 = (bf16[32,2048]{1,0:T(8,128)(2,1)S(1)}, bf16[32,2048]{1,0:T(8,128)(2,1)S(1)}, u32[]{:S(2)}, u32[]{:S(2)}) collective-permute-start(bf16[32,2048]{1,0:T(8,128)(2,1)S(1)} %convert_element_type.74), channel_id=1, source_target_pairs={{0,16},{2,18},{4,20},{6,22},{8,24},{10,26},{12,28},{14,30},{16,0},... | collective-permute-start | bytes 393224 | tf_op jit(solution)/shard_map/ppermute | solution.py:120
  7.6 11.9 %collective-permute-start.1 = (bf16[32,2048]{1,0:T(8,128)(2,1)S(1)}, bf16[32,2048]{1,0:T(8,128)(2,1)S(1)}, u32[]{:S(2)}, u32[]{:S(2)}) collective-permute-start(bf16[32,2048]{1,0:T(8,128)(2,1)S(1)} %convert_element_type.74), channel_id=1, source_target_pairs={{0,8},{2,10},{4,12},{6,14},{8,16},{10,18},{12,20},{14,22},{16,24},... | collective-permute-start | bytes 393224 | tf_op jit(solution)/shard_map/ppermute | solution.py:120
  19.6 8.7 %collective-permute-start.8 = (bf16[32,2048]{1,0:T(8,128)(2,1)S(1)}, bf16[32,2048]{1,0:T(8,128)(2,1)S(1)}, u32[]{:S(2)}, u32[]{:S(2)}) collective-permute-start(bf16[32,2048]{1,0:T(8,128)(2,1)S(1)} %collective-permute-done.4), channel_id=1, source_target_pairs={{0,24},{2,26},{4,28},{6,30},{8,0},{10,2},{12,4},{14,6},{16,8},{18,... | collective-permute-start | bytes 393224 | tf_op jit(solution)/shard_map/ppermute | solution.py:120
  23.0 6.8 %collective-permute-start.7 = (bf16[32,2048]{1,0:T(8,128)(2,1)S(1)}, bf16[32,2048]{1,0:T(8,128)(2,1)S(1)}, u32[]{:S(2)}, u32[]{:S(2)}) collective-permute-start(bf16[32,2048]{1,0:T(8,128)(2,1)S(1)} %collective-permute-done.4), channel_id=1, source_target_pairs={{0,8},{2,10},{4,12},{6,14},{8,16},{10,18},{12,20},{14,22},{16,24},... | collective-permute-start | bytes 393224 | tf_op jit(solution)/shard_map/ppermute | solution.py:120
  23.1 8.4 %collective-permute-start.10 = (bf16[5,32,2048]{2,1,0:T(8,128)(2,1)S(1)}, bf16[5,32,2048]{2,1,0:T(8,128)(2,1)S(1)}, u32[]{:S(2)}, u32[]{:S(2)}) collective-permute-start(bf16[5,32,2048]{2,1,0:T(8,128)(2,1)S(1)} %bitcast_dynamic-update-slice_fusion.5.refs_0_), channel_id=1, source_target_pairs={{0,2},{2,0},{4,6},{6,4},{8,10},{10,8},{12,14},{14,12},{16,18},{18,... | collective-permute-start | bytes 1966088 | tf_op jit(solution)/shard_map/ppermute | solution.py:120
  26.2 14.3 %collective-permute-start.6 = (bf16[4,32,2048]{2,1,0:T(8,128)(2,1)S(1)}, bf16[4,32,2048]{2,1,0:T(8,128)(2,1)S(1)}, u32[]{:S(2)}, u32[]{:S(2)}) collective-permute-start(bf16[4,32,2048]{2,1,0:T(8,128)(2,1)S(1)} %slice.109), channel_id=1, source_target_pairs={{0,4},{2,6},{4,0},{6,2},{8,12},{10,14},{12,8},{14,10},{16,20},{18,... | collective-permute-start | bytes 1572872 | tf_op jit(solution)/shard_map/ppermute | solution.py:120
  37.6 8.9 %collective-permute-start.12 = (bf16[32,2048]{1,0:T(8,128)(2,1)S(1)}, bf16[32,2048]{1,0:T(8,128)(2,1)S(1)}, u32[]{:S(2)}, u32[]{:S(2)}) collective-permute-start(bf16[32,2048]{1,0:T(8,128)(2,1)S(1)} %bitcast.99), channel_id=1, source_target_pairs={{0,1},{1,0},{2,3},{3,2},{4,5},{5,4},{6,7},{7,6},{8,9},{9,8},{10,11... | collective-permute-start | bytes 393224 | tf_op jit(solution)/shard_map/ppermute | solution.py:123
  40.7 7.8 %collective-permute-start.13 = (bf16[32,2048]{1,0:T(8,128)(2,1)S(1)}, bf16[32,2048]{1,0:T(8,128)(2,1)S(1)}, u32[]{:S(2)}, u32[]{:S(2)}) collective-permute-start(bf16[32,2048]{1,0:T(8,128)(2,1)S(1)} %get-tuple-element.70), channel_id=1, source_target_pairs={{0,24},{2,26},{4,28},{6,30},{8,0},{10,2},{12,4},{14,6},{16,8},{18,... | collective-permute-start | bytes 393224 | tf_op jit(solution)/shard_map/ppermute | solution.py:120
  44.5 8.1 %collective-permute-start.15 = (bf16[32,2048]{1,0:T(8,128)(2,1)S(1)}, bf16[32,2048]{1,0:T(8,128)(2,1)S(1)}, u32[]{:S(2)}, u32[]{:S(2)}) collective-permute-start(bf16[32,2048]{1,0:T(8,128)(2,1)S(1)} %get-tuple-element.71), channel_id=1, source_target_pairs={{0,8},{2,10},{4,12},{6,14},{8,16},{10,18},{12,20},{14,22},{16,24},... | collective-permute-start | bytes 393224 | tf_op jit(solution)/shard_map/ppermute | solution.py:120
  44.5 11.3 %collective-permute-start.14 = (bf16[32,2048]{1,0:T(8,128)(2,1)S(1)}, bf16[32,2048]{1,0:T(8,128)(2,1)S(1)}, u32[]{:S(2)}, u32[]{:S(2)}) collective-permute-start(bf16[32,2048]{1,0:T(8,128)(2,1)S(1)} %get-tuple-element.72), channel_id=1, source_target_pairs={{0,16},{2,18},{4,20},{6,22},{8,24},{10,26},{12,28},{14,30},{16,0},... | collective-permute-start | bytes 393224 | tf_op jit(solution)/shard_map/ppermute | solution.py:120
  57.4 9.5 %collective-permute-start.20 = (bf16[32,2048]{1,0:T(8,128)(2,1)S(1)}, bf16[32,2048]{1,0:T(8,128)(2,1)S(1)}, u32[]{:S(2)}, u32[]{:S(2)}) collective-permute-start(bf16[32,2048]{1,0:T(8,128)(2,1)S(1)} %get-tuple-element.48), channel_id=1, source_target_pairs={{0,4},{2,6},{4,0},{6,2},{8,12},{10,14},{12,8},{14,10},{16,20},{18,... | collective-permute-start | bytes 393224 | tf_op jit(solution)/shard_map/ppermute | solution.py:120
  58.0 8.9 %collective-permute-start.19 = (bf16[32,2048]{1,0:T(8,128)(2,1)S(1)}, bf16[32,2048]{1,0:T(8,128)(2,1)S(1)}, u32[]{:S(2)}, u32[]{:S(2)}) collective-permute-start(bf16[32,2048]{1,0:T(8,128)(2,1)S(1)} %get-tuple-element.48), channel_id=1, source_target_pairs={{0,24},{2,26},{4,28},{6,30},{8,0},{10,2},{12,4},{14,6},{16,8},{18,... | collective-permute-start | bytes 393224 | tf_op jit(solution)/shard_map/ppermute | solution.py:120
  59.8 10.1 %collective-permute-start.18 = (bf16[32,2048]{1,0:T(8,128)(2,1)S(1)}, bf16[32,2048]{1,0:T(8,128)(2,1)S(1)}, u32[]{:S(2)}, u32[]{:S(2)}) collective-permute-start(bf16[32,2048]{1,0:T(8,128)(2,1)S(1)} %get-tuple-element.48), channel_id=1, source_target_pairs={{0,16},{2,18},{4,20},{6,22},{8,24},{10,26},{12,28},{14,30},{16,0},... | collective-permute-start | bytes 393224 | tf_op jit(solution)/shard_map/ppermute | solution.py:120
  59.8 10.1 %collective-permute-start.17 = (bf16[32,2048]{1,0:T(8,128)(2,1)S(1)}, bf16[32,2048]{1,0:T(8,128)(2,1)S(1)}, u32[]{:S(2)}, u32[]{:S(2)}) collective-permute-start(bf16[32,2048]{1,0:T(8,128)(2,1)S(1)} %get-tuple-element.48), channel_id=1, source_target_pairs={{0,8},{2,10},{4,12},{6,14},{8,16},{10,18},{12,20},{14,22},{16,24},... | collective-permute-start | bytes 393224 | tf_op jit(solution)/shard_map/ppermute | solution.py:120
  69.9 7.3 %collective-permute-start.24 = (bf16[32,2048]{1,0:T(8,128)(2,1)S(1)}, bf16[32,2048]{1,0:T(8,128)(2,1)S(1)}, u32[]{:S(2)}, u32[]{:S(2)}) collective-permute-start(bf16[32,2048]{1,0:T(8,128)(2,1)S(1)} %collective-permute-done.20), channel_id=1, source_target_pairs={{0,24},{2,26},{4,28},{6,30},{8,0},{10,2},{12,4},{14,6},{16,8},{18,... | collective-permute-start | bytes 393224 | tf_op jit(solution)/shard_map/ppermute | solution.py:120
  71.8 7.5 %collective-permute-start.23 = (bf16[32,2048]{1,0:T(8,128)(2,1)S(1)}, bf16[32,2048]{1,0:T(8,128)(2,1)S(1)}, u32[]{:S(2)}, u32[]{:S(2)}) collective-permute-start(bf16[32,2048]{1,0:T(8,128)(2,1)S(1)} %collective-permute-done.20), channel_id=1, source_target_pairs={{0,8},{2,10},{4,12},{6,14},{8,16},{10,18},{12,20},{14,22},{16,24},... | collective-permute-start | bytes 393224 | tf_op jit(solution)/shard_map/ppermute | solution.py:120
  73.8 7.4 %collective-permute-start.26 = (bf16[5,32,2048]{2,1,0:T(8,128)(2,1)S(1)}, bf16[5,32,2048]{2,1,0:T(8,128)(2,1)S(1)}, u32[]{:S(2)}, u32[]{:S(2)}) collective-permute-start(bf16[5,32,2048]{2,1,0:T(8,128)(2,1)S(1)} %bitcast_dynamic-update-slice_fusion.refs_0_), channel_id=1, source_target_pairs={{0,2},{2,0},{4,6},{6,4},{8,10},{10,8},{12,14},{14,12},{16,18},{18,... | collective-permute-start | bytes 1966088 | tf_op jit(solution)/shard_map/ppermute | solution.py:120
  76.8 14.0 %collective-permute-start.22 = (bf16[4,32,2048]{2,1,0:T(8,128)(2,1)S(1)}, bf16[4,32,2048]{2,1,0:T(8,128)(2,1)S(1)}, u32[]{:S(2)}, u32[]{:S(2)}) collective-permute-start(bf16[4,32,2048]{2,1,0:T(8,128)(2,1)S(1)} %slice.108), channel_id=1, source_target_pairs={{0,4},{2,6},{4,0},{6,2},{8,12},{10,14},{12,8},{14,10},{16,20},{18,... | collective-permute-start | bytes 1572872 | tf_op jit(solution)/shard_map/ppermute | solution.py:120
  87.2 8.7 %collective-permute-start.28 = (bf16[32,2048]{1,0:T(8,128)(2,1)S(1)}, bf16[32,2048]{1,0:T(8,128)(2,1)S(1)}, u32[]{:S(2)}, u32[]{:S(2)}) collective-permute-start(bf16[32,2048]{1,0:T(8,128)(2,1)S(1)} %bitcast.98), channel_id=1, source_target_pairs={{0,1},{1,0},{2,3},{3,2},{4,5},{5,4},{6,7},{7,6},{8,9},{9,8},{10,11... | collective-permute-start | bytes 393224 | tf_op jit(solution)/shard_map/ppermute | solution.py:123
  91.0 7.8 %collective-permute-start.29 = (bf16[32,2048]{1,0:T(8,128)(2,1)S(1)}, bf16[32,2048]{1,0:T(8,128)(2,1)S(1)}, u32[]{:S(2)}, u32[]{:S(2)}) collective-permute-start(bf16[32,2048]{1,0:T(8,128)(2,1)S(1)} %get-tuple-element.67), channel_id=1, source_target_pairs={{0,24},{2,26},{4,28},{6,30},{8,0},{10,2},{12,4},{14,6},{16,8},{18,... | collective-permute-start | bytes 393224 | tf_op jit(solution)/shard_map/ppermute | solution.py:120
  94.8 7.8 %collective-permute-start.31 = (bf16[32,2048]{1,0:T(8,128)(2,1)S(1)}, bf16[32,2048]{1,0:T(8,128)(2,1)S(1)}, u32[]{:S(2)}, u32[]{:S(2)}) collective-permute-start(bf16[32,2048]{1,0:T(8,128)(2,1)S(1)} %get-tuple-element.68), channel_id=1, source_target_pairs={{0,8},{2,10},{4,12},{6,14},{8,16},{10,18},{12,20},{14,22},{16,24},... | collective-permute-start | bytes 393224 | tf_op jit(solution)/shard_map/ppermute | solution.py:120
  94.8 10.9 %collective-permute-start.30 = (bf16[32,2048]{1,0:T(8,128)(2,1)S(1)}, bf16[32,2048]{1,0:T(8,128)(2,1)S(1)}, u32[]{:S(2)}, u32[]{:S(2)}) collective-permute-start(bf16[32,2048]{1,0:T(8,128)(2,1)S(1)} %get-tuple-element.69), channel_id=1, source_target_pairs={{0,16},{2,18},{4,20},{6,22},{8,24},{10,26},{12,28},{14,30},{16,0},... | collective-permute-start | bytes 393224 | tf_op jit(solution)/shard_map/ppermute | solution.py:120
  (9 other events, 47.8 us)

commit v6 on v5

--- a/solution.py
+++ b/solution.py
@@ -160,7 +160,8 @@
             0, mirror_inputs, mirror_outputs, [jnp.bfloat16] * len(mirror_outputs), n_row,
             block_counts, place_rows, put_cols, by_col, block_values,
         )
-        by_col, far, near, mirrors = lax.optimization_barrier((by_col, far, near, mirrors))
+        mirrors = list(mirrors)
+        far, mirrors[0] = lax.optimization_barrier((far, mirrors[0]))
         middle = n_a // 2
         across = [shift(far[middle - 1], db=b) for b in range(1, n_b)] if middle else []
 

time: 107 us -> 103 us (0.963)
  starting transfers between devices: 34.1 us -> 31.4 us
    ppermute x28, starting transfers between devices: 31 us -> 29.4 us  [shift(): return lax.ppermute(value, 'row', pairs)]
    ppermute x4, starting transfers between devices: 3.09 us -> 1.93 us  [shift_col(): lax.ppermute(value, 'col', [(j, (j + d) % n_col) for j in range(n_col)])]
    convert_element_type x2 -> x0, other arithmetic: 1.09 us -> none  [the longest x1 0.96 us: shards(): vectors.astype(jnp.bfloat16)]
    unnamed x0 -> x2, other arithmetic: none -> 1.09 us
  transfers between devices with their start and end apart: 32 -> 32, of which waited for: 17 -> 16; matrix products, arithmetic and copies ran while one was open for 3% -> 2% of each run, Pallas kernels for 22% -> 23%
where the time goes in v6:
time: 103 us
  waiting for transfers between devices  41.4 us (40%)
  starting transfers between devices  31.4 us (30%)
  Pallas kernels  23.8 us (23%)
  other arithmetic  3.75 us (4%)
  between operations  2.24 us (2%)
    ppermute x28, waiting for transfers between devices, shift(): return lax.ppermute(value, 'row', pairs)  38.9 us
    ppermute x28, starting transfers between devices, shift(): return lax.ppermute(value, 'row', pairs)  29.4 us
    pallas_call x4, Pallas kernels, block_product(): pl.pallas_call(functools.partial(product_kernel, contract, inputs, output...  23.8 us
    ppermute x4, waiting for transfers between devices, shift_col(): lax.ppermute(value, 'col', [(j, (j + d) % n_col) for j in range(n_col)])  2.41 us
  transfers between devices with their start and end apart: 32, of which 16 were waited for; matrix products, arithmetic and copies ran while one was open for 2% of the time, Pallas kernels for 23%

profile of v6, /device:TPU:0, one launch (start us, length us, event | category | flops | bytes accessed | tf_op | source)
XLA Modules:
  0.0 102.8 jit_solution(1959587444049656933)
XLA Ops:
  1.0 3.0 %collective-permute-start.6 = (bf16[32,2048]{1,0:T(8,128)(2,1)S(1)}, bf16[32,2048]{1,0:T(8,128)(2,1)S(1)}, u32[]{:S(2)}, u32[]{:S(2)}) collective-permute-start(bf16[32,2048]{1,0:T(8,128)(2,1)S(1)} %get-tuple-element.53), channel_id=1, source_target_pairs={{0,4},{2,6},{4,0},{6,2},{8,12},{10,14},{12,8},{14,10},{16,20},{18,... | collective-permute-start | bytes 393224 | tf_op jit(solution)/shard_map/ppermute | solution.py:120
  5.5 3.6 %collective-permute-start.2 = (bf16[32,2048]{1,0:T(8,128)(2,1)S(1)}, bf16[32,2048]{1,0:T(8,128)(2,1)S(1)}, u32[]{:S(2)}, u32[]{:S(2)}) collective-permute-start(bf16[32,2048]{1,0:T(8,128)(2,1)S(1)} %get-tuple-element.53), channel_id=1, source_target_pairs={{0,24},{2,26},{4,28},{6,30},{8,0},{10,2},{12,4},{14,6},{16,8},{18,... | collective-permute-start | bytes 393224 | tf_op jit(solution)/shard_map/ppermute | solution.py:120
  11.5 5.9 %mirror.2 = (bf16[8,32,2048]{2,1,0:T(8,128)(2,1)S(1)}, bf16[8,32,2048]{2,1,0:T(8,128)(2,1)S(1)}) custom-call(s32[1]{0:T(128)} %copy.16.count_ref, s32[256]{0:T(256)S(1)} %get-tuple-element.55.take_ref, s32[256]{0:T(256)S(1)} %get-tuple-element.64.put_ref, bf16[1,32,2048]{2,1,0:T(8,128)(2,1)S(1)} %bitcast.93, bf16[1,32,2048]{2,1,0:T(8,128)(2,1)S(1)} %bitcast.94, ...), custom_call_target="tpu_custom_call" | custom-call | flops 128 | bytes 128 | tf_op jit(solution)/shard_map/mirror/pallas_call | solution.py:79
  17.5 2.4 %collective-permute-done.1 = bf16[32,2048]{1,0:T(8,128)(2,1)S(1)} collective-permute-done((bf16[32,2048]{1,0:T(8,128)(2,1)S(1)}, bf16[32,2048]{1,0:T(8,128)(2,1)S(1)}, u32[]{:S(2)}, u32[]{:S(2)}) %collective-permute-start.1) | collective-permute-done | bytes 131104 | tf_op jit(solution)/shard_map/ppermute | solution.py:120
  23.5 1.6 %collective-permute-start.5 = (bf16[4,32,2048]{2,1,0:T(8,128)(2,1)S(1)}, bf16[4,32,2048]{2,1,0:T(8,128)(2,1)S(1)}, u32[]{:S(2)}, u32[]{:S(2)}) collective-permute-start(bf16[4,32,2048]{2,1,0:T(8,128)(2,1)S(1)} %slice.109), channel_id=1, source_target_pairs={{0,4},{2,6},{4,0},{6,2},{8,12},{10,14},{12,8},{14,10},{16,20},{18,... | collective-permute-start | bytes 1572872 | tf_op jit(solution)/shard_map/ppermute | solution.py:120
  26.5 4.7 %collective-permute-done.7 = bf16[32,2048]{1,0:T(8,128)(2,1)S(1)} collective-permute-done((bf16[32,2048]{1,0:T(8,128)(2,1)S(1)}, bf16[32,2048]{1,0:T(8,128)(2,1)S(1)}, u32[]{:S(2)}, u32[]{:S(2)}) %collective-permute-start.7) | collective-permute-done | bytes 131104 | tf_op jit(solution)/shard_map/ppermute | solution.py:120
  31.4 1.7 %collective-permute-done.11.refs_3_ = bf16[3,32,2048]{2,1,0:T(8,128)(2,1)S(1)} collective-permute-done((bf16[3,32,2048]{2,1,0:T(8,128)(2,1)S(1)}, bf16[3,32,2048]{2,1,0:T(8,128)(2,1)S(1)}, u32[]{:S(2)}, u32[]{:S(2)}) %collective-permute-start.11) | collective-permute-done | bytes 393248 | tf_op jit(solution)/shard_map/ppermute | solution.py:120
  33.1 6.0 %forward.2 = (f32[1,32,2048]{2,1,0:T(8,128)S(1)}, bf16[1,32,2048]{2,1,0:T(8,128)(2,1)S(1)}) custom-call(s32[1]{0:T(128)} %copy.16.count_ref, s32[256]{0:T(256)S(1)} %get-tuple-element.65.take_ref, s32[256]{0:T(256)S(1)} %get-tuple-element.54.put_ref, bf16[5,32,2048]{2,1,0:T(8,128)(2,1)S(1)} %bitcast_dynamic-update-slice_fusion.4.refs_0_, ...), custom_call_target="tpu_custom_call" | custom-call | flops 128 | bytes 128 | tf_op jit(solution)/shard_map/forward/pallas_call | solution.py:79
  44.1 2.7 %collective-permute-done.13 = bf16[32,2048]{1,0:T(8,128)(2,1)S(1)} collective-permute-done((bf16[32,2048]{1,0:T(8,128)(2,1)S(1)}, bf16[32,2048]{1,0:T(8,128)(2,1)S(1)}, u32[]{:S(2)}, u32[]{:S(2)}) %collective-permute-start.13) | collective-permute-done | bytes 131104 | tf_op jit(solution)/shard_map/ppermute | solution.py:120
  46.8 1.8 %collective-permute-done.15 = bf16[32,2048]{1,0:T(8,128)(2,1)S(1)} collective-permute-done((bf16[32,2048]{1,0:T(8,128)(2,1)S(1)}, bf16[32,2048]{1,0:T(8,128)(2,1)S(1)}, u32[]{:S(2)}, u32[]{:S(2)}) %collective-permute-start.15) | collective-permute-done | bytes 131104 | tf_op jit(solution)/shard_map/ppermute | solution.py:120
  48.6 4.3 %collective-permute-done.14 = bf16[32,2048]{1,0:T(8,128)(2,1)S(1)} collective-permute-done((bf16[32,2048]{1,0:T(8,128)(2,1)S(1)}, bf16[32,2048]{1,0:T(8,128)(2,1)S(1)}, u32[]{:S(2)}, u32[]{:S(2)}) %collective-permute-start.14) | collective-permute-done | bytes 131104 | tf_op jit(solution)/shard_map/ppermute | solution.py:120
  53.4 2.6 %collective-permute-start.18 = (bf16[32,2048]{1,0:T(8,128)(2,1)S(1)}, bf16[32,2048]{1,0:T(8,128)(2,1)S(1)}, u32[]{:S(2)}, u32[]{:S(2)}) collective-permute-start(bf16[32,2048]{1,0:T(8,128)(2,1)S(1)} %get-tuple-element.48), channel_id=1, source_target_pairs={{0,24},{2,26},{4,28},{6,30},{8,0},{10,2},{12,4},{14,6},{16,8},{18,... | collective-permute-start | bytes 393224 | tf_op jit(solution)/shard_map/ppermute | solution.py:120
  56.5 2.3 %collective-permute-start.22 = (bf16[32,2048]{1,0:T(8,128)(2,1)S(1)}, bf16[32,2048]{1,0:T(8,128)(2,1)S(1)}, u32[]{:S(2)}, u32[]{:S(2)}) collective-permute-start(bf16[32,2048]{1,0:T(8,128)(2,1)S(1)} %get-tuple-element.48), channel_id=1, source_target_pairs={{0,4},{2,6},{4,0},{6,2},{8,12},{10,14},{12,8},{14,10},{16,20},{18,... | collective-permute-start | bytes 393224 | tf_op jit(solution)/shard_map/ppermute | solution.py:120
  58.8 5.9 %mirror.3 = (bf16[8,32,2048]{2,1,0:T(8,128)(2,1)S(1)}, bf16[8,32,2048]{2,1,0:T(8,128)(2,1)S(1)}) custom-call(s32[1]{0:T(128)} %copy.16.count_ref, s32[256]{0:T(256)S(1)} %get-tuple-element.55.take_ref, s32[256]{0:T(256)S(1)} %get-tuple-element.64.put_ref, bf16[1,32,2048]{2,1,0:T(8,128)(2,1)S(1)} %bitcast.92, bf16[1,32,2048]{2,1,0:T(8,128)(2,1)S(1)} %bitcast.95, ...), custom_call_target="tpu_custom_call" | custom-call | flops 128 | bytes 128 | tf_op jit(solution)/shard_map/mirror/pallas_call | solution.py:79
  64.7 1.7 %collective-permute-done.17 = bf16[32,2048]{1,0:T(8,128)(2,1)S(1)} collective-permute-done((bf16[32,2048]{1,0:T(8,128)(2,1)S(1)}, bf16[32,2048]{1,0:T(8,128)(2,1)S(1)}, u32[]{:S(2)}, u32[]{:S(2)}) %collective-permute-start.17) | collective-permute-done | bytes 131104 | tf_op jit(solution)/shard_map/ppermute | solution.py:120
  66.5 3.0 %collective-permute-start.25 = (bf16[32,2048]{1,0:T(8,128)(2,1)S(1)}, bf16[32,2048]{1,0:T(8,128)(2,1)S(1)}, u32[]{:S(2)}, u32[]{:S(2)}) collective-permute-start(bf16[32,2048]{1,0:T(8,128)(2,1)S(1)} %collective-permute-done.17), channel_id=1, source_target_pairs={{0,4},{2,6},{4,0},{6,2},{8,12},{10,14},{12,8},{14,10},{16,20},{18,... | collective-permute-start | bytes 393224 | tf_op jit(solution)/shard_map/ppermute | solution.py:120
  72.7 2.9 %collective-permute-done.24 = bf16[32,2048]{1,0:T(8,128)(2,1)S(1)} collective-permute-done((bf16[32,2048]{1,0:T(8,128)(2,1)S(1)}, bf16[32,2048]{1,0:T(8,128)(2,1)S(1)}, u32[]{:S(2)}, u32[]{:S(2)}) %collective-permute-start.24) | collective-permute-done | bytes 131104 | tf_op jit(solution)/shard_map/ppermute | solution.py:120
  75.7 4.6 %collective-permute-done.23 = bf16[32,2048]{1,0:T(8,128)(2,1)S(1)} collective-permute-done((bf16[32,2048]{1,0:T(8,128)(2,1)S(1)}, bf16[32,2048]{1,0:T(8,128)(2,1)S(1)}, u32[]{:S(2)}, u32[]{:S(2)}) %collective-permute-start.23) | collective-permute-done | bytes 131104 | tf_op jit(solution)/shard_map/ppermute | solution.py:120
  80.4 1.7 %collective-permute-done.27.refs_3_ = bf16[3,32,2048]{2,1,0:T(8,128)(2,1)S(1)} collective-permute-done((bf16[3,32,2048]{2,1,0:T(8,128)(2,1)S(1)}, bf16[3,32,2048]{2,1,0:T(8,128)(2,1)S(1)}, u32[]{:S(2)}, u32[]{:S(2)}) %collective-permute-start.27) | collective-permute-done | bytes 393248 | tf_op jit(solution)/shard_map/ppermute | solution.py:120
  82.1 6.0 %forward.3 = (f32[1,32,2048]{2,1,0:T(8,128)S(1)}, bf16[1,32,2048]{2,1,0:T(8,128)(2,1)S(1)}) custom-call(s32[1]{0:T(128)} %copy.16.count_ref, s32[256]{0:T(256)S(1)} %get-tuple-element.65.take_ref, s32[256]{0:T(256)S(1)} %get-tuple-element.54.put_ref, bf16[5,32,2048]{2,1,0:T(8,128)(2,1)S(1)} %bitcast_dynamic-update-slice_fusion.refs_0_, ...), custom_call_target="tpu_custom_call" | custom-call | flops 128 | bytes 128 | tf_op jit(solution)/shard_map/forward/pallas_call | solution.py:79
  91.3 1.8 %collective-permute-done.28 = bf16[32,2048]{1,0:T(8,128)(2,1)S(1)} collective-permute-done((bf16[32,2048]{1,0:T(8,128)(2,1)S(1)}, bf16[32,2048]{1,0:T(8,128)(2,1)S(1)}, u32[]{:S(2)}, u32[]{:S(2)}) %collective-permute-start.28) | collective-permute-done | bytes 131104 | tf_op jit(solution)/shard_map/ppermute | solution.py:123
  93.2 2.3 %collective-permute-done.29 = bf16[32,2048]{1,0:T(8,128)(2,1)S(1)} collective-permute-done((bf16[32,2048]{1,0:T(8,128)(2,1)S(1)}, bf16[32,2048]{1,0:T(8,128)(2,1)S(1)}, u32[]{:S(2)}, u32[]{:S(2)}) %collective-permute-start.29) | collective-permute-done | bytes 131104 | tf_op jit(solution)/shard_map/ppermute | solution.py:120
  95.5 2.3 %collective-permute-done.31 = bf16[32,2048]{1,0:T(8,128)(2,1)S(1)} collective-permute-done((bf16[32,2048]{1,0:T(8,128)(2,1)S(1)}, bf16[32,2048]{1,0:T(8,128)(2,1)S(1)}, u32[]{:S(2)}, u32[]{:S(2)}) %collective-permute-start.31) | collective-permute-done | bytes 131104 | tf_op jit(solution)/shard_map/ppermute | solution.py:120
  97.8 4.1 %collective-permute-done.30 = bf16[32,2048]{1,0:T(8,128)(2,1)S(1)} collective-permute-done((bf16[32,2048]{1,0:T(8,128)(2,1)S(1)}, bf16[32,2048]{1,0:T(8,128)(2,1)S(1)}, u32[]{:S(2)}, u32[]{:S(2)}) %collective-permute-start.30) | collective-permute-done | bytes 131104 | tf_op jit(solution)/shard_map/ppermute | solution.py:120
  (68 shorter events, 21.3 us)
Async XLA Ops:
  1.0 19.4 %collective-permute-start.6 = (bf16[32,2048]{1,0:T(8,128)(2,1)S(1)}, bf16[32,2048]{1,0:T(8,128)(2,1)S(1)}, u32[]{:S(2)}, u32[]{:S(2)}) collective-permute-start(bf16[32,2048]{1,0:T(8,128)(2,1)S(1)} %get-tuple-element.53), channel_id=1, source_target_pairs={{0,4},{2,6},{4,0},{6,2},{8,12},{10,14},{12,8},{14,10},{16,20},{18,... | collective-permute-start | bytes 393224 | tf_op jit(solution)/shard_map/ppermute | solution.py:120
  4.0 7.5 %collective-permute-start.3 = (bf16[32,2048]{1,0:T(8,128)(2,1)S(1)}, bf16[32,2048]{1,0:T(8,128)(2,1)S(1)}, u32[]{:S(2)}, u32[]{:S(2)}) collective-permute-start(bf16[32,2048]{1,0:T(8,128)(2,1)S(1)} %get-tuple-element.53), channel_id=1, source_target_pairs={{0,1},{1,0},{2,3},{3,2},{4,5},{5,4},{6,7},{7,6},{8,9},{9,8},{10,11... | collective-permute-start | bytes 393224 | tf_op jit(solution)/shard_map/ppermute | solution.py:123
  5.5 12.0 %collective-permute-start.2 = (bf16[32,2048]{1,0:T(8,128)(2,1)S(1)}, bf16[32,2048]{1,0:T(8,128)(2,1)S(1)}, u32[]{:S(2)}, u32[]{:S(2)}) collective-permute-start(bf16[32,2048]{1,0:T(8,128)(2,1)S(1)} %get-tuple-element.53), channel_id=1, source_target_pairs={{0,24},{2,26},{4,28},{6,30},{8,0},{10,2},{12,4},{14,6},{16,8},{18,... | collective-permute-start | bytes 393224 | tf_op jit(solution)/shard_map/ppermute | solution.py:120
  9.1 10.8 %collective-permute-start.1 = (bf16[32,2048]{1,0:T(8,128)(2,1)S(1)}, bf16[32,2048]{1,0:T(8,128)(2,1)S(1)}, u32[]{:S(2)}, u32[]{:S(2)}) collective-permute-start(bf16[32,2048]{1,0:T(8,128)(2,1)S(1)} %get-tuple-element.53), channel_id=1, source_target_pairs={{0,16},{2,18},{4,20},{6,22},{8,24},{10,26},{12,28},{14,30},{16,0},... | collective-permute-start | bytes 393224 | tf_op jit(solution)/shard_map/ppermute | solution.py:120
  9.1 10.8 %collective-permute-start = (bf16[32,2048]{1,0:T(8,128)(2,1)S(1)}, bf16[32,2048]{1,0:T(8,128)(2,1)S(1)}, u32[]{:S(2)}, u32[]{:S(2)}) collective-permute-start(bf16[32,2048]{1,0:T(8,128)(2,1)S(1)} %get-tuple-element.53), channel_id=1, source_target_pairs={{0,8},{2,10},{4,12},{6,14},{8,16},{10,18},{12,20},{14,22},{16,24},... | collective-permute-start | bytes 393224 | tf_op jit(solution)/shard_map/ppermute | solution.py:120
  19.9 11.3 %collective-permute-start.9 = (bf16[32,2048]{1,0:T(8,128)(2,1)S(1)}, bf16[32,2048]{1,0:T(8,128)(2,1)S(1)}, u32[]{:S(2)}, u32[]{:S(2)}) collective-permute-start(bf16[32,2048]{1,0:T(8,128)(2,1)S(1)} %collective-permute-done.1), channel_id=1, source_target_pairs={{0,4},{2,6},{4,0},{6,2},{8,12},{10,14},{12,8},{14,10},{16,20},{18,... | collective-permute-start | bytes 393224 | tf_op jit(solution)/shard_map/ppermute | solution.py:120
  20.5 12.6 %collective-permute-start.10 = (bf16[5,32,2048]{2,1,0:T(8,128)(2,1)S(1)}, bf16[5,32,2048]{2,1,0:T(8,128)(2,1)S(1)}, u32[]{:S(2)}, u32[]{:S(2)}) collective-permute-start(bf16[5,32,2048]{2,1,0:T(8,128)(2,1)S(1)} %bitcast_dynamic-update-slice_fusion.4.refs_0_), channel_id=1, source_target_pairs={{0,2},{2,0},{4,6},{6,4},{8,10},{10,8},{12,14},{14,12},{16,18},{18,... | collective-permute-start | bytes 1966088 | tf_op jit(solution)/shard_map/ppermute | solution.py:120
  22.5 8.7 %collective-permute-start.7 = (bf16[32,2048]{1,0:T(8,128)(2,1)S(1)}, bf16[32,2048]{1,0:T(8,128)(2,1)S(1)}, u32[]{:S(2)}, u32[]{:S(2)}) collective-permute-start(bf16[32,2048]{1,0:T(8,128)(2,1)S(1)} %collective-permute-done.6), channel_id=1, source_target_pairs={{0,8},{2,10},{4,12},{6,14},{8,16},{10,18},{12,20},{14,22},{16,24},... | collective-permute-start | bytes 393224 | tf_op jit(solution)/shard_map/ppermute | solution.py:120
  23.5 15.7 %collective-permute-start.5 = (bf16[4,32,2048]{2,1,0:T(8,128)(2,1)S(1)}, bf16[4,32,2048]{2,1,0:T(8,128)(2,1)S(1)}, u32[]{:S(2)}, u32[]{:S(2)}) collective-permute-start(bf16[4,32,2048]{2,1,0:T(8,128)(2,1)S(1)} %slice.109), channel_id=1, source_target_pairs={{0,4},{2,6},{4,0},{6,2},{8,12},{10,14},{12,8},{14,10},{16,20},{18,... | collective-permute-start | bytes 1572872 | tf_op jit(solution)/shard_map/ppermute | solution.py:120
  39.4 7.5 %collective-permute-start.13 = (bf16[32,2048]{1,0:T(8,128)(2,1)S(1)}, bf16[32,2048]{1,0:T(8,128)(2,1)S(1)}, u32[]{:S(2)}, u32[]{:S(2)}) collective-permute-start(bf16[32,2048]{1,0:T(8,128)(2,1)S(1)} %get-tuple-element.61), channel_id=1, source_target_pairs={{0,24},{2,26},{4,28},{6,30},{8,0},{10,2},{12,4},{14,6},{16,8},{18,... | collective-permute-start | bytes 393224 | tf_op jit(solution)/shard_map/ppermute | solution.py:120
  40.4 8.2 %collective-permute-start.15 = (bf16[32,2048]{1,0:T(8,128)(2,1)S(1)}, bf16[32,2048]{1,0:T(8,128)(2,1)S(1)}, u32[]{:S(2)}, u32[]{:S(2)}) collective-permute-start(bf16[32,2048]{1,0:T(8,128)(2,1)S(1)} %get-tuple-element.62), channel_id=1, source_target_pairs={{0,8},{2,10},{4,12},{6,14},{8,16},{10,18},{12,20},{14,22},{16,24},... | collective-permute-start | bytes 393224 | tf_op jit(solution)/shard_map/ppermute | solution.py:120
  41.5 11.5 %collective-permute-start.14 = (bf16[32,2048]{1,0:T(8,128)(2,1)S(1)}, bf16[32,2048]{1,0:T(8,128)(2,1)S(1)}, u32[]{:S(2)}, u32[]{:S(2)}) collective-permute-start(bf16[32,2048]{1,0:T(8,128)(2,1)S(1)} %get-tuple-element.63), channel_id=1, source_target_pairs={{0,16},{2,18},{4,20},{6,22},{8,24},{10,26},{12,28},{14,30},{16,0},... | collective-permute-start | bytes 393224 | tf_op jit(solution)/shard_map/ppermute | solution.py:120
  53.1 5.8 %collective-permute-start.19 = (bf16[32,2048]{1,0:T(8,128)(2,1)S(1)}, bf16[32,2048]{1,0:T(8,128)(2,1)S(1)}, u32[]{:S(2)}, u32[]{:S(2)}) collective-permute-start(bf16[32,2048]{1,0:T(8,128)(2,1)S(1)} %get-tuple-element.48), channel_id=1, source_target_pairs={{0,1},{1,0},{2,3},{3,2},{4,5},{5,4},{6,7},{7,6},{8,9},{9,8},{10,11... | collective-permute-start | bytes 393224 | tf_op jit(solution)/shard_map/ppermute | solution.py:123
  53.4 11.4 %collective-permute-start.18 = (bf16[32,2048]{1,0:T(8,128)(2,1)S(1)}, bf16[32,2048]{1,0:T(8,128)(2,1)S(1)}, u32[]{:S(2)}, u32[]{:S(2)}) collective-permute-start(bf16[32,2048]{1,0:T(8,128)(2,1)S(1)} %get-tuple-element.48), channel_id=1, source_target_pairs={{0,24},{2,26},{4,28},{6,30},{8,0},{10,2},{12,4},{14,6},{16,8},{18,... | collective-permute-start | bytes 393224 | tf_op jit(solution)/shard_map/ppermute | solution.py:120
  55.9 10.6 %collective-permute-start.17 = (bf16[32,2048]{1,0:T(8,128)(2,1)S(1)}, bf16[32,2048]{1,0:T(8,128)(2,1)S(1)}, u32[]{:S(2)}, u32[]{:S(2)}) collective-permute-start(bf16[32,2048]{1,0:T(8,128)(2,1)S(1)} %get-tuple-element.48), channel_id=1, source_target_pairs={{0,16},{2,18},{4,20},{6,22},{8,24},{10,26},{12,28},{14,30},{16,0},... | collective-permute-start | bytes 393224 | tf_op jit(solution)/shard_map/ppermute | solution.py:120
  55.9 10.6 %collective-permute-start.16 = (bf16[32,2048]{1,0:T(8,128)(2,1)S(1)}, bf16[32,2048]{1,0:T(8,128)(2,1)S(1)}, u32[]{:S(2)}, u32[]{:S(2)}) collective-permute-start(bf16[32,2048]{1,0:T(8,128)(2,1)S(1)} %get-tuple-element.48), channel_id=1, source_target_pairs={{0,8},{2,10},{4,12},{6,14},{8,16},{10,18},{12,20},{14,22},{16,24},... | collective-permute-start | bytes 393224 | tf_op jit(solution)/shard_map/ppermute | solution.py:120
  56.5 13.0 %collective-permute-start.22 = (bf16[32,2048]{1,0:T(8,128)(2,1)S(1)}, bf16[32,2048]{1,0:T(8,128)(2,1)S(1)}, u32[]{:S(2)}, u32[]{:S(2)}) collective-permute-start(bf16[32,2048]{1,0:T(8,128)(2,1)S(1)} %get-tuple-element.48), channel_id=1, source_target_pairs={{0,4},{2,6},{4,0},{6,2},{8,12},{10,14},{12,8},{14,10},{16,20},{18,... | collective-permute-start | bytes 393224 | tf_op jit(solution)/shard_map/ppermute | solution.py:120
  66.5 13.8 %collective-permute-start.25 = (bf16[32,2048]{1,0:T(8,128)(2,1)S(1)}, bf16[32,2048]{1,0:T(8,128)(2,1)S(1)}, u32[]{:S(2)}, u32[]{:S(2)}) collective-permute-start(bf16[32,2048]{1,0:T(8,128)(2,1)S(1)} %collective-permute-done.17), channel_id=1, source_target_pairs={{0,4},{2,6},{4,0},{6,2},{8,12},{10,14},{12,8},{14,10},{16,20},{18,... | collective-permute-start | bytes 393224 | tf_op jit(solution)/shard_map/ppermute | solution.py:120
  69.6 12.5 %collective-permute-start.26 = (bf16[5,32,2048]{2,1,0:T(8,128)(2,1)S(1)}, bf16[5,32,2048]{2,1,0:T(8,128)(2,1)S(1)}, u32[]{:S(2)}, u32[]{:S(2)}) collective-permute-start(bf16[5,32,2048]{2,1,0:T(8,128)(2,1)S(1)} %bitcast_dynamic-update-slice_fusion.refs_0_), channel_id=1, source_target_pairs={{0,2},{2,0},{4,6},{6,4},{8,10},{10,8},{12,14},{14,12},{16,18},{18,... | collective-permute-start | bytes 1966088 | tf_op jit(solution)/shard_map/ppermute | solution.py:120
  71.7 8.6 %collective-permute-start.23 = (bf16[32,2048]{1,0:T(8,128)(2,1)S(1)}, bf16[32,2048]{1,0:T(8,128)(2,1)S(1)}, u32[]{:S(2)}, u32[]{:S(2)}) collective-permute-start(bf16[32,2048]{1,0:T(8,128)(2,1)S(1)} %collective-permute-done.22), channel_id=1, source_target_pairs={{0,8},{2,10},{4,12},{6,14},{8,16},{10,18},{12,20},{14,22},{16,24},... | collective-permute-start | bytes 393224 | tf_op jit(solution)/shard_map/ppermute | solution.py:120
  72.6 15.6 %collective-permute-start.21 = (bf16[4,32,2048]{2,1,0:T(8,128)(2,1)S(1)}, bf16[4,32,2048]{2,1,0:T(8,128)(2,1)S(1)}, u32[]{:S(2)}, u32[]{:S(2)}) collective-permute-start(bf16[4,32,2048]{2,1,0:T(8,128)(2,1)S(1)} %slice.108), channel_id=1, source_target_pairs={{0,4},{2,6},{4,0},{6,2},{8,12},{10,14},{12,8},{14,10},{16,20},{18,... | collective-permute-start | bytes 1572872 | tf_op jit(solution)/shard_map/ppermute | solution.py:120
  88.4 7.1 %collective-permute-start.29 = (bf16[32,2048]{1,0:T(8,128)(2,1)S(1)}, bf16[32,2048]{1,0:T(8,128)(2,1)S(1)}, u32[]{:S(2)}, u32[]{:S(2)}) collective-permute-start(bf16[32,2048]{1,0:T(8,128)(2,1)S(1)} %get-tuple-element.58), channel_id=1, source_target_pairs={{0,24},{2,26},{4,28},{6,30},{8,0},{10,2},{12,4},{14,6},{16,8},{18,... | collective-permute-start | bytes 393224 | tf_op jit(solution)/shard_map/ppermute | solution.py:120
  89.6 8.2 %collective-permute-start.31 = (bf16[32,2048]{1,0:T(8,128)(2,1)S(1)}, bf16[32,2048]{1,0:T(8,128)(2,1)S(1)}, u32[]{:S(2)}, u32[]{:S(2)}) collective-permute-start(bf16[32,2048]{1,0:T(8,128)(2,1)S(1)} %get-tuple-element.59), channel_id=1, source_target_pairs={{0,8},{2,10},{4,12},{6,14},{8,16},{10,18},{12,20},{14,22},{16,24},... | collective-permute-start | bytes 393224 | tf_op jit(solution)/shard_map/ppermute | solution.py:120
  90.5 11.5 %collective-permute-start.30 = (bf16[32,2048]{1,0:T(8,128)(2,1)S(1)}, bf16[32,2048]{1,0:T(8,128)(2,1)S(1)}, u32[]{:S(2)}, u32[]{:S(2)}) collective-permute-start(bf16[32,2048]{1,0:T(8,128)(2,1)S(1)} %get-tuple-element.60), channel_id=1, source_target_pairs={{0,16},{2,18},{4,20},{6,22},{8,24},{10,26},{12,28},{14,30},{16,0},... | collective-permute-start | bytes 393224 | tf_op jit(solution)/shard_map/ppermute | solution.py:120
  (9 other events, 43.8 us)

commit v7 on v6

--- a/solution.py
+++ b/solution.py
@@ -141,7 +141,7 @@
     put_rows = jnp.where(live, place_rows, n_col * per_piece)
 
     order = list(range(1, n_a)) + [0]
-    halves = [order]
+    halves = [order[: n_a // 2], order[n_a // 2 :]] if n_a > 1 else [order]
     mirror_outputs = [[piece(a, b, c) for b in range(n_b) for a in order] for c in range(n_c)]
     forward_outputs = [[j] for j in range(n_col)]
     mirror_inputs = [[j] for j in range(n_col)]
@@ -177,8 +177,9 @@
         kept = parts[: len(halves)]
         sends = [part.astype(jnp.bfloat16) for part in parts[len(halves) :]]
         others = [shift(send, db=-(n // len(halves) + 1)) for n, send in enumerate(sends)]
-        firsts = others
+        firsts, rest = others[:: len(halves)], others[1 :: len(halves)]
         far_b = [shift(part, da=a) for part in near[1:] for a in range(1, n_a) if a != middle]
+        far_b, across, firsts = lax.optimization_barrier((far_b, across, firsts))
         early = jnp.stack(near + far)
         by_row = [[early] + [shift(early, dc=c) for c in range(1, n_c)]]
         if far_b + across:
@@ -198,15 +199,20 @@
                 else:
                     own.append(share[n])
 
+        add_up(kept[0], firsts, halves[0])
         forwards = block_product(
             1, forward_inputs, forward_outputs, [jnp.float32] + [jnp.bfloat16] * (n_col - 1), n_col,
             block_counts, place_cols, put_rows, by_row, block_values,
         )
-        firsts, mine = lax.optimization_barrier((firsts, forwards[0]))
-        add_up(kept[0], firsts, halves[0])
+        rest, back[:], mine = lax.optimization_barrier((rest, back, forwards[0]))
+        sent = len(back)
+        if len(halves) > 1:
+            add_up(kept[1], rest, halves[1])
+        crossed = [shift_col(forwards[j][0], -j) for j in range(1, n_col)]
+        crossed, back[:sent] = lax.optimization_barrier((crossed, back[:sent]))
         forward_sum = mine[0]
-        for j in range(1, n_col):
-            forward_sum += shift_col(forwards[j][0], -j).astype(jnp.float32)
+        for other in crossed:
+            forward_sum += other.astype(jnp.float32)
         mirror_sum = sum(own)
         for other in back:
             mirror_sum += other.astype(jnp.float32)

time: 103 us -> 97.9 us (0.950)
  waiting for transfers between devices: 41.4 us -> 36.3 us
  Pallas kernels: 23.8 us -> 21.6 us
  starting transfers between devices: 31.4 us -> 33.2 us
    ppermute x28 -> x30, waiting for transfers between devices: 38.9 us -> 34.7 us  [shift(): return lax.ppermute(value, 'row', pairs)]
    pallas_call x4, Pallas kernels: 23.8 us -> 21.6 us  [block_product(): pl.pallas_call(functools.partial(product_kernel, contract, inputs, output...]
    ppermute x4, starting transfers between devices: 1.93 us -> 3.75 us  [shift_col(): lax.ppermute(value, 'col', [(j, (j + d) % n_col) for j in range(n_col)])]
    ppermute x28 -> x30, starting transfers between devices: 29.4 us -> 29.5 us  [shift(): return lax.ppermute(value, 'row', pairs)]
  transfers between devices with their start and end apart: 32 -> 34, of which waited for: 16 -> 13; matrix products, arithmetic and copies ran while one was open for 2% -> 2% of each run, Pallas kernels for 23% -> 22%
where the time goes in v7:
time: 97.9 us; the launch traced here: 97.6 us
  waiting for transfers between devices  36.3 us (37%)
  starting transfers between devices  33.2 us (34%)
  Pallas kernels  21.6 us (22%)
  other arithmetic  3.89 us (4%)
  between operations  2.34 us (2%)
    ppermute x30, waiting for transfers between devices, shift(): return lax.ppermute(value, 'row', pairs)  34.7 us
    ppermute x30, starting transfers between devices, shift(): return lax.ppermute(value, 'row', pairs)  29.5 us
    pallas_call x4, Pallas kernels, block_product(): pl.pallas_call(functools.partial(product_kernel, contract, inputs, output...  21.6 us
    ppermute x4, starting transfers between devices, shift_col(): lax.ppermute(value, 'col', [(j, (j + d) % n_col) for j in range(n_col)])  3.75 us
  transfers between devices with their start and end apart: 34, of which 13 were waited for; matrix products, arithmetic and copies ran while one was open for 2% of the time, Pallas kernels for 22%

profile of v7, /device:TPU:0, one launch (start us, length us, event | category | flops | bytes accessed | tf_op | source)
XLA Modules:
  0.0 97.6 jit_solution(12158914196167504540)
XLA Ops:
  1.0 3.0 %collective-permute-start.3 = (bf16[32,2048]{1,0:T(8,128)(2,1)S(1)}, bf16[32,2048]{1,0:T(8,128)(2,1)S(1)}, u32[]{:S(2)}, u32[]{:S(2)}) collective-permute-start(bf16[32,2048]{1,0:T(8,128)(2,1)S(1)} %get-tuple-element.85), channel_id=1, source_target_pairs={{0,1},{1,0},{2,3},{3,2},{4,5},{5,4},{6,7},{7,6},{8,9},{9,8},{10,11... | collective-permute-start | bytes 393224 | tf_op jit(solution)/shard_map/ppermute | solution.py:123
  4.0 1.6 %collective-permute-start = (bf16[32,2048]{1,0:T(8,128)(2,1)S(1)}, bf16[32,2048]{1,0:T(8,128)(2,1)S(1)}, u32[]{:S(2)}, u32[]{:S(2)}) collective-permute-start(bf16[32,2048]{1,0:T(8,128)(2,1)S(1)} %get-tuple-element.85), channel_id=1, source_target_pairs={{0,8},{2,10},{4,12},{6,14},{8,16},{10,18},{12,20},{14,22},{16,24},... | collective-permute-start | bytes 393224 | tf_op jit(solution)/shard_map/ppermute | solution.py:120
  5.6 2.6 %collective-permute-start.1 = (bf16[32,2048]{1,0:T(8,128)(2,1)S(1)}, bf16[32,2048]{1,0:T(8,128)(2,1)S(1)}, u32[]{:S(2)}, u32[]{:S(2)}) collective-permute-start(bf16[32,2048]{1,0:T(8,128)(2,1)S(1)} %get-tuple-element.85), channel_id=1, source_target_pairs={{0,16},{2,18},{4,20},{6,22},{8,24},{10,26},{12,28},{14,30},{16,0},... | collective-permute-start | bytes 393224 | tf_op jit(solution)/shard_map/ppermute | solution.py:120
  12.4 5.4 %mirror.2 = (bf16[8,32,2048]{2,1,0:T(8,128)(2,1)S(1)}, bf16[8,32,2048]{2,1,0:T(8,128)(2,1)S(1)}) custom-call(s32[1]{0:T(128)} %copy.16.count_ref, s32[256]{0:T(256)S(1)} %get-tuple-element.87.take_ref, s32[256]{0:T(256)S(1)} %get-tuple-element.102.put_ref, bf16[1,32,2048]{2,1,0:T(8,128)(2,1)S(1)} %bitcast.93, bf16[1,32,2048]{2,1,0:T(8,128)(2,1)S(1)} %bitcast.94, ...), custom_call_target="tpu_custom_call" | custom-call | flops 128 | bytes 128 | tf_op jit(solution)/shard_map/mirror/pallas_call | solution.py:79
  18.1 3.3 %collective-permute-start.7 = (bf16[32,2048]{1,0:T(8,128)(2,1)S(1)}, bf16[32,2048]{1,0:T(8,128)(2,1)S(1)}, u32[]{:S(2)}, u32[]{:S(2)}) collective-permute-start(bf16[32,2048]{1,0:T(8,128)(2,1)S(1)} %collective-permute-done.6), channel_id=1, source_target_pairs={{0,8},{2,10},{4,12},{6,14},{8,16},{10,18},{12,20},{14,22},{16,24},... | collective-permute-start | bytes 393224 | tf_op jit(solution)/shard_map/ppermute | solution.py:120
  22.9 1.5 %collective-permute-start.10 = (bf16[2,32,2048]{2,1,0:T(8,128)(2,1)S(1)}, bf16[2,32,2048]{2,1,0:T(8,128)(2,1)S(1)}, u32[]{:S(2)}, u32[]{:S(2)}) collective-permute-start(bf16[2,32,2048]{2,1,0:T(8,128)(2,1)S(1)} %get-tuple-element.96), channel_id=1, source_target_pairs={{0,4},{2,6},{4,0},{6,2},{8,12},{10,14},{12,8},{14,10},{16,20},{18,... | collective-permute-start | bytes 786440 | tf_op jit(solution)/shard_map/ppermute | solution.py:120
  26.7 2.4 %collective-permute-done.8 = bf16[32,2048]{1,0:T(8,128)(2,1)S(1)} collective-permute-done((bf16[32,2048]{1,0:T(8,128)(2,1)S(1)}, bf16[32,2048]{1,0:T(8,128)(2,1)S(1)}, u32[]{:S(2)}, u32[]{:S(2)}) %collective-permute-start.8) | collective-permute-done | bytes 131104 | tf_op jit(solution)/shard_map/ppermute | solution.py:120
  29.1 3.1 %collective-permute-done.10 = bf16[2,32,2048]{2,1,0:T(8,128)(2,1)S(1)} collective-permute-done((bf16[2,32,2048]{2,1,0:T(8,128)(2,1)S(1)}, bf16[2,32,2048]{2,1,0:T(8,128)(2,1)S(1)}, u32[]{:S(2)}, u32[]{:S(2)}) %collective-permute-start.10) | collective-permute-done | bytes 262176 | tf_op jit(solution)/shard_map/ppermute | solution.py:120
  32.4 2.1 %collective-permute-start.11 = (bf16[32,2048]{1,0:T(8,128)(2,1)S(1)}, bf16[32,2048]{1,0:T(8,128)(2,1)S(1)}, u32[]{:S(2)}, u32[]{:S(2)}) collective-permute-start(bf16[32,2048]{1,0:T(8,128)(2,1)S(1)} %get-tuple-element.101), channel_id=1, source_target_pairs={{0,24},{2,26},{4,28},{6,30},{8,0},{10,2},{12,4},{14,6},{16,8},{18,... | collective-permute-start | bytes 393224 | tf_op jit(solution)/shard_map/ppermute | solution.py:120
  35.0 5.4 %forward.2 = (f32[1,32,2048]{2,1,0:T(8,128)S(1)}, bf16[1,32,2048]{2,1,0:T(8,128)(2,1)S(1)}) custom-call(s32[1]{0:T(128)} %copy.16.count_ref, s32[256]{0:T(256)S(1)} %get-tuple-element.103.take_ref, s32[256]{0:T(256)S(1)} %get-tuple-element.86.put_ref, bf16[5,32,2048]{2,1,0:T(8,128)(2,1)S(1)} %bitcast_dynamic-update-slice_fusion.4.refs_0_, ...), custom_call_target="tpu_custom_call" | custom-call | flops 128 | bytes 128 | tf_op jit(solution)/shard_map/forward/pallas_call | solution.py:79
  40.5 3.9 %collective-permute-done.12 = bf16[32,2048]{1,0:T(8,128)(2,1)S(1)} collective-permute-done((bf16[32,2048]{1,0:T(8,128)(2,1)S(1)}, bf16[32,2048]{1,0:T(8,128)(2,1)S(1)}, u32[]{:S(2)}, u32[]{:S(2)}) %collective-permute-start.12) | collective-permute-done | bytes 131104 | tf_op jit(solution)/shard_map/ppermute | solution.py:120
  45.9 5.6 %collective-permute-done.16 = bf16[32,2048]{1,0:T(8,128)(2,1)S(1)} collective-permute-done((bf16[32,2048]{1,0:T(8,128)(2,1)S(1)}, bf16[32,2048]{1,0:T(8,128)(2,1)S(1)}, u32[]{:S(2)}, u32[]{:S(2)}) %collective-permute-start.16) | collective-permute-done | bytes 131104 | tf_op jit(solution)/shard_map/ppermute | solution.py:120
  53.6 2.5 %collective-permute-start.19 = (bf16[32,2048]{1,0:T(8,128)(2,1)S(1)}, bf16[32,2048]{1,0:T(8,128)(2,1)S(1)}, u32[]{:S(2)}, u32[]{:S(2)}) collective-permute-start(bf16[32,2048]{1,0:T(8,128)(2,1)S(1)} %get-tuple-element.82), channel_id=1, source_target_pairs={{0,24},{2,26},{4,28},{6,30},{8,0},{10,2},{12,4},{14,6},{16,8},{18,... | collective-permute-start | bytes 393224 | tf_op jit(solution)/shard_map/ppermute | solution.py:120
  56.7 5.4 %mirror.3 = (bf16[8,32,2048]{2,1,0:T(8,128)(2,1)S(1)}, bf16[8,32,2048]{2,1,0:T(8,128)(2,1)S(1)}) custom-call(s32[1]{0:T(128)} %copy.16.count_ref, s32[256]{0:T(256)S(1)} %get-tuple-element.87.take_ref, s32[256]{0:T(256)S(1)} %get-tuple-element.102.put_ref, bf16[1,32,2048]{2,1,0:T(8,128)(2,1)S(1)} %bitcast.92, bf16[1,32,2048]{2,1,0:T(8,128)(2,1)S(1)} %bitcast.95, ...), custom_call_target="tpu_custom_call" | custom-call | flops 128 | bytes 128 | tf_op jit(solution)/shard_map/mirror/pallas_call | solution.py:79
  62.1 1.7 %collective-permute-done.18 = bf16[32,2048]{1,0:T(8,128)(2,1)S(1)} collective-permute-done((bf16[32,2048]{1,0:T(8,128)(2,1)S(1)}, bf16[32,2048]{1,0:T(8,128)(2,1)S(1)}, u32[]{:S(2)}, u32[]{:S(2)}) %collective-permute-start.18) | collective-permute-done | bytes 131104 | tf_op jit(solution)/shard_map/ppermute | solution.py:120
  64.3 2.3 %collective-permute-start.24 = (bf16[32,2048]{1,0:T(8,128)(2,1)S(1)}, bf16[32,2048]{1,0:T(8,128)(2,1)S(1)}, u32[]{:S(2)}, u32[]{:S(2)}) collective-permute-start(bf16[32,2048]{1,0:T(8,128)(2,1)S(1)} %collective-permute-done.23), channel_id=1, source_target_pairs={{0,8},{2,10},{4,12},{6,14},{8,16},{10,18},{12,20},{14,22},{16,24},... | collective-permute-start | bytes 393224 | tf_op jit(solution)/shard_map/ppermute | solution.py:120
  68.7 1.6 %collective-permute-start.27 = (bf16[2,32,2048]{2,1,0:T(8,128)(2,1)S(1)}, bf16[2,32,2048]{2,1,0:T(8,128)(2,1)S(1)}, u32[]{:S(2)}, u32[]{:S(2)}) collective-permute-start(bf16[2,32,2048]{2,1,0:T(8,128)(2,1)S(1)} %get-tuple-element.94), channel_id=1, source_target_pairs={{0,4},{2,6},{4,0},{6,2},{8,12},{10,14},{12,8},{14,10},{16,20},{18,... | collective-permute-start | bytes 786440 | tf_op jit(solution)/shard_map/ppermute | solution.py:120
  70.9 1.5 %collective-permute-done.24 = bf16[32,2048]{1,0:T(8,128)(2,1)S(1)} collective-permute-done((bf16[32,2048]{1,0:T(8,128)(2,1)S(1)}, bf16[32,2048]{1,0:T(8,128)(2,1)S(1)}, u32[]{:S(2)}, u32[]{:S(2)}) %collective-permute-start.24) | collective-permute-done | bytes 131104 | tf_op jit(solution)/shard_map/ppermute | solution.py:120
  72.5 2.2 %collective-permute-done.25 = bf16[32,2048]{1,0:T(8,128)(2,1)S(1)} collective-permute-done((bf16[32,2048]{1,0:T(8,128)(2,1)S(1)}, bf16[32,2048]{1,0:T(8,128)(2,1)S(1)}, u32[]{:S(2)}, u32[]{:S(2)}) %collective-permute-start.25) | collective-permute-done | bytes 131104 | tf_op jit(solution)/shard_map/ppermute | solution.py:120
  74.6 3.3 %collective-permute-done.27 = bf16[2,32,2048]{2,1,0:T(8,128)(2,1)S(1)} collective-permute-done((bf16[2,32,2048]{2,1,0:T(8,128)(2,1)S(1)}, bf16[2,32,2048]{2,1,0:T(8,128)(2,1)S(1)}, u32[]{:S(2)}, u32[]{:S(2)}) %collective-permute-start.27) | collective-permute-done | bytes 262176 | tf_op jit(solution)/shard_map/ppermute | solution.py:120
  78.2 2.0 %collective-permute-start.29 = (bf16[32,2048]{1,0:T(8,128)(2,1)S(1)}, bf16[32,2048]{1,0:T(8,128)(2,1)S(1)}, u32[]{:S(2)}, u32[]{:S(2)}) collective-permute-start(bf16[32,2048]{1,0:T(8,128)(2,1)S(1)} %get-tuple-element.98), channel_id=1, source_target_pairs={{0,16},{2,18},{4,20},{6,22},{8,24},{10,26},{12,28},{14,30},{16,0},... | collective-permute-start | bytes 393224 | tf_op jit(solution)/shard_map/ppermute | solution.py:120
  80.2 5.4 %forward.3 = (f32[1,32,2048]{2,1,0:T(8,128)S(1)}, bf16[1,32,2048]{2,1,0:T(8,128)(2,1)S(1)}) custom-call(s32[1]{0:T(128)} %copy.16.count_ref, s32[256]{0:T(256)S(1)} %get-tuple-element.103.take_ref, s32[256]{0:T(256)S(1)} %get-tuple-element.86.put_ref, bf16[5,32,2048]{2,1,0:T(8,128)(2,1)S(1)} %bitcast_dynamic-update-slice_fusion.refs_0_, ...), custom_call_target="tpu_custom_call" | custom-call | flops 128 | bytes 128 | tf_op jit(solution)/shard_map/forward/pallas_call | solution.py:79
  85.7 4.0 %collective-permute-done.29 = bf16[32,2048]{1,0:T(8,128)(2,1)S(1)} collective-permute-done((bf16[32,2048]{1,0:T(8,128)(2,1)S(1)}, bf16[32,2048]{1,0:T(8,128)(2,1)S(1)}, u32[]{:S(2)}, u32[]{:S(2)}) %collective-permute-start.29) | collective-permute-done | bytes 131104 | tf_op jit(solution)/shard_map/ppermute | solution.py:120
  91.4 5.4 %collective-permute-done.33 = bf16[32,2048]{1,0:T(8,128)(2,1)S(1)} collective-permute-done((bf16[32,2048]{1,0:T(8,128)(2,1)S(1)}, bf16[32,2048]{1,0:T(8,128)(2,1)S(1)}, u32[]{:S(2)}, u32[]{:S(2)}) %collective-permute-start.33) | collective-permute-done | bytes 131104 | tf_op jit(solution)/shard_map/ppermute | solution.py:120
  (76 shorter events, 18.0 us)
Async XLA Ops:
  1.0 11.4 %collective-permute-start.3 = (bf16[32,2048]{1,0:T(8,128)(2,1)S(1)}, bf16[32,2048]{1,0:T(8,128)(2,1)S(1)}, u32[]{:S(2)}, u32[]{:S(2)}) collective-permute-start(bf16[32,2048]{1,0:T(8,128)(2,1)S(1)} %get-tuple-element.85), channel_id=1, source_target_pairs={{0,1},{1,0},{2,3},{3,2},{4,5},{5,4},{6,7},{7,6},{8,9},{9,8},{10,11... | collective-permute-start | bytes 393224 | tf_op jit(solution)/shard_map/ppermute | solution.py:123
  4.0 13.8 %collective-permute-start = (bf16[32,2048]{1,0:T(8,128)(2,1)S(1)}, bf16[32,2048]{1,0:T(8,128)(2,1)S(1)}, u32[]{:S(2)}, u32[]{:S(2)}) collective-permute-start(bf16[32,2048]{1,0:T(8,128)(2,1)S(1)} %get-tuple-element.85), channel_id=1, source_target_pairs={{0,8},{2,10},{4,12},{6,14},{8,16},{10,18},{12,20},{14,22},{16,24},... | collective-permute-start | bytes 393224 | tf_op jit(solution)/shard_map/ppermute | solution.py:120
  5.6 12.3 %collective-permute-start.1 = (bf16[32,2048]{1,0:T(8,128)(2,1)S(1)}, bf16[32,2048]{1,0:T(8,128)(2,1)S(1)}, u32[]{:S(2)}, u32[]{:S(2)}) collective-permute-start(bf16[32,2048]{1,0:T(8,128)(2,1)S(1)} %get-tuple-element.85), channel_id=1, source_target_pairs={{0,16},{2,18},{4,20},{6,22},{8,24},{10,26},{12,28},{14,30},{16,0},... | collective-permute-start | bytes 393224 | tf_op jit(solution)/shard_map/ppermute | solution.py:120
  8.1 9.7 %collective-permute-start.2 = (bf16[32,2048]{1,0:T(8,128)(2,1)S(1)}, bf16[32,2048]{1,0:T(8,128)(2,1)S(1)}, u32[]{:S(2)}, u32[]{:S(2)}) collective-permute-start(bf16[32,2048]{1,0:T(8,128)(2,1)S(1)} %get-tuple-element.85), channel_id=1, source_target_pairs={{0,24},{2,26},{4,28},{6,30},{8,0},{10,2},{12,4},{14,6},{16,8},{18,... | collective-permute-start | bytes 393224 | tf_op jit(solution)/shard_map/ppermute | solution.py:120
  9.5 8.6 %collective-permute-start.6 = (bf16[32,2048]{1,0:T(8,128)(2,1)S(1)}, bf16[32,2048]{1,0:T(8,128)(2,1)S(1)}, u32[]{:S(2)}, u32[]{:S(2)}) collective-permute-start(bf16[32,2048]{1,0:T(8,128)(2,1)S(1)} %get-tuple-element.85), channel_id=1, source_target_pairs={{0,4},{2,6},{4,0},{6,2},{8,12},{10,14},{12,8},{14,10},{16,20},{18,... | collective-permute-start | bytes 393224 | tf_op jit(solution)/shard_map/ppermute | solution.py:120
  18.1 8.6 %collective-permute-start.7 = (bf16[32,2048]{1,0:T(8,128)(2,1)S(1)}, bf16[32,2048]{1,0:T(8,128)(2,1)S(1)}, u32[]{:S(2)}, u32[]{:S(2)}) collective-permute-start(bf16[32,2048]{1,0:T(8,128)(2,1)S(1)} %collective-permute-done.6), channel_id=1, source_target_pairs={{0,8},{2,10},{4,12},{6,14},{8,16},{10,18},{12,20},{14,22},{16,24},... | collective-permute-start | bytes 393224 | tf_op jit(solution)/shard_map/ppermute | solution.py:120
  21.4 7.7 %collective-permute-start.8 = (bf16[32,2048]{1,0:T(8,128)(2,1)S(1)}, bf16[32,2048]{1,0:T(8,128)(2,1)S(1)}, u32[]{:S(2)}, u32[]{:S(2)}) collective-permute-start(bf16[32,2048]{1,0:T(8,128)(2,1)S(1)} %collective-permute-done.6), channel_id=1, source_target_pairs={{0,24},{2,26},{4,28},{6,30},{8,0},{10,2},{12,4},{14,6},{16,8},{18,... | collective-permute-start | bytes 393224 | tf_op jit(solution)/shard_map/ppermute | solution.py:120
  22.9 9.2 %collective-permute-start.10 = (bf16[2,32,2048]{2,1,0:T(8,128)(2,1)S(1)}, bf16[2,32,2048]{2,1,0:T(8,128)(2,1)S(1)}, u32[]{:S(2)}, u32[]{:S(2)}) collective-permute-start(bf16[2,32,2048]{2,1,0:T(8,128)(2,1)S(1)} %get-tuple-element.96), channel_id=1, source_target_pairs={{0,4},{2,6},{4,0},{6,2},{8,12},{10,14},{12,8},{14,10},{16,20},{18,... | collective-permute-start | bytes 786440 | tf_op jit(solution)/shard_map/ppermute | solution.py:120
  24.5 10.5 %collective-permute-start.13 = (bf16[5,32,2048]{2,1,0:T(8,128)(2,1)S(1)}, bf16[5,32,2048]{2,1,0:T(8,128)(2,1)S(1)}, u32[]{:S(2)}, u32[]{:S(2)}) collective-permute-start(bf16[5,32,2048]{2,1,0:T(8,128)(2,1)S(1)} %bitcast_dynamic-update-slice_fusion.4.refs_0_), channel_id=1, source_target_pairs={{0,2},{2,0},{4,6},{6,4},{8,10},{10,8},{12,14},{14,12},{16,18},{18,... | collective-permute-start | bytes 1966088 | tf_op jit(solution)/shard_map/ppermute | solution.py:120
  24.6 15.9 %collective-permute-start.5 = (bf16[2,32,2048]{2,1,0:T(8,128)(2,1)S(1)}, bf16[2,32,2048]{2,1,0:T(8,128)(2,1)S(1)}, u32[]{:S(2)}, u32[]{:S(2)}) collective-permute-start(bf16[2,32,2048]{2,1,0:T(8,128)(2,1)S(1)} %get-tuple-element.97), channel_id=1, source_target_pairs={{0,4},{2,6},{4,0},{6,2},{8,12},{10,14},{12,8},{14,10},{16,20},{18,... | collective-permute-start | bytes 786440 | tf_op jit(solution)/shard_map/ppermute | solution.py:120
  32.4 8.1 %collective-permute-start.11 = (bf16[32,2048]{1,0:T(8,128)(2,1)S(1)}, bf16[32,2048]{1,0:T(8,128)(2,1)S(1)}, u32[]{:S(2)}, u32[]{:S(2)}) collective-permute-start(bf16[32,2048]{1,0:T(8,128)(2,1)S(1)} %get-tuple-element.101), channel_id=1, source_target_pairs={{0,24},{2,26},{4,28},{6,30},{8,0},{10,2},{12,4},{14,6},{16,8},{18,... | collective-permute-start | bytes 393224 | tf_op jit(solution)/shard_map/ppermute | solution.py:120
  34.5 9.9 %collective-permute-start.12 = (bf16[32,2048]{1,0:T(8,128)(2,1)S(1)}, bf16[32,2048]{1,0:T(8,128)(2,1)S(1)}, u32[]{:S(2)}, u32[]{:S(2)}) collective-permute-start(bf16[32,2048]{1,0:T(8,128)(2,1)S(1)} %get-tuple-element.100), channel_id=1, source_target_pairs={{0,16},{2,18},{4,20},{6,22},{8,24},{10,26},{12,28},{14,30},{16,0},... | collective-permute-start | bytes 393224 | tf_op jit(solution)/shard_map/ppermute | solution.py:120
  52.2 9.8 %collective-permute-start.17 = (bf16[32,2048]{1,0:T(8,128)(2,1)S(1)}, bf16[32,2048]{1,0:T(8,128)(2,1)S(1)}, u32[]{:S(2)}, u32[]{:S(2)}) collective-permute-start(bf16[32,2048]{1,0:T(8,128)(2,1)S(1)} %get-tuple-element.82), channel_id=1, source_target_pairs={{0,8},{2,10},{4,12},{6,14},{8,16},{10,18},{12,20},{14,22},{16,24},... | collective-permute-start | bytes 393224 | tf_op jit(solution)/shard_map/ppermute | solution.py:120
  52.2 11.6 %collective-permute-start.18 = (bf16[32,2048]{1,0:T(8,128)(2,1)S(1)}, bf16[32,2048]{1,0:T(8,128)(2,1)S(1)}, u32[]{:S(2)}, u32[]{:S(2)}) collective-permute-start(bf16[32,2048]{1,0:T(8,128)(2,1)S(1)} %get-tuple-element.82), channel_id=1, source_target_pairs={{0,16},{2,18},{4,20},{6,22},{8,24},{10,26},{12,28},{14,30},{16,0},... | collective-permute-start | bytes 393224 | tf_op jit(solution)/shard_map/ppermute | solution.py:120
  53.6 10.2 %collective-permute-start.19 = (bf16[32,2048]{1,0:T(8,128)(2,1)S(1)}, bf16[32,2048]{1,0:T(8,128)(2,1)S(1)}, u32[]{:S(2)}, u32[]{:S(2)}) collective-permute-start(bf16[32,2048]{1,0:T(8,128)(2,1)S(1)} %get-tuple-element.82), channel_id=1, source_target_pairs={{0,24},{2,26},{4,28},{6,30},{8,0},{10,2},{12,4},{14,6},{16,8},{18,... | collective-permute-start | bytes 393224 | tf_op jit(solution)/shard_map/ppermute | solution.py:120
  56.1 8.2 %collective-permute-start.23 = (bf16[32,2048]{1,0:T(8,128)(2,1)S(1)}, bf16[32,2048]{1,0:T(8,128)(2,1)S(1)}, u32[]{:S(2)}, u32[]{:S(2)}) collective-permute-start(bf16[32,2048]{1,0:T(8,128)(2,1)S(1)} %get-tuple-element.82), channel_id=1, source_target_pairs={{0,4},{2,6},{4,0},{6,2},{8,12},{10,14},{12,8},{14,10},{16,20},{18,... | collective-permute-start | bytes 393224 | tf_op jit(solution)/shard_map/ppermute | solution.py:120
  64.3 8.2 %collective-permute-start.24 = (bf16[32,2048]{1,0:T(8,128)(2,1)S(1)}, bf16[32,2048]{1,0:T(8,128)(2,1)S(1)}, u32[]{:S(2)}, u32[]{:S(2)}) collective-permute-start(bf16[32,2048]{1,0:T(8,128)(2,1)S(1)} %collective-permute-done.23), channel_id=1, source_target_pairs={{0,8},{2,10},{4,12},{6,14},{8,16},{10,18},{12,20},{14,22},{16,24},... | collective-permute-start | bytes 393224 | tf_op jit(solution)/shard_map/ppermute | solution.py:120
  66.6 8.0 %collective-permute-start.25 = (bf16[32,2048]{1,0:T(8,128)(2,1)S(1)}, bf16[32,2048]{1,0:T(8,128)(2,1)S(1)}, u32[]{:S(2)}, u32[]{:S(2)}) collective-permute-start(bf16[32,2048]{1,0:T(8,128)(2,1)S(1)} %collective-permute-done.23), channel_id=1, source_target_pairs={{0,24},{2,26},{4,28},{6,30},{8,0},{10,2},{12,4},{14,6},{16,8},{18,... | collective-permute-start | bytes 393224 | tf_op jit(solution)/shard_map/ppermute | solution.py:120
  68.7 9.3 %collective-permute-start.27 = (bf16[2,32,2048]{2,1,0:T(8,128)(2,1)S(1)}, bf16[2,32,2048]{2,1,0:T(8,128)(2,1)S(1)}, u32[]{:S(2)}, u32[]{:S(2)}) collective-permute-start(bf16[2,32,2048]{2,1,0:T(8,128)(2,1)S(1)} %get-tuple-element.94), channel_id=1, source_target_pairs={{0,4},{2,6},{4,0},{6,2},{8,12},{10,14},{12,8},{14,10},{16,20},{18,... | collective-permute-start | bytes 786440 | tf_op jit(solution)/shard_map/ppermute | solution.py:120
  70.3 9.9 %collective-permute-start.30 = (bf16[5,32,2048]{2,1,0:T(8,128)(2,1)S(1)}, bf16[5,32,2048]{2,1,0:T(8,128)(2,1)S(1)}, u32[]{:S(2)}, u32[]{:S(2)}) collective-permute-start(bf16[5,32,2048]{2,1,0:T(8,128)(2,1)S(1)} %bitcast_dynamic-update-slice_fusion.refs_0_), channel_id=1, source_target_pairs={{0,2},{2,0},{4,6},{6,4},{8,10},{10,8},{12,14},{14,12},{16,18},{18,... | collective-permute-start | bytes 1966088 | tf_op jit(solution)/shard_map/ppermute | solution.py:120
  70.4 15.3 %collective-permute-start.22 = (bf16[2,32,2048]{2,1,0:T(8,128)(2,1)S(1)}, bf16[2,32,2048]{2,1,0:T(8,128)(2,1)S(1)}, u32[]{:S(2)}, u32[]{:S(2)}) collective-permute-start(bf16[2,32,2048]{2,1,0:T(8,128)(2,1)S(1)} %get-tuple-element.95), channel_id=1, source_target_pairs={{0,4},{2,6},{4,0},{6,2},{8,12},{10,14},{12,8},{14,10},{16,20},{18,... | collective-permute-start | bytes 786440 | tf_op jit(solution)/shard_map/ppermute | solution.py:120
  78.2 7.6 %collective-permute-start.28 = (bf16[32,2048]{1,0:T(8,128)(2,1)S(1)}, bf16[32,2048]{1,0:T(8,128)(2,1)S(1)}, u32[]{:S(2)}, u32[]{:S(2)}) collective-permute-start(bf16[32,2048]{1,0:T(8,128)(2,1)S(1)} %get-tuple-element.99), channel_id=1, source_target_pairs={{0,24},{2,26},{4,28},{6,30},{8,0},{10,2},{12,4},{14,6},{16,8},{18,... | collective-permute-start | bytes 393224 | tf_op jit(solution)/shard_map/ppermute | solution.py:120
  78.2 11.5 %collective-permute-start.29 = (bf16[32,2048]{1,0:T(8,128)(2,1)S(1)}, bf16[32,2048]{1,0:T(8,128)(2,1)S(1)}, u32[]{:S(2)}, u32[]{:S(2)}) collective-permute-start(bf16[32,2048]{1,0:T(8,128)(2,1)S(1)} %get-tuple-element.98), channel_id=1, source_target_pairs={{0,16},{2,18},{4,20},{6,22},{8,24},{10,26},{12,28},{14,30},{16,0},... | collective-permute-start | bytes 393224 | tf_op jit(solution)/shard_map/ppermute | solution.py:120
  89.8 7.0 %collective-permute-start.33 = (bf16[32,2048]{1,0:T(8,128)(2,1)S(1)}, bf16[32,2048]{1,0:T(8,128)(2,1)S(1)}, u32[]{:S(2)}, u32[]{:S(2)}) collective-permute-start(bf16[32,2048]{1,0:T(8,128)(2,1)S(1)} %fusion.17), channel_id=1, source_target_pairs={{0,8},{2,10},{4,12},{6,14},{8,16},{10,18},{12,20},{14,22},{16,24},... | collective-permute-start | bytes 393224 | tf_op jit(solution)/shard_map/ppermute | solution.py:120
  (11 other events, 66.9 us)

commit v8 on v7

--- a/solution.py
+++ b/solution.py
@@ -8,7 +8,7 @@
 from jax.sharding import PartitionSpec as P
 
 CHUNK = 32
-UNROLL = 32
+UNROLL = 64
 
 
 def product_kernel(contract, inputs, outputs, count_ref, take_ref, put_ref, *refs):
@@ -27,7 +27,7 @@
         return pltpu.make_async_copy(blocks.at[part], held_blocks.at[part], block_sems.at[g])
 
     for g in range(chunks):
-        @pl.when(g * CHUNK < count)
+        @pl.when(g * CHUNK // UNROLL * UNROLL < count)
         def _(g=g):
             block_copy(g).start()
 
@@ -57,11 +57,11 @@
         for n, product in enumerate(products):
             total[place(put_ref[first + n])] += product
 
-    @pl.loop(0, (count + CHUNK - 1) // CHUNK)
+    @pl.loop(0, (count + UNROLL - 1) // UNROLL)
     def _(g):
-        block_copy(g).wait()
-        for n in range(0, CHUNK, UNROLL):
-            group(g * CHUNK + n)
+        for n in range(UNROLL // CHUNK):
+            block_copy(g * (UNROLL // CHUNK) + n).wait()
+        group(g * UNROLL)
 
     for out, held_pieces in zip(outs, outputs):
         for n, p in enumerate(held_pieces):
@@ -141,7 +141,7 @@
     put_rows = jnp.where(live, place_rows, n_col * per_piece)
 
     order = list(range(1, n_a)) + [0]
-    halves = [order[: n_a // 2], order[n_a // 2 :]] if n_a > 1 else [order]
+    halves = [order[:-1], order[-1:]] if n_a > 1 else [order]
     mirror_outputs = [[piece(a, b, c) for b in range(n_b) for a in order] for c in range(n_c)]
     forward_outputs = [[j] for j in range(n_col)]
     mirror_inputs = [[j] for j in range(n_col)]

time: 97.9 us -> 96.3 us (0.984)
  waiting for transfers between devices: 36.3 us -> 28.7 us
  Pallas kernels: 21.6 us -> 25.5 us
  starting transfers between devices: 33.2 us -> 35.8 us
    ppermute x30, waiting for transfers between devices: 34.7 us -> 28.7 us  [shift(): return lax.ppermute(value, 'row', pairs)]
    pallas_call x4, Pallas kernels: 21.6 us -> 25.5 us  [block_product(): pl.pallas_call(functools.partial(product_kernel, contract, inputs, output...]
    ppermute x30, starting transfers between devices: 29.5 us -> 32 us  [shift(): return lax.ppermute(value, 'row', pairs)]
    ppermute x4, waiting for transfers between devices: 1.64 us -> 0.01 us  [shift_col(): lax.ppermute(value, 'col', [(j, (j + d) % n_col) for j in range(n_col)])]
  transfers between devices with their start and end apart: 34 -> 34, of which waited for: 13 -> 8; matrix products, arithmetic and copies ran while one was open for 2% -> 2% of each run, Pallas kernels for 22% -> 26%
where the time goes in v8:
time: 96.3 us; the launch traced here: 96.4 us
  starting transfers between devices  35.8 us (37%)
  waiting for transfers between devices  28.7 us (30%)
  Pallas kernels  25.5 us (26%)
  other arithmetic  3.86 us (4%)
  between operations  2.35 us (2%)
    ppermute x30, starting transfers between devices, shift(): return lax.ppermute(value, 'row', pairs)  32 us
    ppermute x30, waiting for transfers between devices, shift(): return lax.ppermute(value, 'row', pairs)  28.7 us
    pallas_call x4, Pallas kernels, block_product(): pl.pallas_call(functools.partial(product_kernel, contract, inputs, output...  25.5 us
    ppermute x4, starting transfers between devices, shift_col(): lax.ppermute(value, 'col', [(j, (j + d) % n_col) for j in range(n_col)])  3.75 us
  transfers between devices with their start and end apart: 34, of which 8 were waited for; matrix products, arithmetic and copies ran while one was open for 2% of the time, Pallas kernels for 26%

profile of v8, /device:TPU:0, one launch (start us, length us, event | category | flops | bytes accessed | tf_op | source)
XLA Modules:
  0.0 96.4 jit_solution(2116991122752702435)
XLA Ops:
  1.0 3.0 %collective-permute-start.3 = (bf16[32,2048]{1,0:T(8,128)(2,1)S(1)}, bf16[32,2048]{1,0:T(8,128)(2,1)S(1)}, u32[]{:S(2)}, u32[]{:S(2)}) collective-permute-start(bf16[32,2048]{1,0:T(8,128)(2,1)S(1)} %get-tuple-element.93), channel_id=1, source_target_pairs={{0,1},{1,0},{2,3},{3,2},{4,5},{5,4},{6,7},{7,6},{8,9},{9,8},{10,11... | collective-permute-start | bytes 393224 | tf_op jit(solution)/shard_map/ppermute | solution.py:123
  4.0 1.6 %collective-permute-start = (bf16[32,2048]{1,0:T(8,128)(2,1)S(1)}, bf16[32,2048]{1,0:T(8,128)(2,1)S(1)}, u32[]{:S(2)}, u32[]{:S(2)}) collective-permute-start(bf16[32,2048]{1,0:T(8,128)(2,1)S(1)} %get-tuple-element.93), channel_id=1, source_target_pairs={{0,8},{2,10},{4,12},{6,14},{8,16},{10,18},{12,20},{14,22},{16,24},... | collective-permute-start | bytes 393224 | tf_op jit(solution)/shard_map/ppermute | solution.py:120
  5.6 2.6 %collective-permute-start.1 = (bf16[32,2048]{1,0:T(8,128)(2,1)S(1)}, bf16[32,2048]{1,0:T(8,128)(2,1)S(1)}, u32[]{:S(2)}, u32[]{:S(2)}) collective-permute-start(bf16[32,2048]{1,0:T(8,128)(2,1)S(1)} %get-tuple-element.93), channel_id=1, source_target_pairs={{0,16},{2,18},{4,20},{6,22},{8,24},{10,26},{12,28},{14,30},{16,0},... | collective-permute-start | bytes 393224 | tf_op jit(solution)/shard_map/ppermute | solution.py:120
  9.5 1.5 %collective-permute-start.6 = (bf16[32,2048]{1,0:T(8,128)(2,1)S(1)}, bf16[32,2048]{1,0:T(8,128)(2,1)S(1)}, u32[]{:S(2)}, u32[]{:S(2)}) collective-permute-start(bf16[32,2048]{1,0:T(8,128)(2,1)S(1)} %get-tuple-element.93), channel_id=1, source_target_pairs={{0,4},{2,6},{4,0},{6,2},{8,12},{10,14},{12,8},{14,10},{16,20},{18,... | collective-permute-start | bytes 393224 | tf_op jit(solution)/shard_map/ppermute | solution.py:120
  12.4 6.4 %mirror.2 = (bf16[8,32,2048]{2,1,0:T(8,128)(2,1)S(1)}, bf16[8,32,2048]{2,1,0:T(8,128)(2,1)S(1)}) custom-call(s32[1]{0:T(128)} %copy.16.count_ref, s32[256]{0:T(256)S(1)} %get-tuple-element.95.take_ref, s32[256]{0:T(256)S(1)} %get-tuple-element.108.put_ref, bf16[1,32,2048]{2,1,0:T(8,128)(2,1)S(1)} %bitcast.93, bf16[1,32,2048]{2,1,0:T(8,128)(2,1)S(1)} %bitcast.94, ...), custom_call_target="tpu_custom_call" | custom-call | flops 128 | bytes 128 | tf_op jit(solution)/shard_map/mirror/pallas_call | solution.py:79
  19.0 2.3 %collective-permute-start.7 = (bf16[32,2048]{1,0:T(8,128)(2,1)S(1)}, bf16[32,2048]{1,0:T(8,128)(2,1)S(1)}, u32[]{:S(2)}, u32[]{:S(2)}) collective-permute-start(bf16[32,2048]{1,0:T(8,128)(2,1)S(1)} %collective-permute-done.6), channel_id=1, source_target_pairs={{0,8},{2,10},{4,12},{6,14},{8,16},{10,18},{12,20},{14,22},{16,24},... | collective-permute-start | bytes 393224 | tf_op jit(solution)/shard_map/ppermute | solution.py:120
  21.4 1.5 %collective-permute-start.8 = (bf16[32,2048]{1,0:T(8,128)(2,1)S(1)}, bf16[32,2048]{1,0:T(8,128)(2,1)S(1)}, u32[]{:S(2)}, u32[]{:S(2)}) collective-permute-start(bf16[32,2048]{1,0:T(8,128)(2,1)S(1)} %collective-permute-done.6), channel_id=1, source_target_pairs={{0,24},{2,26},{4,28},{6,30},{8,0},{10,2},{12,4},{14,6},{16,8},{18,... | collective-permute-start | bytes 393224 | tf_op jit(solution)/shard_map/ppermute | solution.py:120
  23.5 2.0 %collective-permute-start.10 = (bf16[3,32,2048]{2,1,0:T(8,128)(2,1)S(1)}, bf16[3,32,2048]{2,1,0:T(8,128)(2,1)S(1)}, u32[]{:S(2)}, u32[]{:S(2)}) collective-permute-start(bf16[3,32,2048]{2,1,0:T(8,128)(2,1)S(1)} %slice.68), channel_id=1, source_target_pairs={{0,4},{2,6},{4,0},{6,2},{8,12},{10,14},{12,8},{14,10},{16,20},{18,... | collective-permute-start | bytes 1179656 | tf_op jit(solution)/shard_map/ppermute | solution.py:120
  27.2 1.8 %collective-permute-done.8 = bf16[32,2048]{1,0:T(8,128)(2,1)S(1)} collective-permute-done((bf16[32,2048]{1,0:T(8,128)(2,1)S(1)}, bf16[32,2048]{1,0:T(8,128)(2,1)S(1)}, u32[]{:S(2)}, u32[]{:S(2)}) %collective-permute-start.8) | collective-permute-done | bytes 131104 | tf_op jit(solution)/shard_map/ppermute | solution.py:120
  29.0 6.5 %collective-permute-done.10 = bf16[3,32,2048]{2,1,0:T(8,128)(2,1)S(1)} collective-permute-done((bf16[3,32,2048]{2,1,0:T(8,128)(2,1)S(1)}, bf16[3,32,2048]{2,1,0:T(8,128)(2,1)S(1)}, u32[]{:S(2)}, u32[]{:S(2)}) %collective-permute-start.10) | collective-permute-done | bytes 393248 | tf_op jit(solution)/shard_map/ppermute | solution.py:120
  37.8 6.4 %forward.2 = (f32[1,32,2048]{2,1,0:T(8,128)S(1)}, bf16[1,32,2048]{2,1,0:T(8,128)(2,1)S(1)}) custom-call(s32[1]{0:T(128)} %copy.16.count_ref, s32[256]{0:T(256)S(1)} %get-tuple-element.109.take_ref, s32[256]{0:T(256)S(1)} %get-tuple-element.94.put_ref, bf16[5,32,2048]{2,1,0:T(8,128)(2,1)S(1)} %bitcast_dynamic-update-slice_fusion.4.refs_0_, ...), custom_call_target="tpu_custom_call" | custom-call | flops 128 | bytes 128 | tf_op jit(solution)/shard_map/forward/pallas_call | solution.py:79
  45.6 4.0 %collective-permute-done.12 = bf16[32,2048]{1,0:T(8,128)(2,1)S(1)} collective-permute-done((bf16[32,2048]{1,0:T(8,128)(2,1)S(1)}, bf16[32,2048]{1,0:T(8,128)(2,1)S(1)}, u32[]{:S(2)}, u32[]{:S(2)}) %collective-permute-start.12) | collective-permute-done | bytes 131104 | tf_op jit(solution)/shard_map/ppermute | solution.py:120
  51.6 1.9 %collective-permute-start.18 = (bf16[32,2048]{1,0:T(8,128)(2,1)S(1)}, bf16[32,2048]{1,0:T(8,128)(2,1)S(1)}, u32[]{:S(2)}, u32[]{:S(2)}) collective-permute-start(bf16[32,2048]{1,0:T(8,128)(2,1)S(1)} %get-tuple-element.90), channel_id=1, source_target_pairs={{0,16},{2,18},{4,20},{6,22},{8,24},{10,26},{12,28},{14,30},{16,0},... | collective-permute-start | bytes 393224 | tf_op jit(solution)/shard_map/ppermute | solution.py:120
  54.9 1.7 %collective-permute-start.23 = (bf16[32,2048]{1,0:T(8,128)(2,1)S(1)}, bf16[32,2048]{1,0:T(8,128)(2,1)S(1)}, u32[]{:S(2)}, u32[]{:S(2)}) collective-permute-start(bf16[32,2048]{1,0:T(8,128)(2,1)S(1)} %get-tuple-element.90), channel_id=1, source_target_pairs={{0,4},{2,6},{4,0},{6,2},{8,12},{10,14},{12,8},{14,10},{16,20},{18,... | collective-permute-start | bytes 393224 | tf_op jit(solution)/shard_map/ppermute | solution.py:120
  56.5 6.4 %mirror.3 = (bf16[8,32,2048]{2,1,0:T(8,128)(2,1)S(1)}, bf16[8,32,2048]{2,1,0:T(8,128)(2,1)S(1)}) custom-call(s32[1]{0:T(128)} %copy.16.count_ref, s32[256]{0:T(256)S(1)} %get-tuple-element.95.take_ref, s32[256]{0:T(256)S(1)} %get-tuple-element.108.put_ref, bf16[1,32,2048]{2,1,0:T(8,128)(2,1)S(1)} %bitcast.92, bf16[1,32,2048]{2,1,0:T(8,128)(2,1)S(1)} %bitcast.95, ...), custom_call_target="tpu_custom_call" | custom-call | flops 128 | bytes 128 | tf_op jit(solution)/shard_map/mirror/pallas_call | solution.py:79
  63.7 3.1 %collective-permute-start.24 = (bf16[32,2048]{1,0:T(8,128)(2,1)S(1)}, bf16[32,2048]{1,0:T(8,128)(2,1)S(1)}, u32[]{:S(2)}, u32[]{:S(2)}) collective-permute-start(bf16[32,2048]{1,0:T(8,128)(2,1)S(1)} %collective-permute-done.23), channel_id=1, source_target_pairs={{0,8},{2,10},{4,12},{6,14},{8,16},{10,18},{12,20},{14,22},{16,24},... | collective-permute-start | bytes 393224 | tf_op jit(solution)/shard_map/ppermute | solution.py:120
  66.8 1.6 %collective-permute-start.25 = (bf16[32,2048]{1,0:T(8,128)(2,1)S(1)}, bf16[32,2048]{1,0:T(8,128)(2,1)S(1)}, u32[]{:S(2)}, u32[]{:S(2)}) collective-permute-start(bf16[32,2048]{1,0:T(8,128)(2,1)S(1)} %collective-permute-done.23), channel_id=1, source_target_pairs={{0,24},{2,26},{4,28},{6,30},{8,0},{10,2},{12,4},{14,6},{16,8},{18,... | collective-permute-start | bytes 393224 | tf_op jit(solution)/shard_map/ppermute | solution.py:120
  69.7 1.5 %collective-permute-start.22 = (bf16[1,32,2048]{2,1,0:T(8,128)(2,1)S(1)}, bf16[1,32,2048]{2,1,0:T(8,128)(2,1)S(1)}, u32[]{:S(2)}, u32[]{:S(2)}) collective-permute-start(bf16[1,32,2048]{2,1,0:T(8,128)(2,1)S(1)} %slice.73), channel_id=1, source_target_pairs={{0,4},{2,6},{4,0},{6,2},{8,12},{10,14},{12,8},{14,10},{16,20},{18,... | collective-permute-start | bytes 393224 | tf_op jit(solution)/shard_map/ppermute | solution.py:120
  71.2 1.5 %collective-permute-done.24 = bf16[32,2048]{1,0:T(8,128)(2,1)S(1)} collective-permute-done((bf16[32,2048]{1,0:T(8,128)(2,1)S(1)}, bf16[32,2048]{1,0:T(8,128)(2,1)S(1)}, u32[]{:S(2)}, u32[]{:S(2)}) %collective-permute-start.24) | collective-permute-done | bytes 131104 | tf_op jit(solution)/shard_map/ppermute | solution.py:120
  72.7 2.2 %collective-permute-done.25 = bf16[32,2048]{1,0:T(8,128)(2,1)S(1)} collective-permute-done((bf16[32,2048]{1,0:T(8,128)(2,1)S(1)}, bf16[32,2048]{1,0:T(8,128)(2,1)S(1)}, u32[]{:S(2)}, u32[]{:S(2)}) %collective-permute-start.25) | collective-permute-done | bytes 131104 | tf_op jit(solution)/shard_map/ppermute | solution.py:120
  74.9 6.1 %collective-permute-done.27 = bf16[3,32,2048]{2,1,0:T(8,128)(2,1)S(1)} collective-permute-done((bf16[3,32,2048]{2,1,0:T(8,128)(2,1)S(1)}, bf16[3,32,2048]{2,1,0:T(8,128)(2,1)S(1)}, u32[]{:S(2)}, u32[]{:S(2)}) %collective-permute-start.27) | collective-permute-done | bytes 393248 | tf_op jit(solution)/shard_map/ppermute | solution.py:120
  81.3 2.1 %collective-permute-start.28 = (bf16[32,2048]{1,0:T(8,128)(2,1)S(1)}, bf16[32,2048]{1,0:T(8,128)(2,1)S(1)}, u32[]{:S(2)}, u32[]{:S(2)}) collective-permute-start(bf16[32,2048]{1,0:T(8,128)(2,1)S(1)} %get-tuple-element.104), channel_id=1, source_target_pairs={{0,24},{2,26},{4,28},{6,30},{8,0},{10,2},{12,4},{14,6},{16,8},{18,... | collective-permute-start | bytes 393224 | tf_op jit(solution)/shard_map/ppermute | solution.py:120
  84.0 6.4 %forward.3 = (f32[1,32,2048]{2,1,0:T(8,128)S(1)}, bf16[1,32,2048]{2,1,0:T(8,128)(2,1)S(1)}) custom-call(s32[1]{0:T(128)} %copy.16.count_ref, s32[256]{0:T(256)S(1)} %get-tuple-element.109.take_ref, s32[256]{0:T(256)S(1)} %get-tuple-element.94.put_ref, bf16[5,32,2048]{2,1,0:T(8,128)(2,1)S(1)} %bitcast_dynamic-update-slice_fusion.refs_0_, ...), custom_call_target="tpu_custom_call" | custom-call | flops 128 | bytes 128 | tf_op jit(solution)/shard_map/forward/pallas_call | solution.py:79
  90.5 5.0 %collective-permute-done.29 = bf16[32,2048]{1,0:T(8,128)(2,1)S(1)} collective-permute-done((bf16[32,2048]{1,0:T(8,128)(2,1)S(1)}, bf16[32,2048]{1,0:T(8,128)(2,1)S(1)}, u32[]{:S(2)}, u32[]{:S(2)}) %collective-permute-start.29) | collective-permute-done | bytes 131104 | tf_op jit(solution)/shard_map/ppermute | solution.py:120
  (74 shorter events, 14.9 us)
Async XLA Ops:
  1.0 11.4 %collective-permute-start.3 = (bf16[32,2048]{1,0:T(8,128)(2,1)S(1)}, bf16[32,2048]{1,0:T(8,128)(2,1)S(1)}, u32[]{:S(2)}, u32[]{:S(2)}) collective-permute-start(bf16[32,2048]{1,0:T(8,128)(2,1)S(1)} %get-tuple-element.93), channel_id=1, source_target_pairs={{0,1},{1,0},{2,3},{3,2},{4,5},{5,4},{6,7},{7,6},{8,9},{9,8},{10,11... | collective-permute-start | bytes 393224 | tf_op jit(solution)/shard_map/ppermute | solution.py:123
  4.0 14.9 %collective-permute-start = (bf16[32,2048]{1,0:T(8,128)(2,1)S(1)}, bf16[32,2048]{1,0:T(8,128)(2,1)S(1)}, u32[]{:S(2)}, u32[]{:S(2)}) collective-permute-start(bf16[32,2048]{1,0:T(8,128)(2,1)S(1)} %get-tuple-element.93), channel_id=1, source_target_pairs={{0,8},{2,10},{4,12},{6,14},{8,16},{10,18},{12,20},{14,22},{16,24},... | collective-permute-start | bytes 393224 | tf_op jit(solution)/shard_map/ppermute | solution.py:120
  5.6 13.4 %collective-permute-start.1 = (bf16[32,2048]{1,0:T(8,128)(2,1)S(1)}, bf16[32,2048]{1,0:T(8,128)(2,1)S(1)}, u32[]{:S(2)}, u32[]{:S(2)}) collective-permute-start(bf16[32,2048]{1,0:T(8,128)(2,1)S(1)} %get-tuple-element.93), channel_id=1, source_target_pairs={{0,16},{2,18},{4,20},{6,22},{8,24},{10,26},{12,28},{14,30},{16,0},... | collective-permute-start | bytes 393224 | tf_op jit(solution)/shard_map/ppermute | solution.py:120
  8.1 10.8 %collective-permute-start.2 = (bf16[32,2048]{1,0:T(8,128)(2,1)S(1)}, bf16[32,2048]{1,0:T(8,128)(2,1)S(1)}, u32[]{:S(2)}, u32[]{:S(2)}) collective-permute-start(bf16[32,2048]{1,0:T(8,128)(2,1)S(1)} %get-tuple-element.93), channel_id=1, source_target_pairs={{0,24},{2,26},{4,28},{6,30},{8,0},{10,2},{12,4},{14,6},{16,8},{18,... | collective-permute-start | bytes 393224 | tf_op jit(solution)/shard_map/ppermute | solution.py:120
  9.5 9.5 %collective-permute-start.6 = (bf16[32,2048]{1,0:T(8,128)(2,1)S(1)}, bf16[32,2048]{1,0:T(8,128)(2,1)S(1)}, u32[]{:S(2)}, u32[]{:S(2)}) collective-permute-start(bf16[32,2048]{1,0:T(8,128)(2,1)S(1)} %get-tuple-element.93), channel_id=1, source_target_pairs={{0,4},{2,6},{4,0},{6,2},{8,12},{10,14},{12,8},{14,10},{16,20},{18,... | collective-permute-start | bytes 393224 | tf_op jit(solution)/shard_map/ppermute | solution.py:120
  19.0 8.2 %collective-permute-start.7 = (bf16[32,2048]{1,0:T(8,128)(2,1)S(1)}, bf16[32,2048]{1,0:T(8,128)(2,1)S(1)}, u32[]{:S(2)}, u32[]{:S(2)}) collective-permute-start(bf16[32,2048]{1,0:T(8,128)(2,1)S(1)} %collective-permute-done.6), channel_id=1, source_target_pairs={{0,8},{2,10},{4,12},{6,14},{8,16},{10,18},{12,20},{14,22},{16,24},... | collective-permute-start | bytes 393224 | tf_op jit(solution)/shard_map/ppermute | solution.py:120
  23.5 12.1 %collective-permute-start.10 = (bf16[3,32,2048]{2,1,0:T(8,128)(2,1)S(1)}, bf16[3,32,2048]{2,1,0:T(8,128)(2,1)S(1)}, u32[]{:S(2)}, u32[]{:S(2)}) collective-permute-start(bf16[3,32,2048]{2,1,0:T(8,128)(2,1)S(1)} %slice.68), channel_id=1, source_target_pairs={{0,4},{2,6},{4,0},{6,2},{8,12},{10,14},{12,8},{14,10},{16,20},{18,... | collective-permute-start | bytes 1179656 | tf_op jit(solution)/shard_map/ppermute | solution.py:120
  25.5 11.9 %collective-permute-start.14 = (bf16[5,32,2048]{2,1,0:T(8,128)(2,1)S(1)}, bf16[5,32,2048]{2,1,0:T(8,128)(2,1)S(1)}, u32[]{:S(2)}, u32[]{:S(2)}) collective-permute-start(bf16[5,32,2048]{2,1,0:T(8,128)(2,1)S(1)} %bitcast_dynamic-update-slice_fusion.4.refs_0_), channel_id=1, source_target_pairs={{0,2},{2,0},{4,6},{6,4},{8,10},{10,8},{12,14},{14,12},{16,18},{18,... | collective-permute-start | bytes 1966088 | tf_op jit(solution)/shard_map/ppermute | solution.py:120
  25.6 20.0 %collective-permute-start.5 = (bf16[1,32,2048]{2,1,0:T(8,128)(2,1)S(1)}, bf16[1,32,2048]{2,1,0:T(8,128)(2,1)S(1)}, u32[]{:S(2)}, u32[]{:S(2)}) collective-permute-start(bf16[1,32,2048]{2,1,0:T(8,128)(2,1)S(1)} %slice.66), channel_id=1, source_target_pairs={{0,4},{2,6},{4,0},{6,2},{8,12},{10,14},{12,8},{14,10},{16,20},{18,... | collective-permute-start | bytes 393224 | tf_op jit(solution)/shard_map/ppermute | solution.py:120
  35.8 9.8 %collective-permute-start.11 = (bf16[32,2048]{1,0:T(8,128)(2,1)S(1)}, bf16[32,2048]{1,0:T(8,128)(2,1)S(1)}, u32[]{:S(2)}, u32[]{:S(2)}) collective-permute-start(bf16[32,2048]{1,0:T(8,128)(2,1)S(1)} %get-tuple-element.107), channel_id=1, source_target_pairs={{0,24},{2,26},{4,28},{6,30},{8,0},{10,2},{12,4},{14,6},{16,8},{18,... | collective-permute-start | bytes 393224 | tf_op jit(solution)/shard_map/ppermute | solution.py:120
  36.4 13.2 %collective-permute-start.12 = (bf16[32,2048]{1,0:T(8,128)(2,1)S(1)}, bf16[32,2048]{1,0:T(8,128)(2,1)S(1)}, u32[]{:S(2)}, u32[]{:S(2)}) collective-permute-start(bf16[32,2048]{1,0:T(8,128)(2,1)S(1)} %get-tuple-element.106), channel_id=1, source_target_pairs={{0,16},{2,18},{4,20},{6,22},{8,24},{10,26},{12,28},{14,30},{16,0},... | collective-permute-start | bytes 393224 | tf_op jit(solution)/shard_map/ppermute | solution.py:120
  37.4 12.3 %collective-permute-start.13 = (bf16[32,2048]{1,0:T(8,128)(2,1)S(1)}, bf16[32,2048]{1,0:T(8,128)(2,1)S(1)}, u32[]{:S(2)}, u32[]{:S(2)}) collective-permute-start(bf16[32,2048]{1,0:T(8,128)(2,1)S(1)} %get-tuple-element.105), channel_id=1, source_target_pairs={{0,8},{2,10},{4,12},{6,14},{8,16},{10,18},{12,20},{14,22},{16,24},... | collective-permute-start | bytes 393224 | tf_op jit(solution)/shard_map/ppermute | solution.py:120
  50.4 12.5 %collective-permute-start.17 = (bf16[32,2048]{1,0:T(8,128)(2,1)S(1)}, bf16[32,2048]{1,0:T(8,128)(2,1)S(1)}, u32[]{:S(2)}, u32[]{:S(2)}) collective-permute-start(bf16[32,2048]{1,0:T(8,128)(2,1)S(1)} %get-tuple-element.90), channel_id=1, source_target_pairs={{0,8},{2,10},{4,12},{6,14},{8,16},{10,18},{12,20},{14,22},{16,24},... | collective-permute-start | bytes 393224 | tf_op jit(solution)/shard_map/ppermute | solution.py:120
  51.6 11.3 %collective-permute-start.18 = (bf16[32,2048]{1,0:T(8,128)(2,1)S(1)}, bf16[32,2048]{1,0:T(8,128)(2,1)S(1)}, u32[]{:S(2)}, u32[]{:S(2)}) collective-permute-start(bf16[32,2048]{1,0:T(8,128)(2,1)S(1)} %get-tuple-element.90), channel_id=1, source_target_pairs={{0,16},{2,18},{4,20},{6,22},{8,24},{10,26},{12,28},{14,30},{16,0},... | collective-permute-start | bytes 393224 | tf_op jit(solution)/shard_map/ppermute | solution.py:120
  53.5 9.4 %collective-permute-start.19 = (bf16[32,2048]{1,0:T(8,128)(2,1)S(1)}, bf16[32,2048]{1,0:T(8,128)(2,1)S(1)}, u32[]{:S(2)}, u32[]{:S(2)}) collective-permute-start(bf16[32,2048]{1,0:T(8,128)(2,1)S(1)} %get-tuple-element.90), channel_id=1, source_target_pairs={{0,24},{2,26},{4,28},{6,30},{8,0},{10,2},{12,4},{14,6},{16,8},{18,... | collective-permute-start | bytes 393224 | tf_op jit(solution)/shard_map/ppermute | solution.py:120
  54.9 8.9 %collective-permute-start.23 = (bf16[32,2048]{1,0:T(8,128)(2,1)S(1)}, bf16[32,2048]{1,0:T(8,128)(2,1)S(1)}, u32[]{:S(2)}, u32[]{:S(2)}) collective-permute-start(bf16[32,2048]{1,0:T(8,128)(2,1)S(1)} %get-tuple-element.90), channel_id=1, source_target_pairs={{0,4},{2,6},{4,0},{6,2},{8,12},{10,14},{12,8},{14,10},{16,20},{18,... | collective-permute-start | bytes 393224 | tf_op jit(solution)/shard_map/ppermute | solution.py:120
  63.7 9.0 %collective-permute-start.24 = (bf16[32,2048]{1,0:T(8,128)(2,1)S(1)}, bf16[32,2048]{1,0:T(8,128)(2,1)S(1)}, u32[]{:S(2)}, u32[]{:S(2)}) collective-permute-start(bf16[32,2048]{1,0:T(8,128)(2,1)S(1)} %collective-permute-done.23), channel_id=1, source_target_pairs={{0,8},{2,10},{4,12},{6,14},{8,16},{10,18},{12,20},{14,22},{16,24},... | collective-permute-start | bytes 393224 | tf_op jit(solution)/shard_map/ppermute | solution.py:120
  66.8 8.2 %collective-permute-start.25 = (bf16[32,2048]{1,0:T(8,128)(2,1)S(1)}, bf16[32,2048]{1,0:T(8,128)(2,1)S(1)}, u32[]{:S(2)}, u32[]{:S(2)}) collective-permute-start(bf16[32,2048]{1,0:T(8,128)(2,1)S(1)} %collective-permute-done.23), channel_id=1, source_target_pairs={{0,24},{2,26},{4,28},{6,30},{8,0},{10,2},{12,4},{14,6},{16,8},{18,... | collective-permute-start | bytes 393224 | tf_op jit(solution)/shard_map/ppermute | solution.py:120
  69.0 12.1 %collective-permute-start.27 = (bf16[3,32,2048]{2,1,0:T(8,128)(2,1)S(1)}, bf16[3,32,2048]{2,1,0:T(8,128)(2,1)S(1)}, u32[]{:S(2)}, u32[]{:S(2)}) collective-permute-start(bf16[3,32,2048]{2,1,0:T(8,128)(2,1)S(1)} %slice.75), channel_id=1, source_target_pairs={{0,4},{2,6},{4,0},{6,2},{8,12},{10,14},{12,8},{14,10},{16,20},{18,... | collective-permute-start | bytes 1179656 | tf_op jit(solution)/shard_map/ppermute | solution.py:120
  69.6 13.8 %collective-permute-start.31 = (bf16[5,32,2048]{2,1,0:T(8,128)(2,1)S(1)}, bf16[5,32,2048]{2,1,0:T(8,128)(2,1)S(1)}, u32[]{:S(2)}, u32[]{:S(2)}) collective-permute-start(bf16[5,32,2048]{2,1,0:T(8,128)(2,1)S(1)} %bitcast_dynamic-update-slice_fusion.refs_0_), channel_id=1, source_target_pairs={{0,2},{2,0},{4,6},{6,4},{8,10},{10,8},{12,14},{14,12},{16,18},{18,... | collective-permute-start | bytes 1966088 | tf_op jit(solution)/shard_map/ppermute | solution.py:120
  69.7 20.8 %collective-permute-start.22 = (bf16[1,32,2048]{2,1,0:T(8,128)(2,1)S(1)}, bf16[1,32,2048]{2,1,0:T(8,128)(2,1)S(1)}, u32[]{:S(2)}, u32[]{:S(2)}) collective-permute-start(bf16[1,32,2048]{2,1,0:T(8,128)(2,1)S(1)} %slice.73), channel_id=1, source_target_pairs={{0,4},{2,6},{4,0},{6,2},{8,12},{10,14},{12,8},{14,10},{16,20},{18,... | collective-permute-start | bytes 393224 | tf_op jit(solution)/shard_map/ppermute | solution.py:120
  81.3 9.2 %collective-permute-start.28 = (bf16[32,2048]{1,0:T(8,128)(2,1)S(1)}, bf16[32,2048]{1,0:T(8,128)(2,1)S(1)}, u32[]{:S(2)}, u32[]{:S(2)}) collective-permute-start(bf16[32,2048]{1,0:T(8,128)(2,1)S(1)} %get-tuple-element.104), channel_id=1, source_target_pairs={{0,24},{2,26},{4,28},{6,30},{8,0},{10,2},{12,4},{14,6},{16,8},{18,... | collective-permute-start | bytes 393224 | tf_op jit(solution)/shard_map/ppermute | solution.py:120
  83.4 12.1 %collective-permute-start.29 = (bf16[32,2048]{1,0:T(8,128)(2,1)S(1)}, bf16[32,2048]{1,0:T(8,128)(2,1)S(1)}, u32[]{:S(2)}, u32[]{:S(2)}) collective-permute-start(bf16[32,2048]{1,0:T(8,128)(2,1)S(1)} %get-tuple-element.103), channel_id=1, source_target_pairs={{0,16},{2,18},{4,20},{6,22},{8,24},{10,26},{12,28},{14,30},{16,0},... | collective-permute-start | bytes 393224 | tf_op jit(solution)/shard_map/ppermute | solution.py:120
  83.4 12.1 %collective-permute-start.30 = (bf16[32,2048]{1,0:T(8,128)(2,1)S(1)}, bf16[32,2048]{1,0:T(8,128)(2,1)S(1)}, u32[]{:S(2)}, u32[]{:S(2)}) collective-permute-start(bf16[32,2048]{1,0:T(8,128)(2,1)S(1)} %get-tuple-element.102), channel_id=1, source_target_pairs={{0,8},{2,10},{4,12},{6,14},{8,16},{10,18},{12,20},{14,22},{16,24},... | collective-permute-start | bytes 393224 | tf_op jit(solution)/shard_map/ppermute | solution.py:120
  (11 other events, 64.9 us)

commit v9 on v8

--- a/solution.py
+++ b/solution.py
@@ -176,15 +176,16 @@
                 first += len(half)
         kept = parts[: len(halves)]
         sends = [part.astype(jnp.bfloat16) for part in parts[len(halves) :]]
-        others = [shift(send, db=-(n // len(halves) + 1)) for n, send in enumerate(sends)]
-        firsts, rest = others[:: len(halves)], others[1 :: len(halves)]
+        firsts = [shift(send, db=-(b + 1)) for b, send in enumerate(sends[:: len(halves)])]
         far_b = [shift(part, da=a) for part in near[1:] for a in range(1, n_a) if a != middle]
-        far_b, across, firsts = lax.optimization_barrier((far_b, across, firsts))
+        last = sends[1 :: len(halves)]
+        far_b, across, firsts, last = lax.optimization_barrier((far_b, across, firsts, last))
+        rest = [shift(send, db=-(b + 1)) for b, send in enumerate(last)]
         early = jnp.stack(near + far)
         by_row = [[early] + [shift(early, dc=c) for c in range(1, n_c)]]
         if far_b + across:
-            last = jnp.stack(far_b + across)
-            by_row.append([last] + [shift(last, dc=c) for c in range(1, n_c)])
+            late = jnp.stack(far_b + across)
+            by_row.append([late] + [shift(late, dc=c) for c in range(1, n_c)])
         by_row = [part[c] for c in range(n_c) for part in by_row]
 
         own = []

time: 96.3 us -> 94.2 us (0.978)
  Pallas kernels: 25.5 us -> 17.4 us
  starting transfers between devices: 35.8 us -> 39 us
  waiting for transfers between devices: 28.7 us -> 31.3 us
    pallas_call x4, Pallas kernels: 25.5 us -> 17.4 us  [block_product(): pl.pallas_call(functools.partial(product_kernel, contract, inputs, output...]
    ppermute x30, waiting for transfers between devices: 28.7 us -> 31.3 us  [shift(): return lax.ppermute(value, 'row', pairs)]
    ppermute x4, starting transfers between devices: 3.75 us -> 5.73 us  [shift_col(): lax.ppermute(value, 'col', [(j, (j + d) % n_col) for j in range(n_col)])]
    ppermute x30, starting transfers between devices: 32 us -> 33.2 us  [shift(): return lax.ppermute(value, 'row', pairs)]
  transfers between devices with their start and end apart: 34 -> 34, of which waited for: 8 -> 9; matrix products, arithmetic and copies ran while one was open for 2% -> 2% of each run, Pallas kernels for 26% -> 18%
where the time goes in v9:
time: 94.2 us; the launch traced here: 94 us
  starting transfers between devices  39 us (41%)
  waiting for transfers between devices  31.3 us (33%)
  Pallas kernels  17.4 us (18%)
  other arithmetic  3.86 us (4%)
  between operations  2.29 us (2%)
    ppermute x30, starting transfers between devices, shift(): return lax.ppermute(value, 'row', pairs)  33.2 us
    ppermute x30, waiting for transfers between devices, shift(): return lax.ppermute(value, 'row', pairs)  31.3 us
    pallas_call x4, Pallas kernels, block_product(): pl.pallas_call(functools.partial(product_kernel, contract, inputs, output...  17.4 us
    ppermute x4, starting transfers between devices, shift_col(): lax.ppermute(value, 'col', [(j, (j + d) % n_col) for j in range(n_col)])  5.73 us
  transfers between devices with their start and end apart: 34, of which 9 were waited for; matrix products, arithmetic and copies ran while one was open for 2% of the time, Pallas kernels for 18%

profile of v9, /device:TPU:0, one launch (start us, length us, event | category | flops | bytes accessed | tf_op | source)
XLA Modules:
  0.0 94.0 jit_solution(950102728241756192)
XLA Ops:
  1.0 3.0 %collective-permute-start.6 = (bf16[32,2048]{1,0:T(8,128)(2,1)S(1)}, bf16[32,2048]{1,0:T(8,128)(2,1)S(1)}, u32[]{:S(2)}, u32[]{:S(2)}) collective-permute-start(bf16[32,2048]{1,0:T(8,128)(2,1)S(1)} %get-tuple-element.97), channel_id=1, source_target_pairs={{0,1},{1,0},{2,3},{3,2},{4,5},{5,4},{6,7},{7,6},{8,9},{9,8},{10,11... | collective-permute-start | bytes 393224 | tf_op jit(solution)/shard_map/ppermute | solution.py:123
  4.0 1.6 %collective-permute-start.3 = (bf16[32,2048]{1,0:T(8,128)(2,1)S(1)}, bf16[32,2048]{1,0:T(8,128)(2,1)S(1)}, u32[]{:S(2)}, u32[]{:S(2)}) collective-permute-start(bf16[32,2048]{1,0:T(8,128)(2,1)S(1)} %get-tuple-element.97), channel_id=1, source_target_pairs={{0,8},{2,10},{4,12},{6,14},{8,16},{10,18},{12,20},{14,22},{16,24},... | collective-permute-start | bytes 393224 | tf_op jit(solution)/shard_map/ppermute | solution.py:120
  5.6 2.6 %collective-permute-start.4 = (bf16[32,2048]{1,0:T(8,128)(2,1)S(1)}, bf16[32,2048]{1,0:T(8,128)(2,1)S(1)}, u32[]{:S(2)}, u32[]{:S(2)}) collective-permute-start(bf16[32,2048]{1,0:T(8,128)(2,1)S(1)} %get-tuple-element.97), channel_id=1, source_target_pairs={{0,16},{2,18},{4,20},{6,22},{8,24},{10,26},{12,28},{14,30},{16,0},... | collective-permute-start | bytes 393224 | tf_op jit(solution)/shard_map/ppermute | solution.py:120
  9.5 1.5 %collective-permute-start = (bf16[32,2048]{1,0:T(8,128)(2,1)S(1)}, bf16[32,2048]{1,0:T(8,128)(2,1)S(1)}, u32[]{:S(2)}, u32[]{:S(2)}) collective-permute-start(bf16[32,2048]{1,0:T(8,128)(2,1)S(1)} %get-tuple-element.97), channel_id=1, source_target_pairs={{0,4},{2,6},{4,0},{6,2},{8,12},{10,14},{12,8},{14,10},{16,20},{18,... | collective-permute-start | bytes 393224 | tf_op jit(solution)/shard_map/ppermute | solution.py:120
  12.4 4.4 %mirror.2 = (bf16[8,32,2048]{2,1,0:T(8,128)(2,1)S(1)}, bf16[8,32,2048]{2,1,0:T(8,128)(2,1)S(1)}) custom-call(s32[1]{0:T(128)} %copy.16.count_ref, s32[256]{0:T(256)S(1)} %get-tuple-element.99.take_ref, s32[256]{0:T(256)S(1)} %get-tuple-element.112.put_ref, bf16[1,32,2048]{2,1,0:T(8,128)(2,1)S(1)} %bitcast.93, bf16[1,32,2048]{2,1,0:T(8,128)(2,1)S(1)} %bitcast.94, ...), custom_call_target="tpu_custom_call" | custom-call | flops 128 | bytes 128 | tf_op jit(solution)/shard_map/mirror/pallas_call | solution.py:79
  18.1 3.3 %collective-permute-start.1 = (bf16[32,2048]{1,0:T(8,128)(2,1)S(1)}, bf16[32,2048]{1,0:T(8,128)(2,1)S(1)}, u32[]{:S(2)}, u32[]{:S(2)}) collective-permute-start(bf16[32,2048]{1,0:T(8,128)(2,1)S(1)} %collective-permute-done), channel_id=1, source_target_pairs={{0,8},{2,10},{4,12},{6,14},{8,16},{10,18},{12,20},{14,22},{16,24},... | collective-permute-start | bytes 393224 | tf_op jit(solution)/shard_map/ppermute | solution.py:120
  23.6 2.7 %collective-permute-done.1 = bf16[32,2048]{1,0:T(8,128)(2,1)S(1)} collective-permute-done((bf16[32,2048]{1,0:T(8,128)(2,1)S(1)}, bf16[32,2048]{1,0:T(8,128)(2,1)S(1)}, u32[]{:S(2)}, u32[]{:S(2)}) %collective-permute-start.1) | collective-permute-done | bytes 131104 | tf_op jit(solution)/shard_map/ppermute | solution.py:120
  26.4 1.4 %collective-permute-done.2 = bf16[32,2048]{1,0:T(8,128)(2,1)S(1)} collective-permute-done((bf16[32,2048]{1,0:T(8,128)(2,1)S(1)}, bf16[32,2048]{1,0:T(8,128)(2,1)S(1)}, u32[]{:S(2)}, u32[]{:S(2)}) %collective-permute-start.2) | collective-permute-done | bytes 131104 | tf_op jit(solution)/shard_map/ppermute | solution.py:120
  27.8 4.9 %collective-permute-done.9 = bf16[3,32,2048]{2,1,0:T(8,128)(2,1)S(1)} collective-permute-done((bf16[3,32,2048]{2,1,0:T(8,128)(2,1)S(1)}, bf16[3,32,2048]{2,1,0:T(8,128)(2,1)S(1)}, u32[]{:S(2)}, u32[]{:S(2)}) %collective-permute-start.9) | collective-permute-done | bytes 393248 | tf_op jit(solution)/shard_map/ppermute | solution.py:120
  32.9 1.7 %collective-permute-start.11 = (bf16[32,2048]{1,0:T(8,128)(2,1)S(1)}, bf16[32,2048]{1,0:T(8,128)(2,1)S(1)}, u32[]{:S(2)}, u32[]{:S(2)}) collective-permute-start(bf16[32,2048]{1,0:T(8,128)(2,1)S(1)} %get-tuple-element.111), channel_id=1, source_target_pairs={{0,24},{2,26},{4,28},{6,30},{8,0},{10,2},{12,4},{14,6},{16,8},{18,... | collective-permute-start | bytes 393224 | tf_op jit(solution)/shard_map/ppermute | solution.py:120
  34.5 1.4 %collective-permute-start.12 = (bf16[32,2048]{1,0:T(8,128)(2,1)S(1)}, bf16[32,2048]{1,0:T(8,128)(2,1)S(1)}, u32[]{:S(2)}, u32[]{:S(2)}) collective-permute-start(bf16[32,2048]{1,0:T(8,128)(2,1)S(1)} %get-tuple-element.110), channel_id=1, source_target_pairs={{0,16},{2,18},{4,20},{6,22},{8,24},{10,26},{12,28},{14,30},{16,0},... | collective-permute-start | bytes 393224 | tf_op jit(solution)/shard_map/ppermute | solution.py:120
  37.0 4.3 %forward.2 = (f32[1,32,2048]{2,1,0:T(8,128)S(1)}, bf16[1,32,2048]{2,1,0:T(8,128)(2,1)S(1)}) custom-call(s32[1]{0:T(128)} %copy.16.count_ref, s32[256]{0:T(256)S(1)} %get-tuple-element.113.take_ref, s32[256]{0:T(256)S(1)} %get-tuple-element.98.put_ref, bf16[5,32,2048]{2,1,0:T(8,128)(2,1)S(1)} %bitcast_dynamic-update-slice_fusion.4.refs_0_, ...), custom_call_target="tpu_custom_call" | custom-call | flops 128 | bytes 128 | tf_op jit(solution)/shard_map/forward/pallas_call | solution.py:79
  43.2 5.1 %collective-permute-done.12 = bf16[32,2048]{1,0:T(8,128)(2,1)S(1)} collective-permute-done((bf16[32,2048]{1,0:T(8,128)(2,1)S(1)}, bf16[32,2048]{1,0:T(8,128)(2,1)S(1)}, u32[]{:S(2)}, u32[]{:S(2)}) %collective-permute-start.12) | collective-permute-done | bytes 131104 | tf_op jit(solution)/shard_map/ppermute | solution.py:120
  50.2 4.6 %collective-permute-start.21 = (bf16[32,2048]{1,0:T(8,128)(2,1)S(1)}, bf16[32,2048]{1,0:T(8,128)(2,1)S(1)}, u32[]{:S(2)}, u32[]{:S(2)}) collective-permute-start(bf16[32,2048]{1,0:T(8,128)(2,1)S(1)} %get-tuple-element.94), channel_id=1, source_target_pairs={{0,16},{2,18},{4,20},{6,22},{8,24},{10,26},{12,28},{14,30},{16,0},... | collective-permute-start | bytes 393224 | tf_op jit(solution)/shard_map/ppermute | solution.py:120
  54.9 4.4 %mirror.3 = (bf16[8,32,2048]{2,1,0:T(8,128)(2,1)S(1)}, bf16[8,32,2048]{2,1,0:T(8,128)(2,1)S(1)}) custom-call(s32[1]{0:T(128)} %copy.16.count_ref, s32[256]{0:T(256)S(1)} %get-tuple-element.99.take_ref, s32[256]{0:T(256)S(1)} %get-tuple-element.112.put_ref, bf16[1,32,2048]{2,1,0:T(8,128)(2,1)S(1)} %bitcast.92, bf16[1,32,2048]{2,1,0:T(8,128)(2,1)S(1)} %bitcast.95, ...), custom_call_target="tpu_custom_call" | custom-call | flops 128 | bytes 128 | tf_op jit(solution)/shard_map/mirror/pallas_call | solution.py:79
  59.4 2.3 %collective-permute-done.21 = bf16[32,2048]{1,0:T(8,128)(2,1)S(1)} collective-permute-done((bf16[32,2048]{1,0:T(8,128)(2,1)S(1)}, bf16[32,2048]{1,0:T(8,128)(2,1)S(1)}, u32[]{:S(2)}, u32[]{:S(2)}) %collective-permute-start.21) | collective-permute-done | bytes 131104 | tf_op jit(solution)/shard_map/ppermute | solution.py:120
  62.4 3.1 %collective-permute-start.18 = (bf16[32,2048]{1,0:T(8,128)(2,1)S(1)}, bf16[32,2048]{1,0:T(8,128)(2,1)S(1)}, u32[]{:S(2)}, u32[]{:S(2)}) collective-permute-start(bf16[32,2048]{1,0:T(8,128)(2,1)S(1)} %collective-permute-done.17), channel_id=1, source_target_pairs={{0,8},{2,10},{4,12},{6,14},{8,16},{10,18},{12,20},{14,22},{16,24},... | collective-permute-start | bytes 393224 | tf_op jit(solution)/shard_map/ppermute | solution.py:120
  68.3 2.3 %collective-permute-done.18 = bf16[32,2048]{1,0:T(8,128)(2,1)S(1)} collective-permute-done((bf16[32,2048]{1,0:T(8,128)(2,1)S(1)}, bf16[32,2048]{1,0:T(8,128)(2,1)S(1)}, u32[]{:S(2)}, u32[]{:S(2)}) %collective-permute-start.18) | collective-permute-done | bytes 131104 | tf_op jit(solution)/shard_map/ppermute | solution.py:120
  70.6 2.4 %collective-permute-done.19 = bf16[32,2048]{1,0:T(8,128)(2,1)S(1)} collective-permute-done((bf16[32,2048]{1,0:T(8,128)(2,1)S(1)}, bf16[32,2048]{1,0:T(8,128)(2,1)S(1)}, u32[]{:S(2)}, u32[]{:S(2)}) %collective-permute-start.19) | collective-permute-done | bytes 131104 | tf_op jit(solution)/shard_map/ppermute | solution.py:120
  73.0 4.9 %collective-permute-done.26 = bf16[3,32,2048]{2,1,0:T(8,128)(2,1)S(1)} collective-permute-done((bf16[3,32,2048]{2,1,0:T(8,128)(2,1)S(1)}, bf16[3,32,2048]{2,1,0:T(8,128)(2,1)S(1)}, u32[]{:S(2)}, u32[]{:S(2)}) %collective-permute-start.26) | collective-permute-done | bytes 393248 | tf_op jit(solution)/shard_map/ppermute | solution.py:120
  78.1 1.8 %collective-permute-start.28 = (bf16[32,2048]{1,0:T(8,128)(2,1)S(1)}, bf16[32,2048]{1,0:T(8,128)(2,1)S(1)}, u32[]{:S(2)}, u32[]{:S(2)}) collective-permute-start(bf16[32,2048]{1,0:T(8,128)(2,1)S(1)} %get-tuple-element.108), channel_id=1, source_target_pairs={{0,24},{2,26},{4,28},{6,30},{8,0},{10,2},{12,4},{14,6},{16,8},{18,... | collective-permute-start | bytes 393224 | tf_op jit(solution)/shard_map/ppermute | solution.py:120
  82.1 4.3 %forward.3 = (f32[1,32,2048]{2,1,0:T(8,128)S(1)}, bf16[1,32,2048]{2,1,0:T(8,128)(2,1)S(1)}) custom-call(s32[1]{0:T(128)} %copy.16.count_ref, s32[256]{0:T(256)S(1)} %get-tuple-element.113.take_ref, s32[256]{0:T(256)S(1)} %get-tuple-element.98.put_ref, bf16[5,32,2048]{2,1,0:T(8,128)(2,1)S(1)} %bitcast_dynamic-update-slice_fusion.refs_0_, ...), custom_call_target="tpu_custom_call" | custom-call | flops 128 | bytes 128 | tf_op jit(solution)/shard_map/forward/pallas_call | solution.py:79
  86.4 1.5 %collective-permute-start.33 = (bf16[32,2048]{1,0:T(8,128)(2,1)S(1)}, bf16[32,2048]{1,0:T(8,128)(2,1)S(1)}, u32[]{:S(2)}, u32[]{:S(2)}) collective-permute-start(bf16[32,2048]{1,0:T(8,128)(2,1)S(1)} %bitcast.96), channel_id=1, source_target_pairs={{0,1},{1,0},{2,3},{3,2},{4,5},{5,4},{6,7},{7,6},{8,9},{9,8},{10,11... | collective-permute-start | bytes 393224 | tf_op jit(solution)/shard_map/ppermute | solution.py:123
  87.9 5.2 %collective-permute-done.29 = bf16[32,2048]{1,0:T(8,128)(2,1)S(1)} collective-permute-done((bf16[32,2048]{1,0:T(8,128)(2,1)S(1)}, bf16[32,2048]{1,0:T(8,128)(2,1)S(1)}, u32[]{:S(2)}, u32[]{:S(2)}) %collective-permute-start.29) | collective-permute-done | bytes 131104 | tf_op jit(solution)/shard_map/ppermute | solution.py:120
  (74 shorter events, 17.1 us)
Async XLA Ops:
  1.0 11.4 %collective-permute-start.6 = (bf16[32,2048]{1,0:T(8,128)(2,1)S(1)}, bf16[32,2048]{1,0:T(8,128)(2,1)S(1)}, u32[]{:S(2)}, u32[]{:S(2)}) collective-permute-start(bf16[32,2048]{1,0:T(8,128)(2,1)S(1)} %get-tuple-element.97), channel_id=1, source_target_pairs={{0,1},{1,0},{2,3},{3,2},{4,5},{5,4},{6,7},{7,6},{8,9},{9,8},{10,11... | collective-permute-start | bytes 393224 | tf_op jit(solution)/shard_map/ppermute | solution.py:123
  4.0 12.9 %collective-permute-start.3 = (bf16[32,2048]{1,0:T(8,128)(2,1)S(1)}, bf16[32,2048]{1,0:T(8,128)(2,1)S(1)}, u32[]{:S(2)}, u32[]{:S(2)}) collective-permute-start(bf16[32,2048]{1,0:T(8,128)(2,1)S(1)} %get-tuple-element.97), channel_id=1, source_target_pairs={{0,8},{2,10},{4,12},{6,14},{8,16},{10,18},{12,20},{14,22},{16,24},... | collective-permute-start | bytes 393224 | tf_op jit(solution)/shard_map/ppermute | solution.py:120
  5.6 11.4 %collective-permute-start.4 = (bf16[32,2048]{1,0:T(8,128)(2,1)S(1)}, bf16[32,2048]{1,0:T(8,128)(2,1)S(1)}, u32[]{:S(2)}, u32[]{:S(2)}) collective-permute-start(bf16[32,2048]{1,0:T(8,128)(2,1)S(1)} %get-tuple-element.97), channel_id=1, source_target_pairs={{0,16},{2,18},{4,20},{6,22},{8,24},{10,26},{12,28},{14,30},{16,0},... | collective-permute-start | bytes 393224 | tf_op jit(solution)/shard_map/ppermute | solution.py:120
  8.1 8.8 %collective-permute-start.5 = (bf16[32,2048]{1,0:T(8,128)(2,1)S(1)}, bf16[32,2048]{1,0:T(8,128)(2,1)S(1)}, u32[]{:S(2)}, u32[]{:S(2)}) collective-permute-start(bf16[32,2048]{1,0:T(8,128)(2,1)S(1)} %get-tuple-element.97), channel_id=1, source_target_pairs={{0,24},{2,26},{4,28},{6,30},{8,0},{10,2},{12,4},{14,6},{16,8},{18,... | collective-permute-start | bytes 393224 | tf_op jit(solution)/shard_map/ppermute | solution.py:120
  9.5 8.6 %collective-permute-start = (bf16[32,2048]{1,0:T(8,128)(2,1)S(1)}, bf16[32,2048]{1,0:T(8,128)(2,1)S(1)}, u32[]{:S(2)}, u32[]{:S(2)}) collective-permute-start(bf16[32,2048]{1,0:T(8,128)(2,1)S(1)} %get-tuple-element.97), channel_id=1, source_target_pairs={{0,4},{2,6},{4,0},{6,2},{8,12},{10,14},{12,8},{14,10},{16,20},{18,... | collective-permute-start | bytes 393224 | tf_op jit(solution)/shard_map/ppermute | solution.py:120
  18.1 8.3 %collective-permute-start.1 = (bf16[32,2048]{1,0:T(8,128)(2,1)S(1)}, bf16[32,2048]{1,0:T(8,128)(2,1)S(1)}, u32[]{:S(2)}, u32[]{:S(2)}) collective-permute-start(bf16[32,2048]{1,0:T(8,128)(2,1)S(1)} %collective-permute-done), channel_id=1, source_target_pairs={{0,8},{2,10},{4,12},{6,14},{8,16},{10,18},{12,20},{14,22},{16,24},... | collective-permute-start | bytes 393224 | tf_op jit(solution)/shard_map/ppermute | solution.py:120
  22.9 9.7 %collective-permute-start.9 = (bf16[3,32,2048]{2,1,0:T(8,128)(2,1)S(1)}, bf16[3,32,2048]{2,1,0:T(8,128)(2,1)S(1)}, u32[]{:S(2)}, u32[]{:S(2)}) collective-permute-start(bf16[3,32,2048]{2,1,0:T(8,128)(2,1)S(1)} %slice.66), channel_id=1, source_target_pairs={{0,4},{2,6},{4,0},{6,2},{8,12},{10,14},{12,8},{14,10},{16,20},{18,... | collective-permute-start | bytes 1179656 | tf_op jit(solution)/shard_map/ppermute | solution.py:120
  23.5 12.7 %collective-permute-start.14 = (bf16[5,32,2048]{2,1,0:T(8,128)(2,1)S(1)}, bf16[5,32,2048]{2,1,0:T(8,128)(2,1)S(1)}, u32[]{:S(2)}, u32[]{:S(2)}) collective-permute-start(bf16[5,32,2048]{2,1,0:T(8,128)(2,1)S(1)} %bitcast_dynamic-update-slice_fusion.4.refs_0_), channel_id=1, source_target_pairs={{0,2},{2,0},{4,6},{6,4},{8,10},{10,8},{12,14},{14,12},{16,18},{18,... | collective-permute-start | bytes 1966088 | tf_op jit(solution)/shard_map/ppermute | solution.py:120
  32.9 10.3 %collective-permute-start.11 = (bf16[32,2048]{1,0:T(8,128)(2,1)S(1)}, bf16[32,2048]{1,0:T(8,128)(2,1)S(1)}, u32[]{:S(2)}, u32[]{:S(2)}) collective-permute-start(bf16[32,2048]{1,0:T(8,128)(2,1)S(1)} %get-tuple-element.111), channel_id=1, source_target_pairs={{0,24},{2,26},{4,28},{6,30},{8,0},{10,2},{12,4},{14,6},{16,8},{18,... | collective-permute-start | bytes 393224 | tf_op jit(solution)/shard_map/ppermute | solution.py:120
  34.5 13.7 %collective-permute-start.12 = (bf16[32,2048]{1,0:T(8,128)(2,1)S(1)}, bf16[32,2048]{1,0:T(8,128)(2,1)S(1)}, u32[]{:S(2)}, u32[]{:S(2)}) collective-permute-start(bf16[32,2048]{1,0:T(8,128)(2,1)S(1)} %get-tuple-element.110), channel_id=1, source_target_pairs={{0,16},{2,18},{4,20},{6,22},{8,24},{10,26},{12,28},{14,30},{16,0},... | collective-permute-start | bytes 393224 | tf_op jit(solution)/shard_map/ppermute | solution.py:120
  36.0 12.3 %collective-permute-start.13 = (bf16[32,2048]{1,0:T(8,128)(2,1)S(1)}, bf16[32,2048]{1,0:T(8,128)(2,1)S(1)}, u32[]{:S(2)}, u32[]{:S(2)}) collective-permute-start(bf16[32,2048]{1,0:T(8,128)(2,1)S(1)} %get-tuple-element.109), channel_id=1, source_target_pairs={{0,8},{2,10},{4,12},{6,14},{8,16},{10,18},{12,20},{14,22},{16,24},... | collective-permute-start | bytes 393224 | tf_op jit(solution)/shard_map/ppermute | solution.py:120
  36.2 12.0 %collective-permute-start.10 = (bf16[1,32,2048]{2,1,0:T(8,128)(2,1)S(1)}, bf16[1,32,2048]{2,1,0:T(8,128)(2,1)S(1)}, u32[]{:S(2)}, u32[]{:S(2)}) collective-permute-start(bf16[1,32,2048]{2,1,0:T(8,128)(2,1)S(1)} %slice.67), channel_id=1, source_target_pairs={{0,4},{2,6},{4,0},{6,2},{8,12},{10,14},{12,8},{14,10},{16,20},{18,... | collective-permute-start | bytes 393224 | tf_op jit(solution)/shard_map/ppermute | solution.py:120
  41.3 7.0 %collective-permute-start.16 = (bf16[32,2048]{1,0:T(8,128)(2,1)S(1)}, bf16[32,2048]{1,0:T(8,128)(2,1)S(1)}, u32[]{:S(2)}, u32[]{:S(2)}) collective-permute-start(bf16[32,2048]{1,0:T(8,128)(2,1)S(1)} %bitcast.97), channel_id=1, source_target_pairs={{0,1},{1,0},{2,3},{3,2},{4,5},{5,4},{6,7},{7,6},{8,9},{9,8},{10,11... | collective-permute-start | bytes 393224 | tf_op jit(solution)/shard_map/ppermute | solution.py:123
  49.0 10.3 %collective-permute-start.20 = (bf16[32,2048]{1,0:T(8,128)(2,1)S(1)}, bf16[32,2048]{1,0:T(8,128)(2,1)S(1)}, u32[]{:S(2)}, u32[]{:S(2)}) collective-permute-start(bf16[32,2048]{1,0:T(8,128)(2,1)S(1)} %get-tuple-element.94), channel_id=1, source_target_pairs={{0,8},{2,10},{4,12},{6,14},{8,16},{10,18},{12,20},{14,22},{16,24},... | collective-permute-start | bytes 393224 | tf_op jit(solution)/shard_map/ppermute | solution.py:120
  50.2 11.5 %collective-permute-start.21 = (bf16[32,2048]{1,0:T(8,128)(2,1)S(1)}, bf16[32,2048]{1,0:T(8,128)(2,1)S(1)}, u32[]{:S(2)}, u32[]{:S(2)}) collective-permute-start(bf16[32,2048]{1,0:T(8,128)(2,1)S(1)} %get-tuple-element.94), channel_id=1, source_target_pairs={{0,16},{2,18},{4,20},{6,22},{8,24},{10,26},{12,28},{14,30},{16,0},... | collective-permute-start | bytes 393224 | tf_op jit(solution)/shard_map/ppermute | solution.py:120
  54.7 7.7 %collective-permute-start.17 = (bf16[32,2048]{1,0:T(8,128)(2,1)S(1)}, bf16[32,2048]{1,0:T(8,128)(2,1)S(1)}, u32[]{:S(2)}, u32[]{:S(2)}) collective-permute-start(bf16[32,2048]{1,0:T(8,128)(2,1)S(1)} %get-tuple-element.94), channel_id=1, source_target_pairs={{0,4},{2,6},{4,0},{6,2},{8,12},{10,14},{12,8},{14,10},{16,20},{18,... | collective-permute-start | bytes 393224 | tf_op jit(solution)/shard_map/ppermute | solution.py:120
  62.4 8.2 %collective-permute-start.18 = (bf16[32,2048]{1,0:T(8,128)(2,1)S(1)}, bf16[32,2048]{1,0:T(8,128)(2,1)S(1)}, u32[]{:S(2)}, u32[]{:S(2)}) collective-permute-start(bf16[32,2048]{1,0:T(8,128)(2,1)S(1)} %collective-permute-done.17), channel_id=1, source_target_pairs={{0,8},{2,10},{4,12},{6,14},{8,16},{10,18},{12,20},{14,22},{16,24},... | collective-permute-start | bytes 393224 | tf_op jit(solution)/shard_map/ppermute | solution.py:120
  65.5 7.5 %collective-permute-start.19 = (bf16[32,2048]{1,0:T(8,128)(2,1)S(1)}, bf16[32,2048]{1,0:T(8,128)(2,1)S(1)}, u32[]{:S(2)}, u32[]{:S(2)}) collective-permute-start(bf16[32,2048]{1,0:T(8,128)(2,1)S(1)} %collective-permute-done.17), channel_id=1, source_target_pairs={{0,24},{2,26},{4,28},{6,30},{8,0},{10,2},{12,4},{14,6},{16,8},{18,... | collective-permute-start | bytes 393224 | tf_op jit(solution)/shard_map/ppermute | solution.py:120
  66.9 11.0 %collective-permute-start.26 = (bf16[3,32,2048]{2,1,0:T(8,128)(2,1)S(1)}, bf16[3,32,2048]{2,1,0:T(8,128)(2,1)S(1)}, u32[]{:S(2)}, u32[]{:S(2)}) collective-permute-start(bf16[3,32,2048]{2,1,0:T(8,128)(2,1)S(1)} %slice.73), channel_id=1, source_target_pairs={{0,4},{2,6},{4,0},{6,2},{8,12},{10,14},{12,8},{14,10},{16,20},{18,... | collective-permute-start | bytes 1179656 | tf_op jit(solution)/shard_map/ppermute | solution.py:120
  68.2 12.7 %collective-permute-start.31 = (bf16[5,32,2048]{2,1,0:T(8,128)(2,1)S(1)}, bf16[5,32,2048]{2,1,0:T(8,128)(2,1)S(1)}, u32[]{:S(2)}, u32[]{:S(2)}) collective-permute-start(bf16[5,32,2048]{2,1,0:T(8,128)(2,1)S(1)} %bitcast_dynamic-update-slice_fusion.refs_0_), channel_id=1, source_target_pairs={{0,2},{2,0},{4,6},{6,4},{8,10},{10,8},{12,14},{14,12},{16,18},{18,... | collective-permute-start | bytes 1966088 | tf_op jit(solution)/shard_map/ppermute | solution.py:120
  78.1 9.8 %collective-permute-start.28 = (bf16[32,2048]{1,0:T(8,128)(2,1)S(1)}, bf16[32,2048]{1,0:T(8,128)(2,1)S(1)}, u32[]{:S(2)}, u32[]{:S(2)}) collective-permute-start(bf16[32,2048]{1,0:T(8,128)(2,1)S(1)} %get-tuple-element.108), channel_id=1, source_target_pairs={{0,24},{2,26},{4,28},{6,30},{8,0},{10,2},{12,4},{14,6},{16,8},{18,... | collective-permute-start | bytes 393224 | tf_op jit(solution)/shard_map/ppermute | solution.py:120
  79.9 13.1 %collective-permute-start.29 = (bf16[32,2048]{1,0:T(8,128)(2,1)S(1)}, bf16[32,2048]{1,0:T(8,128)(2,1)S(1)}, u32[]{:S(2)}, u32[]{:S(2)}) collective-permute-start(bf16[32,2048]{1,0:T(8,128)(2,1)S(1)} %get-tuple-element.107), channel_id=1, source_target_pairs={{0,16},{2,18},{4,20},{6,22},{8,24},{10,26},{12,28},{14,30},{16,0},... | collective-permute-start | bytes 393224 | tf_op jit(solution)/shard_map/ppermute | solution.py:120
  80.8 12.3 %collective-permute-start.30 = (bf16[32,2048]{1,0:T(8,128)(2,1)S(1)}, bf16[32,2048]{1,0:T(8,128)(2,1)S(1)}, u32[]{:S(2)}, u32[]{:S(2)}) collective-permute-start(bf16[32,2048]{1,0:T(8,128)(2,1)S(1)} %get-tuple-element.106), channel_id=1, source_target_pairs={{0,8},{2,10},{4,12},{6,14},{8,16},{10,18},{12,20},{14,22},{16,24},... | collective-permute-start | bytes 393224 | tf_op jit(solution)/shard_map/ppermute | solution.py:120
  80.9 12.2 %collective-permute-start.27 = (bf16[1,32,2048]{2,1,0:T(8,128)(2,1)S(1)}, bf16[1,32,2048]{2,1,0:T(8,128)(2,1)S(1)}, u32[]{:S(2)}, u32[]{:S(2)}) collective-permute-start(bf16[1,32,2048]{2,1,0:T(8,128)(2,1)S(1)} %slice.74), channel_id=1, source_target_pairs={{0,4},{2,6},{4,0},{6,2},{8,12},{10,14},{12,8},{14,10},{16,20},{18,... | collective-permute-start | bytes 393224 | tf_op jit(solution)/shard_map/ppermute | solution.py:120
  (11 other events, 69.8 us)

commit v10 on v9

--- a/solution.py
+++ b/solution.py
@@ -154,14 +154,14 @@
 
     def apply_operator(narrow):
         by_col = [narrow] + [shift_col(narrow, j) for j in range(1, n_col)]
-        near = [narrow] + [shift(narrow, db=b) for b in range(1, n_b)]
         far = [shift(narrow, da=a) for a in range(1, n_a)]
         mirrors = block_product(
             0, mirror_inputs, mirror_outputs, [jnp.bfloat16] * len(mirror_outputs), n_row,
             block_counts, place_rows, put_cols, by_col, block_values,
         )
         mirrors = list(mirrors)
-        far, mirrors[0] = lax.optimization_barrier((far, mirrors[0]))
+        far, mirrors[0], held = lax.optimization_barrier((far, mirrors[0], narrow))
+        near = [held] + [shift(held, db=b) for b in range(1, n_b)]
         middle = n_a // 2
         across = [shift(far[middle - 1], db=b) for b in range(1, n_b)] if middle else []
 

time: 94.2 us -> 100 us (1.062)
  starting transfers between devices: 39 us -> 50 us
  Pallas kernels: 17.4 us -> 13.3 us
  waiting for transfers between devices: 31.3 us -> 28.6 us
    ppermute x4, starting transfers between devices: 5.73 us -> 13.1 us  [shift_col(): lax.ppermute(value, 'col', [(j, (j + d) % n_col) for j in range(n_col)])]
    pallas_call x4, Pallas kernels: 17.4 us -> 13.3 us  [block_product(): pl.pallas_call(functools.partial(product_kernel, contract, inputs, output...]
    ppermute x30, starting transfers between devices: 33.2 us -> 36.9 us  [shift(): return lax.ppermute(value, 'row', pairs)]
    ppermute x30, waiting for transfers between devices: 31.3 us -> 27.8 us  [shift(): return lax.ppermute(value, 'row', pairs)]
    unnamed x2 -> x0, other arithmetic: 1.12 us -> none
    convert_element_type x0 -> x2, other arithmetic: none -> 1.12 us  [the longest x1 0.96 us: shards(): vectors.astype(jnp.bfloat16)]
  transfers between devices with their start and end apart: 34 -> 34, of which waited for: 9 -> 13; matrix products, arithmetic and copies ran while one was open for 2% -> 3% of each run, Pallas kernels for 18% -> 13%
where the time goes in v10:
time: 100 us; the launch traced here: 99.2 us
  starting transfers between devices  50 us (50%)
  waiting for transfers between devices  28.6 us (29%)
  Pallas kernels  13.3 us (13%)
  other arithmetic  4.82 us (5%)
  between operations  2.3 us (2%)
    ppermute x30, starting transfers between devices, shift(): return lax.ppermute(value, 'row', pairs)  36.9 us
    ppermute x30, waiting for transfers between devices, shift(): return lax.ppermute(value, 'row', pairs)  27.8 us
    pallas_call x4, Pallas kernels, block_product(): pl.pallas_call(functools.partial(product_kernel, contract, inputs, output...  13.3 us
    ppermute x4, starting transfers between devices, shift_col(): lax.ppermute(value, 'col', [(j, (j + d) % n_col) for j in range(n_col)])  13.1 us
  transfers between devices with their start and end apart: 34, of which 13 were waited for; matrix products, arithmetic and copies ran while one was open for 3% of the time, Pallas kernels for 13%

profile of v10, /device:TPU:0, one launch (start us, length us, event | category | flops | bytes accessed | tf_op | source)
XLA Modules:
  0.0 99.2 jit_solution(12252916424847634418)
XLA Ops:
  1.0 3.0 %collective-permute-start.3 = (bf16[32,2048]{1,0:T(8,128)(2,1)S(1)}, bf16[32,2048]{1,0:T(8,128)(2,1)S(1)}, u32[]{:S(2)}, u32[]{:S(2)}) collective-permute-start(bf16[32,2048]{1,0:T(8,128)(2,1)S(1)} %convert_element_type.82), channel_id=1, source_target_pairs={{0,1},{1,0},{2,3},{3,2},{4,5},{5,4},{6,7},{7,6},{8,9},{9,8},{10,11... | collective-permute-start | bytes 393224 | tf_op jit(solution)/shard_map/ppermute | solution.py:123
  5.5 2.6 %collective-permute-start.1 = (bf16[32,2048]{1,0:T(8,128)(2,1)S(1)}, bf16[32,2048]{1,0:T(8,128)(2,1)S(1)}, u32[]{:S(2)}, u32[]{:S(2)}) collective-permute-start(bf16[32,2048]{1,0:T(8,128)(2,1)S(1)} %convert_element_type.82), channel_id=1, source_target_pairs={{0,16},{2,18},{4,20},{6,22},{8,24},{10,26},{12,28},{14,30},{16,0},... | collective-permute-start | bytes 393224 | tf_op jit(solution)/shard_map/ppermute | solution.py:120
  11.9 3.4 %mirror.2 = (bf16[8,32,2048]{2,1,0:T(8,128)(2,1)S(1)}, bf16[8,32,2048]{2,1,0:T(8,128)(2,1)S(1)}) custom-call(s32[1]{0:T(128)} %copy.16.count_ref, s32[256]{0:T(256)S(1)} %get-tuple-element.100.take_ref, s32[256]{0:T(256)S(1)} %get-tuple-element.113.put_ref, bf16[1,32,2048]{2,1,0:T(8,128)(2,1)S(1)} %convert_bitcast_fusion.refs_0_, ...), custom_call_target="tpu_custom_call" | custom-call | flops 128 | bytes 128 | tf_op jit(solution)/shard_map/mirror/pallas_call | solution.py:79
  16.5 3.4 %collective-permute-start.4 = (bf16[32,2048]{1,0:T(8,128)(2,1)S(1)}, bf16[32,2048]{1,0:T(8,128)(2,1)S(1)}, u32[]{:S(2)}, u32[]{:S(2)}) collective-permute-start(bf16[32,2048]{1,0:T(8,128)(2,1)S(1)} %convert_element_type.82), channel_id=1, source_target_pairs={{0,4},{2,6},{4,0},{6,2},{8,12},{10,14},{12,8},{14,10},{16,20},{18,... | collective-permute-start | bytes 393224 | tf_op jit(solution)/shard_map/ppermute | solution.py:120
  20.1 3.6 %collective-permute-done.4 = bf16[32,2048]{1,0:T(8,128)(2,1)S(1)} collective-permute-done((bf16[32,2048]{1,0:T(8,128)(2,1)S(1)}, bf16[32,2048]{1,0:T(8,128)(2,1)S(1)}, u32[]{:S(2)}, u32[]{:S(2)}) %collective-permute-start.4) | collective-permute-done | bytes 131104 | tf_op jit(solution)/shard_map/ppermute | solution.py:120
  23.7 2.2 %collective-permute-start.5 = (bf16[32,2048]{1,0:T(8,128)(2,1)S(1)}, bf16[32,2048]{1,0:T(8,128)(2,1)S(1)}, u32[]{:S(2)}, u32[]{:S(2)}) collective-permute-start(bf16[32,2048]{1,0:T(8,128)(2,1)S(1)} %collective-permute-done.4), channel_id=1, source_target_pairs={{0,8},{2,10},{4,12},{6,14},{8,16},{10,18},{12,20},{14,22},{16,24},... | collective-permute-start | bytes 393224 | tf_op jit(solution)/shard_map/ppermute | solution.py:120
  28.1 2.5 %collective-permute-start.9 = (bf16[3,32,2048]{2,1,0:T(8,128)(2,1)S(1)}, bf16[3,32,2048]{2,1,0:T(8,128)(2,1)S(1)}, u32[]{:S(2)}, u32[]{:S(2)}) collective-permute-start(bf16[3,32,2048]{2,1,0:T(8,128)(2,1)S(1)} %slice.66), channel_id=1, source_target_pairs={{0,4},{2,6},{4,0},{6,2},{8,12},{10,14},{12,8},{14,10},{16,20},{18,... | collective-permute-start | bytes 1179656 | tf_op jit(solution)/shard_map/ppermute | solution.py:120
  32.0 4.4 %collective-permute-done.9 = bf16[3,32,2048]{2,1,0:T(8,128)(2,1)S(1)} collective-permute-done((bf16[3,32,2048]{2,1,0:T(8,128)(2,1)S(1)}, bf16[3,32,2048]{2,1,0:T(8,128)(2,1)S(1)}, u32[]{:S(2)}, u32[]{:S(2)}) %collective-permute-start.9) | collective-permute-done | bytes 393248 | tf_op jit(solution)/shard_map/ppermute | solution.py:120
  37.4 1.9 %collective-permute-start.12 = (bf16[32,2048]{1,0:T(8,128)(2,1)S(1)}, bf16[32,2048]{1,0:T(8,128)(2,1)S(1)}, u32[]{:S(2)}, u32[]{:S(2)}) collective-permute-start(bf16[32,2048]{1,0:T(8,128)(2,1)S(1)} %get-tuple-element.111), channel_id=1, source_target_pairs={{0,16},{2,18},{4,20},{6,22},{8,24},{10,26},{12,28},{14,30},{16,0},... | collective-permute-start | bytes 393224 | tf_op jit(solution)/shard_map/ppermute | solution.py:120
  41.1 3.2 %forward.2 = (f32[1,32,2048]{2,1,0:T(8,128)S(1)}, bf16[1,32,2048]{2,1,0:T(8,128)(2,1)S(1)}) custom-call(s32[1]{0:T(128)} %copy.16.count_ref, s32[256]{0:T(256)S(1)} %get-tuple-element.114.take_ref, s32[256]{0:T(256)S(1)} %get-tuple-element.99.put_ref, bf16[5,32,2048]{2,1,0:T(8,128)(2,1)S(1)} %bitcast_dynamic-update-slice_fusion.5.refs_0_, ...), custom_call_target="tpu_custom_call" | custom-call | flops 128 | bytes 128 | tf_op jit(solution)/shard_map/forward/pallas_call | solution.py:79
  44.4 3.7 %collective-permute-start.16 = (bf16[32,2048]{1,0:T(8,128)(2,1)S(1)}, bf16[32,2048]{1,0:T(8,128)(2,1)S(1)}, u32[]{:S(2)}, u32[]{:S(2)}) collective-permute-start(bf16[32,2048]{1,0:T(8,128)(2,1)S(1)} %bitcast.99), channel_id=1, source_target_pairs={{0,1},{1,0},{2,3},{3,2},{4,5},{5,4},{6,7},{7,6},{8,9},{9,8},{10,11... | collective-permute-start | bytes 393224 | tf_op jit(solution)/shard_map/ppermute | solution.py:123
  49.4 2.2 %collective-permute-done.12 = bf16[32,2048]{1,0:T(8,128)(2,1)S(1)} collective-permute-done((bf16[32,2048]{1,0:T(8,128)(2,1)S(1)}, bf16[32,2048]{1,0:T(8,128)(2,1)S(1)}, u32[]{:S(2)}, u32[]{:S(2)}) %collective-permute-start.12) | collective-permute-done | bytes 131104 | tf_op jit(solution)/shard_map/ppermute | solution.py:120
  53.2 4.8 %collective-permute-start.18 = (bf16[32,2048]{1,0:T(8,128)(2,1)S(1)}, bf16[32,2048]{1,0:T(8,128)(2,1)S(1)}, u32[]{:S(2)}, u32[]{:S(2)}) collective-permute-start(bf16[32,2048]{1,0:T(8,128)(2,1)S(1)} %get-tuple-element.75), channel_id=1, source_target_pairs={{0,16},{2,18},{4,20},{6,22},{8,24},{10,26},{12,28},{14,30},{16,0},... | collective-permute-start | bytes 393224 | tf_op jit(solution)/shard_map/ppermute | solution.py:120
  58.0 3.4 %mirror.3 = (bf16[8,32,2048]{2,1,0:T(8,128)(2,1)S(1)}, bf16[8,32,2048]{2,1,0:T(8,128)(2,1)S(1)}) custom-call(s32[1]{0:T(128)} %copy.16.count_ref, s32[256]{0:T(256)S(1)} %get-tuple-element.100.take_ref, s32[256]{0:T(256)S(1)} %get-tuple-element.113.put_ref, bf16[1,32,2048]{2,1,0:T(8,128)(2,1)S(1)} %bitcast.95, bf16[1,32,2048]{2,1,0:T(8,128)(2,1)S(1)} %bitcast.97, ...), custom_call_target="tpu_custom_call" | custom-call | flops 128 | bytes 128 | tf_op jit(solution)/shard_map/mirror/pallas_call | solution.py:79
  61.8 3.2 %collective-permute-done.18 = bf16[32,2048]{1,0:T(8,128)(2,1)S(1)} collective-permute-done((bf16[32,2048]{1,0:T(8,128)(2,1)S(1)}, bf16[32,2048]{1,0:T(8,128)(2,1)S(1)}, u32[]{:S(2)}, u32[]{:S(2)}) %collective-permute-start.18) | collective-permute-done | bytes 131104 | tf_op jit(solution)/shard_map/ppermute | solution.py:120
  67.2 3.3 %collective-permute-done.21 = bf16[32,2048]{1,0:T(8,128)(2,1)S(1)} collective-permute-done((bf16[32,2048]{1,0:T(8,128)(2,1)S(1)}, bf16[32,2048]{1,0:T(8,128)(2,1)S(1)}, u32[]{:S(2)}, u32[]{:S(2)}) %collective-permute-start.21) | collective-permute-done | bytes 131104 | tf_op jit(solution)/shard_map/ppermute | solution.py:120
  70.5 1.9 %collective-permute-start.22 = (bf16[32,2048]{1,0:T(8,128)(2,1)S(1)}, bf16[32,2048]{1,0:T(8,128)(2,1)S(1)}, u32[]{:S(2)}, u32[]{:S(2)}) collective-permute-start(bf16[32,2048]{1,0:T(8,128)(2,1)S(1)} %collective-permute-done.21), channel_id=1, source_target_pairs={{0,8},{2,10},{4,12},{6,14},{8,16},{10,18},{12,20},{14,22},{16,24},... | collective-permute-start | bytes 393224 | tf_op jit(solution)/shard_map/ppermute | solution.py:120
  72.4 2.2 %collective-permute-start.23 = (bf16[32,2048]{1,0:T(8,128)(2,1)S(1)}, bf16[32,2048]{1,0:T(8,128)(2,1)S(1)}, u32[]{:S(2)}, u32[]{:S(2)}) collective-permute-start(bf16[32,2048]{1,0:T(8,128)(2,1)S(1)} %collective-permute-done.21), channel_id=1, source_target_pairs={{0,24},{2,26},{4,28},{6,30},{8,0},{10,2},{12,4},{14,6},{16,8},{18,... | collective-permute-start | bytes 393224 | tf_op jit(solution)/shard_map/ppermute | solution.py:120
  75.1 1.7 %collective-permute-start.26 = (bf16[3,32,2048]{2,1,0:T(8,128)(2,1)S(1)}, bf16[3,32,2048]{2,1,0:T(8,128)(2,1)S(1)}, u32[]{:S(2)}, u32[]{:S(2)}) collective-permute-start(bf16[3,32,2048]{2,1,0:T(8,128)(2,1)S(1)} %slice.73), channel_id=1, source_target_pairs={{0,4},{2,6},{4,0},{6,2},{8,12},{10,14},{12,8},{14,10},{16,20},{18,... | collective-permute-start | bytes 1179656 | tf_op jit(solution)/shard_map/ppermute | solution.py:120
  78.8 4.2 %collective-permute-done.26 = bf16[3,32,2048]{2,1,0:T(8,128)(2,1)S(1)} collective-permute-done((bf16[3,32,2048]{2,1,0:T(8,128)(2,1)S(1)}, bf16[3,32,2048]{2,1,0:T(8,128)(2,1)S(1)}, u32[]{:S(2)}, u32[]{:S(2)}) %collective-permute-start.26) | collective-permute-done | bytes 393248 | tf_op jit(solution)/shard_map/ppermute | solution.py:120
  83.2 2.2 %collective-permute-start.28 = (bf16[32,2048]{1,0:T(8,128)(2,1)S(1)}, bf16[32,2048]{1,0:T(8,128)(2,1)S(1)}, u32[]{:S(2)}, u32[]{:S(2)}) collective-permute-start(bf16[32,2048]{1,0:T(8,128)(2,1)S(1)} %get-tuple-element.109), channel_id=1, source_target_pairs={{0,24},{2,26},{4,28},{6,30},{8,0},{10,2},{12,4},{14,6},{16,8},{18,... | collective-permute-start | bytes 393224 | tf_op jit(solution)/shard_map/ppermute | solution.py:120
  87.2 3.2 %forward.3 = (f32[1,32,2048]{2,1,0:T(8,128)S(1)}, bf16[1,32,2048]{2,1,0:T(8,128)(2,1)S(1)}) custom-call(s32[1]{0:T(128)} %copy.16.count_ref, s32[256]{0:T(256)S(1)} %get-tuple-element.114.take_ref, s32[256]{0:T(256)S(1)} %get-tuple-element.99.put_ref, bf16[5,32,2048]{2,1,0:T(8,128)(2,1)S(1)} %bitcast_dynamic-update-slice_fusion.refs_0_, ...), custom_call_target="tpu_custom_call" | custom-call | flops 128 | bytes 128 | tf_op jit(solution)/shard_map/forward/pallas_call | solution.py:79
  90.5 4.9 %collective-permute-start.33 = (bf16[32,2048]{1,0:T(8,128)(2,1)S(1)}, bf16[32,2048]{1,0:T(8,128)(2,1)S(1)}, u32[]{:S(2)}, u32[]{:S(2)}) collective-permute-start(bf16[32,2048]{1,0:T(8,128)(2,1)S(1)} %bitcast.98), channel_id=1, source_target_pairs={{0,1},{1,0},{2,3},{3,2},{4,5},{5,4},{6,7},{7,6},{8,9},{9,8},{10,11... | collective-permute-start | bytes 393224 | tf_op jit(solution)/shard_map/ppermute | solution.py:123
  95.4 2.2 %collective-permute-done.29 = bf16[32,2048]{1,0:T(8,128)(2,1)S(1)} collective-permute-done((bf16[32,2048]{1,0:T(8,128)(2,1)S(1)}, bf16[32,2048]{1,0:T(8,128)(2,1)S(1)}, u32[]{:S(2)}, u32[]{:S(2)}) %collective-permute-start.29) | collective-permute-done | bytes 131104 | tf_op jit(solution)/shard_map/ppermute | solution.py:120
  (77 shorter events, 23.6 us)
Async XLA Ops:
  1.0 10.9 %collective-permute-start.3 = (bf16[32,2048]{1,0:T(8,128)(2,1)S(1)}, bf16[32,2048]{1,0:T(8,128)(2,1)S(1)}, u32[]{:S(2)}, u32[]{:S(2)}) collective-permute-start(bf16[32,2048]{1,0:T(8,128)(2,1)S(1)} %convert_element_type.82), channel_id=1, source_target_pairs={{0,1},{1,0},{2,3},{3,2},{4,5},{5,4},{6,7},{7,6},{8,9},{9,8},{10,11... | collective-permute-start | bytes 393224 | tf_op jit(solution)/shard_map/ppermute | solution.py:123
  4.0 11.3 %collective-permute-start = (bf16[32,2048]{1,0:T(8,128)(2,1)S(1)}, bf16[32,2048]{1,0:T(8,128)(2,1)S(1)}, u32[]{:S(2)}, u32[]{:S(2)}) collective-permute-start(bf16[32,2048]{1,0:T(8,128)(2,1)S(1)} %convert_element_type.82), channel_id=1, source_target_pairs={{0,8},{2,10},{4,12},{6,14},{8,16},{10,18},{12,20},{14,22},{16,24},... | collective-permute-start | bytes 393224 | tf_op jit(solution)/shard_map/ppermute | solution.py:120
  5.5 11.0 %collective-permute-start.1 = (bf16[32,2048]{1,0:T(8,128)(2,1)S(1)}, bf16[32,2048]{1,0:T(8,128)(2,1)S(1)}, u32[]{:S(2)}, u32[]{:S(2)}) collective-permute-start(bf16[32,2048]{1,0:T(8,128)(2,1)S(1)} %convert_element_type.82), channel_id=1, source_target_pairs={{0,16},{2,18},{4,20},{6,22},{8,24},{10,26},{12,28},{14,30},{16,0},... | collective-permute-start | bytes 393224 | tf_op jit(solution)/shard_map/ppermute | solution.py:120
  8.1 8.4 %collective-permute-start.2 = (bf16[32,2048]{1,0:T(8,128)(2,1)S(1)}, bf16[32,2048]{1,0:T(8,128)(2,1)S(1)}, u32[]{:S(2)}, u32[]{:S(2)}) collective-permute-start(bf16[32,2048]{1,0:T(8,128)(2,1)S(1)} %convert_element_type.82), channel_id=1, source_target_pairs={{0,24},{2,26},{4,28},{6,30},{8,0},{10,2},{12,4},{14,6},{16,8},{18,... | collective-permute-start | bytes 393224 | tf_op jit(solution)/shard_map/ppermute | solution.py:120
  19.9 7.7 %collective-permute-start.8 = (bf16[8,32,2048]{2,1,0:T(8,128)(2,1)S(1)}, bf16[8,32,2048]{2,1,0:T(8,128)(2,1)S(1)}, u32[]{:S(2)}, u32[]{:S(2)}) collective-permute-start(bf16[8,32,2048]{2,1,0:T(8,128)(2,1)S(1)} %get-tuple-element.55), channel_id=1, source_target_pairs={{0,2},{2,0},{4,6},{6,4},{8,10},{10,8},{12,14},{14,12},{16,18},{18,... | collective-permute-start | bytes 3145736 | tf_op jit(solution)/shard_map/ppermute | solution.py:120
  20.0 10.7 %collective-permute-start.7 = (bf16[32,2048]{1,0:T(8,128)(2,1)S(1)}, bf16[32,2048]{1,0:T(8,128)(2,1)S(1)}, u32[]{:S(2)}, u32[]{:S(2)}) collective-permute-start(bf16[32,2048]{1,0:T(8,128)(2,1)S(1)} %collective-permute-done.1), channel_id=1, source_target_pairs={{0,4},{2,6},{4,0},{6,2},{8,12},{10,14},{12,8},{14,10},{16,20},{18,... | collective-permute-start | bytes 393224 | tf_op jit(solution)/shard_map/ppermute | solution.py:120
  28.1 8.3 %collective-permute-start.9 = (bf16[3,32,2048]{2,1,0:T(8,128)(2,1)S(1)}, bf16[3,32,2048]{2,1,0:T(8,128)(2,1)S(1)}, u32[]{:S(2)}, u32[]{:S(2)}) collective-permute-start(bf16[3,32,2048]{2,1,0:T(8,128)(2,1)S(1)} %slice.66), channel_id=1, source_target_pairs={{0,4},{2,6},{4,0},{6,2},{8,12},{10,14},{12,8},{14,10},{16,20},{18,... | collective-permute-start | bytes 1179656 | tf_op jit(solution)/shard_map/ppermute | solution.py:120
  30.6 9.0 %collective-permute-start.14 = (bf16[5,32,2048]{2,1,0:T(8,128)(2,1)S(1)}, bf16[5,32,2048]{2,1,0:T(8,128)(2,1)S(1)}, u32[]{:S(2)}, u32[]{:S(2)}) collective-permute-start(bf16[5,32,2048]{2,1,0:T(8,128)(2,1)S(1)} %bitcast_dynamic-update-slice_fusion.5.refs_0_), channel_id=1, source_target_pairs={{0,2},{2,0},{4,6},{6,4},{8,10},{10,8},{12,14},{14,12},{16,18},{18,... | collective-permute-start | bytes 1966088 | tf_op jit(solution)/shard_map/ppermute | solution.py:120
  36.6 12.7 %collective-permute-start.11 = (bf16[32,2048]{1,0:T(8,128)(2,1)S(1)}, bf16[32,2048]{1,0:T(8,128)(2,1)S(1)}, u32[]{:S(2)}, u32[]{:S(2)}) collective-permute-start(bf16[32,2048]{1,0:T(8,128)(2,1)S(1)} %get-tuple-element.112), channel_id=1, source_target_pairs={{0,24},{2,26},{4,28},{6,30},{8,0},{10,2},{12,4},{14,6},{16,8},{18,... | collective-permute-start | bytes 393224 | tf_op jit(solution)/shard_map/ppermute | solution.py:120
  37.4 14.2 %collective-permute-start.12 = (bf16[32,2048]{1,0:T(8,128)(2,1)S(1)}, bf16[32,2048]{1,0:T(8,128)(2,1)S(1)}, u32[]{:S(2)}, u32[]{:S(2)}) collective-permute-start(bf16[32,2048]{1,0:T(8,128)(2,1)S(1)} %get-tuple-element.111), channel_id=1, source_target_pairs={{0,16},{2,18},{4,20},{6,22},{8,24},{10,26},{12,28},{14,30},{16,0},... | collective-permute-start | bytes 393224 | tf_op jit(solution)/shard_map/ppermute | solution.py:120
  39.3 12.3 %collective-permute-start.13 = (bf16[32,2048]{1,0:T(8,128)(2,1)S(1)}, bf16[32,2048]{1,0:T(8,128)(2,1)S(1)}, u32[]{:S(2)}, u32[]{:S(2)}) collective-permute-start(bf16[32,2048]{1,0:T(8,128)(2,1)S(1)} %get-tuple-element.110), channel_id=1, source_target_pairs={{0,8},{2,10},{4,12},{6,14},{8,16},{10,18},{12,20},{14,22},{16,24},... | collective-permute-start | bytes 393224 | tf_op jit(solution)/shard_map/ppermute | solution.py:120
  39.6 12.0 %collective-permute-start.10 = (bf16[1,32,2048]{2,1,0:T(8,128)(2,1)S(1)}, bf16[1,32,2048]{2,1,0:T(8,128)(2,1)S(1)}, u32[]{:S(2)}, u32[]{:S(2)}) collective-permute-start(bf16[1,32,2048]{2,1,0:T(8,128)(2,1)S(1)} %slice.67), channel_id=1, source_target_pairs={{0,4},{2,6},{4,0},{6,2},{8,12},{10,14},{12,8},{14,10},{16,20},{18,... | collective-permute-start | bytes 393224 | tf_op jit(solution)/shard_map/ppermute | solution.py:120
  44.4 7.2 %collective-permute-start.16 = (bf16[32,2048]{1,0:T(8,128)(2,1)S(1)}, bf16[32,2048]{1,0:T(8,128)(2,1)S(1)}, u32[]{:S(2)}, u32[]{:S(2)}) collective-permute-start(bf16[32,2048]{1,0:T(8,128)(2,1)S(1)} %bitcast.99), channel_id=1, source_target_pairs={{0,1},{1,0},{2,3},{3,2},{4,5},{5,4},{6,7},{7,6},{8,9},{9,8},{10,11... | collective-permute-start | bytes 393224 | tf_op jit(solution)/shard_map/ppermute | solution.py:123
  53.2 8.6 %collective-permute-start.17 = (bf16[32,2048]{1,0:T(8,128)(2,1)S(1)}, bf16[32,2048]{1,0:T(8,128)(2,1)S(1)}, u32[]{:S(2)}, u32[]{:S(2)}) collective-permute-start(bf16[32,2048]{1,0:T(8,128)(2,1)S(1)} %get-tuple-element.75), channel_id=1, source_target_pairs={{0,8},{2,10},{4,12},{6,14},{8,16},{10,18},{12,20},{14,22},{16,24},... | collective-permute-start | bytes 393224 | tf_op jit(solution)/shard_map/ppermute | solution.py:120
  53.2 11.8 %collective-permute-start.18 = (bf16[32,2048]{1,0:T(8,128)(2,1)S(1)}, bf16[32,2048]{1,0:T(8,128)(2,1)S(1)}, u32[]{:S(2)}, u32[]{:S(2)}) collective-permute-start(bf16[32,2048]{1,0:T(8,128)(2,1)S(1)} %get-tuple-element.75), channel_id=1, source_target_pairs={{0,16},{2,18},{4,20},{6,22},{8,24},{10,26},{12,28},{14,30},{16,0},... | collective-permute-start | bytes 393224 | tf_op jit(solution)/shard_map/ppermute | solution.py:120
  66.3 8.3 %collective-permute-start.25 = (bf16[8,32,2048]{2,1,0:T(8,128)(2,1)S(1)}, bf16[8,32,2048]{2,1,0:T(8,128)(2,1)S(1)}, u32[]{:S(2)}, u32[]{:S(2)}) collective-permute-start(bf16[8,32,2048]{2,1,0:T(8,128)(2,1)S(1)} %get-tuple-element.78), channel_id=1, source_target_pairs={{0,2},{2,0},{4,6},{6,4},{8,10},{10,8},{12,14},{14,12},{16,18},{18,... | collective-permute-start | bytes 3145736 | tf_op jit(solution)/shard_map/ppermute | solution.py:120
  66.4 10.5 %collective-permute-start.24 = (bf16[32,2048]{1,0:T(8,128)(2,1)S(1)}, bf16[32,2048]{1,0:T(8,128)(2,1)S(1)}, u32[]{:S(2)}, u32[]{:S(2)}) collective-permute-start(bf16[32,2048]{1,0:T(8,128)(2,1)S(1)} %collective-permute-done.18), channel_id=1, source_target_pairs={{0,4},{2,6},{4,0},{6,2},{8,12},{10,14},{12,8},{14,10},{16,20},{18,... | collective-permute-start | bytes 393224 | tf_op jit(solution)/shard_map/ppermute | solution.py:120
  75.1 7.8 %collective-permute-start.26 = (bf16[3,32,2048]{2,1,0:T(8,128)(2,1)S(1)}, bf16[3,32,2048]{2,1,0:T(8,128)(2,1)S(1)}, u32[]{:S(2)}, u32[]{:S(2)}) collective-permute-start(bf16[3,32,2048]{2,1,0:T(8,128)(2,1)S(1)} %slice.73), channel_id=1, source_target_pairs={{0,4},{2,6},{4,0},{6,2},{8,12},{10,14},{12,8},{14,10},{16,20},{18,... | collective-permute-start | bytes 1179656 | tf_op jit(solution)/shard_map/ppermute | solution.py:120
  76.8 9.2 %collective-permute-start.31 = (bf16[5,32,2048]{2,1,0:T(8,128)(2,1)S(1)}, bf16[5,32,2048]{2,1,0:T(8,128)(2,1)S(1)}, u32[]{:S(2)}, u32[]{:S(2)}) collective-permute-start(bf16[5,32,2048]{2,1,0:T(8,128)(2,1)S(1)} %bitcast_dynamic-update-slice_fusion.refs_0_), channel_id=1, source_target_pairs={{0,2},{2,0},{4,6},{6,4},{8,10},{10,8},{12,14},{14,12},{16,18},{18,... | collective-permute-start | bytes 1966088 | tf_op jit(solution)/shard_map/ppermute | solution.py:120
  83.2 12.2 %collective-permute-start.28 = (bf16[32,2048]{1,0:T(8,128)(2,1)S(1)}, bf16[32,2048]{1,0:T(8,128)(2,1)S(1)}, u32[]{:S(2)}, u32[]{:S(2)}) collective-permute-start(bf16[32,2048]{1,0:T(8,128)(2,1)S(1)} %get-tuple-element.109), channel_id=1, source_target_pairs={{0,24},{2,26},{4,28},{6,30},{8,0},{10,2},{12,4},{14,6},{16,8},{18,... | collective-permute-start | bytes 393224 | tf_op jit(solution)/shard_map/ppermute | solution.py:120
  85.4 12.1 %collective-permute-start.29 = (bf16[32,2048]{1,0:T(8,128)(2,1)S(1)}, bf16[32,2048]{1,0:T(8,128)(2,1)S(1)}, u32[]{:S(2)}, u32[]{:S(2)}) collective-permute-start(bf16[32,2048]{1,0:T(8,128)(2,1)S(1)} %get-tuple-element.108), channel_id=1, source_target_pairs={{0,16},{2,18},{4,20},{6,22},{8,24},{10,26},{12,28},{14,30},{16,0},... | collective-permute-start | bytes 393224 | tf_op jit(solution)/shard_map/ppermute | solution.py:120
  85.4 12.1 %collective-permute-start.30 = (bf16[32,2048]{1,0:T(8,128)(2,1)S(1)}, bf16[32,2048]{1,0:T(8,128)(2,1)S(1)}, u32[]{:S(2)}, u32[]{:S(2)}) collective-permute-start(bf16[32,2048]{1,0:T(8,128)(2,1)S(1)} %get-tuple-element.107), channel_id=1, source_target_pairs={{0,8},{2,10},{4,12},{6,14},{8,16},{10,18},{12,20},{14,22},{16,24},... | collective-permute-start | bytes 393224 | tf_op jit(solution)/shard_map/ppermute | solution.py:120
  86.0 11.5 %collective-permute-start.27 = (bf16[1,32,2048]{2,1,0:T(8,128)(2,1)S(1)}, bf16[1,32,2048]{2,1,0:T(8,128)(2,1)S(1)}, u32[]{:S(2)}, u32[]{:S(2)}) collective-permute-start(bf16[1,32,2048]{2,1,0:T(8,128)(2,1)S(1)} %slice.74), channel_id=1, source_target_pairs={{0,4},{2,6},{4,0},{6,2},{8,12},{10,14},{12,8},{14,10},{16,20},{18,... | collective-permute-start | bytes 393224 | tf_op jit(solution)/shard_map/ppermute | solution.py:120
  90.5 7.8 %collective-permute-start.33 = (bf16[32,2048]{1,0:T(8,128)(2,1)S(1)}, bf16[32,2048]{1,0:T(8,128)(2,1)S(1)}, u32[]{:S(2)}, u32[]{:S(2)}) collective-permute-start(bf16[32,2048]{1,0:T(8,128)(2,1)S(1)} %bitcast.98), channel_id=1, source_target_pairs={{0,1},{1,0},{2,3},{3,2},{4,5},{5,4},{6,7},{7,6},{8,9},{9,8},{10,11... | collective-permute-start | bytes 393224 | tf_op jit(solution)/shard_map/ppermute | solution.py:123
  (11 other events, 71.9 us)

commit v11 on v9

--- a/solution.py
+++ b/solution.py
@@ -148,8 +148,7 @@
     chip = [[(0, b) for b in range(n_b)] + [(a, 0) for a in range(1, n_a)]]
     rest_of_chip = [(a, b) for b in range(1, n_b) for a in range(1, n_a) if a != n_a // 2]
     rest_of_chip += [(n_a // 2, b) for b in range(1, n_b) if n_a > 1]
-    if rest_of_chip:
-        chip.append(rest_of_chip)
+    chip += [[spot] for spot in rest_of_chip]
     forward_inputs = [[piece(a, b, c) for a, b in part] for c in range(n_c) for part in chip]
 
     def apply_operator(narrow):
@@ -183,9 +182,7 @@
         rest = [shift(send, db=-(b + 1)) for b, send in enumerate(last)]
         early = jnp.stack(near + far)
         by_row = [[early] + [shift(early, dc=c) for c in range(1, n_c)]]
-        if far_b + across:
-            late = jnp.stack(far_b + across)
-            by_row.append([late] + [shift(late, dc=c) for c in range(1, n_c)])
+        by_row += [[part] + [shift(part, dc=c) for c in range(1, n_c)] for part in far_b + across]
         by_row = [part[c] for c in range(n_c) for part in by_row]
 
         own = []

time: 94.2 us -> 98.1 us (1.041)
  starting transfers between devices: 39 us -> 43.5 us
  Pallas kernels: 17.4 us -> 13.3 us
  waiting for transfers between devices: 31.3 us -> 34.4 us
    pallas_call x4, Pallas kernels: 17.4 us -> 13.3 us  [block_product(): pl.pallas_call(functools.partial(product_kernel, contract, inputs, output...]
    ppermute x30 -> x34, starting transfers between devices: 33.2 us -> 36 us  [shift(): return lax.ppermute(value, 'row', pairs)]
    ppermute x4, waiting for transfers between devices: 0.01 us -> 2.08 us  [shift_col(): lax.ppermute(value, 'col', [(j, (j + d) % n_col) for j in range(n_col)])]
    ppermute x4, starting transfers between devices: 5.73 us -> 7.53 us  [shift_col(): lax.ppermute(value, 'col', [(j, (j + d) % n_col) for j in range(n_col)])]
    ppermute x30 -> x34, waiting for transfers between devices: 31.3 us -> 32.3 us  [shift(): return lax.ppermute(value, 'row', pairs)]
  transfers between devices with their start and end apart: 34 -> 38, of which waited for: 9 -> 10; matrix products, arithmetic and copies ran while one was open for 2% -> 2% of each run, Pallas kernels for 18% -> 14%
where the time goes in v11:
time: 98.1 us; the launch traced here: 97.4 us
  starting transfers between devices  43.5 us (44%)
  waiting for transfers between devices  34.4 us (35%)
  Pallas kernels  13.3 us (14%)
  other arithmetic  3.76 us (4%)
  between operations  2.26 us (2%)
    ppermute x34, starting transfers between devices, shift(): return lax.ppermute(value, 'row', pairs)  36 us
    ppermute x34, waiting for transfers between devices, shift(): return lax.ppermute(value, 'row', pairs)  32.3 us
    pallas_call x4, Pallas kernels, block_product(): pl.pallas_call(functools.partial(product_kernel, contract, inputs, output...  13.3 us
    ppermute x4, starting transfers between devices, shift_col(): lax.ppermute(value, 'col', [(j, (j + d) % n_col) for j in range(n_col)])  7.53 us
    ppermute x4, waiting for transfers between devices, shift_col(): lax.ppermute(value, 'col', [(j, (j + d) % n_col) for j in range(n_col)])  2.08 us
  transfers between devices with their start and end apart: 38, of which 10 were waited for; matrix products, arithmetic and copies ran while one was open for 2% of the time, Pallas kernels for 14%

profile of v11, /device:TPU:0, one launch (start us, length us, event | category | flops | bytes accessed | tf_op | source)
XLA Modules:
  0.0 97.4 jit_solution(12065400344805283857)
XLA Ops:
  1.0 3.0 %collective-permute-start = (bf16[32,2048]{1,0:T(8,128)(2,1)S(1)}, bf16[32,2048]{1,0:T(8,128)(2,1)S(1)}, u32[]{:S(2)}, u32[]{:S(2)}) collective-permute-start(bf16[32,2048]{1,0:T(8,128)(2,1)S(1)} %get-tuple-element.97), channel_id=1, source_target_pairs={{0,4},{2,6},{4,0},{6,2},{8,12},{10,14},{12,8},{14,10},{16,20},{18,... | collective-permute-start | bytes 393224 | tf_op jit(solution)/shard_map/ppermute | solution.py:120
  4.0 1.6 %collective-permute-start.3 = (bf16[32,2048]{1,0:T(8,128)(2,1)S(1)}, bf16[32,2048]{1,0:T(8,128)(2,1)S(1)}, u32[]{:S(2)}, u32[]{:S(2)}) collective-permute-start(bf16[32,2048]{1,0:T(8,128)(2,1)S(1)} %get-tuple-element.97), channel_id=1, source_target_pairs={{0,8},{2,10},{4,12},{6,14},{8,16},{10,18},{12,20},{14,22},{16,24},... | collective-permute-start | bytes 393224 | tf_op jit(solution)/shard_map/ppermute | solution.py:120
  5.6 2.6 %collective-permute-start.4 = (bf16[32,2048]{1,0:T(8,128)(2,1)S(1)}, bf16[32,2048]{1,0:T(8,128)(2,1)S(1)}, u32[]{:S(2)}, u32[]{:S(2)}) collective-permute-start(bf16[32,2048]{1,0:T(8,128)(2,1)S(1)} %get-tuple-element.97), channel_id=1, source_target_pairs={{0,16},{2,18},{4,20},{6,22},{8,24},{10,26},{12,28},{14,30},{16,0},... | collective-permute-start | bytes 393224 | tf_op jit(solution)/shard_map/ppermute | solution.py:120
  12.4 2.1 %collective-permute-done.6 = bf16[32,2048]{1,0:T(8,128)(2,1)S(1)} collective-permute-done((bf16[32,2048]{1,0:T(8,128)(2,1)S(1)}, bf16[32,2048]{1,0:T(8,128)(2,1)S(1)}, u32[]{:S(2)}, u32[]{:S(2)}) %collective-permute-start.6) | collective-permute-done | bytes 131104 | tf_op jit(solution)/shard_map/ppermute | solution.py:123
  14.5 3.4 %mirror.2 = (bf16[8,32,2048]{2,1,0:T(8,128)(2,1)S(1)}, bf16[8,32,2048]{2,1,0:T(8,128)(2,1)S(1)}) custom-call(s32[1]{0:T(128)} %copy.16.count_ref, s32[256]{0:T(256)S(1)} %get-tuple-element.99.take_ref, s32[256]{0:T(256)S(1)} %get-tuple-element.112.put_ref, bf16[1,32,2048]{2,1,0:T(8,128)(2,1)S(1)} %bitcast.99, bf16[1,32,2048]{2,1,0:T(8,128)(2,1)S(1)} %bitcast.102, ...), custom_call_target="tpu_custom_call" | custom-call | flops 128 | bytes 128 | tf_op jit(solution)/shard_map/mirror/pallas_call | solution.py:79
  17.9 1.6 %collective-permute-start.7 = (bf16[32,2048]{1,0:T(8,128)(2,1)S(1)}, bf16[32,2048]{1,0:T(8,128)(2,1)S(1)}, u32[]{:S(2)}, u32[]{:S(2)}) collective-permute-start(bf16[32,2048]{1,0:T(8,128)(2,1)S(1)} %collective-permute-done.4), channel_id=1, source_target_pairs={{0,4},{2,6},{4,0},{6,2},{8,12},{10,14},{12,8},{14,10},{16,20},{18,... | collective-permute-start | bytes 393224 | tf_op jit(solution)/shard_map/ppermute | solution.py:120
  19.5 2.7 %collective-permute-start.1 = (bf16[32,2048]{1,0:T(8,128)(2,1)S(1)}, bf16[32,2048]{1,0:T(8,128)(2,1)S(1)}, u32[]{:S(2)}, u32[]{:S(2)}) collective-permute-start(bf16[32,2048]{1,0:T(8,128)(2,1)S(1)} %collective-permute-done), channel_id=1, source_target_pairs={{0,8},{2,10},{4,12},{6,14},{8,16},{10,18},{12,20},{14,22},{16,24},... | collective-permute-start | bytes 393224 | tf_op jit(solution)/shard_map/ppermute | solution.py:120
  24.6 3.1 %collective-permute-done.1 = bf16[32,2048]{1,0:T(8,128)(2,1)S(1)} collective-permute-done((bf16[32,2048]{1,0:T(8,128)(2,1)S(1)}, bf16[32,2048]{1,0:T(8,128)(2,1)S(1)}, u32[]{:S(2)}, u32[]{:S(2)}) %collective-permute-start.1) | collective-permute-done | bytes 131104 | tf_op jit(solution)/shard_map/ppermute | solution.py:120
  27.6 2.4 %collective-permute-done.2 = bf16[32,2048]{1,0:T(8,128)(2,1)S(1)} collective-permute-done((bf16[32,2048]{1,0:T(8,128)(2,1)S(1)}, bf16[32,2048]{1,0:T(8,128)(2,1)S(1)}, u32[]{:S(2)}, u32[]{:S(2)}) %collective-permute-start.2) | collective-permute-done | bytes 131104 | tf_op jit(solution)/shard_map/ppermute | solution.py:120
  30.0 4.8 %collective-permute-done.9 = bf16[3,32,2048]{2,1,0:T(8,128)(2,1)S(1)} collective-permute-done((bf16[3,32,2048]{2,1,0:T(8,128)(2,1)S(1)}, bf16[3,32,2048]{2,1,0:T(8,128)(2,1)S(1)}, u32[]{:S(2)}, u32[]{:S(2)}) %collective-permute-start.9) | collective-permute-done | bytes 393248 | tf_op jit(solution)/shard_map/ppermute | solution.py:120
  36.0 1.9 %collective-permute-start.11 = (bf16[32,2048]{1,0:T(8,128)(2,1)S(1)}, bf16[32,2048]{1,0:T(8,128)(2,1)S(1)}, u32[]{:S(2)}, u32[]{:S(2)}) collective-permute-start(bf16[32,2048]{1,0:T(8,128)(2,1)S(1)} %get-tuple-element.111), channel_id=1, source_target_pairs={{0,24},{2,26},{4,28},{6,30},{8,0},{10,2},{12,4},{14,6},{16,8},{18,... | collective-permute-start | bytes 393224 | tf_op jit(solution)/shard_map/ppermute | solution.py:120
  39.0 3.3 %forward.2 = (f32[1,32,2048]{2,1,0:T(8,128)S(1)}, bf16[1,32,2048]{2,1,0:T(8,128)(2,1)S(1)}) custom-call(s32[1]{0:T(128)} %copy.16.count_ref, s32[256]{0:T(256)S(1)} %get-tuple-element.113.take_ref, s32[256]{0:T(256)S(1)} %get-tuple-element.98.put_ref, bf16[5,32,2048]{2,1,0:T(8,128)(2,1)S(1)} %bitcast_dynamic-update-slice_fusion.4.refs_0_, ...), custom_call_target="tpu_custom_call" | custom-call | flops 128 | bytes 128 | tf_op jit(solution)/shard_map/forward/pallas_call | solution.py:79
  42.3 3.0 %collective-permute-start.18 = (bf16[32,2048]{1,0:T(8,128)(2,1)S(1)}, bf16[32,2048]{1,0:T(8,128)(2,1)S(1)}, u32[]{:S(2)}, u32[]{:S(2)}) collective-permute-start(bf16[32,2048]{1,0:T(8,128)(2,1)S(1)} %bitcast.115), channel_id=1, source_target_pairs={{0,1},{1,0},{2,3},{3,2},{4,5},{5,4},{6,7},{7,6},{8,9},{9,8},{10,11... | collective-permute-start | bytes 393224 | tf_op jit(solution)/shard_map/ppermute | solution.py:123
  46.6 4.4 %collective-permute-done.12 = bf16[32,2048]{1,0:T(8,128)(2,1)S(1)} collective-permute-done((bf16[32,2048]{1,0:T(8,128)(2,1)S(1)}, bf16[32,2048]{1,0:T(8,128)(2,1)S(1)}, u32[]{:S(2)}, u32[]{:S(2)}) %collective-permute-start.12) | collective-permute-done | bytes 131104 | tf_op jit(solution)/shard_map/ppermute | solution.py:120
  52.4 1.9 %collective-permute-start.23 = (bf16[32,2048]{1,0:T(8,128)(2,1)S(1)}, bf16[32,2048]{1,0:T(8,128)(2,1)S(1)}, u32[]{:S(2)}, u32[]{:S(2)}) collective-permute-start(bf16[32,2048]{1,0:T(8,128)(2,1)S(1)} %get-tuple-element.94), channel_id=1, source_target_pairs={{0,16},{2,18},{4,20},{6,22},{8,24},{10,26},{12,28},{14,30},{16,0},... | collective-permute-start | bytes 393224 | tf_op jit(solution)/shard_map/ppermute | solution.py:120
  54.4 2.9 %collective-permute-start.24 = (bf16[32,2048]{1,0:T(8,128)(2,1)S(1)}, bf16[32,2048]{1,0:T(8,128)(2,1)S(1)}, u32[]{:S(2)}, u32[]{:S(2)}) collective-permute-start(bf16[32,2048]{1,0:T(8,128)(2,1)S(1)} %get-tuple-element.94), channel_id=1, source_target_pairs={{0,24},{2,26},{4,28},{6,30},{8,0},{10,2},{12,4},{14,6},{16,8},{18,... | collective-permute-start | bytes 393224 | tf_op jit(solution)/shard_map/ppermute | solution.py:120
  57.6 3.4 %mirror.3 = (bf16[8,32,2048]{2,1,0:T(8,128)(2,1)S(1)}, bf16[8,32,2048]{2,1,0:T(8,128)(2,1)S(1)}) custom-call(s32[1]{0:T(128)} %copy.16.count_ref, s32[256]{0:T(256)S(1)} %get-tuple-element.99.take_ref, s32[256]{0:T(256)S(1)} %get-tuple-element.112.put_ref, bf16[1,32,2048]{2,1,0:T(8,128)(2,1)S(1)} %bitcast.98, bf16[1,32,2048]{2,1,0:T(8,128)(2,1)S(1)} %bitcast.113, ...), custom_call_target="tpu_custom_call" | custom-call | flops 128 | bytes 128 | tf_op jit(solution)/shard_map/mirror/pallas_call | solution.py:79
  61.4 3.0 %collective-permute-done.23 = bf16[32,2048]{1,0:T(8,128)(2,1)S(1)} collective-permute-done((bf16[32,2048]{1,0:T(8,128)(2,1)S(1)}, bf16[32,2048]{1,0:T(8,128)(2,1)S(1)}, u32[]{:S(2)}, u32[]{:S(2)}) %collective-permute-start.23) | collective-permute-done | bytes 131104 | tf_op jit(solution)/shard_map/ppermute | solution.py:120
  65.4 2.4 %collective-permute-start.20 = (bf16[32,2048]{1,0:T(8,128)(2,1)S(1)}, bf16[32,2048]{1,0:T(8,128)(2,1)S(1)}, u32[]{:S(2)}, u32[]{:S(2)}) collective-permute-start(bf16[32,2048]{1,0:T(8,128)(2,1)S(1)} %collective-permute-done.19), channel_id=1, source_target_pairs={{0,8},{2,10},{4,12},{6,14},{8,16},{10,18},{12,20},{14,22},{16,24},... | collective-permute-start | bytes 393224 | tf_op jit(solution)/shard_map/ppermute | solution.py:120
  74.1 5.0 %collective-permute-done.28 = bf16[3,32,2048]{2,1,0:T(8,128)(2,1)S(1)} collective-permute-done((bf16[3,32,2048]{2,1,0:T(8,128)(2,1)S(1)}, bf16[3,32,2048]{2,1,0:T(8,128)(2,1)S(1)}, u32[]{:S(2)}, u32[]{:S(2)}) %collective-permute-start.28) | collective-permute-done | bytes 393248 | tf_op jit(solution)/shard_map/ppermute | solution.py:120
  81.2 1.6 %collective-permute-start.30 = (bf16[32,2048]{1,0:T(8,128)(2,1)S(1)}, bf16[32,2048]{1,0:T(8,128)(2,1)S(1)}, u32[]{:S(2)}, u32[]{:S(2)}) collective-permute-start(bf16[32,2048]{1,0:T(8,128)(2,1)S(1)} %get-tuple-element.108), channel_id=1, source_target_pairs={{0,24},{2,26},{4,28},{6,30},{8,0},{10,2},{12,4},{14,6},{16,8},{18,... | collective-permute-start | bytes 393224 | tf_op jit(solution)/shard_map/ppermute | solution.py:120
  84.5 3.2 %forward.3 = (f32[1,32,2048]{2,1,0:T(8,128)S(1)}, bf16[1,32,2048]{2,1,0:T(8,128)(2,1)S(1)}) custom-call(s32[1]{0:T(128)} %copy.16.count_ref, s32[256]{0:T(256)S(1)} %get-tuple-element.113.take_ref, s32[256]{0:T(256)S(1)} %get-tuple-element.98.put_ref, bf16[5,32,2048]{2,1,0:T(8,128)(2,1)S(1)} %bitcast_dynamic-update-slice_fusion.refs_0_, ...), custom_call_target="tpu_custom_call" | custom-call | flops 128 | bytes 128 | tf_op jit(solution)/shard_map/forward/pallas_call | solution.py:79
  87.8 2.0 %collective-permute-start.37 = (bf16[32,2048]{1,0:T(8,128)(2,1)S(1)}, bf16[32,2048]{1,0:T(8,128)(2,1)S(1)}, u32[]{:S(2)}, u32[]{:S(2)}) collective-permute-start(bf16[32,2048]{1,0:T(8,128)(2,1)S(1)} %bitcast.114), channel_id=1, source_target_pairs={{0,1},{1,0},{2,3},{3,2},{4,5},{5,4},{6,7},{7,6},{8,9},{9,8},{10,11... | collective-permute-start | bytes 393224 | tf_op jit(solution)/shard_map/ppermute | solution.py:123
  89.8 6.7 %collective-permute-done.31 = bf16[32,2048]{1,0:T(8,128)(2,1)S(1)} collective-permute-done((bf16[32,2048]{1,0:T(8,128)(2,1)S(1)}, bf16[32,2048]{1,0:T(8,128)(2,1)S(1)}, u32[]{:S(2)}, u32[]{:S(2)}) %collective-permute-start.31) | collective-permute-done | bytes 131104 | tf_op jit(solution)/shard_map/ppermute | solution.py:120
  (80 shorter events, 23.1 us)
Async XLA Ops:
  1.0 18.5 %collective-permute-start = (bf16[32,2048]{1,0:T(8,128)(2,1)S(1)}, bf16[32,2048]{1,0:T(8,128)(2,1)S(1)}, u32[]{:S(2)}, u32[]{:S(2)}) collective-permute-start(bf16[32,2048]{1,0:T(8,128)(2,1)S(1)} %get-tuple-element.97), channel_id=1, source_target_pairs={{0,4},{2,6},{4,0},{6,2},{8,12},{10,14},{12,8},{14,10},{16,20},{18,... | collective-permute-start | bytes 393224 | tf_op jit(solution)/shard_map/ppermute | solution.py:120
  4.0 13.9 %collective-permute-start.3 = (bf16[32,2048]{1,0:T(8,128)(2,1)S(1)}, bf16[32,2048]{1,0:T(8,128)(2,1)S(1)}, u32[]{:S(2)}, u32[]{:S(2)}) collective-permute-start(bf16[32,2048]{1,0:T(8,128)(2,1)S(1)} %get-tuple-element.97), channel_id=1, source_target_pairs={{0,8},{2,10},{4,12},{6,14},{8,16},{10,18},{12,20},{14,22},{16,24},... | collective-permute-start | bytes 393224 | tf_op jit(solution)/shard_map/ppermute | solution.py:120
  5.6 12.3 %collective-permute-start.4 = (bf16[32,2048]{1,0:T(8,128)(2,1)S(1)}, bf16[32,2048]{1,0:T(8,128)(2,1)S(1)}, u32[]{:S(2)}, u32[]{:S(2)}) collective-permute-start(bf16[32,2048]{1,0:T(8,128)(2,1)S(1)} %get-tuple-element.97), channel_id=1, source_target_pairs={{0,16},{2,18},{4,20},{6,22},{8,24},{10,26},{12,28},{14,30},{16,0},... | collective-permute-start | bytes 393224 | tf_op jit(solution)/shard_map/ppermute | solution.py:120
  8.2 9.7 %collective-permute-start.5 = (bf16[32,2048]{1,0:T(8,128)(2,1)S(1)}, bf16[32,2048]{1,0:T(8,128)(2,1)S(1)}, u32[]{:S(2)}, u32[]{:S(2)}) collective-permute-start(bf16[32,2048]{1,0:T(8,128)(2,1)S(1)} %get-tuple-element.97), channel_id=1, source_target_pairs={{0,24},{2,26},{4,28},{6,30},{8,0},{10,2},{12,4},{14,6},{16,8},{18,... | collective-permute-start | bytes 393224 | tf_op jit(solution)/shard_map/ppermute | solution.py:120
  17.9 12.1 %collective-permute-start.7 = (bf16[32,2048]{1,0:T(8,128)(2,1)S(1)}, bf16[32,2048]{1,0:T(8,128)(2,1)S(1)}, u32[]{:S(2)}, u32[]{:S(2)}) collective-permute-start(bf16[32,2048]{1,0:T(8,128)(2,1)S(1)} %collective-permute-done.4), channel_id=1, source_target_pairs={{0,4},{2,6},{4,0},{6,2},{8,12},{10,14},{12,8},{14,10},{16,20},{18,... | collective-permute-start | bytes 393224 | tf_op jit(solution)/shard_map/ppermute | solution.py:120
  23.8 11.0 %collective-permute-start.9 = (bf16[3,32,2048]{2,1,0:T(8,128)(2,1)S(1)}, bf16[3,32,2048]{2,1,0:T(8,128)(2,1)S(1)}, u32[]{:S(2)}, u32[]{:S(2)}) collective-permute-start(bf16[3,32,2048]{2,1,0:T(8,128)(2,1)S(1)} %slice.66), channel_id=1, source_target_pairs={{0,4},{2,6},{4,0},{6,2},{8,12},{10,14},{12,8},{14,10},{16,20},{18,... | collective-permute-start | bytes 1179656 | tf_op jit(solution)/shard_map/ppermute | solution.py:120
  24.5 11.6 %collective-permute-start.14 = (bf16[5,32,2048]{2,1,0:T(8,128)(2,1)S(1)}, bf16[5,32,2048]{2,1,0:T(8,128)(2,1)S(1)}, u32[]{:S(2)}, u32[]{:S(2)}) collective-permute-start(bf16[5,32,2048]{2,1,0:T(8,128)(2,1)S(1)} %bitcast_dynamic-update-slice_fusion.4.refs_0_), channel_id=1, source_target_pairs={{0,2},{2,0},{4,6},{6,4},{8,10},{10,8},{12,14},{14,12},{16,18},{18,... | collective-permute-start | bytes 1966088 | tf_op jit(solution)/shard_map/ppermute | solution.py:120
  35.4 11.2 %collective-permute-start.10 = (bf16[1,32,2048]{2,1,0:T(8,128)(2,1)S(1)}, bf16[1,32,2048]{2,1,0:T(8,128)(2,1)S(1)}, u32[]{:S(2)}, u32[]{:S(2)}) collective-permute-start(bf16[1,32,2048]{2,1,0:T(8,128)(2,1)S(1)} %slice.67), channel_id=1, source_target_pairs={{0,4},{2,6},{4,0},{6,2},{8,12},{10,14},{12,8},{14,10},{16,20},{18,... | collective-permute-start | bytes 393224 | tf_op jit(solution)/shard_map/ppermute | solution.py:120
  36.0 10.6 %collective-permute-start.11 = (bf16[32,2048]{1,0:T(8,128)(2,1)S(1)}, bf16[32,2048]{1,0:T(8,128)(2,1)S(1)}, u32[]{:S(2)}, u32[]{:S(2)}) collective-permute-start(bf16[32,2048]{1,0:T(8,128)(2,1)S(1)} %get-tuple-element.111), channel_id=1, source_target_pairs={{0,24},{2,26},{4,28},{6,30},{8,0},{10,2},{12,4},{14,6},{16,8},{18,... | collective-permute-start | bytes 393224 | tf_op jit(solution)/shard_map/ppermute | solution.py:120
  38.0 13.0 %collective-permute-start.12 = (bf16[32,2048]{1,0:T(8,128)(2,1)S(1)}, bf16[32,2048]{1,0:T(8,128)(2,1)S(1)}, u32[]{:S(2)}, u32[]{:S(2)}) collective-permute-start(bf16[32,2048]{1,0:T(8,128)(2,1)S(1)} %get-tuple-element.110), channel_id=1, source_target_pairs={{0,16},{2,18},{4,20},{6,22},{8,24},{10,26},{12,28},{14,30},{16,0},... | collective-permute-start | bytes 393224 | tf_op jit(solution)/shard_map/ppermute | solution.py:120
  39.0 12.0 %collective-permute-start.13 = (bf16[32,2048]{1,0:T(8,128)(2,1)S(1)}, bf16[32,2048]{1,0:T(8,128)(2,1)S(1)}, u32[]{:S(2)}, u32[]{:S(2)}) collective-permute-start(bf16[32,2048]{1,0:T(8,128)(2,1)S(1)} %get-tuple-element.109), channel_id=1, source_target_pairs={{0,8},{2,10},{4,12},{6,14},{8,16},{10,18},{12,20},{14,22},{16,24},... | collective-permute-start | bytes 393224 | tf_op jit(solution)/shard_map/ppermute | solution.py:120
  42.3 8.7 %collective-permute-start.18 = (bf16[32,2048]{1,0:T(8,128)(2,1)S(1)}, bf16[32,2048]{1,0:T(8,128)(2,1)S(1)}, u32[]{:S(2)}, u32[]{:S(2)}) collective-permute-start(bf16[32,2048]{1,0:T(8,128)(2,1)S(1)} %bitcast.115), channel_id=1, source_target_pairs={{0,1},{1,0},{2,3},{3,2},{4,5},{5,4},{6,7},{7,6},{8,9},{9,8},{10,11... | collective-permute-start | bytes 393224 | tf_op jit(solution)/shard_map/ppermute | solution.py:123
  52.1 9.2 %collective-permute-start.22 = (bf16[32,2048]{1,0:T(8,128)(2,1)S(1)}, bf16[32,2048]{1,0:T(8,128)(2,1)S(1)}, u32[]{:S(2)}, u32[]{:S(2)}) collective-permute-start(bf16[32,2048]{1,0:T(8,128)(2,1)S(1)} %get-tuple-element.94), channel_id=1, source_target_pairs={{0,8},{2,10},{4,12},{6,14},{8,16},{10,18},{12,20},{14,22},{16,24},... | collective-permute-start | bytes 393224 | tf_op jit(solution)/shard_map/ppermute | solution.py:120
  52.4 11.9 %collective-permute-start.23 = (bf16[32,2048]{1,0:T(8,128)(2,1)S(1)}, bf16[32,2048]{1,0:T(8,128)(2,1)S(1)}, u32[]{:S(2)}, u32[]{:S(2)}) collective-permute-start(bf16[32,2048]{1,0:T(8,128)(2,1)S(1)} %get-tuple-element.94), channel_id=1, source_target_pairs={{0,16},{2,18},{4,20},{6,22},{8,24},{10,26},{12,28},{14,30},{16,0},... | collective-permute-start | bytes 393224 | tf_op jit(solution)/shard_map/ppermute | solution.py:120
  54.4 10.0 %collective-permute-start.24 = (bf16[32,2048]{1,0:T(8,128)(2,1)S(1)}, bf16[32,2048]{1,0:T(8,128)(2,1)S(1)}, u32[]{:S(2)}, u32[]{:S(2)}) collective-permute-start(bf16[32,2048]{1,0:T(8,128)(2,1)S(1)} %get-tuple-element.94), channel_id=1, source_target_pairs={{0,24},{2,26},{4,28},{6,30},{8,0},{10,2},{12,4},{14,6},{16,8},{18,... | collective-permute-start | bytes 393224 | tf_op jit(solution)/shard_map/ppermute | solution.py:120
  61.0 8.3 %collective-permute-start.27 = (bf16[8,32,2048]{2,1,0:T(8,128)(2,1)S(1)}, bf16[8,32,2048]{2,1,0:T(8,128)(2,1)S(1)}, u32[]{:S(2)}, u32[]{:S(2)}) collective-permute-start(bf16[8,32,2048]{2,1,0:T(8,128)(2,1)S(1)} %get-tuple-element.74), channel_id=1, source_target_pairs={{0,2},{2,0},{4,6},{6,4},{8,10},{10,8},{12,14},{14,12},{16,18},{18,... | collective-permute-start | bytes 3145736 | tf_op jit(solution)/shard_map/ppermute | solution.py:120
  64.4 9.8 %collective-permute-start.26 = (bf16[32,2048]{1,0:T(8,128)(2,1)S(1)}, bf16[32,2048]{1,0:T(8,128)(2,1)S(1)}, u32[]{:S(2)}, u32[]{:S(2)}) collective-permute-start(bf16[32,2048]{1,0:T(8,128)(2,1)S(1)} %collective-permute-done.23), channel_id=1, source_target_pairs={{0,4},{2,6},{4,0},{6,2},{8,12},{10,14},{12,8},{14,10},{16,20},{18,... | collective-permute-start | bytes 393224 | tf_op jit(solution)/shard_map/ppermute | solution.py:120
  69.8 9.3 %collective-permute-start.28 = (bf16[3,32,2048]{2,1,0:T(8,128)(2,1)S(1)}, bf16[3,32,2048]{2,1,0:T(8,128)(2,1)S(1)}, u32[]{:S(2)}, u32[]{:S(2)}) collective-permute-start(bf16[3,32,2048]{2,1,0:T(8,128)(2,1)S(1)} %slice.73), channel_id=1, source_target_pairs={{0,4},{2,6},{4,0},{6,2},{8,12},{10,14},{12,8},{14,10},{16,20},{18,... | collective-permute-start | bytes 1179656 | tf_op jit(solution)/shard_map/ppermute | solution.py:120
  71.2 9.9 %collective-permute-start.33 = (bf16[5,32,2048]{2,1,0:T(8,128)(2,1)S(1)}, bf16[5,32,2048]{2,1,0:T(8,128)(2,1)S(1)}, u32[]{:S(2)}, u32[]{:S(2)}) collective-permute-start(bf16[5,32,2048]{2,1,0:T(8,128)(2,1)S(1)} %bitcast_dynamic-update-slice_fusion.refs_0_), channel_id=1, source_target_pairs={{0,2},{2,0},{4,6},{6,4},{8,10},{10,8},{12,14},{14,12},{16,18},{18,... | collective-permute-start | bytes 1966088 | tf_op jit(solution)/shard_map/ppermute | solution.py:120
  79.1 10.7 %collective-permute-start.29 = (bf16[1,32,2048]{2,1,0:T(8,128)(2,1)S(1)}, bf16[1,32,2048]{2,1,0:T(8,128)(2,1)S(1)}, u32[]{:S(2)}, u32[]{:S(2)}) collective-permute-start(bf16[1,32,2048]{2,1,0:T(8,128)(2,1)S(1)} %slice.74), channel_id=1, source_target_pairs={{0,4},{2,6},{4,0},{6,2},{8,12},{10,14},{12,8},{14,10},{16,20},{18,... | collective-permute-start | bytes 393224 | tf_op jit(solution)/shard_map/ppermute | solution.py:120
  81.2 8.7 %collective-permute-start.30 = (bf16[32,2048]{1,0:T(8,128)(2,1)S(1)}, bf16[32,2048]{1,0:T(8,128)(2,1)S(1)}, u32[]{:S(2)}, u32[]{:S(2)}) collective-permute-start(bf16[32,2048]{1,0:T(8,128)(2,1)S(1)} %get-tuple-element.108), channel_id=1, source_target_pairs={{0,24},{2,26},{4,28},{6,30},{8,0},{10,2},{12,4},{14,6},{16,8},{18,... | collective-permute-start | bytes 393224 | tf_op jit(solution)/shard_map/ppermute | solution.py:120
  82.8 13.8 %collective-permute-start.31 = (bf16[32,2048]{1,0:T(8,128)(2,1)S(1)}, bf16[32,2048]{1,0:T(8,128)(2,1)S(1)}, u32[]{:S(2)}, u32[]{:S(2)}) collective-permute-start(bf16[32,2048]{1,0:T(8,128)(2,1)S(1)} %get-tuple-element.107), channel_id=1, source_target_pairs={{0,16},{2,18},{4,20},{6,22},{8,24},{10,26},{12,28},{14,30},{16,0},... | collective-permute-start | bytes 393224 | tf_op jit(solution)/shard_map/ppermute | solution.py:120
  84.2 12.3 %collective-permute-start.32 = (bf16[32,2048]{1,0:T(8,128)(2,1)S(1)}, bf16[32,2048]{1,0:T(8,128)(2,1)S(1)}, u32[]{:S(2)}, u32[]{:S(2)}) collective-permute-start(bf16[32,2048]{1,0:T(8,128)(2,1)S(1)} %get-tuple-element.106), channel_id=1, source_target_pairs={{0,8},{2,10},{4,12},{6,14},{8,16},{10,18},{12,20},{14,22},{16,24},... | collective-permute-start | bytes 393224 | tf_op jit(solution)/shard_map/ppermute | solution.py:120
  87.8 8.8 %collective-permute-start.37 = (bf16[32,2048]{1,0:T(8,128)(2,1)S(1)}, bf16[32,2048]{1,0:T(8,128)(2,1)S(1)}, u32[]{:S(2)}, u32[]{:S(2)}) collective-permute-start(bf16[32,2048]{1,0:T(8,128)(2,1)S(1)} %bitcast.114), channel_id=1, source_target_pairs={{0,1},{1,0},{2,3},{3,2},{4,5},{5,4},{6,7},{7,6},{8,9},{9,8},{10,11... | collective-permute-start | bytes 393224 | tf_op jit(solution)/shard_map/ppermute | solution.py:123
  (15 other events, 85.4 us)
